TPU v7x, 32 devices: a whole 2x2x4 slice. The times are simulated.
32 devices in a mesh: row: 4 (over x, core), col: 8 (over z, y).
Axes of the slice: x: 2, y: 2, z: 4, core: 2. Of those that a mesh axis runs over, the one named last changes fastest.
Arguments:
- observed: bfloat16 [512, 8, 128, 128], P(('row', 'col')), may hold values from -6 to 6
- sku_ids: int32 [512], P(('row', 'col')), may hold values from 0 to 15
- store_ids: int32 [512, 8], P(('row', 'col')), may hold values from 0 to 39
- live_slot_counts: int32 [4, 8, 4], P('row', 'col'), may hold values from 0 to 4, as said below
- sku_factors: float32 [65536, 256], P(('row', 'col')), may hold values from -1.5 to 1.5
- store_factors: float32 [20480, 256], P(('row', 'col')), may hold values from -1.5 to 1.5
Outputs:
- new_sku_factors: float32 [65536, 256], P(('row', 'col'))
- new_store_factors: float32 [20480, 256], P(('row', 'col'))
Inputs may be any that keep to these rules, and one draw needn't show every extreme that they name: `live_slot_counts`: in every column index some owner row's slots are full from every device of that column.
All inputs are finite; a program needn't handle non-finite values.
Results may differ from a plain program's by a relative error of at most 0.023.
Values may be sent and summed in bfloat16 or wider, within the bound.
No kernel may reach another device: no remote copies, remote signals or barrier semaphores. Data moves between devices by JAX's collectives and lax.ppermute only.
A program may use at most 192 MiB of HBM per device.

v0:
```python
import jax
import jax.numpy as jnp
from jax import lax
from jax.sharding import PartitionSpec as P

learn_rate = 0.01
weight_decay = 0.05
group_rows = 8


def one_hot_of(ids, count):
    return (
        ids[..., None] == lax.broadcasted_iota(jnp.int32, ids.shape + (count,), ids.ndim)
    ).astype(jnp.bfloat16)


def pick_blocks(table, ids):
    selector = one_hot_of(ids.reshape(-1), table.shape[0])
    flat_table = table.reshape(table.shape[0], -1)
    picked = jnp.dot(selector, flat_table, preferred_element_type=jnp.float32).astype(jnp.bfloat16)
    return picked.reshape(ids.shape + table.shape[1:])


def sum_into_blocks(selector, values):
    flat_values = values.reshape(values.shape[0], -1)
    high_part = flat_values.astype(jnp.bfloat16)
    low_part = (flat_values - high_part.astype(jnp.float32)).astype(jnp.bfloat16)
    upper = jnp.einsum("nv,nx->vx", selector, high_part, preferred_element_type=jnp.float32)
    lower = jnp.einsum("nv,nx->vx", selector, low_part, preferred_element_type=jnp.float32)
    return upper + lower


def local(observed, sku_ids, store_ids, live_slot_counts, sku_factors, store_factors):
    rows_per_owner = lax.axis_size("row")
    total_live_slots = observed.shape[0]
    owner_wise = total_live_slots // rows_per_owner
    block_len = observed.shape[2]
    rank_len = sku_factors.shape[1]
    slot_alive_mask = lax.broadcasted_iota(
        jnp.int32, (rows_per_owner, owner_wise), 1
    ) < live_slot_counts.reshape(rows_per_owner, 1)
    slot_alive_mask = slot_alive_mask.reshape(total_live_slots).astype(jnp.float32)
    own_sku = sku_factors.reshape(-1, block_len, rank_len)
    own_table = own_sku.astype(jnp.bfloat16)
    own_store = store_factors.reshape(-1, block_len, rank_len)
    requested_ids = sku_ids.reshape(rows_per_owner, owner_wise)
    all_tables = lax.all_gather(own_table, "row", axis=0, tiled=True)
    owner_row = jnp.arange(total_live_slots, dtype=jnp.int32) // owner_wise
    fetched = pick_blocks(all_tables, owner_row * own_table.shape[0] + sku_ids)
    group_low = lax.all_gather(own_store.astype(jnp.bfloat16), "col", axis=0, tiled=True)
    group_count = group_low.shape[0]
    count_groups = total_live_slots // group_rows

    def split_into_groups(array_in):
        return array_in.reshape((count_groups, group_rows) + array_in.shape[1:])

    input_arrays = (
        split_into_groups(fetched),
        split_into_groups(observed),
        split_into_groups(store_ids),
        split_into_groups(slot_alive_mask),
    )

    def misfit_of(factor_rows, measured, store_pick, store_table):
        selected = pick_blocks(store_table, store_pick)
        predicted = jnp.einsum(
            "sar,skbr->skab", factor_rows, selected, preferred_element_type=jnp.float32
        )
        misfit = (predicted - measured.astype(jnp.float32)).astype(jnp.bfloat16)
        return (misfit, selected)

    def first_pass(running, inputs_now):
        factor_rows, measured, store_pick, alive = inputs_now
        misfit, selected = misfit_of(factor_rows, measured, store_pick, group_low)
        partial_value = jnp.einsum(
            "skab,sar->skbr", misfit, factor_rows, preferred_element_type=jnp.float32
        )
        selector = one_hot_of(store_pick, group_count) * alive[:, None, None].astype(jnp.bfloat16)
        selector = selector.reshape(-1, group_count)
        added = sum_into_blocks(selector, partial_value.reshape(-1, block_len, rank_len))
        return (running + added.reshape(running.shape), None)

    store_grad, _ = lax.scan(first_pass, jnp.zeros(group_low.shape, jnp.float32), input_arrays)
    own_grad = lax.psum_scatter(
        store_grad.astype(jnp.bfloat16), "col", scatter_dimension=0, tiled=True
    ).astype(jnp.float32)
    new_store = own_store - learn_rate * (own_grad + weight_decay * own_store)
    new_low = lax.all_gather(new_store.astype(jnp.bfloat16), "col", axis=0, tiled=True)

    def second_pass(running, inputs_now):
        factor_rows, measured, store_pick, alive = inputs_now
        misfit, selected = misfit_of(factor_rows, measured, store_pick, new_low)
        partial_value = jnp.einsum(
            "skab,skbr->sar", misfit, selected, preferred_element_type=jnp.float32
        )
        return (running, partial_value * alive[:, None, None])

    _, sku_terms = lax.scan(second_pass, jnp.zeros((), jnp.float32), input_arrays)
    sku_terms = sku_terms.reshape(rows_per_owner, owner_wise, block_len, rank_len)
    arrived, requested = (
        lax.all_to_all(
            sku_terms.astype(jnp.bfloat16), "row", split_axis=0, concat_axis=0, tiled=True
        ).astype(sku_terms.dtype),
        lax.all_to_all(requested_ids, "row", split_axis=0, concat_axis=0, tiled=True),
    )
    owner_selector = one_hot_of(requested.reshape(-1), own_sku.shape[0])
    sku_grad = sum_into_blocks(owner_selector, arrived.reshape(-1, block_len, rank_len)).reshape(
        own_sku.shape
    )
    new_sku = own_sku - learn_rate * (sku_grad + weight_decay * own_sku)
    return (new_sku.reshape(sku_factors.shape), new_store.reshape(store_factors.shape))


def solution(mesh):
    placed = (
        P(("row", "col"), None, None, None),
        P(("row", "col")),
        P(("row", "col"), None),
        P("row", "col", None),
        P(("row", "col"), None),
        P(("row", "col"), None),
    )
    return jax.shard_map(
        local,
        mesh=mesh,
        in_specs=placed,
        out_specs=(P(("row", "col"), None), P(("row", "col"), None)),
        check_vma=False,
    )
```

profile of v0, /device:TPU:0, one launch (start us, length us, event | category | flops | bytes accessed | tf_op | source)
XLA Modules:
  0.0 369.9 jit_solution(10197465241156663328)
XLA Ops:
  7.2 2.7 convert_element_type.96
  10.0 0.0 all-gather.4.cloned.1.call-start
  10.0 0.8 convert_element_type.95
  10.8 0.0 reduce-scatter.2.cloned.1.call-start
  10.9 0.6 broadcast.121
  11.5 0.7 reduce.6
  12.2 0.1 lt.20
  12.3 0.1 lt.21
  12.3 0.1 lt.22
  12.4 0.1 iota.41
  12.5 0.1 copy.28
  12.6 6.3 %copy.17 = bf16[16,8,128,128]{2,3,1,0:T(8,128)(2,1)} copy(bf16[16,8,128,128]{3,2,1,0:T(8,128)(2,1)} %param.10) | data formatting | bytes 8388608 | tf_op args[0]
  19.0 28.4 %all-gather.6.cloned.1.call-done = bf16[64,128,256]{2,1,0:T(8,128)(2,1)} async-done(((bf16[16,128,256]{2,1,0:T(8,128)(2,1)}), bf16[64,128,256]{2,1,0:T(8,128)(2,1)}) %all-gather.6.cloned.1.call-update) | async-done | bytes 4194320 | tf_op jit(solution)/shard_map/all_gather | solution.py:47
  47.4 4.7 %copy.34 = bf16[8,8,128,256]{3,1,2,0:T(8,128)(2,1)S(1)} copy(bf16[8,8,128,256]{3,2,1,0:T(8,128)(2,1)} %bitcast.189) | data formatting | bytes 8388608
  52.1 0.7 convolution_convert_fusion.2
  52.8 0.2 copy.19
  53.1 51.7 %all-gather.4.cloned.1.call-done = bf16[40,128,256]{2,1,0:T(8,128)(2,1)} async-done(((bf16[5,128,256]{2,1,0:T(8,128)(2,1)}), bf16[40,128,256]{2,1,0:T(8,128)(2,1)}) %all-gather.4.cloned.1.call-update) | async-done | bytes 2621456 | tf_op jit(solution)/shard_map/all_gather | solution.py:50
  104.8 72.9 %while.22 = (s32[]{:T(128)}, f32[40,128,256]{2,1,0:T(8,128)}, s32[2,8,8]{2,1,0:T(8,128)S(1)}, bf16[2,8]{1,0:T(2,128)(2,1)S(1)}, bf16[40,128,256]{2,1,0:T(8,128)(...) while((s32[]{:T(128)}, f32[40,128,256]{2,1,0:T(8,128)}, ...), condition=%wide.region_1.2_spmd.clone, body=%wide.region_0.1_spmd.clone.sunk | while | flops 1594634752 | bytes 111677384 | solution.py:83
  104.8 0.1 eq.134
  104.9 3.3 copy.80
  108.2 3.2 convolution_convert_fusion.6
  111.4 8.6 %fusion.141 = (bf16[8,8,128,256]{3,2,1,0:T(8,128)(2,1)}, bf16[8,8,128,256]{3,2,1,0:T(8,128)(2,1)}) fusion(bf16[2,8,128,256]{3,2,1,0:T(8,128)(2,1)S(1)} %get-tuple-element.277, s32[]{:T(128)} %get-tuple-element.263, bf16[8,8,128,256]{3,1,2,0:T(8,128)(2,1)} %bitcast.175, bf16[2,8,8,128,128]{3,4,2,1,0:T(8,128)(2,1)} %get-tuple-element.278), kind=kOutput, calls=%fused_computation.25.clone.1 | convolution fusion | flops 1085276160 | bytes 15730176 | tf_op jit(solution)/shard_map/while/body/eval_jaxpr/skab,sar->skbr/dot_general | solution.py:75
  120.1 4.7 %copy.81 = bf16[8,8,128,256]{3,1,2,0:T(8,128)(2,1)S(1)} copy(bf16[8,8,128,256]{3,2,1,0:T(8,128)(2,1)} %get-tuple-element.252) | data formatting | bytes 8388608 | tf_op jit(solution)/shard_map/while
  124.9 1.0 fusion.144
  125.8 1.2 copy-done
  127.0 2.6 copy.82
  129.6 1.0 convolution_add_fusion.3
  130.6 3.9 %copy.83 = f32[5,8,128,256]{3,2,1,0:T(8,128)} copy(f32[5,8,128,256]{3,1,2,0:T(8,128)S(1)} %bitcast.174) | data formatting | bytes 10485760 | tf_op jit(solution)/shard_map/while
  134.5 6.0 %bitcast_add_fusion.2 = f32[40,128,256]{2,1,0:T(8,128)} fusion(f32[5,8,128,256]{3,2,1,0:T(8,128)} %copy.83, f32[40,128,256]{2,1,0:T(8,128)} %get-tuple-element.264, pred[]{:T(512)S(6)} %compare.5), kind=kLoop, calls=%fused_computation.24.clone.1 | loop fusion | flops 2621440 | bytes 15728641 | tf_op jit(solution)/shard_map/while/body/eval_jaxpr/add | solution.py:81
  140.5 0.1 eq.134
  140.6 3.3 copy.80
  143.9 3.2 convolution_convert_fusion.6
  147.1 8.6 %fusion.141 = (bf16[8,8,128,256]{3,2,1,0:T(8,128)(2,1)}, bf16[8,8,128,256]{3,2,1,0:T(8,128)(2,1)}) fusion(bf16[2,8,128,256]{3,2,1,0:T(8,128)(2,1)S(1)} %get-tuple-element.277, s32[]{:T(128)} %get-tuple-element.263, bf16[8,8,128,256]{3,1,2,0:T(8,128)(2,1)} %bitcast.175, bf16[2,8,8,128,128]{3,4,2,1,0:T(8,128)(2,1)} %get-tuple-element.278), kind=kOutput, calls=%fused_computation.25.clone.1 | convolution fusion | flops 1085276160 | bytes 15730176 | tf_op jit(solution)/shard_map/while/body/eval_jaxpr/skab,sar->skbr/dot_general | solution.py:75
  155.7 4.7 %copy.81 = bf16[8,8,128,256]{3,1,2,0:T(8,128)(2,1)S(1)} copy(bf16[8,8,128,256]{3,2,1,0:T(8,128)(2,1)} %get-tuple-element.252) | data formatting | bytes 8388608 | tf_op jit(solution)/shard_map/while
  160.5 1.0 fusion.144
  161.5 1.2 copy-done
  162.7 2.6 copy.82
  165.3 1.0 convolution_add_fusion.3
  166.3 3.9 %copy.83 = f32[5,8,128,256]{3,2,1,0:T(8,128)} copy(f32[5,8,128,256]{3,1,2,0:T(8,128)S(1)} %bitcast.174) | data formatting | bytes 10485760 | tf_op jit(solution)/shard_map/while
  170.2 7.6 %bitcast_add_fusion.2 = f32[40,128,256]{2,1,0:T(8,128)} fusion(f32[5,8,128,256]{3,2,1,0:T(8,128)} %copy.83, f32[40,128,256]{2,1,0:T(8,128)} %get-tuple-element.264, pred[]{:T(512)S(6)} %compare.5), kind=kLoop, calls=%fused_computation.24.clone.1 | loop fusion | flops 2621440 | bytes 15728641 | tf_op jit(solution)/shard_map/while/body/eval_jaxpr/add | solution.py:81
  177.8 4.3 %convert_element_type.99 = bf16[40,128,256]{2,1,0:T(8,128)(2,1)} convert(f32[40,128,256]{2,1,0:T(8,128)} %get-tuple-element.76) | non-fusion elementwise | flops 1310720 | bytes 7864320 | tf_op jit(solution)/shard_map/convert_element_type | solution.py:85
  182.1 69.2 %reduce-scatter.2.cloned.1.call-done = bf16[5,128,256]{2,1,0:T(8,128)(2,1)} async-done(((bf16[40,128,256]{2,1,0:T(8,128)(2,1)}), bf16[5,128,256]{2,1,0:T(8,128)(2,1)}) %reduce-scatter.2.cloned.1.call-update) | async-done | bytes 327696 | tf_op jit(solution)/shard_map/reduce_scatter | solution.py:84
  251.3 2.0 fusion.88
  253.4 0.7 all_to_all.9
  254.1 3.2 all-to-all-start
  257.3 49.9 %all-gather.8.cloned.1.call-done = bf16[40,128,256]{2,1,0:T(8,128)(2,1)} async-done(((bf16[5,128,256]{2,1,0:T(8,128)(2,1)}), bf16[40,128,256]{2,1,0:T(8,128)(2,1)}) %all-gather.8.cloned.1.call-update) | async-done | bytes 2621456 | tf_op jit(solution)/shard_map/all_gather | solution.py:88
  307.1 29.3 %while.21 = (s32[]{:T(128)}, bf16[2,8,128,256]{3,2,1,0:T(8,128)(2,1)}, s32[2,8,8]{2,1,0:T(8,128)S(1)}, bf16[40,128,256]{2,1,0:T(8,128)(2,1)}, bf16[2,8,128,256]{...) while((s32[]{:T(128)}, ...), condition=%wide.region_4.5_spmd, body=%wide.region_3.4_spmd.sunk | while | flops 1247021568 | bytes 24120732 | solution.py:98
  307.2 0.1 eq.127
  307.2 3.3 copy.78
  310.5 3.4 convolution_convert_fusion.5
  313.9 7.9 %fusion.131 = bf16[2,8,128,256]{3,2,1,0:T(8,128)(2,1)} fusion(bf16[2,8,128,256]{3,2,1,0:T(8,128)(2,1)} %get-tuple-element.290, s32[]{:T(128)} %get-tuple-element.289, bf16[8,8,128,256]{3,1,2,0:T(8,128)(2,1)} %bitcast.180, bf16[2,8,8,128,128]{4,3,2,1,0:T(8,128)(2,1)} %get-tuple-element.302, f32[8]{0:T(128)S(1)} %fusion.130, ...), kind=kOutput, calls=%fused_computation.12.clone.1 | convolution fusion | flops 1077149696 | bytes 12060672 | tf_op jit(solution)/shard_map/while/body/eval_jaxpr/skab,skbr->sar/dot_general | solution.py:93
  321.8 0.1 eq.127
  321.9 3.3 copy.78
  325.2 3.4 convolution_convert_fusion.5
  328.5 7.9 %fusion.131 = bf16[2,8,128,256]{3,2,1,0:T(8,128)(2,1)} fusion(bf16[2,8,128,256]{3,2,1,0:T(8,128)(2,1)} %get-tuple-element.290, s32[]{:T(128)} %get-tuple-element.289, bf16[8,8,128,256]{3,1,2,0:T(8,128)(2,1)} %bitcast.180, bf16[2,8,8,128,128]{4,3,2,1,0:T(8,128)(2,1)} %get-tuple-element.302, f32[8]{0:T(128)S(1)} %fusion.130, ...), kind=kOutput, calls=%fused_computation.12.clone.1 | convolution fusion | flops 1077149696 | bytes 12060672 | tf_op jit(solution)/shard_map/while/body/eval_jaxpr/skab,skbr->sar/dot_general | solution.py:93
  336.5 3.5 all-to-all-start.1
  340.0 0.7 reduce.7
  340.7 0.1 eq.60
  340.8 13.6 %all-to-all-done.1 = bf16[4,4,128,256]{3,2,1,0:T(8,128)(2,1)S(1)} async-done(((bf16[4,4,128,256]{3,2,1,0:T(8,128)(2,1)}), bf16[4,4,128,256]{3,2,1,0:T(8,128)(2,1)S(1)}, u32[]{:S(2)}, u32[]{:S(2)}) %all-to-all-start.1) | async-done | bytes 1048608 | tf_op jit(solution)/shard_map/all_to_all | solution.py:101
  354.4 0.6 copy.35
  355.0 0.5 fusion.82
  355.6 1.9 convolution_add_fusion.1
  357.4 2.7 reshape.197
  360.2 3.2 multiply_subtract_fusion
  (34 shorter events, 0.3 us)
Async XLA Ops:
  7.2 2.9 copy-start.2
  7.2 4.3 %copy-start.5 = (s32[1,1,4]{2,1,0:T(1,128)S(1)}, s32[1,1,4]{2,1,0:T(1,128)}, u32[]{:S(2)}) copy-start(s32[1,1,4]{2,1,0:T(1,128)} %param.13) | copy-start | bytes 52
  7.2 5.3 %copy-start.3 = (s32[16,8]{0,1:T(8,128)S(1)}, s32[16,8]{0,1:T(8,128)}, u32[]{:S(2)}) copy-start(s32[16,8]{0,1:T(8,128)} %param.12) | copy-start | bytes 1540
  7.2 40.2 %all-gather.6.cloned.1.call-start = ((), (), s32[]{:S(2)}) async-start(), calls=%async_computation.4 | async-start | bytes 5242880 | tf_op jit(solution)/shard_map/all_gather | solution.py:47
  10.0 94.8 %all-gather.4.cloned.1.call-start = ((), (), s32[]{:S(2)}) async-start(), calls=%async_computation.3 | async-start | bytes 2949120 | tf_op jit(solution)/shard_map/all_gather | solution.py:50
  10.8 240.5 %reduce-scatter.2.cloned.1.call-start = ((), (), s32[]{:S(2)}) async-start(), calls=%async_computation.5 | async-start | bytes 2949120 | tf_op jit(solution)/shard_map/reduce_scatter | solution.py:84
  12.6 6.3 %copy-start.4 = (s32[16]{0:T(128)S(1)}, s32[16]{0:T(128)}, u32[]{:S(2)}) copy-start(s32[16]{0:T(128)} %param.11) | copy-start | bytes 196
  124.8 2.2 copy-start
  160.5 2.2 copy-start
  182.1 125.0 %all-gather.8.cloned.1.call-start = ((), (), s32[]{:S(2)}) async-start(), calls=%async_computation.6 | async-start | bytes 2949120 | tf_op jit(solution)/shard_map/all_gather | solution.py:88
  254.1 82.4 %all-to-all-start = ((s32[4,1,4]{2,1,0:T(1,128)}), s32[4,1,4]{2,1,0:T(1,128)S(1)}, u32[]{:S(2)}, u32[]{:S(2)}) async-start(s32[4,1,4]{2,1,0:T(1,128)} %bitcast.10), calls=%async_computation | async-start | bytes 4096 | tf_op jit(solution)/shard_map/all_to_all | solution.py:104
  336.5 18.0 %all-to-all-start.1 = ((bf16[4,4,128,256]{3,2,1,0:T(8,128)(2,1)}), bf16[4,4,128,256]{3,2,1,0:T(8,128)(2,1)S(1)}, u32[]{:S(2)}, u32[]{:S(2)}) async-start(bf16[4,4,128,256]{3,2,1,0:T(8,128)(2,1)} %bitcast.16), calls=%async_computation.2 | async-start | bytes 2097152 | tf_op jit(solution)/shard_map/all_to_all | solution.py:101
  355.5 4.6 %copy-start.1 = (f32[2048,256]{1,0:T(8,128)S(1)}, f32[2048,256]{1,0:T(8,128)}, u32[]{:S(2)}) copy-start(f32[2048,256]{1,0:T(8,128)} %param.14) | copy-start | bytes 6291460
Sparse Core Ops, SparseCore 0:
  10.2 37.1 all-gather.5
  50.1 54.6 all-gather.3
  182.2 69.0 reduce-scatter.1
  253.5 53.5 all-gather.7
where the time goes:
time: 371 us; the launch traced here: 370 us
  waiting for transfers between devices  213 us (57%)
  local copies, waits for them, and re-layouts  54.8 us (15%)
  matrix products  53.3 us (14%)
  other arithmetic  28.1 us (8%)
  between operations  13.9 us (4%)
  starting transfers between devices  6.85 us (2%)
    reduce_scatter x1, waiting for transfers between devices, local(): lax.psum_scatter(store_grad.astype(jnp.bfloat16), 'col', scatter_dimensio...  69.2 us
    all_gather x1, waiting for transfers between devices, local(): lax.all_gather(own_store.astype(jnp.bfloat16), 'col', axis=0, tiled=True)  51.7 us
    all_gather x1, waiting for transfers between devices, local(): lax.all_gather(new_store.astype(jnp.bfloat16), 'col', axis=0, tiled=True)  49.9 us
    while x14, local copies, waits for them, and re-layouts  38 us
    all_gather x1, waiting for transfers between devices, local(): all_tables = lax.all_gather(own_table, 'row', axis=0, tiled=True)  28.4 us
    dot_general x2, matrix products, first_pass(): jnp.einsum('skab,sar->skbr', misfit, factor_rows, preferred_element_type=...  17.3 us
    dot_general x2, matrix products, second_pass(): jnp.einsum('skab,skbr->sar', misfit, selected, preferred_element_type=jnp...  15.8 us
    dot_general x5, matrix products, pick_blocks(): jnp.dot(selector, flat_table, preferred_element_type=jnp.float32)  13.9 us
  transfers between devices with their start and end apart: 6, of which 5 were waited for; matrix products, arithmetic and copies ran while one was open for 12% of the time, Pallas kernels for 0%

commit v1 on v0

v1 whole, which is shorter than its diff:
```python
import functools

import jax
import jax.numpy as jnp
from jax import lax
from jax.experimental import pallas as pl
from jax.experimental.pallas import tpu as pltpu
from jax.sharding import PartitionSpec as P

learn_rate = 0.01
weight_decay = 0.05
line_len = 4

VMEM = pltpu.VMEM
SMEM = pltpu.SMEM


def ring_place(col, col_count):
    width = max(col_count // line_len, 1)
    depth = col_count // width
    across, along = col % width, col // width
    return across * depth + jnp.where(across % 2 == 0, along, depth - 1 - along)


def ring_steps(col_count):
    width = max(col_count // line_len, 1)
    depth = col_count // width
    order = []
    for place in range(col_count):
        across, along = divmod(place, depth)
        along = along if across % 2 == 0 else depth - 1 - along
        order.append(along * width + across)
    ahead = [(order[p], order[(p + 1) % col_count]) for p in range(col_count)]
    back = [(b, a) for a, b in ahead]
    return ahead, back


def spec(space):
    return pl.BlockSpec(memory_space=space)


def gather_ring(rows, col_count):
    ahead, back = ring_steps(col_count)
    half = rows.shape[0] // 2
    far = col_count // 2
    parts = [rows[:half], rows[half:]]
    from_behind, from_front = list(parts), list(parts)
    pieces = {(0, 0): parts[0], (0, 1): parts[1]}
    for step in range(1, far + 1):
        for h in (0, 1):
            if step < far or h == 0:
                from_behind[h] = lax.ppermute(from_behind[h], "col", ahead)
                pieces[(col_count - step, h)] = from_behind[h]
            if step < far or h == 1:
                from_front[h] = lax.ppermute(from_front[h], "col", back)
                pieces[(step, h)] = from_front[h]
    return pieces


def scatter_ring(pieces, col_count):
    ahead, back = ring_steps(col_count)
    far = col_count // 2
    sums = []
    to_front = [pieces[(far, 0)], pieces[(far - 1, 1)]]
    to_back = [pieces[(col_count - far + 1, 0)], pieces[(far, 1)]]
    for step in range(far, 0, -1):
        for h in (0, 1):
            if step < far or h == 0:
                moved = lax.ppermute(to_front[h], "col", ahead)
                if step > 1:
                    moved = (
                        moved.astype(jnp.float32) + pieces[(step - 1, h)].astype(jnp.float32)
                    ).astype(jnp.bfloat16)
                to_front[h] = moved
            if step < far or h == 1:
                moved = lax.ppermute(to_back[h], "col", back)
                if step > 1:
                    moved = (
                        moved.astype(jnp.float32)
                        + pieces[(col_count - step + 1, h)].astype(jnp.float32)
                    ).astype(jnp.bfloat16)
                to_back[h] = moved
    for h in (0, 1):
        sums.append(
            pieces[(0, h)].astype(jnp.float32)
            + to_front[h].astype(jnp.float32)
            + to_back[h].astype(jnp.float32)
        )
    return jnp.concatenate(sums, axis=0)


def pick_kernel(row_count, per_owner, row_ref, *refs):
    ids = refs[:row_count]
    table = refs[row_count]
    outs = refs[row_count + 1 : 2 * row_count + 1]
    held, sems = refs[2 * row_count + 1 :]
    row = row_ref[0]

    def copy_of(k, i):
        block = ids[k][row * per_owner + i]
        n = k * per_owner + i
        return pltpu.make_async_copy(table.at[block], held.at[n], sems.at[n])

    for k in range(row_count):
        for i in range(per_owner):
            copy_of(k, i).start()
    for k in range(row_count):
        for i in range(per_owner):
            copy_of(k, i).wait()
            outs[k][i] = held[k * per_owner + i].astype(jnp.bfloat16)


def pick(row, ids, table, per_owner):
    row_count = len(ids)
    block = table.shape[1:]
    return pl.pallas_call(
        functools.partial(pick_kernel, row_count, per_owner),
        out_shape=[jax.ShapeDtypeStruct((per_owner,) + block, jnp.bfloat16)] * row_count,
        in_specs=[spec(SMEM)] * (row_count + 1) + [spec(pl.ANY)],
        out_specs=[spec(VMEM)] * row_count,
        scratch_shapes=[
            VMEM((row_count * per_owner,) + block, jnp.float32),
            pltpu.SemaphoreType.DMA((row_count * per_owner,)),
        ],
        compiler_params=pltpu.CompilerParams(vmem_limit_bytes=48 * 1024 * 1024),
    )(row, *ids, table)


def load_table(table, names, refs, rows):
    half = rows // 2
    for (offset, h), ref in zip(names, refs):
        table[pl.ds(offset * rows + h * half, half), :] = ref[...]


def first_kernel(cfg, row_ref, live_ref, ids_ref, observed, *refs):
    row_count, per_owner, kinds, block, rows, names = cfg
    skus = refs[:row_count]
    pieces = refs[row_count : row_count + len(names)]
    outs = refs[row_count + len(names) : row_count + 2 * len(names)]
    table, grad = refs[row_count + 2 * len(names) :]
    row = row_ref[0]
    load_table(table, names, pieces, rows)
    grad[...] = jnp.zeros_like(grad)
    for k in range(row_count):
        owner = row ^ k

        @pl.loop(0, live_ref[owner])
        def _(i):
            slot = owner * per_owner + i
            sku = skus[k][i]
            terms = []
            for n in range(kinds):
                at = pl.multiple_of(ids_ref[slot * kinds + n] * block, block)
                store = table[pl.ds(at, block), :]
                predicted = lax.dot_general(
                    sku, store, (((1,), (1,)), ((), ())), preferred_element_type=jnp.float32
                )
                misfit = (predicted - observed[slot, n].astype(jnp.float32)).astype(jnp.bfloat16)
                terms.append(
                    lax.dot_general(
                        misfit, sku, (((0,), (0,)), ((), ())), preferred_element_type=jnp.float32
                    )
                )
            for n in range(kinds):
                at = pl.multiple_of(ids_ref[slot * kinds + n] * block, block)
                grad[pl.ds(at, block), :] += terms[n]

    half = rows // 2
    for (offset, h), out in zip(names, outs):
        out[...] = grad[pl.ds(offset * rows + h * half, half), :].astype(jnp.bfloat16)


def second_kernel(cfg, row_ref, live_ref, ids_ref, observed, *refs):
    row_count, per_owner, kinds, block, rows, names = cfg
    skus = refs[:row_count]
    pieces = refs[row_count : row_count + len(names)]
    outs = refs[row_count + len(names) : 2 * row_count + len(names)]
    (table,) = refs[2 * row_count + len(names) :]
    row = row_ref[0]
    load_table(table, names, pieces, rows)
    for k in range(row_count):
        owner = row ^ k
        outs[k][...] = jnp.zeros_like(outs[k])

        @pl.loop(0, live_ref[owner])
        def _(i):
            slot = owner * per_owner + i
            sku = skus[k][i]
            total = None
            for n in range(kinds):
                at = pl.multiple_of(ids_ref[slot * kinds + n] * block, block)
                store = table[pl.ds(at, block), :]
                predicted = lax.dot_general(
                    sku, store, (((1,), (1,)), ((), ())), preferred_element_type=jnp.float32
                )
                misfit = (predicted - observed[slot, n].astype(jnp.float32)).astype(jnp.bfloat16)
                term = jnp.dot(misfit, store, preferred_element_type=jnp.float32)
                total = term if total is None else total + term
            outs[k][i] = total.astype(jnp.bfloat16)


def run_pass(kernel, second, row, live, ids, observed, skus, pieces, cfg):
    row_count, per_owner, kinds, block, rows, names = cfg
    rank = skus[0].shape[2]
    columns = max(offset for offset, _ in names) + 1
    if second:
        outs = [jax.ShapeDtypeStruct(skus[0].shape, jnp.bfloat16)] * row_count
        scratch = [VMEM((columns * rows, rank), jnp.bfloat16)]
    else:
        outs = [jax.ShapeDtypeStruct((rows // 2, rank), jnp.bfloat16)] * len(names)
        scratch = [
            VMEM((columns * rows, rank), jnp.bfloat16),
            VMEM((columns * rows, rank), jnp.float32),
        ]
    return pl.pallas_call(
        functools.partial(kernel, cfg),
        out_shape=outs,
        in_specs=[spec(SMEM)] * 3 + [spec(VMEM)] * (1 + row_count + len(names)),
        out_specs=[spec(VMEM)] * len(outs),
        scratch_shapes=scratch,
        compiler_params=pltpu.CompilerParams(vmem_limit_bytes=56 * 1024 * 1024),
    )(row, live, ids, observed, *skus, *[pieces[name] for name in names])


def finish_kernel(row_count, per_owner, row_ref, *refs):
    ids = refs[:row_count]
    sku = refs[row_count]
    terms = refs[row_count + 1 : 2 * row_count + 1]
    out = refs[2 * row_count + 1]
    (grad,) = refs[2 * row_count + 2 :]
    row = row_ref[0]
    grad[...] = jnp.zeros_like(grad)
    for k in range(row_count):
        for i in range(per_owner):
            block = ids[k][row * per_owner + i]
            grad[block] += terms[k][i].astype(jnp.float32)
    out[...] = sku[...] - learn_rate * (grad[...] + weight_decay * sku[...])


def finish(row, ids, sku, terms, per_owner):
    row_count = len(ids)
    return pl.pallas_call(
        functools.partial(finish_kernel, row_count, per_owner),
        out_shape=jax.ShapeDtypeStruct(sku.shape, jnp.float32),
        in_specs=[spec(SMEM)] * (row_count + 1) + [spec(VMEM)] * (1 + row_count),
        out_specs=spec(VMEM),
        scratch_shapes=[VMEM(sku.shape, jnp.float32)],
        compiler_params=pltpu.CompilerParams(vmem_limit_bytes=48 * 1024 * 1024),
    )(row, *ids, sku, *terms)


def local(observed, sku_ids, store_ids, live_slot_counts, sku_factors, store_factors):
    row_count = lax.axis_size("row")
    col_count = lax.axis_size("col")
    per_owner = observed.shape[0] // row_count
    kinds, block = observed.shape[1:3]
    rank = sku_factors.shape[1]
    rows = store_factors.shape[0]
    store_blocks = rows // block
    row = lax.axis_index("row")
    row_vec = row.reshape(1).astype(jnp.int32)
    live = live_slot_counts.reshape(row_count)
    sku = sku_factors.reshape(-1, block, rank)

    swaps = [[(r, r ^ k) for r in range(row_count)] for k in range(row_count)]
    asked = [sku_ids] + [lax.ppermute(sku_ids, "row", swaps[k]) for k in range(1, row_count)]

    place = ring_place(lax.axis_index("col"), col_count)
    owner_place = ring_place(store_ids // store_blocks, col_count)
    near_ids = ((owner_place - place) % col_count) * store_blocks + store_ids % store_blocks
    near_ids = near_ids.reshape(-1)

    names = [(d, h) for d in range(col_count) for h in (0, 1)]
    cfg = (row_count, per_owner, kinds, block, rows, names)

    pieces = gather_ring(store_factors.astype(jnp.bfloat16), col_count)
    picked = pick(row_vec, asked, sku, per_owner)
    skus = [picked[0]] + [
        lax.ppermute(picked[k], "row", swaps[k]) for k in range(1, row_count)
    ]
    grads = run_pass(first_kernel, False, row_vec, live, near_ids, observed, skus, pieces, cfg)
    own_grad = scatter_ring(dict(zip(names, grads)), col_count)
    new_store = store_factors - learn_rate * (own_grad + weight_decay * store_factors)
    new_pieces = gather_ring(new_store.astype(jnp.bfloat16), col_count)
    terms = run_pass(second_kernel, True, row_vec, live, near_ids, observed, skus, new_pieces, cfg)
    arrived = [terms[0]] + [
        lax.ppermute(terms[k], "row", swaps[k]) for k in range(1, row_count)
    ]
    new_sku = finish(row_vec, asked, sku, arrived, per_owner)
    return new_sku.reshape(sku_factors.shape), new_store


def solution(mesh):
    placed = (
        P(("row", "col"), None, None, None),
        P(("row", "col")),
        P(("row", "col"), None),
        P("row", "col", None),
        P(("row", "col"), None),
        P(("row", "col"), None),
    )
    return jax.shard_map(
        local,
        mesh=mesh,
        in_specs=placed,
        out_specs=(P(("row", "col"), None), P(("row", "col"), None)),
        check_vma=False,
    )
```

time: 371 us -> 151 us (0.41)
  waiting for transfers between devices: 213 us -> 50.9 us
  matrix products: 53.3 us -> 0 us
  local copies, waits for them, and re-layouts: 54.8 us -> 6.01 us
  starting transfers between devices: 6.85 us -> 54.2 us
  Pallas kernels: 0 us -> 29.9 us
  other arithmetic: 28.1 us -> 7.29 us
  between operations: 13.9 us -> 1.21 us
    all_gather x3 -> x0, waiting for transfers between devices: 130 us -> none  [the longest x1 51.7 us: local(): lax.all_gather(own_store.astype(jnp.bfloat16), 'col', axis=0, tiled=True)]
    reduce_scatter x1 -> x0, waiting for transfers between devices: 69.2 us -> none  [local(): lax.psum_scatter(store_grad.astype(jnp.bfloat16), 'col', scatter_dimensio...]
    ppermute x0 -> x51, starting transfers between devices: none -> 54.2 us  [the longest x7 18.4 us: scatter_ring(): moved = lax.ppermute(to_front[h], 'col', ahead)]
    dot_general x15 -> x0, matrix products: 53.3 us -> none  [the longest x2 17.3 us: first_pass(): jnp.einsum('skab,sar->skbr', misfit, factor_rows, preferred_element_type=...]
    ppermute x0 -> x51, waiting for transfers between devices: none -> 50.9 us  [the longest x14 16.8 us: gather_ring(): from_front[h] = lax.ppermute(from_front[h], 'col', back)]
    while x15 -> x0, local copies, waits for them, and re-layouts: 38.1 us -> none
    pallas_call x0 -> x4, Pallas kernels: none -> 29.9 us  [the longest x2 23.4 us: run_pass(): pl.pallas_call(functools.partial(kernel, cfg), out_shape=outs, in_specs=[...]
    all_to_all x2 -> x0, waiting for transfers between devices: 13.6 us -> none  [the longest x1 13.6 us: local(): lax.all_to_all(sku_terms.astype(jnp.bfloat16), 'row', split_axis=0, conca...]
  transfers between devices with their start and end apart: 6 -> 51, of which waited for: 5 -> 29; matrix products, arithmetic and copies ran while one was open for 12% -> 4% of each run, Pallas kernels for 0% -> 2%
where the time goes in v1:
time: 151 us; the launch traced here: 149 us
  starting transfers between devices  54.2 us (36%)
  waiting for transfers between devices  50.9 us (34%)
  Pallas kernels  29.9 us (20%)
  other arithmetic  7.29 us (5%)
  local copies, waits for them, and re-layouts  6.01 us (4%)
    pallas_call x2, Pallas kernels, run_pass(): pl.pallas_call(functools.partial(kernel, cfg), out_shape=outs, in_specs=[...  23.4 us
    ppermute x7, starting transfers between devices, scatter_ring(): moved = lax.ppermute(to_front[h], 'col', ahead)  18.4 us
    ppermute x14, starting transfers between devices, gather_ring(): from_behind[h] = lax.ppermute(from_behind[h], 'col', ahead)  17.7 us
    ppermute x14, waiting for transfers between devices, gather_ring(): from_front[h] = lax.ppermute(from_front[h], 'col', back)  16.8 us
    ppermute x3, waiting for transfers between devices, local(): lax.ppermute(terms[k], 'row', swaps[k])  12.2 us
    ppermute x14, starting transfers between devices, gather_ring(): from_front[h] = lax.ppermute(from_front[h], 'col', back)  11 us
    ppermute x7, waiting for transfers between devices, scatter_ring(): moved = lax.ppermute(to_back[h], 'col', back)  9.49 us
    ppermute x14, waiting for transfers between devices, gather_ring(): from_behind[h] = lax.ppermute(from_behind[h], 'col', ahead)  7.36 us
  transfers between devices with their start and end apart: 51, of which 29 were waited for; matrix products, arithmetic and copies ran while one was open for 4% of the time, Pallas kernels for 2%

profile of v1, /device:TPU:0, one launch (start us, length us, event | category | flops | bytes accessed | tf_op | source)
XLA Modules:
  0.0 149.5 jit_solution(8304023062360216749)
XLA Ops:
  0.6 1.1 convert_element_type.114
  1.8 3.0 %collective-permute-start.7 = (bf16[320,256]{1,0:T(8,128)(2,1)S(1)}, bf16[320,256]{1,0:T(8,128)(2,1)S(1)}, u32[]{:S(2)}, u32[]{:S(2)}) collective-permute-start(bf16[320,256]{1,0:T(8,128)(2,1)S(1)} %get-tuple-element.54.refs_5_), channel_id=1, source_target_pairs={{2,0},{4,2},{6,4},{7,6},{5,7},{3,5},{1,3},{0,1},{10,8},{12,10},{14... | collective-permute-start | bytes 491528 | tf_op jit(solution)/shard_map/ppermute | solution.py:55
  5.0 2.0 %collective-permute-start.17 = (bf16[320,256]{1,0:T(8,128)(2,1)S(1)}, bf16[320,256]{1,0:T(8,128)(2,1)S(1)}, u32[]{:S(2)}, u32[]{:S(2)}) collective-permute-start(bf16[320,256]{1,0:T(8,128)(2,1)S(1)} %get-tuple-element.54.refs_5_), channel_id=1, source_target_pairs={{0,2},{2,4},{4,6},{6,7},{7,5},{5,3},{3,1},{1,0},{8,10},{10,12},{12... | collective-permute-start | bytes 491528 | tf_op jit(solution)/shard_map/ppermute | solution.py:52
  7.0 1.4 collective-permute-start.1
  8.5 1.6 %collective-permute-done.2.refs_3_ = s32[16]{0:T(128)S(1)} collective-permute-done((s32[16]{0:T(128)}, s32[16]{0:T(128)S(1)}, u32[]{:S(2)}, u32[]{:S(2)}) %collective-permute-start.2) | collective-permute-done | bytes 96 | tf_op jit(solution)/shard_map/ppermute | solution.py:266
  11.3 1.6 %copy-done = f32[2048,256]{1,0:T(8,128)S(1)} copy-done((f32[2048,256]{1,0:T(8,128)S(1)}, f32[2048,256]{1,0:T(8,128)}, u32[]{:S(2)}) %copy-start) | copy-done | bytes 2097176
  12.9 0.7 copy-done.4
  13.5 3.6 %shard_map.77 = (bf16[4,128,256]{2,1,0:T(8,128)(2,1)S(1)}, bf16[4,128,256]{2,1,0:T(8,128)(2,1)S(1)}, bf16[4,128,256]{2,1,0:T(8,128)(2,1)S(1)}, bf16[4,128,256]{2,1,0:T(8,128)(2,1)S(1)}) custom-call(s32[1]{0:T(128)} %bitcast.row_ref, s32[16]{0:T(128)S(1)} %copy-done.4, s32[16]{0:T(128)S(1)} %collective-permute-done.refs_1_, ...), custom_call_target="tpu_custom_call" | custom-call | tf_op jit(solution)/shard_map/pallas_call | solution.py:116
  17.2 0.7 copy-done.2
  18.5 1.6 %collective-permute-start.9 = (bf16[320,256]{1,0:T(8,128)(2,1)S(1)}, bf16[320,256]{1,0:T(8,128)(2,1)S(1)}, u32[]{:S(2)}, u32[]{:S(2)}) collective-permute-start(bf16[320,256]{1,0:T(8,128)(2,1)S(1)} %collective-permute-done.7.refs_7_), channel_id=1, source_target_pairs={{2,0},{4,2},{6,4},{7,6},{5,7},{3,5},{1,3},{0,1},{10,8},{12,10},{14... | collective-permute-start | bytes 491528 | tf_op jit(solution)/shard_map/ppermute | solution.py:55
  20.5 1.5 %collective-permute-start.4 = (bf16[4,128,256]{2,1,0:T(8,128)(2,1)S(1)}, bf16[4,128,256]{2,1,0:T(8,128)(2,1)S(1)}, u32[]{:S(2)}, u32[]{:S(2)}) collective-permute-start(bf16[4,128,256]{2,1,0:T(8,128)(2,1)S(1)} %get-tuple-element.28), channel_id=1, source_target_pairs={{0,16},{8,24},{16,0},{24,8},{1,17},{9,25},{17,1},{25,9},{2,18},{10... | collective-permute-start | bytes 786440 | tf_op jit(solution)/shard_map/ppermute | solution.py:279
  22.0 3.1 %collective-permute-done.6.refs_6_ = bf16[320,256]{1,0:T(8,128)(2,1)S(1)} collective-permute-done((bf16[320,256]{1,0:T(8,128)(2,1)S(1)}, bf16[320,256]{1,0:T(8,128)(2,1)S(1)}, u32[]{:S(2)}, u32[]{:S(2)}) %collective-permute-start.6) | collective-permute-done | bytes 163872 | tf_op jit(solution)/shard_map/ppermute | solution.py:55
  25.1 1.6 %collective-permute-start.18 = (bf16[320,256]{1,0:T(8,128)(2,1)S(1)}, bf16[320,256]{1,0:T(8,128)(2,1)S(1)}, u32[]{:S(2)}, u32[]{:S(2)}) collective-permute-start(bf16[320,256]{1,0:T(8,128)(2,1)S(1)} %collective-permute-done.17.refs_19_), channel_id=1, source_target_pairs={{0,2},{2,4},{4,6},{6,7},{7,5},{5,3},{3,1},{1,0},{8,10},{10,12},{12... | collective-permute-start | bytes 491528 | tf_op jit(solution)/shard_map/ppermute | solution.py:52
  27.1 0.9 collective-permute-done.9.refs_9_
  28.3 1.8 %collective-permute-start.14 = (bf16[320,256]{1,0:T(8,128)(2,1)S(1)}, bf16[320,256]{1,0:T(8,128)(2,1)S(1)}, u32[]{:S(2)}, u32[]{:S(2)}) collective-permute-start(bf16[320,256]{1,0:T(8,128)(2,1)S(1)} %collective-permute-done.13.refs_16_), channel_id=1, source_target_pairs={{0,2},{2,4},{4,6},{6,7},{7,5},{5,3},{3,1},{1,0},{8,10},{10,12},{12... | collective-permute-start | bytes 491528 | tf_op jit(solution)/shard_map/ppermute | solution.py:52
  30.6 1.4 collective-permute-start.19
  32.1 1.5 collective-permute-done.8.refs_8_
  33.8 1.5 collective-permute-done.11.refs_11_
  35.6 1.7 %collective-permute-start.15 = (bf16[320,256]{1,0:T(8,128)(2,1)S(1)}, bf16[320,256]{1,0:T(8,128)(2,1)}, u32[]{:S(2)}, u32[]{:S(2)}) collective-permute-start(bf16[320,256]{1,0:T(8,128)(2,1)S(1)} %collective-permute-done.14.refs_14_), channel_id=1, source_target_pairs={{0,2},{2,4},{4,6},{6,7},{7,5},{5,3},{3,1},{1,0},{8,10},{10,12},{12... | collective-permute-start | bytes 491528 | tf_op jit(solution)/shard_map/ppermute | solution.py:52
  37.5 0.7 reshape.22.ids_ref
  38.6 2.1 %collective-permute-done.10.refs_10_ = bf16[320,256]{1,0:T(8,128)(2,1)S(1)} collective-permute-done((bf16[320,256]{1,0:T(8,128)(2,1)S(1)}, bf16[320,256]{1,0:T(8,128)(2,1)S(1)}, u32[]{:S(2)}, u32[]{:S(2)}) %collective-permute-start.10) | collective-permute-done | bytes 163872 | tf_op jit(solution)/shard_map/ppermute | solution.py:55
  40.7 1.9 %collective-permute-done.16.refs_13_ = bf16[320,256]{1,0:T(8,128)(2,1)S(1)} collective-permute-done((bf16[320,256]{1,0:T(8,128)(2,1)S(1)}, bf16[320,256]{1,0:T(8,128)(2,1)S(1)}, u32[]{:S(2)}, u32[]{:S(2)}) %collective-permute-start.16) | collective-permute-done | bytes 163872 | tf_op jit(solution)/shard_map/ppermute | solution.py:55
  43.3 13.2 %shard_map.78 = (bf16[320,256]{1,0:T(8,128)(2,1)}, bf16[320,256]{1,0:T(8,128)(2,1)}, bf16[320,256]{1,0:T(8,128)(2,1)}, bf16[320,256]{1,0:T(8,128)(2,1)}, bf16[32...) custom-call(s32[1]{0:T(128)} %bitcast.row_ref, ...), custom_call_target="tpu_custom_call" | custom-call | tf_op jit(solution)/shard_map/pallas_call | solution.py:215
  56.5 2.8 %collective-permute-start.20 = (bf16[320,256]{1,0:T(8,128)(2,1)}, bf16[320,256]{1,0:T(8,128)(2,1)S(1)}, u32[]{:S(2)}, u32[]{:S(2)}) collective-permute-start(bf16[320,256]{1,0:T(8,128)(2,1)} %get-tuple-element.31), channel_id=1, source_target_pairs={{0,2},{2,4},{4,6},{6,7},{7,5},{5,3},{3,1},{1,0},{8,10},{10,12},{12... | collective-permute-start | bytes 491528 | tf_op jit(solution)/shard_map/ppermute | solution.py:69
  59.3 4.1 %collective-permute-start.27 = (bf16[320,256]{1,0:T(8,128)(2,1)}, bf16[320,256]{1,0:T(8,128)(2,1)S(1)}, u32[]{:S(2)}, u32[]{:S(2)}) collective-permute-start(bf16[320,256]{1,0:T(8,128)(2,1)} %get-tuple-element.39), channel_id=1, source_target_pairs={{0,2},{2,4},{4,6},{6,7},{7,5},{5,3},{3,1},{1,0},{8,10},{10,12},{12... | collective-permute-start | bytes 491528 | tf_op jit(solution)/shard_map/ppermute | solution.py:69
  63.8 1.0 add_convert_fusion.9
  64.8 3.7 %collective-permute-start.21 = (bf16[320,256]{1,0:T(8,128)(2,1)S(1)}, bf16[320,256]{1,0:T(8,128)(2,1)S(1)}, u32[]{:S(2)}, u32[]{:S(2)}) collective-permute-start(bf16[320,256]{1,0:T(8,128)(2,1)S(1)} %add_convert_fusion.9), channel_id=1, source_target_pairs={{0,2},{2,4},{4,6},{6,7},{7,5},{5,3},{3,1},{1,0},{8,10},{10,12},{12... | collective-permute-start | bytes 491528 | tf_op jit(solution)/shard_map/ppermute | solution.py:69
  68.5 1.0 add_convert_fusion.6
  69.5 1.0 add_convert_fusion.4
  70.5 2.4 %collective-permute-start.28 = (bf16[320,256]{1,0:T(8,128)(2,1)S(1)}, bf16[320,256]{1,0:T(8,128)(2,1)S(1)}, u32[]{:S(2)}, u32[]{:S(2)}) collective-permute-start(bf16[320,256]{1,0:T(8,128)(2,1)S(1)} %add_convert_fusion.4), channel_id=1, source_target_pairs={{0,2},{2,4},{4,6},{6,7},{7,5},{5,3},{3,1},{1,0},{8,10},{10,12},{12... | collective-permute-start | bytes 491528 | tf_op jit(solution)/shard_map/ppermute | solution.py:69
  72.9 1.0 add_convert_fusion.2
  74.0 1.0 add_convert_fusion.8
  75.0 2.1 %collective-permute-start.22 = (bf16[320,256]{1,0:T(8,128)(2,1)S(1)}, bf16[320,256]{1,0:T(8,128)(2,1)S(1)}, u32[]{:S(2)}, u32[]{:S(2)}) collective-permute-start(bf16[320,256]{1,0:T(8,128)(2,1)S(1)} %add_convert_fusion.8), channel_id=1, source_target_pairs={{0,2},{2,4},{4,6},{6,7},{7,5},{5,3},{3,1},{1,0},{8,10},{10,12},{12... | collective-permute-start | bytes 491528 | tf_op jit(solution)/shard_map/ppermute | solution.py:69
  77.6 2.1 %collective-permute-start.29 = (bf16[320,256]{1,0:T(8,128)(2,1)S(1)}, bf16[320,256]{1,0:T(8,128)(2,1)S(1)}, u32[]{:S(2)}, u32[]{:S(2)}) collective-permute-start(bf16[320,256]{1,0:T(8,128)(2,1)S(1)} %add_convert_fusion.3), channel_id=1, source_target_pairs={{0,2},{2,4},{4,6},{6,7},{7,5},{5,3},{3,1},{1,0},{8,10},{10,12},{12... | collective-permute-start | bytes 491528 | tf_op jit(solution)/shard_map/ppermute | solution.py:69
  79.7 0.8 collective-permute-done.31
  80.9 1.0 collective-permute-done.22
  81.9 1.3 collective-permute-start.23
  83.1 3.0 %collective-permute-done.32 = bf16[320,256]{1,0:T(8,128)(2,1)S(1)} collective-permute-done((bf16[320,256]{1,0:T(8,128)(2,1)S(1)}, bf16[320,256]{1,0:T(8,128)(2,1)S(1)}, u32[]{:S(2)}, u32[]{:S(2)}) %collective-permute-start.32) | collective-permute-done | bytes 163872 | tf_op jit(solution)/shard_map/ppermute | solution.py:76
  86.2 1.2 collective-permute-start.33
  87.5 5.7 %collective-permute-done.33 = bf16[320,256]{1,0:T(8,128)(2,1)S(1)} collective-permute-done((bf16[320,256]{1,0:T(8,128)(2,1)S(1)}, bf16[320,256]{1,0:T(8,128)(2,1)S(1)}, u32[]{:S(2)}, u32[]{:S(2)}) %collective-permute-start.33) | collective-permute-done | bytes 163872 | tf_op jit(solution)/shard_map/ppermute | solution.py:76
  93.3 1.0 fusion.13
  94.8 1.6 %collective-permute-start.40 = (bf16[320,256]{1,0:T(8,128)(2,1)S(1)}, bf16[320,256]{1,0:T(8,128)(2,1)S(1)}, u32[]{:S(2)}, u32[]{:S(2)}) collective-permute-start(bf16[320,256]{1,0:T(8,128)(2,1)S(1)} %get-tuple-element.53.refs_4_), channel_id=1, source_target_pairs={{0,2},{2,4},{4,6},{6,7},{7,5},{5,3},{3,1},{1,0},{8,10},{10,12},{12... | collective-permute-start | bytes 491528 | tf_op jit(solution)/shard_map/ppermute | solution.py:52
  96.4 1.9 %collective-permute-start.45 = (bf16[320,256]{1,0:T(8,128)(2,1)S(1)}, bf16[320,256]{1,0:T(8,128)(2,1)S(1)}, u32[]{:S(2)}, u32[]{:S(2)}) collective-permute-start(bf16[320,256]{1,0:T(8,128)(2,1)S(1)} %get-tuple-element.52.refs_5_), channel_id=1, source_target_pairs={{0,2},{2,4},{4,6},{6,7},{7,5},{5,3},{3,1},{1,0},{8,10},{10,12},{12... | collective-permute-start | bytes 491528 | tf_op jit(solution)/shard_map/ppermute | solution.py:52
  98.4 3.0 %collective-permute-done.35.refs_7_ = bf16[320,256]{1,0:T(8,128)(2,1)S(1)} collective-permute-done((bf16[320,256]{1,0:T(8,128)(2,1)S(1)}, bf16[320,256]{1,0:T(8,128)(2,1)S(1)}, u32[]{:S(2)}, u32[]{:S(2)}) %collective-permute-start.35) | collective-permute-done | bytes 163872 | tf_op jit(solution)/shard_map/ppermute | solution.py:55
  102.0 1.5 %collective-permute-start.41 = (bf16[320,256]{1,0:T(8,128)(2,1)S(1)}, bf16[320,256]{1,0:T(8,128)(2,1)S(1)}, u32[]{:S(2)}, u32[]{:S(2)}) collective-permute-start(bf16[320,256]{1,0:T(8,128)(2,1)S(1)} %collective-permute-done.40.refs_18_), channel_id=1, source_target_pairs={{0,2},{2,4},{4,6},{6,7},{7,5},{5,3},{3,1},{1,0},{8,10},{10,12},{12... | collective-permute-start | bytes 491528 | tf_op jit(solution)/shard_map/ppermute | solution.py:52
  103.5 2.0 %collective-permute-done.45.refs_19_ = bf16[320,256]{1,0:T(8,128)(2,1)S(1)} collective-permute-done((bf16[320,256]{1,0:T(8,128)(2,1)S(1)}, bf16[320,256]{1,0:T(8,128)(2,1)S(1)}, u32[]{:S(2)}, u32[]{:S(2)}) %collective-permute-start.45) | collective-permute-done | bytes 163872 | tf_op jit(solution)/shard_map/ppermute | solution.py:52
  105.5 0.7 collective-permute-start.46
  106.2 1.3 collective-permute-start.36
  107.5 0.9 collective-permute-done.37.refs_9_
  109.1 1.4 collective-permute-start.42
  110.5 2.0 %collective-permute-done.46.refs_17_ = bf16[320,256]{1,0:T(8,128)(2,1)S(1)} collective-permute-done((bf16[320,256]{1,0:T(8,128)(2,1)S(1)}, bf16[320,256]{1,0:T(8,128)(2,1)S(1)}, u32[]{:S(2)}, u32[]{:S(2)}) %collective-permute-start.46) | collective-permute-done | bytes 163872 | tf_op jit(solution)/shard_map/ppermute | solution.py:52
  112.7 1.7 %collective-permute-start.38 = (bf16[320,256]{1,0:T(8,128)(2,1)S(1)}, bf16[320,256]{1,0:T(8,128)(2,1)S(1)}, u32[]{:S(2)}, u32[]{:S(2)}) collective-permute-start(bf16[320,256]{1,0:T(8,128)(2,1)S(1)} %collective-permute-done.36.refs_8_), channel_id=1, source_target_pairs={{2,0},{4,2},{6,4},{7,6},{5,7},{3,5},{1,3},{0,1},{10,8},{12,10},{14... | collective-permute-start | bytes 491528 | tf_op jit(solution)/shard_map/ppermute | solution.py:55
  114.5 0.7 collective-permute-start.44
  115.2 1.3 collective-permute-start.43
  116.5 1.2 collective-permute-done.47.refs_15_
  118.0 1.8 %collective-permute-done.44.refs_13_ = bf16[320,256]{1,0:T(8,128)(2,1)S(1)} collective-permute-done((bf16[320,256]{1,0:T(8,128)(2,1)S(1)}, bf16[320,256]{1,0:T(8,128)(2,1)S(1)}, u32[]{:S(2)}, u32[]{:S(2)}) %collective-permute-start.44) | collective-permute-done | bytes 163872 | tf_op jit(solution)/shard_map/ppermute | solution.py:55
  119.8 0.7 collective-permute-done.43.refs_12_
  120.6 0.7 copy-done.47
  121.3 10.2 %shard_map.79 = (bf16[4,128,256]{2,1,0:T(8,128)(2,1)}, bf16[4,128,256]{2,1,0:T(8,128)(2,1)}, bf16[4,128,256]{2,1,0:T(8,128)(2,1)}, bf16[4,128,256]{2,1,0:T(8,128)(2,1)}) custom-call(s32[1]{0:T(128)} %bitcast.row_ref, s32[4]{0:T(128)} %bitcast.8, s32[128]{0:T(128)} %reshape.22.ids_ref, bf16[16,8,128,128]{3,2,1,0:T(8,128)(2,1)} %observed.3, ...), custom_call_target="tpu_custom_call" | custom-call | tf_op jit(solution)/shard_map/pallas_call | solution.py:215
  131.6 1.5 collective-permute-start.49
  133.4 7.5 %collective-permute-done.49.refs_7_ = bf16[4,128,256]{2,1,0:T(8,128)(2,1)S(1)} collective-permute-done((bf16[4,128,256]{2,1,0:T(8,128)(2,1)}, bf16[4,128,256]{2,1,0:T(8,128)(2,1)S(1)}, u32[]{:S(2)}, u32[]{:S(2)}) %collective-permute-start.49) | collective-permute-done | bytes 262176 | tf_op jit(solution)/shard_map/ppermute | solution.py:287
  140.9 4.7 %collective-permute-done.50.refs_8_ = bf16[4,128,256]{2,1,0:T(8,128)(2,1)S(1)} collective-permute-done((bf16[4,128,256]{2,1,0:T(8,128)(2,1)}, bf16[4,128,256]{2,1,0:T(8,128)(2,1)S(1)}, u32[]{:S(2)}, u32[]{:S(2)}) %collective-permute-start.50) | collective-permute-done | bytes 262176 | tf_op jit(solution)/shard_map/ppermute | solution.py:287
  145.7 0.9 copy-done.3
  146.6 2.9 %shard_map.80 = f32[16,128,256]{2,1,0:T(8,128)} custom-call(s32[1]{0:T(128)} %bitcast.row_ref, s32[16]{0:T(128)S(1)} %copy-done.5, s32[16]{0:T(128)S(1)} %collective-permute-done.refs_1_, s32[16]{0:T(128)S(1)} %collective-permute-done.1.refs_2_, s32[16]{0:T(128)S(1)} %collective-permute-done.2.refs_3_, f32[16,128,256]{2,1,0:T(8,128)S(1)} %bitcast.5, ...), custom_call_target="tpu_custom_call" | custom-call | tf_op jit(solution)/shard_map/pallas_call | solution.py:242
  (159 shorter events, 10.3 us)
Async XLA Ops:
  0.6 36.7 %copy-start.48 = (s32[16,8]{0,1:T(8,128)S(1)}, s32[16,8]{0,1:T(8,128)}, u32[]{:S(2)}) copy-start(s32[16,8]{0,1:T(8,128)} %param.8) | copy-start | bytes 1540
  1.8 40.8 %copy-start.10 = (bf16[320,256]{1,0:T(8,128)(2,1)}, bf16[320,256]{1,0:T(8,128)(2,1)S(1)}, u32[]{:S(2)}) copy-start(bf16[320,256]{1,0:T(8,128)(2,1)S(1)} %get-tuple-element.54.refs_5_) | copy-start | bytes 491524
  1.8 40.8 %copy-start.11 = (bf16[320,256]{1,0:T(8,128)(2,1)}, bf16[320,256]{1,0:T(8,128)(2,1)S(1)}, u32[]{:S(2)}) copy-start(bf16[320,256]{1,0:T(8,128)(2,1)S(1)} %get-tuple-element.55.refs_4_) | copy-start | bytes 491524
  1.8 16.6 %collective-permute-start.7 = (bf16[320,256]{1,0:T(8,128)(2,1)S(1)}, bf16[320,256]{1,0:T(8,128)(2,1)S(1)}, u32[]{:S(2)}, u32[]{:S(2)}) collective-permute-start(bf16[320,256]{1,0:T(8,128)(2,1)S(1)} %get-tuple-element.54.refs_5_), channel_id=1, source_target_pairs={{2,0},{4,2},{6,4},{7,6},{5,7},{3,5},{1,3},{0,1},{10,8},{12,10},{14... | collective-permute-start | bytes 491528 | tf_op jit(solution)/shard_map/ppermute | solution.py:55
  4.8 15.2 %collective-permute-start.12 = (bf16[320,256]{1,0:T(8,128)(2,1)S(1)}, bf16[320,256]{1,0:T(8,128)(2,1)S(1)}, u32[]{:S(2)}, u32[]{:S(2)}) collective-permute-start(bf16[320,256]{1,0:T(8,128)(2,1)S(1)} %get-tuple-element.55.refs_4_), channel_id=1, source_target_pairs={{0,2},{2,4},{4,6},{6,7},{7,5},{5,3},{3,1},{1,0},{8,10},{10,12},{12... | collective-permute-start | bytes 491528 | tf_op jit(solution)/shard_map/ppermute | solution.py:52
  5.0 15.5 %collective-permute-start.17 = (bf16[320,256]{1,0:T(8,128)(2,1)S(1)}, bf16[320,256]{1,0:T(8,128)(2,1)S(1)}, u32[]{:S(2)}, u32[]{:S(2)}) collective-permute-start(bf16[320,256]{1,0:T(8,128)(2,1)S(1)} %get-tuple-element.54.refs_5_), channel_id=1, source_target_pairs={{0,2},{2,4},{4,6},{6,7},{7,5},{5,3},{3,1},{1,0},{8,10},{10,12},{12... | collective-permute-start | bytes 491528 | tf_op jit(solution)/shard_map/ppermute | solution.py:52
  6.9 3.1 %collective-permute-start.2 = (s32[16]{0:T(128)}, s32[16]{0:T(128)S(1)}, u32[]{:S(2)}, u32[]{:S(2)}) collective-permute-start(s32[16]{0:T(128)} %refs_0_.3), channel_id=1, source_target_pairs={{0,24},{8,16},{16,8},{24,0},{1,25},{9,17},{17,9},{25,1},{2,26},{10... | collective-permute-start | bytes 200 | tf_op jit(solution)/shard_map/ppermute | solution.py:266
  7.0 3.7 %collective-permute-start.1 = (s32[16]{0:T(128)}, s32[16]{0:T(128)S(1)}, u32[]{:S(2)}, u32[]{:S(2)}) collective-permute-start(s32[16]{0:T(128)} %refs_0_.3), channel_id=1, source_target_pairs={{0,16},{8,24},{16,0},{24,8},{1,17},{9,25},{17,1},{25,9},{2,18},{10... | collective-permute-start | bytes 200 | tf_op jit(solution)/shard_map/ppermute | solution.py:266
  10.0 1.3 collective-permute-start
  17.8 8.8 %collective-permute-start.3 = (bf16[4,128,256]{2,1,0:T(8,128)(2,1)S(1)}, bf16[4,128,256]{2,1,0:T(8,128)(2,1)S(1)}, u32[]{:S(2)}, u32[]{:S(2)}) collective-permute-start(bf16[4,128,256]{2,1,0:T(8,128)(2,1)S(1)} %get-tuple-element.27), channel_id=1, source_target_pairs={{0,8},{8,0},{16,24},{24,16},{1,9},{9,1},{17,25},{25,17},{2,10},{10... | collective-permute-start | bytes 786440 | tf_op jit(solution)/shard_map/ppermute | solution.py:279
  18.1 7.0 %collective-permute-start.6 = (bf16[320,256]{1,0:T(8,128)(2,1)S(1)}, bf16[320,256]{1,0:T(8,128)(2,1)S(1)}, u32[]{:S(2)}, u32[]{:S(2)}) collective-permute-start(bf16[320,256]{1,0:T(8,128)(2,1)S(1)} %get-tuple-element.55.refs_4_), channel_id=1, source_target_pairs={{2,0},{4,2},{6,4},{7,6},{5,7},{3,5},{1,3},{0,1},{10,8},{12,10},{14... | collective-permute-start | bytes 491528 | tf_op jit(solution)/shard_map/ppermute | solution.py:55
  18.5 24.2 %copy-start.21 = (bf16[320,256]{1,0:T(8,128)(2,1)}, bf16[320,256]{1,0:T(8,128)(2,1)S(1)}, u32[]{:S(2)}) copy-start(bf16[320,256]{1,0:T(8,128)(2,1)S(1)} %collective-permute-done.7.refs_7_) | copy-start | bytes 491524
  18.5 9.6 %collective-permute-start.9 = (bf16[320,256]{1,0:T(8,128)(2,1)S(1)}, bf16[320,256]{1,0:T(8,128)(2,1)S(1)}, u32[]{:S(2)}, u32[]{:S(2)}) collective-permute-start(bf16[320,256]{1,0:T(8,128)(2,1)S(1)} %collective-permute-done.7.refs_7_), channel_id=1, source_target_pairs={{2,0},{4,2},{6,4},{7,6},{5,7},{3,5},{1,3},{0,1},{10,8},{12,10},{14... | collective-permute-start | bytes 491528 | tf_op jit(solution)/shard_map/ppermute | solution.py:55
  20.0 22.6 %copy-start.22 = (bf16[320,256]{1,0:T(8,128)(2,1)}, bf16[320,256]{1,0:T(8,128)(2,1)S(1)}, u32[]{:S(2)}) copy-start(bf16[320,256]{1,0:T(8,128)(2,1)S(1)} %collective-permute-done.12.refs_18_) | copy-start | bytes 491524
  20.0 8.2 %collective-permute-start.13 = (bf16[320,256]{1,0:T(8,128)(2,1)S(1)}, bf16[320,256]{1,0:T(8,128)(2,1)S(1)}, u32[]{:S(2)}, u32[]{:S(2)}) collective-permute-start(bf16[320,256]{1,0:T(8,128)(2,1)S(1)} %collective-permute-done.12.refs_18_), channel_id=1, source_target_pairs={{0,2},{2,4},{4,6},{6,7},{7,5},{5,3},{3,1},{1,0},{8,10},{10,12},{12... | collective-permute-start | bytes 491528 | tf_op jit(solution)/shard_map/ppermute | solution.py:52
  20.5 22.1 %copy-start.23 = (bf16[320,256]{1,0:T(8,128)(2,1)}, bf16[320,256]{1,0:T(8,128)(2,1)S(1)}, u32[]{:S(2)}) copy-start(bf16[320,256]{1,0:T(8,128)(2,1)S(1)} %collective-permute-done.17.refs_19_) | copy-start | bytes 491524
  20.5 9.6 %collective-permute-start.4 = (bf16[4,128,256]{2,1,0:T(8,128)(2,1)S(1)}, bf16[4,128,256]{2,1,0:T(8,128)(2,1)S(1)}, u32[]{:S(2)}, u32[]{:S(2)}) collective-permute-start(bf16[4,128,256]{2,1,0:T(8,128)(2,1)S(1)} %get-tuple-element.28), channel_id=1, source_target_pairs={{0,16},{8,24},{16,0},{24,8},{1,17},{9,25},{17,1},{25,9},{2,18},{10... | collective-permute-start | bytes 786440 | tf_op jit(solution)/shard_map/ppermute | solution.py:279
  25.1 5.5 %collective-permute-start.18 = (bf16[320,256]{1,0:T(8,128)(2,1)S(1)}, bf16[320,256]{1,0:T(8,128)(2,1)S(1)}, u32[]{:S(2)}, u32[]{:S(2)}) collective-permute-start(bf16[320,256]{1,0:T(8,128)(2,1)S(1)} %collective-permute-done.17.refs_19_), channel_id=1, source_target_pairs={{0,2},{2,4},{4,6},{6,7},{7,5},{5,3},{3,1},{1,0},{8,10},{10,12},{12... | collective-permute-start | bytes 491528 | tf_op jit(solution)/shard_map/ppermute | solution.py:52
  26.7 6.9 %collective-permute-start.8 = (bf16[320,256]{1,0:T(8,128)(2,1)S(1)}, bf16[320,256]{1,0:T(8,128)(2,1)S(1)}, u32[]{:S(2)}, u32[]{:S(2)}) collective-permute-start(bf16[320,256]{1,0:T(8,128)(2,1)S(1)} %collective-permute-done.6.refs_6_), channel_id=1, source_target_pairs={{2,0},{4,2},{6,4},{7,6},{5,7},{3,5},{1,3},{0,1},{10,8},{12,10},{14... | collective-permute-start | bytes 491528 | tf_op jit(solution)/shard_map/ppermute | solution.py:55
  28.0 7.3 %collective-permute-start.11 = (bf16[320,256]{1,0:T(8,128)(2,1)S(1)}, bf16[320,256]{1,0:T(8,128)(2,1)S(1)}, u32[]{:S(2)}, u32[]{:S(2)}) collective-permute-start(bf16[320,256]{1,0:T(8,128)(2,1)S(1)} %collective-permute-done.9.refs_9_), channel_id=1, source_target_pairs={{2,0},{4,2},{6,4},{7,6},{5,7},{3,5},{1,3},{0,1},{10,8},{12,10},{14... | collective-permute-start | bytes 491528 | tf_op jit(solution)/shard_map/ppermute | solution.py:55
  28.3 7.3 %collective-permute-start.14 = (bf16[320,256]{1,0:T(8,128)(2,1)S(1)}, bf16[320,256]{1,0:T(8,128)(2,1)S(1)}, u32[]{:S(2)}, u32[]{:S(2)}) collective-permute-start(bf16[320,256]{1,0:T(8,128)(2,1)S(1)} %collective-permute-done.13.refs_16_), channel_id=1, source_target_pairs={{0,2},{2,4},{4,6},{6,7},{7,5},{5,3},{3,1},{1,0},{8,10},{10,12},{12... | collective-permute-start | bytes 491528 | tf_op jit(solution)/shard_map/ppermute | solution.py:52
  30.1 8.6 %collective-permute-start.5 = (bf16[4,128,256]{2,1,0:T(8,128)(2,1)S(1)}, bf16[4,128,256]{2,1,0:T(8,128)(2,1)S(1)}, u32[]{:S(2)}, u32[]{:S(2)}) collective-permute-start(bf16[4,128,256]{2,1,0:T(8,128)(2,1)S(1)} %get-tuple-element.29), channel_id=1, source_target_pairs={{0,24},{8,16},{16,8},{24,0},{1,25},{9,17},{17,9},{25,1},{2,26},{10... | collective-permute-start | bytes 786440 | tf_op jit(solution)/shard_map/ppermute | solution.py:279
  30.6 8.0 %collective-permute-start.19 = (bf16[320,256]{1,0:T(8,128)(2,1)S(1)}, bf16[320,256]{1,0:T(8,128)(2,1)S(1)}, u32[]{:S(2)}, u32[]{:S(2)}) collective-permute-start(bf16[320,256]{1,0:T(8,128)(2,1)S(1)} %collective-permute-done.18.refs_17_), channel_id=1, source_target_pairs={{0,2},{2,4},{4,6},{6,7},{7,5},{5,3},{3,1},{1,0},{8,10},{10,12},{12... | collective-permute-start | bytes 491528 | tf_op jit(solution)/shard_map/ppermute | solution.py:52
  33.6 7.1 %collective-permute-start.10 = (bf16[320,256]{1,0:T(8,128)(2,1)S(1)}, bf16[320,256]{1,0:T(8,128)(2,1)S(1)}, u32[]{:S(2)}, u32[]{:S(2)}) collective-permute-start(bf16[320,256]{1,0:T(8,128)(2,1)S(1)} %collective-permute-done.8.refs_8_), channel_id=1, source_target_pairs={{2,0},{4,2},{6,4},{7,6},{5,7},{3,5},{1,3},{0,1},{10,8},{12,10},{14... | collective-permute-start | bytes 491528 | tf_op jit(solution)/shard_map/ppermute | solution.py:55
  35.3 7.3 %collective-permute-start.16 = (bf16[320,256]{1,0:T(8,128)(2,1)S(1)}, bf16[320,256]{1,0:T(8,128)(2,1)S(1)}, u32[]{:S(2)}, u32[]{:S(2)}) collective-permute-start(bf16[320,256]{1,0:T(8,128)(2,1)S(1)} %collective-permute-done.11.refs_11_), channel_id=1, source_target_pairs={{2,0},{4,2},{6,4},{7,6},{5,7},{3,5},{1,3},{0,1},{10,8},{12,10},{14... | collective-permute-start | bytes 491528 | tf_op jit(solution)/shard_map/ppermute | solution.py:55
  35.6 7.0 %collective-permute-start.15 = (bf16[320,256]{1,0:T(8,128)(2,1)S(1)}, bf16[320,256]{1,0:T(8,128)(2,1)}, u32[]{:S(2)}, u32[]{:S(2)}) collective-permute-start(bf16[320,256]{1,0:T(8,128)(2,1)S(1)} %collective-permute-done.14.refs_14_), channel_id=1, source_target_pairs={{0,2},{2,4},{4,6},{6,7},{7,5},{5,3},{3,1},{1,0},{8,10},{10,12},{12... | collective-permute-start | bytes 491528 | tf_op jit(solution)/shard_map/ppermute | solution.py:52
  56.5 23.9 %copy-start.18 = (bf16[320,256]{1,0:T(8,128)(2,1)S(1)}, bf16[320,256]{1,0:T(8,128)(2,1)}, u32[]{:S(2)}) copy-start(bf16[320,256]{1,0:T(8,128)(2,1)} %get-tuple-element.44) | copy-start | bytes 491524
  56.5 25.3 %copy-start.17 = (bf16[320,256]{1,0:T(8,128)(2,1)S(1)}, bf16[320,256]{1,0:T(8,128)(2,1)}, u32[]{:S(2)}) copy-start(bf16[320,256]{1,0:T(8,128)(2,1)} %get-tuple-element.34) | copy-start | bytes 491524
  56.5 7.3 %collective-permute-start.20 = (bf16[320,256]{1,0:T(8,128)(2,1)}, bf16[320,256]{1,0:T(8,128)(2,1)S(1)}, u32[]{:S(2)}, u32[]{:S(2)}) collective-permute-start(bf16[320,256]{1,0:T(8,128)(2,1)} %get-tuple-element.31), channel_id=1, source_target_pairs={{0,2},{2,4},{4,6},{6,7},{7,5},{5,3},{3,1},{1,0},{8,10},{10,12},{12... | collective-permute-start | bytes 491528 | tf_op jit(solution)/shard_map/ppermute | solution.py:69
  59.3 9.2 %collective-permute-start.24 = (bf16[320,256]{1,0:T(8,128)(2,1)}, bf16[320,256]{1,0:T(8,128)(2,1)S(1)}, u32[]{:S(2)}, u32[]{:S(2)}) collective-permute-start(bf16[320,256]{1,0:T(8,128)(2,1)} %get-tuple-element.35), channel_id=1, source_target_pairs={{2,0},{4,2},{6,4},{7,6},{5,7},{3,5},{1,3},{0,1},{10,8},{12,10},{14... | collective-permute-start | bytes 491528 | tf_op jit(solution)/shard_map/ppermute | solution.py:76
  59.3 10.2 %collective-permute-start.27 = (bf16[320,256]{1,0:T(8,128)(2,1)}, bf16[320,256]{1,0:T(8,128)(2,1)S(1)}, u32[]{:S(2)}, u32[]{:S(2)}) collective-permute-start(bf16[320,256]{1,0:T(8,128)(2,1)} %get-tuple-element.39), channel_id=1, source_target_pairs={{0,2},{2,4},{4,6},{6,7},{7,5},{5,3},{3,1},{1,0},{8,10},{10,12},{12... | collective-permute-start | bytes 491528 | tf_op jit(solution)/shard_map/ppermute | solution.py:69
  63.4 9.5 %collective-permute-start.30 = (bf16[320,256]{1,0:T(8,128)(2,1)}, bf16[320,256]{1,0:T(8,128)(2,1)S(1)}, u32[]{:S(2)}, u32[]{:S(2)}) collective-permute-start(bf16[320,256]{1,0:T(8,128)(2,1)} %get-tuple-element.42), channel_id=1, source_target_pairs={{2,0},{4,2},{6,4},{7,6},{5,7},{3,5},{1,3},{0,1},{10,8},{12,10},{14... | collective-permute-start | bytes 491528 | tf_op jit(solution)/shard_map/ppermute | solution.py:76
  64.8 21.3 %copy-start.16 = (bf16[320,256]{1,0:T(8,128)(2,1)S(1)}, bf16[320,256]{1,0:T(8,128)(2,1)}, u32[]{:S(2)}) copy-start(bf16[320,256]{1,0:T(8,128)(2,1)} %get-tuple-element.45) | copy-start | bytes 491524
  64.8 9.2 %collective-permute-start.21 = (bf16[320,256]{1,0:T(8,128)(2,1)S(1)}, bf16[320,256]{1,0:T(8,128)(2,1)S(1)}, u32[]{:S(2)}, u32[]{:S(2)}) collective-permute-start(bf16[320,256]{1,0:T(8,128)(2,1)S(1)} %add_convert_fusion.9), channel_id=1, source_target_pairs={{0,2},{2,4},{4,6},{6,7},{7,5},{5,3},{3,1},{1,0},{8,10},{10,12},{12... | collective-permute-start | bytes 491528 | tf_op jit(solution)/shard_map/ppermute | solution.py:69
  69.4 7.6 %collective-permute-start.25 = (bf16[320,256]{1,0:T(8,128)(2,1)S(1)}, bf16[320,256]{1,0:T(8,128)(2,1)S(1)}, u32[]{:S(2)}, u32[]{:S(2)}) collective-permute-start(bf16[320,256]{1,0:T(8,128)(2,1)S(1)} %add_convert_fusion.6), channel_id=1, source_target_pairs={{2,0},{4,2},{6,4},{7,6},{5,7},{3,5},{1,3},{0,1},{10,8},{12,10},{14... | collective-permute-start | bytes 491528 | tf_op jit(solution)/shard_map/ppermute | solution.py:76
  70.5 7.1 %collective-permute-start.28 = (bf16[320,256]{1,0:T(8,128)(2,1)S(1)}, bf16[320,256]{1,0:T(8,128)(2,1)S(1)}, u32[]{:S(2)}, u32[]{:S(2)}) collective-permute-start(bf16[320,256]{1,0:T(8,128)(2,1)S(1)} %add_convert_fusion.4), channel_id=1, source_target_pairs={{0,2},{2,4},{4,6},{6,7},{7,5},{5,3},{3,1},{1,0},{8,10},{10,12},{12... | collective-permute-start | bytes 491528 | tf_op jit(solution)/shard_map/ppermute | solution.py:69
  73.9 6.5 %collective-permute-start.31 = (bf16[320,256]{1,0:T(8,128)(2,1)S(1)}, bf16[320,256]{1,0:T(8,128)(2,1)S(1)}, u32[]{:S(2)}, u32[]{:S(2)}) collective-permute-start(bf16[320,256]{1,0:T(8,128)(2,1)S(1)} %add_convert_fusion.2), channel_id=1, source_target_pairs={{2,0},{4,2},{6,4},{7,6},{5,7},{3,5},{1,3},{0,1},{10,8},{12,10},{14... | collective-permute-start | bytes 491528 | tf_op jit(solution)/shard_map/ppermute | solution.py:76
  75.0 6.9 %collective-permute-start.22 = (bf16[320,256]{1,0:T(8,128)(2,1)S(1)}, bf16[320,256]{1,0:T(8,128)(2,1)S(1)}, u32[]{:S(2)}, u32[]{:S(2)}) collective-permute-start(bf16[320,256]{1,0:T(8,128)(2,1)S(1)} %add_convert_fusion.8), channel_id=1, source_target_pairs={{0,2},{2,4},{4,6},{6,7},{7,5},{5,3},{3,1},{1,0},{8,10},{10,12},{12... | collective-permute-start | bytes 491528 | tf_op jit(solution)/shard_map/ppermute | solution.py:69
  77.1 10.3 %collective-permute-start.26 = (bf16[320,256]{1,0:T(8,128)(2,1)S(1)}, bf16[320,256]{1,0:T(8,128)(2,1)S(1)}, u32[]{:S(2)}, u32[]{:S(2)}) collective-permute-start(bf16[320,256]{1,0:T(8,128)(2,1)S(1)} %add_convert_fusion.5), channel_id=1, source_target_pairs={{2,0},{4,2},{6,4},{7,6},{5,7},{3,5},{1,3},{0,1},{10,8},{12,10},{14... | collective-permute-start | bytes 491528 | tf_op jit(solution)/shard_map/ppermute | solution.py:76
  77.6 9.9 %collective-permute-start.29 = (bf16[320,256]{1,0:T(8,128)(2,1)S(1)}, bf16[320,256]{1,0:T(8,128)(2,1)S(1)}, u32[]{:S(2)}, u32[]{:S(2)}) collective-permute-start(bf16[320,256]{1,0:T(8,128)(2,1)S(1)} %add_convert_fusion.3), channel_id=1, source_target_pairs={{0,2},{2,4},{4,6},{6,7},{7,5},{5,3},{3,1},{1,0},{8,10},{10,12},{12... | collective-permute-start | bytes 491528 | tf_op jit(solution)/shard_map/ppermute | solution.py:69
  80.5 5.6 %collective-permute-start.32 = (bf16[320,256]{1,0:T(8,128)(2,1)S(1)}, bf16[320,256]{1,0:T(8,128)(2,1)S(1)}, u32[]{:S(2)}, u32[]{:S(2)}) collective-permute-start(bf16[320,256]{1,0:T(8,128)(2,1)S(1)} %add_convert_fusion.1), channel_id=1, source_target_pairs={{2,0},{4,2},{6,4},{7,6},{5,7},{3,5},{1,3},{0,1},{10,8},{12,10},{14... | collective-permute-start | bytes 491528 | tf_op jit(solution)/shard_map/ppermute | solution.py:76
  81.9 5.5 %collective-permute-start.23 = (bf16[320,256]{1,0:T(8,128)(2,1)S(1)}, bf16[320,256]{1,0:T(8,128)(2,1)S(1)}, u32[]{:S(2)}, u32[]{:S(2)}) collective-permute-start(bf16[320,256]{1,0:T(8,128)(2,1)S(1)} %add_convert_fusion.7), channel_id=1, source_target_pairs={{0,2},{2,4},{4,6},{6,7},{7,5},{5,3},{3,1},{1,0},{8,10},{10,12},{12... | collective-permute-start | bytes 491528 | tf_op jit(solution)/shard_map/ppermute | solution.py:69
  86.2 7.1 %collective-permute-start.33 = (bf16[320,256]{1,0:T(8,128)(2,1)S(1)}, bf16[320,256]{1,0:T(8,128)(2,1)S(1)}, u32[]{:S(2)}, u32[]{:S(2)}) collective-permute-start(bf16[320,256]{1,0:T(8,128)(2,1)S(1)} %add_convert_fusion), channel_id=1, source_target_pairs={{2,0},{4,2},{6,4},{7,6},{5,7},{3,5},{1,3},{0,1},{10,8},{12,10},{14... | collective-permute-start | bytes 491528 | tf_op jit(solution)/shard_map/ppermute | solution.py:76
  94.3 26.2 %copy-start.12 = (bf16[320,256]{1,0:T(8,128)(2,1)}, bf16[320,256]{1,0:T(8,128)(2,1)S(1)}, u32[]{:S(2)}) copy-start(bf16[320,256]{1,0:T(8,128)(2,1)S(1)} %get-tuple-element.52.refs_5_) | copy-start | bytes 491524
  94.3 26.2 %copy-start.13 = (bf16[320,256]{1,0:T(8,128)(2,1)}, bf16[320,256]{1,0:T(8,128)(2,1)S(1)}, u32[]{:S(2)}) copy-start(bf16[320,256]{1,0:T(8,128)(2,1)S(1)} %get-tuple-element.53.refs_4_) | copy-start | bytes 491524
  94.3 7.1 %collective-permute-start.35 = (bf16[320,256]{1,0:T(8,128)(2,1)S(1)}, bf16[320,256]{1,0:T(8,128)(2,1)S(1)}, u32[]{:S(2)}, u32[]{:S(2)}) collective-permute-start(bf16[320,256]{1,0:T(8,128)(2,1)S(1)} %get-tuple-element.52.refs_5_), channel_id=1, source_target_pairs={{2,0},{4,2},{6,4},{7,6},{5,7},{3,5},{1,3},{0,1},{10,8},{12,10},{14... | collective-permute-start | bytes 491528 | tf_op jit(solution)/shard_map/ppermute | solution.py:55
  94.8 50.8 %copy-start.1 = (f32[2048,256]{1,0:T(8,128)S(1)}, f32[2048,256]{1,0:T(8,128)}, u32[]{:S(2)}) copy-start(f32[2048,256]{1,0:T(8,128)} %param.10) | copy-start | bytes 6291460
  94.8 50.8 %copy-start.5 = (s32[16]{0:T(128)S(1)}, s32[16]{0:T(128)}, u32[]{:S(2)}) copy-start(s32[16]{0:T(128)} %refs_0_.3) | copy-start | bytes 196
  94.8 7.1 %collective-permute-start.40 = (bf16[320,256]{1,0:T(8,128)(2,1)S(1)}, bf16[320,256]{1,0:T(8,128)(2,1)S(1)}, u32[]{:S(2)}, u32[]{:S(2)}) collective-permute-start(bf16[320,256]{1,0:T(8,128)(2,1)S(1)} %get-tuple-element.53.refs_4_), channel_id=1, source_target_pairs={{0,2},{2,4},{4,6},{6,7},{7,5},{5,3},{3,1},{1,0},{8,10},{10,12},{12... | collective-permute-start | bytes 491528 | tf_op jit(solution)/shard_map/ppermute | solution.py:52
  96.4 9.1 %collective-permute-start.45 = (bf16[320,256]{1,0:T(8,128)(2,1)S(1)}, bf16[320,256]{1,0:T(8,128)(2,1)S(1)}, u32[]{:S(2)}, u32[]{:S(2)}) collective-permute-start(bf16[320,256]{1,0:T(8,128)(2,1)S(1)} %get-tuple-element.52.refs_5_), channel_id=1, source_target_pairs={{0,2},{2,4},{4,6},{6,7},{7,5},{5,3},{3,1},{1,0},{8,10},{10,12},{12... | collective-permute-start | bytes 491528 | tf_op jit(solution)/shard_map/ppermute | solution.py:52
  98.3 7.9 %collective-permute-start.34 = (bf16[320,256]{1,0:T(8,128)(2,1)S(1)}, bf16[320,256]{1,0:T(8,128)(2,1)S(1)}, u32[]{:S(2)}, u32[]{:S(2)}) collective-permute-start(bf16[320,256]{1,0:T(8,128)(2,1)S(1)} %get-tuple-element.53.refs_4_), channel_id=1, source_target_pairs={{2,0},{4,2},{6,4},{7,6},{5,7},{3,5},{1,3},{0,1},{10,8},{12,10},{14... | collective-permute-start | bytes 491528 | tf_op jit(solution)/shard_map/ppermute | solution.py:55
  101.4 7.0 %collective-permute-start.37 = (bf16[320,256]{1,0:T(8,128)(2,1)S(1)}, bf16[320,256]{1,0:T(8,128)(2,1)S(1)}, u32[]{:S(2)}, u32[]{:S(2)}) collective-permute-start(bf16[320,256]{1,0:T(8,128)(2,1)S(1)} %collective-permute-done.35.refs_7_), channel_id=1, source_target_pairs={{2,0},{4,2},{6,4},{7,6},{5,7},{3,5},{1,3},{0,1},{10,8},{12,10},{14... | collective-permute-start | bytes 491528 | tf_op jit(solution)/shard_map/ppermute | solution.py:55
  102.0 7.1 %collective-permute-start.41 = (bf16[320,256]{1,0:T(8,128)(2,1)S(1)}, bf16[320,256]{1,0:T(8,128)(2,1)S(1)}, u32[]{:S(2)}, u32[]{:S(2)}) collective-permute-start(bf16[320,256]{1,0:T(8,128)(2,1)S(1)} %collective-permute-done.40.refs_18_), channel_id=1, source_target_pairs={{0,2},{2,4},{4,6},{6,7},{7,5},{5,3},{3,1},{1,0},{8,10},{10,12},{12... | collective-permute-start | bytes 491528 | tf_op jit(solution)/shard_map/ppermute | solution.py:52
  105.5 6.9 %collective-permute-start.46 = (bf16[320,256]{1,0:T(8,128)(2,1)S(1)}, bf16[320,256]{1,0:T(8,128)(2,1)S(1)}, u32[]{:S(2)}, u32[]{:S(2)}) collective-permute-start(bf16[320,256]{1,0:T(8,128)(2,1)S(1)} %collective-permute-done.45.refs_19_), channel_id=1, source_target_pairs={{0,2},{2,4},{4,6},{6,7},{7,5},{5,3},{3,1},{1,0},{8,10},{10,12},{12... | collective-permute-start | bytes 491528 | tf_op jit(solution)/shard_map/ppermute | solution.py:52
  106.2 6.5 %collective-permute-start.36 = (bf16[320,256]{1,0:T(8,128)(2,1)S(1)}, bf16[320,256]{1,0:T(8,128)(2,1)S(1)}, u32[]{:S(2)}, u32[]{:S(2)}) collective-permute-start(bf16[320,256]{1,0:T(8,128)(2,1)S(1)} %collective-permute-done.34.refs_6_), channel_id=1, source_target_pairs={{2,0},{4,2},{6,4},{7,6},{5,7},{3,5},{1,3},{0,1},{10,8},{12,10},{14... | collective-permute-start | bytes 491528 | tf_op jit(solution)/shard_map/ppermute | solution.py:55
  108.4 6.0 %collective-permute-start.39 = (bf16[320,256]{1,0:T(8,128)(2,1)S(1)}, bf16[320,256]{1,0:T(8,128)(2,1)S(1)}, u32[]{:S(2)}, u32[]{:S(2)}) collective-permute-start(bf16[320,256]{1,0:T(8,128)(2,1)S(1)} %collective-permute-done.37.refs_9_), channel_id=1, source_target_pairs={{2,0},{4,2},{6,4},{7,6},{5,7},{3,5},{1,3},{0,1},{10,8},{12,10},{14... | collective-permute-start | bytes 491528 | tf_op jit(solution)/shard_map/ppermute | solution.py:55
  109.1 6.1 %collective-permute-start.42 = (bf16[320,256]{1,0:T(8,128)(2,1)S(1)}, bf16[320,256]{1,0:T(8,128)(2,1)S(1)}, u32[]{:S(2)}, u32[]{:S(2)}) collective-permute-start(bf16[320,256]{1,0:T(8,128)(2,1)S(1)} %collective-permute-done.41.refs_16_), channel_id=1, source_target_pairs={{0,2},{2,4},{4,6},{6,7},{7,5},{5,3},{3,1},{1,0},{8,10},{10,12},{12... | collective-permute-start | bytes 491528 | tf_op jit(solution)/shard_map/ppermute | solution.py:52
  112.4 5.3 %collective-permute-start.47 = (bf16[320,256]{1,0:T(8,128)(2,1)S(1)}, bf16[320,256]{1,0:T(8,128)(2,1)S(1)}, u32[]{:S(2)}, u32[]{:S(2)}) collective-permute-start(bf16[320,256]{1,0:T(8,128)(2,1)S(1)} %collective-permute-done.46.refs_17_), channel_id=1, source_target_pairs={{0,2},{2,4},{4,6},{6,7},{7,5},{5,3},{3,1},{1,0},{8,10},{10,12},{12... | collective-permute-start | bytes 491528 | tf_op jit(solution)/shard_map/ppermute | solution.py:52
  112.7 5.3 %collective-permute-start.38 = (bf16[320,256]{1,0:T(8,128)(2,1)S(1)}, bf16[320,256]{1,0:T(8,128)(2,1)S(1)}, u32[]{:S(2)}, u32[]{:S(2)}) collective-permute-start(bf16[320,256]{1,0:T(8,128)(2,1)S(1)} %collective-permute-done.36.refs_8_), channel_id=1, source_target_pairs={{2,0},{4,2},{6,4},{7,6},{5,7},{3,5},{1,3},{0,1},{10,8},{12,10},{14... | collective-permute-start | bytes 491528 | tf_op jit(solution)/shard_map/ppermute | solution.py:55
  114.5 5.3 %collective-permute-start.44 = (bf16[320,256]{1,0:T(8,128)(2,1)S(1)}, bf16[320,256]{1,0:T(8,128)(2,1)S(1)}, u32[]{:S(2)}, u32[]{:S(2)}) collective-permute-start(bf16[320,256]{1,0:T(8,128)(2,1)S(1)} %collective-permute-done.39.refs_11_), channel_id=1, source_target_pairs={{2,0},{4,2},{6,4},{7,6},{5,7},{3,5},{1,3},{0,1},{10,8},{12,10},{14... | collective-permute-start | bytes 491528 | tf_op jit(solution)/shard_map/ppermute | solution.py:55
  115.2 5.3 %collective-permute-start.43 = (bf16[320,256]{1,0:T(8,128)(2,1)S(1)}, bf16[320,256]{1,0:T(8,128)(2,1)S(1)}, u32[]{:S(2)}, u32[]{:S(2)}) collective-permute-start(bf16[320,256]{1,0:T(8,128)(2,1)S(1)} %collective-permute-done.42.refs_14_), channel_id=1, source_target_pairs={{0,2},{2,4},{4,6},{6,7},{7,5},{5,3},{3,1},{1,0},{8,10},{10,12},{12... | collective-permute-start | bytes 491528 | tf_op jit(solution)/shard_map/ppermute | solution.py:52
  131.5 1.9 %collective-permute-start.48 = (bf16[4,128,256]{2,1,0:T(8,128)(2,1)}, bf16[4,128,256]{2,1,0:T(8,128)(2,1)S(1)}, u32[]{:S(2)}, u32[]{:S(2)}) collective-permute-start(bf16[4,128,256]{2,1,0:T(8,128)(2,1)} %get-tuple-element.47), channel_id=1, source_target_pairs={{0,8},{8,0},{16,24},{24,16},{1,9},{9,1},{17,25},{25,17},{2,10},{10... | collective-permute-start | bytes 786440 | tf_op jit(solution)/shard_map/ppermute | solution.py:287
  131.6 9.4 %collective-permute-start.49 = (bf16[4,128,256]{2,1,0:T(8,128)(2,1)}, bf16[4,128,256]{2,1,0:T(8,128)(2,1)S(1)}, u32[]{:S(2)}, u32[]{:S(2)}) collective-permute-start(bf16[4,128,256]{2,1,0:T(8,128)(2,1)} %get-tuple-element.48), channel_id=1, source_target_pairs={{0,16},{8,24},{16,0},{24,8},{1,17},{9,25},{17,1},{25,9},{2,18},{10... | collective-permute-start | bytes 786440 | tf_op jit(solution)/shard_map/ppermute | solution.py:287
  133.1 12.6 %collective-permute-start.50 = (bf16[4,128,256]{2,1,0:T(8,128)(2,1)}, bf16[4,128,256]{2,1,0:T(8,128)(2,1)S(1)}, u32[]{:S(2)}, u32[]{:S(2)}) collective-permute-start(bf16[4,128,256]{2,1,0:T(8,128)(2,1)} %get-tuple-element.49), channel_id=1, source_target_pairs={{0,24},{8,16},{16,8},{24,0},{1,25},{9,17},{17,9},{25,1},{2,26},{10... | collective-permute-start | bytes 786440 | tf_op jit(solution)/shard_map/ppermute | solution.py:287
  (36 other events, 349.1 us)

commit v2 on v0

v2 whole, which is shorter than its diff:
```python
import functools

import jax
import jax.numpy as jnp
from jax import lax
from jax.experimental import pallas as pl
from jax.experimental.pallas import tpu as pltpu
from jax.sharding import PartitionSpec as P

learn_rate = 0.01
weight_decay = 0.05
line_len = 4
batch = 8

VMEM = pltpu.VMEM
SMEM = pltpu.SMEM
NT = (((1,), (1,)), ((), ()))


def spec(space):
    return pl.BlockSpec(memory_space=space)


def near(array):
    return pltpu.with_memory_space_constraint(array, VMEM)


def away(array):
    return pltpu.with_memory_space_constraint(array, pltpu.HBM)


def params(mib):
    return pltpu.CompilerParams(vmem_limit_bytes=mib * 1024 * 1024)


def cost(pairs, block, rank):
    return pl.CostEstimate(
        flops=pairs * 4 * block * block * rank,
        bytes_accessed=pairs * 256 * 1024,
        transcendentals=0,
    )


def ring_place(col, col_count):
    width = max(col_count // line_len, 1)
    depth = col_count // width
    across, along = col % width, col // width
    return across * depth + jnp.where(across % 2 == 0, along, depth - 1 - along)


def ring_steps(col_count):
    width = max(col_count // line_len, 1)
    depth = col_count // width
    order = []
    for place in range(col_count):
        across, along = divmod(place, depth)
        along = along if across % 2 == 0 else depth - 1 - along
        order.append(along * width + across)
    ahead = [(order[p], order[(p + 1) % col_count]) for p in range(col_count)]
    back = [(b, a) for a, b in ahead]
    return ahead, back


class Plan:
    def __init__(self, col_count, rows, block):
        self.count = col_count
        self.far = col_count // 2
        self.rows, self.block = rows, block
        self.blocks = rows // block
        first = (self.blocks + 1) // 2 * block
        self.halves = [(0, first), (first, rows)]
        self.order = [0]
        for m in range(1, self.far):
            self.order += [m, col_count - m]
        self.order.append(self.far)
        self.groups = [self.order[:3], self.order[3:-3], self.order[-3:]]
        self.starts = [self.order.index(g[0]) * self.blocks for g in self.groups]

    def arrival(self, offset):
        back = self.count - offset
        return jnp.where(
            offset == 0,
            0,
            jnp.where(
                offset == self.far,
                self.count - 1,
                jnp.where(offset < self.far, 2 * offset - 1, 2 * back),
            ),
        )

    def cuts(self, offset):
        return self.halves if offset == self.far else [(0, self.rows)]


def after(value, mark):
    return jnp.where(mark[0, :1] < jnp.inf, value, jnp.zeros_like(value))


def gather_ring(low, plan, mark_last=lambda pieces: None):
    steps = ring_steps(plan.count)
    moved = [low, low]
    pieces = {0: [low]}
    for step in range(1, plan.far):
        for way in (0, 1):
            moved[way] = lax.ppermute(moved[way], "col", steps[way])
            pieces[step if way else plan.count - step] = [moved[way]]
    mark = mark_last(pieces)
    parts = [moved[way][a:b] for way, (a, b) in enumerate(plan.halves)]
    if mark is not None:
        parts = [after(part, mark) for part in parts]
    pieces[plan.far] = [lax.ppermute(parts[way], "col", steps[way]) for way in (0, 1)]
    return pieces


def add_up(moved, piece):
    return (moved.astype(jnp.float32) + piece.astype(jnp.float32)).astype(jnp.bfloat16)


def scatter_ring(pieces, plan):
    steps = ring_steps(plan.count)
    first = plan.halves[0][1]
    moved = [lax.ppermute(pieces[plan.far][way], "col", steps[way]) for way in (0, 1)]
    for step in range(plan.far - 1, 0, -1):
        for way in (0, 1):
            (value,) = pieces[plan.count - step if way else step]
            if step == plan.far - 1:
                parts = [value[:first], value[first:]]
                parts[way] = add_up(moved[way], parts[way])
                value = jnp.concatenate(parts, axis=0)
            else:
                value = add_up(moved[way], value)
            moved[way] = lax.ppermute(value, "col", steps[way])
    return (
        pieces[0][0].astype(jnp.float32)
        + moved[0].astype(jnp.float32)
        + moved[1].astype(jnp.float32)
    )


def pick_kernel(row_count, per_owner, row_ref, *refs):
    ids = refs[:row_count]
    table, *outs = refs[row_count:-2]
    held, sems = refs[-2:]
    row = row_ref[0]

    def block_of(k, i):
        n = k * per_owner + i
        block = ids[k][row * per_owner + i]
        return pltpu.make_async_copy(table.at[block], held.at[n], sems.at[n])

    order = [(k, i) for k in reversed(range(row_count)) for i in range(per_owner)]
    for k, i in order:
        block_of(k, i).start()
    for k, i in order:
        block_of(k, i).wait()
        out = outs[k] if k < 2 else outs[1 + k // 2]
        at = i if k < 2 else k % 2 * per_owner + i
        out[at] = held[k * per_owner + i].astype(jnp.bfloat16)


def pick(row, ids, table, per_owner):
    row_count = len(ids)
    block, rank = table.shape[1:]
    heights = [per_owner] * 2 + [2 * per_owner] * (row_count // 2 - 1)
    shapes = [VMEM((height, block, rank), jnp.bfloat16) for height in heights]
    asked = row_count * per_owner
    return pl.pallas_call(
        functools.partial(pick_kernel, row_count, per_owner),
        out_shape=shapes,
        in_specs=[spec(SMEM)] * (row_count + 1) + [spec(pltpu.HBM)],
        out_specs=[spec(VMEM)] * len(shapes),
        scratch_shapes=[
            VMEM((asked, block, rank), jnp.float32),
            pltpu.SemaphoreType.DMA((asked,)),
        ],
        compiler_params=params(8),
    )(row, *ids, away(table))


def join_kernel(per_owner, first, *refs):
    out = refs[-1]
    out[0:per_owner] = first[...]
    for x in range(1, out.shape[0] // per_owner):
        out[x * per_owner : (x + 1) * per_owner] = refs[x - 1][per_owner:]


def join(first, moved, per_owner, marks):
    shape = ((1 + len(moved)) * per_owner,) + first.shape[1:]
    inputs = [first, *moved, *marks]
    return pl.pallas_call(
        functools.partial(join_kernel, per_owner),
        out_shape=VMEM(shape, first.dtype),
        in_specs=[spec(VMEM)] * len(inputs),
        out_specs=spec(VMEM),
        compiler_params=params(1),
    )(*map(near, inputs))


def list_kernel(cfg, row_ref, live_ref, ids_ref, observed, *refs):
    row_count, per_owner, kinds, starts, room = cfg
    pairs_ref, counts_ref, held, sem = refs[-4:]
    copy = pltpu.make_async_copy(observed, held, sem)
    copy.start()
    row = row_ref[0]
    for g in range(len(starts)):
        counts_ref[g] = 0
    for owner in range(row_count):

        @pl.loop(0, live_ref[owner])
        def _(i):
            slot = owner * per_owner + i
            sku_at = (row ^ owner) * per_owner + i
            for n in range(kinds):
                at = ids_ref[slot, n]
                group = jnp.int32(0)
                for start in starts[1:]:
                    group += (at >= start).astype(jnp.int32)
                filled = counts_ref[group]
                pairs_ref[group * room + filled] = at + n * 256 + sku_at * 4096 + slot * 1048576
                counts_ref[group] = filled + 1

    for g, start in enumerate(starts):
        for q in range(batch - 1):
            blank = start + row_count * per_owner * 4096
            pairs_ref[g * room + counts_ref[g] + q] = jnp.int32(blank)
    copy.wait()


def list_pairs(row, live, ids, observed, plan, row_count, per_owner, kinds, marks):
    room = row_count * per_owner * kinds + batch
    groups = len(plan.groups)
    return pl.pallas_call(
        functools.partial(list_kernel, (row_count, per_owner, kinds, plan.starts, room)),
        out_shape=[
            jax.ShapeDtypeStruct((groups * room,), jnp.int32),
            jax.ShapeDtypeStruct((groups,), jnp.int32),
            VMEM(observed.shape, observed.dtype),
        ],
        in_specs=[spec(SMEM)] * 3 + [spec(pltpu.HBM)] + [spec(VMEM)] * len(marks),
        out_specs=[spec(SMEM)] * 2 + [spec(VMEM)],
        scratch_shapes=[pltpu.SemaphoreType.DMA],
        compiler_params=params(1),
    )(row, live, ids, away(observed), *map(near, marks))


def load_skus(held, refs, starts):
    count = refs[0].shape[0]
    for k, (ref, start) in enumerate(zip(refs, starts)):
        held[pl.ds(k * count, count)] = ref[start : start + count]
    held[len(refs) * count] = jnp.zeros_like(held[0])


def load_table(table, refs):
    at = 0
    for ref in refs:
        table[pl.ds(at, ref.shape[0]), :] = ref[...]
        at += ref.shape[0]


def for_pairs(pairs_ref, counts_ref, room, groups, base, block, body):
    for g in groups:

        @pl.loop(0, pl.cdiv(counts_ref[g], batch))
        def _(b):
            entries = []
            for q in range(batch):
                e = pairs_ref[g * room + b * batch + q]
                at = pl.multiple_of(((e & 255) - base) * block, block)
                entries.append((at, (e >> 8) & 15, (e >> 12) & 255, e >> 20))
            body(entries)


def first_kernel(cfg, pairs_ref, counts_ref, observed, *refs):
    sku_starts, piece_count, out_count, room, groups, base, block = cfg
    sku_count = len(sku_starts)
    skus = refs[:sku_count]
    pieces = refs[sku_count : sku_count + piece_count]
    outs = refs[-3 - out_count : -3]
    held, table, grad = refs[-3:]
    load_skus(held, skus, sku_starts)
    load_table(table, pieces)
    grad[...] = jnp.zeros_like(grad)

    def body(entries):
        terms = []
        for at, n, sku_at, slot in entries:
            sku = held[sku_at]
            predicted = lax.dot_general(
                table[pl.ds(at, block), :], sku, NT, preferred_element_type=jnp.float32
            )
            misfit = predicted - observed[slot, n].T.astype(jnp.float32)
            terms.append(
                jnp.dot(misfit.astype(jnp.bfloat16), sku, preferred_element_type=jnp.float32)
            )
        for (at, _, _, _), term in zip(entries, terms):
            grad[pl.ds(at, block), :] += term

    for_pairs(pairs_ref, counts_ref, room, groups, base, block, body)
    at = 0
    for out in outs:
        out[...] = grad[pl.ds(at, out.shape[0]), :].astype(jnp.bfloat16)
        at += out.shape[0]


def first_pass(pairs, counts, observed, skus, pieces, plan, groups, marks):
    offsets = [d for g in groups for d in plan.groups[g]]
    given = [piece for d in offsets for piece in pieces[d]]
    cuts = [plan.cuts(d) for d in offsets]
    heights = [b - a for spans in cuts for a, b in spans]
    skus, sku_starts = zip(*skus)
    block, rank = plan.block, skus[0].shape[2]
    room = pairs.shape[0] // len(plan.groups)
    slots = len(skus) * skus[0].shape[0]
    cfg = (sku_starts, len(given), len(heights), room, groups, plan.starts[groups[0]], block)
    table = (len(offsets) * plan.rows, rank)
    inputs = [observed, *skus, *given, *marks]
    out = pl.pallas_call(
        functools.partial(first_kernel, cfg),
        out_shape=[VMEM((height, rank), jnp.bfloat16) for height in heights],
        in_specs=[spec(SMEM)] * 2 + [spec(VMEM)] * len(inputs),
        out_specs=[spec(VMEM)] * len(heights),
        scratch_shapes=[
            VMEM((slots + 1, block, rank), jnp.bfloat16),
            VMEM(table, jnp.bfloat16),
            VMEM(table, jnp.float32),
        ],
        compiler_params=params(24),
        cost_estimate=cost(len(offsets) * room // plan.count, block, rank),
    )(pairs, counts, *map(near, inputs))
    out = list(out)
    return {d: [out.pop(0) for _ in spans] for d, spans in zip(offsets, cuts)}


def second_kernel(cfg, row_ref, live_ref, ids_ref, observed, *refs):
    ks, sku_starts, per_owner, kinds, block = cfg
    skus, pieces = refs[: len(ks)], refs[len(ks) : -1 - len(ks)]
    outs, table = refs[-1 - len(ks) : -1], refs[-1]
    load_table(table, pieces)
    row = row_ref[0]
    for k, sku_ref, start, out in zip(ks, skus, sku_starts, outs):
        out[...] = jnp.zeros_like(out)
        owner = row ^ k

        @pl.loop(0, live_ref[owner])
        def _(i):
            slot = owner * per_owner + i
            stores, measured = [], []
            for n in range(kinds):
                at = pl.multiple_of(ids_ref[slot, n] * block, block)
                stores.append(table[pl.ds(at, block), :])
                measured.append(observed[slot, n])
            store = jnp.concatenate(stores, axis=0)
            predicted = lax.dot_general(
                sku_ref[start + i], store, NT, preferred_element_type=jnp.float32
            )
            misfit = predicted - jnp.concatenate(measured, axis=1).astype(jnp.float32)
            out[i] = jnp.dot(
                misfit.astype(jnp.bfloat16), store, preferred_element_type=jnp.float32
            ).astype(jnp.bfloat16)


def second_pass(ks, row, live, ids, observed, skus, pieces, plan, per_owner):
    kept, sku_starts = zip(*[skus[k] for k in ks])
    kinds, block, rank = observed.shape[1], plan.block, kept[0].shape[2]
    shape = (per_owner, block, rank)
    inputs = [observed, *kept, *[piece for d in plan.order for piece in pieces[d]]]
    return pl.pallas_call(
        functools.partial(second_kernel, (ks, sku_starts, per_owner, kinds, block)),
        out_shape=[VMEM(shape, jnp.bfloat16)] * len(ks),
        in_specs=[spec(SMEM)] * 3 + [spec(VMEM)] * len(inputs),
        out_specs=[spec(VMEM)] * len(ks),
        scratch_shapes=[VMEM((plan.count * plan.rows, rank), jnp.bfloat16)],
        compiler_params=params(16),
        cost_estimate=cost(len(ks) * per_owner * kinds, block, rank),
    )(row, live, ids, *map(near, inputs))


def take_terms(held, ids, terms, row, per_owner):
    blocks = []
    for block_ids, term in zip(ids, terms):
        for i in range(per_owner):
            block = block_ids[row * per_owner + i]
            held[block] -= learn_rate * term[i].astype(jnp.float32)
            blocks.append(block)
    return blocks


def copy_out(held, out, blocks, sems):
    copies = [
        pltpu.make_async_copy(held.at[block], out.at[block], sems.at[n])
        for n, block in enumerate(blocks)
    ]
    for copy in copies:
        copy.start()
    for copy in copies:
        copy.wait()


def base_kernel(count, per_owner, row_ref, *refs):
    ids, sku, terms = refs[:count], refs[count], refs[count + 1 : -3]
    held, out, sems = refs[-3:]
    held[...] = sku[...] * (1.0 - learn_rate * weight_decay)
    take_terms(held, ids, terms, row_ref[0], per_owner)
    copy_out(held, out, range(sku.shape[0]), sems)


def base_step(row, ids, sku, terms, per_owner):
    return pl.pallas_call(
        functools.partial(base_kernel, len(ids), per_owner),
        out_shape=[VMEM(sku.shape, jnp.float32), pltpu.HBM(sku.shape, jnp.float32)],
        in_specs=[spec(SMEM)] * (len(ids) + 1) + [spec(VMEM)] * (1 + len(ids)),
        out_specs=[spec(VMEM), spec(pltpu.HBM)],
        scratch_shapes=[pltpu.SemaphoreType.DMA((sku.shape[0],))],
        compiler_params=params(8),
    )(row, *ids, sku, *map(near, terms))


def finish_kernel(count, per_owner, row_ref, *refs):
    ids, sku, terms = refs[:count], refs[count], refs[count + 1 : 2 * count + 1]
    out, held, sems = refs[-3:]
    for block_ids in ids:
        for i in range(per_owner):
            block = block_ids[row_ref[0] * per_owner + i]
            held[block] = sku[block]
    blocks = take_terms(held, ids, terms, row_ref[0], per_owner)
    copy_out(held, out, blocks, sems)


def finish_step(row, ids, held, out, terms, per_owner):
    return pl.pallas_call(
        functools.partial(finish_kernel, len(ids), per_owner),
        out_shape=pltpu.HBM(out.shape, jnp.float32),
        in_specs=[spec(SMEM)] * (len(ids) + 1)
        + [spec(VMEM)] * (1 + len(ids))
        + [spec(pltpu.HBM)],
        out_specs=spec(pltpu.HBM),
        scratch_shapes=[
            VMEM(out.shape, jnp.float32),
            pltpu.SemaphoreType.DMA((len(ids) * per_owner,)),
        ],
        input_output_aliases={2 + 2 * len(ids): 0},
        compiler_params=params(4),
    )(row, *ids, near(held), *map(near, terms), away(out))


def local(observed, sku_ids, store_ids, live_slot_counts, sku_factors, store_factors):
    row_count = lax.axis_size("row")
    per_owner = observed.shape[0] // row_count
    kinds, block = observed.shape[1:3]
    rank = sku_factors.shape[1]
    plan = Plan(lax.axis_size("col"), store_factors.shape[0], block)
    row_vec = lax.axis_index("row").reshape(1).astype(jnp.int32)
    live = live_slot_counts.reshape(row_count)
    sku = sku_factors.reshape(-1, block, rank)

    swaps = [[(r, r ^ k) for r in range(row_count)] for k in range(row_count)]
    asked = [sku_ids] + [lax.ppermute(sku_ids, "row", swaps[k]) for k in range(1, row_count)]
    picked = pick(row_vec, asked, sku, per_owner)
    moved = [
        lax.ppermute(picked[1 + x], "row", swaps[2 * x]) for x in range(1, row_count // 2)
    ]

    place = ring_place(lax.axis_index("col"), plan.count)
    owner_place = ring_place(store_ids // plan.blocks, plan.count)
    arrival = plan.arrival((owner_place - place) % plan.count)
    ids = arrival * plan.blocks + store_ids % plan.blocks
    made = []

    def prepare(pieces):
        early = pieces[1] + pieces[plan.count - 1]
        made.extend(
            list_pairs(
                row_vec, live, ids, observed, plan, row_count, per_owner, kinds, early
            )
        )
        late = pieces[plan.far - 2] + pieces[plan.far + 2] + [made[2]]
        made.append(
            lax.ppermute(join(picked[1], moved, per_owner, late), "row", swaps[1])
        )
        return made[3][0]

    pieces = gather_ring(store_factors.astype(jnp.bfloat16), plan, prepare)
    pairs, counts, observed, passed = made
    skus = [(picked[0], 0), (passed, 0)]
    for x, both in enumerate(moved, 1):
        skus += [(both, 0), (passed, x * per_owner)]

    grads, marks = {}, []
    for group in (0, 2, 1):
        if plan.groups[group]:
            some = first_pass(pairs, counts, observed, skus, pieces, plan, [group], marks)
            grads.update(some)
            marks = some[plan.groups[group][0]][:1]
    own_grad = scatter_ring(grads, plan)
    new_store = store_factors - learn_rate * (own_grad + weight_decay * store_factors)
    new_pieces = gather_ring(new_store.astype(jnp.bfloat16), plan)

    terms = [None] * row_count
    for ks in (list(range(2, row_count)), [1, 0]):
        out = second_pass(ks, row_vec, live, ids, observed, skus, new_pieces, plan, per_owner)
        for k, term in zip(ks, out):
            terms[k] = lax.ppermute(term, "row", swaps[k]) if k else term
    held, new_sku = base_step(row_vec, asked[:2], sku, terms[:2], per_owner)
    new_sku = finish_step(row_vec, asked[2:], held, new_sku, terms[2:], per_owner)
    return new_sku.reshape(sku_factors.shape), new_store


def solution(mesh):
    placed = (
        P(("row", "col"), None, None, None),
        P(("row", "col")),
        P(("row", "col"), None),
        P("row", "col", None),
        P(("row", "col"), None),
        P(("row", "col"), None),
    )
    return jax.shard_map(
        local,
        mesh=mesh,
        in_specs=placed,
        out_specs=(P(("row", "col"), None), P(("row", "col"), None)),
        check_vma=False,
    )
```

time: 371 us -> 141 us (0.38)
  waiting for transfers between devices: 213 us -> 73 us
  local copies, waits for them, and re-layouts: 54.8 us -> 1.32 us
  matrix products: 53.3 us -> 0 us
  starting transfers between devices: 6.85 us -> 34.3 us
  Pallas kernels: 0 us -> 26 us
  other arithmetic: 28.1 us -> 2.76 us
  between operations: 13.9 us -> 1.55 us
    all_gather x3 -> x0, waiting for transfers between devices: 130 us -> none  [the longest x1 51.7 us: local(): lax.all_gather(own_store.astype(jnp.bfloat16), 'col', axis=0, tiled=True)]
    ppermute x0 -> x32, waiting for transfers between devices: none -> 73 us  [the longest x12 25.6 us: gather_ring(): moved[way] = lax.ppermute(moved[way], 'col', steps[way])]
    reduce_scatter x1 -> x0, waiting for transfers between devices: 69.2 us -> none  [local(): lax.psum_scatter(store_grad.astype(jnp.bfloat16), 'col', scatter_dimensio...]
    dot_general x15 -> x0, matrix products: 53.3 us -> none  [the longest x2 17.3 us: first_pass(): jnp.einsum('skab,sar->skbr', misfit, factor_rows, preferred_element_type=...]
    while x15 -> x0, local copies, waits for them, and re-layouts: 38.1 us -> none
    ppermute x0 -> x32, starting transfers between devices: none -> 34.3 us  [the longest x12 14.6 us: gather_ring(): moved[way] = lax.ppermute(moved[way], 'col', steps[way])]
    pallas_call x0 -> x10, Pallas kernels: none -> 26 us  [the longest x3 10 us: first_pass(): pl.pallas_call(functools.partial(first_kernel, cfg), out_shape=[VMEM((hei...]
    all_to_all x2 -> x0, waiting for transfers between devices: 13.6 us -> none  [the longest x1 13.6 us: local(): lax.all_to_all(sku_terms.astype(jnp.bfloat16), 'row', split_axis=0, conca...]
  transfers between devices with their start and end apart: 6 -> 32, of which waited for: 5 -> 20; matrix products, arithmetic and copies ran while one was open for 12% -> 1% of each run, Pallas kernels for 0% -> 14%
where the time goes in v2:
time: 141 us; the launch traced here: 139 us
  waiting for transfers between devices  73 us (52%)
  starting transfers between devices  34.3 us (24%)
  Pallas kernels  26 us (18%)
  other arithmetic  2.76 us (2%)
  between operations  1.55 us (1%)
    ppermute x12, waiting for transfers between devices, gather_ring(): moved[way] = lax.ppermute(moved[way], 'col', steps[way])  25.6 us
    ppermute x6, waiting for transfers between devices, scatter_ring(): moved[way] = lax.ppermute(value, 'col', steps[way])  20.6 us
    ppermute x12, starting transfers between devices, gather_ring(): moved[way] = lax.ppermute(moved[way], 'col', steps[way])  14.6 us
    pallas_call x3, Pallas kernels, first_pass(): pl.pallas_call(functools.partial(first_kernel, cfg), out_shape=[VMEM((hei...  10 us
    ppermute x6, starting transfers between devices, scatter_ring(): moved[way] = lax.ppermute(value, 'col', steps[way])  9.35 us
    ppermute x3, waiting for transfers between devices, local(): terms[k] = lax.ppermute(term, 'row', swaps[k]) if k else term  8.55 us
    ppermute x1, waiting for transfers between devices, local(): lax.ppermute(picked[1 + x], 'row', swaps[2 * x])  7.16 us
    pallas_call x2, Pallas kernels, second_pass(): pl.pallas_call(functools.partial(second_kernel, (ks, sku_starts, per_owne...  6.16 us
  transfers between devices with their start and end apart: 32, of which 20 were waited for; matrix products, arithmetic and copies ran while one was open for 1% of the time, Pallas kernels for 14%

profile of v2, /device:TPU:0, one launch (start us, length us, event | category | flops | bytes accessed | tf_op | source)
XLA Modules:
  0.0 139.0 jit_solution(5890796872307253728)
XLA Ops:
  0.6 1.1 convert_element_type.69.refs_4_
  1.8 3.1 %collective-permute-start.4 = (bf16[640,256]{1,0:T(8,128)(2,1)S(1)}, bf16[640,256]{1,0:T(8,128)(2,1)S(1)}, u32[]{:S(2)}, u32[]{:S(2)}) collective-permute-start(bf16[640,256]{1,0:T(8,128)(2,1)S(1)} %convert_element_type.69.refs_4_), channel_id=1, source_target_pairs={{0,2},{2,4},{4,6},{6,7},{7,5},{5,3},{3,1},{1,0},{8,10},{10,12},{12... | collective-permute-start | bytes 983048 | tf_op jit(solution)/shard_map/ppermute | solution.py:105
  4.9 2.0 %collective-permute-start.1 = (s32[16]{0:T(128)}, s32[16]{0:T(128)S(1)}, u32[]{:S(2)}, u32[]{:S(2)}) collective-permute-start(s32[16]{0:T(128)} %refs_0_.3), channel_id=1, source_target_pairs={{0,24},{8,16},{16,8},{24,0},{1,25},{9,17},{17,9},{25,1},{2,26},{10... | collective-permute-start | bytes 200 | tf_op jit(solution)/shard_map/ppermute | solution.py:457
  6.9 0.1 collective-permute-start
  7.0 1.3 collective-permute-done.1.refs_3_.refs_1_
  8.3 2.2 %collective-permute-done.refs_2_.refs_0_ = s32[16]{0:T(128)S(1)} collective-permute-done((s32[16]{0:T(128)}, s32[16]{0:T(128)S(1)}, u32[]{:S(2)}, u32[]{:S(2)}) %collective-permute-start) | collective-permute-done | bytes 96 | tf_op jit(solution)/shard_map/ppermute | solution.py:457
  10.6 0.7 copy-done.2
  11.2 2.3 %shard_map.78 = (bf16[4,128,256]{2,1,0:T(8,128)(2,1)S(1)}, bf16[4,128,256]{2,1,0:T(8,128)(2,1)S(1)}, bf16[8,128,256]{2,1,0:T(8,128)(2,1)S(1)}) custom-call(s32[1]{0:T(128)} %bitcast.row_ref, s32[16]{0:T(128)S(1)} %copy-done.2, s32[16]{0:T(128)S(1)} %collective-permute-done.2.refs_1_, s32[16]{0:T(128)S(1)} %collective-permute-done.refs_2_.refs_0_, ...), custom_call_target="tpu_custom_call" | custom-call | tf_op jit(solution)/shard_map/pallas_call | solution.py:167
  13.6 0.2 collective-permute-start.5
  13.8 2.0 %collective-permute-start.7 = (bf16[640,256]{1,0:T(8,128)(2,1)S(1)}, bf16[640,256]{1,0:T(8,128)(2,1)S(1)}, u32[]{:S(2)}, u32[]{:S(2)}) collective-permute-start(bf16[640,256]{1,0:T(8,128)(2,1)S(1)} %collective-permute-done.4.refs_1_.refs_6_), channel_id=1, source_target_pairs={{0,2},{2,4},{4,6},{6,7},{7,5},{5,3},{3,1},{1,0},{8,10},{10,12},{12... | collective-permute-start | bytes 983048 | tf_op jit(solution)/shard_map/ppermute | solution.py:105
  15.8 0.1 collective-permute-start.6
  15.8 0.1 copy.9
  16.0 3.5 %shard_map.77 = (s32[408]{0:T(512)S(1)}, s32[3]{0:T(128)S(1)}, bf16[16,8,128,128]{3,2,1,0:T(8,128)(2,1)S(1)}) custom-call(s32[1]{0:T(128)} %bitcast.row_ref, s32[4]{0:T(128)S(1)} %bitcast.9, s32[16,8]{1,0:T(8,128)S(1)} %fusion.5.ids_ref, bf16[16,8,128,128]{3,2,1,0:T(8,128)(2,1)} %observed.1, bf16[640,256]{1,0:T(8,128)(2,1)S(1)} %collective-permute-done.3.refs_0_.refs_5_, ...), custom_call_target="tpu_custom_call" | custom-call | tf_op jit(solution)/shard_map/pallas_call | solution.py:232
  19.5 7.2 %collective-permute-done.5.refs_0_.refs_2_ = bf16[8,128,256]{2,1,0:T(8,128)(2,1)S(1)} collective-permute-done((bf16[8,128,256]{2,1,0:T(8,128)(2,1)S(1)}, bf16[8,128,256]{2,1,0:T(8,128)(2,1)S(1)}, u32[]{:S(2)}, u32[]{:S(2)}) %collective-permute-start.5) | collective-permute-done | bytes 524320 | tf_op jit(solution)/shard_map/ppermute | solution.py:460
  26.7 0.1 collective-permute-start.8
  26.7 1.6 %collective-permute-start.10 = (bf16[640,256]{1,0:T(8,128)(2,1)S(1)}, bf16[640,256]{1,0:T(8,128)(2,1)S(1)}, u32[]{:S(2)}, u32[]{:S(2)}) collective-permute-start(bf16[640,256]{1,0:T(8,128)(2,1)S(1)} %collective-permute-done.7.refs_2_.refs_5_), channel_id=1, source_target_pairs={{0,2},{2,4},{4,6},{6,7},{7,5},{5,3},{3,1},{1,0},{8,10},{10,12},{12... | collective-permute-start | bytes 983048 | tf_op jit(solution)/shard_map/ppermute | solution.py:105
  28.4 0.4 collective-permute-start.9
  28.8 0.5 slice.42
  30.0 6.9 %collective-permute-done.10.refs_5_ = bf16[640,256]{1,0:T(8,128)(2,1)S(1)} collective-permute-done((bf16[640,256]{1,0:T(8,128)(2,1)S(1)}, bf16[640,256]{1,0:T(8,128)(2,1)S(1)}, u32[]{:S(2)}, u32[]{:S(2)}) %collective-permute-start.10) | collective-permute-done | bytes 327712 | tf_op jit(solution)/shard_map/ppermute | solution.py:105
  36.9 1.6 %collective-permute-start.11 = (bf16[384,256]{1,0:T(8,128)(2,1)S(1)}, bf16[384,256]{1,0:T(8,128)(2,1)S(1)}, u32[]{:S(2)}, u32[]{:S(2)}) collective-permute-start(bf16[384,256]{1,0:T(8,128)(2,1)S(1)} %slice_select_fusion), channel_id=1, source_target_pairs={{0,2},{2,4},{4,6},{6,7},{7,5},{5,3},{3,1},{1,0},{8,10},{10,12},{12... | collective-permute-start | bytes 589832 | tf_op jit(solution)/shard_map/ppermute | solution.py:111
  38.5 0.5 collective-permute-start.12
  39.0 4.3 %shard_map.80 = (bf16[640,256]{1,0:T(8,128)(2,1)S(1)}, bf16[640,256]{1,0:T(8,128)(2,1)S(1)}, bf16[640,256]{1,0:T(8,128)(2,1)S(1)}) custom-call(s32[408]{0:T(512)S(1)} %get-tuple-element.27.pairs_ref, s32[3]{0:T(128)S(1)} %get-tuple-element.28.counts_ref, bf16[16,8,128,128]{3,2,1,0:T(8,128)(2,1)S(1)} %get-tuple-element.23.refs_3_.observed, ...), custom_call_target="tpu_custom_call" | custom-call | flops 855638016 | bytes 13369344 | tf_op jit(solution)/shard_map/pallas_call | solution.py:317
  43.3 0.3 collective-permute-done.12.refs_7_
  43.5 3.6 %shard_map.81 = (bf16[640,256]{1,0:T(8,128)(2,1)S(1)}, bf16[640,256]{1,0:T(8,128)(2,1)S(1)}, bf16[384,256]{1,0:T(8,128)(2,1)S(1)}, bf16[256,256]{1,0:T(8,128)(2,1)S(1)}) custom-call(s32[408]{0:T(512)S(1)} %get-tuple-element.27.pairs_ref, s32[3]{0:T(128)S(1)} %get-tuple-element.28.counts_ref, ...), custom_call_target="tpu_custom_call" | custom-call | flops 855638016 | bytes 13369344 | tf_op jit(solution)/shard_map/pallas_call | solution.py:317
  47.1 0.7 collective-permute-start.17
  47.9 1.4 collective-permute-start.13
  49.3 2.9 %collective-permute-done.17 = bf16[256,256]{1,0:T(8,128)(2,1)S(1)} collective-permute-done((bf16[256,256]{1,0:T(8,128)(2,1)S(1)}, bf16[256,256]{1,0:T(8,128)(2,1)S(1)}, u32[]{:S(2)}, u32[]{:S(2)}) %collective-permute-start.17) | collective-permute-done | bytes 131104 | tf_op jit(solution)/shard_map/ppermute | solution.py:122
  52.2 0.7 collective-permute-start.18
  53.0 0.8 collective-permute-done.13
  53.9 1.5 %collective-permute-start.14 = (bf16[640,256]{1,0:T(8,128)(2,1)S(1)}, bf16[640,256]{1,0:T(8,128)(2,1)S(1)}, u32[]{:S(2)}, u32[]{:S(2)}) collective-permute-start(bf16[640,256]{1,0:T(8,128)(2,1)S(1)} %pad_maximum_fusion), channel_id=1, source_target_pairs={{0,2},{2,4},{4,6},{6,7},{7,5},{5,3},{3,1},{1,0},{8,10},{10,12},{12... | collective-permute-start | bytes 983048 | tf_op jit(solution)/shard_map/ppermute | solution.py:132
  55.4 2.2 %shard_map.82 = (bf16[640,256]{1,0:T(8,128)(2,1)S(1)}, bf16[640,256]{1,0:T(8,128)(2,1)S(1)}) custom-call(s32[408]{0:T(512)S(1)} %get-tuple-element.27.pairs_ref, s32[3]{0:T(128)S(1)} %get-tuple-element.28.counts_ref, bf16[16,8,128,128]{3,2,1,0:T(8,128)(2,1)S(1)} %get-tuple-element.23.refs_3_.observed, ...), custom_call_target="tpu_custom_call" | custom-call | flops 570425344 | bytes 8912896 | tf_op jit(solution)/shard_map/pallas_call | solution.py:317
  57.5 2.6 %collective-permute-done.18 = bf16[640,256]{1,0:T(8,128)(2,1)S(1)} collective-permute-done((bf16[640,256]{1,0:T(8,128)(2,1)S(1)}, bf16[640,256]{1,0:T(8,128)(2,1)S(1)}, u32[]{:S(2)}, u32[]{:S(2)}) %collective-permute-start.18) | collective-permute-done | bytes 327712 | tf_op jit(solution)/shard_map/ppermute | solution.py:132
  60.1 0.1 add_convert_fusion.1
  60.2 0.3 collective-permute-start.19
  60.5 1.2 collective-permute-done.14
  61.8 0.1 add_convert_fusion.3
  61.9 1.4 %collective-permute-start.15 = (bf16[640,256]{1,0:T(8,128)(2,1)S(1)}, bf16[640,256]{1,0:T(8,128)(2,1)S(1)}, u32[]{:S(2)}, u32[]{:S(2)}) collective-permute-start(bf16[640,256]{1,0:T(8,128)(2,1)S(1)} %add_convert_fusion.3), channel_id=1, source_target_pairs={{0,2},{2,4},{4,6},{6,7},{7,5},{5,3},{3,1},{1,0},{8,10},{10,12},{12... | collective-permute-start | bytes 983048 | tf_op jit(solution)/shard_map/ppermute | solution.py:132
  63.3 5.1 %collective-permute-done.19 = bf16[640,256]{1,0:T(8,128)(2,1)S(1)} collective-permute-done((bf16[640,256]{1,0:T(8,128)(2,1)S(1)}, bf16[640,256]{1,0:T(8,128)(2,1)S(1)}, u32[]{:S(2)}, u32[]{:S(2)}) %collective-permute-start.19) | collective-permute-done | bytes 327712 | tf_op jit(solution)/shard_map/ppermute | solution.py:132
  68.4 0.1 add_convert_fusion
  68.5 5.3 %collective-permute-start.20 = (bf16[640,256]{1,0:T(8,128)(2,1)S(1)}, bf16[640,256]{1,0:T(8,128)(2,1)S(1)}, u32[]{:S(2)}, u32[]{:S(2)}) collective-permute-start(bf16[640,256]{1,0:T(8,128)(2,1)S(1)} %add_convert_fusion), channel_id=1, source_target_pairs={{2,0},{4,2},{6,4},{7,6},{5,7},{3,5},{1,3},{0,1},{10,8},{12,10},{14... | collective-permute-start | bytes 983048 | tf_op jit(solution)/shard_map/ppermute | solution.py:132
  73.8 1.5 %collective-permute-done.15 = bf16[640,256]{1,0:T(8,128)(2,1)S(1)} collective-permute-done((bf16[640,256]{1,0:T(8,128)(2,1)S(1)}, bf16[640,256]{1,0:T(8,128)(2,1)S(1)}, u32[]{:S(2)}, u32[]{:S(2)}) %collective-permute-start.15) | collective-permute-done | bytes 327712 | tf_op jit(solution)/shard_map/ppermute | solution.py:132
  75.3 0.1 add_convert_fusion.2
  75.4 2.9 %collective-permute-done.20 = bf16[640,256]{1,0:T(8,128)(2,1)S(1)} collective-permute-done((bf16[640,256]{1,0:T(8,128)(2,1)S(1)}, bf16[640,256]{1,0:T(8,128)(2,1)S(1)}, u32[]{:S(2)}, u32[]{:S(2)}) %collective-permute-start.20) | collective-permute-done | bytes 327712 | tf_op jit(solution)/shard_map/ppermute | solution.py:132
  78.4 7.3 %collective-permute-done.16 = bf16[640,256]{1,0:T(8,128)(2,1)S(1)} collective-permute-done((bf16[640,256]{1,0:T(8,128)(2,1)S(1)}, bf16[640,256]{1,0:T(8,128)(2,1)S(1)}, u32[]{:S(2)}, u32[]{:S(2)}) %collective-permute-start.16) | collective-permute-done | bytes 327712 | tf_op jit(solution)/shard_map/ppermute | solution.py:132
  85.7 1.1 fusion.10
  86.7 3.1 %collective-permute-start.21 = (bf16[640,256]{1,0:T(8,128)(2,1)S(1)}, bf16[640,256]{1,0:T(8,128)(2,1)S(1)}, u32[]{:S(2)}, u32[]{:S(2)}) collective-permute-start(bf16[640,256]{1,0:T(8,128)(2,1)S(1)} %get-tuple-element.44.refs_2_), channel_id=1, source_target_pairs={{2,0},{4,2},{6,4},{7,6},{5,7},{3,5},{1,3},{0,1},{10,8},{12,10},{14... | collective-permute-start | bytes 983048 | tf_op jit(solution)/shard_map/ppermute | solution.py:105
  89.8 7.3 %collective-permute-done.22.refs_4_ = bf16[640,256]{1,0:T(8,128)(2,1)S(1)} collective-permute-done((bf16[640,256]{1,0:T(8,128)(2,1)S(1)}, bf16[640,256]{1,0:T(8,128)(2,1)S(1)}, u32[]{:S(2)}, u32[]{:S(2)}) %collective-permute-start.22) | collective-permute-done | bytes 327712 | tf_op jit(solution)/shard_map/ppermute | solution.py:105
  97.1 2.2 %collective-permute-start.23 = (bf16[640,256]{1,0:T(8,128)(2,1)S(1)}, bf16[640,256]{1,0:T(8,128)(2,1)S(1)}, u32[]{:S(2)}, u32[]{:S(2)}) collective-permute-start(bf16[640,256]{1,0:T(8,128)(2,1)S(1)} %collective-permute-done.21.refs_3_), channel_id=1, source_target_pairs={{2,0},{4,2},{6,4},{7,6},{5,7},{3,5},{1,3},{0,1},{10,8},{12,10},{14... | collective-permute-start | bytes 983048 | tf_op jit(solution)/shard_map/ppermute | solution.py:105
  99.3 6.4 %collective-permute-done.24.refs_6_ = bf16[640,256]{1,0:T(8,128)(2,1)S(1)} collective-permute-done((bf16[640,256]{1,0:T(8,128)(2,1)S(1)}, bf16[640,256]{1,0:T(8,128)(2,1)S(1)}, u32[]{:S(2)}, u32[]{:S(2)}) %collective-permute-start.24) | collective-permute-done | bytes 327712 | tf_op jit(solution)/shard_map/ppermute | solution.py:105
  105.8 0.1 collective-permute-start.26
  105.8 2.0 %collective-permute-start.25 = (bf16[640,256]{1,0:T(8,128)(2,1)S(1)}, bf16[640,256]{1,0:T(8,128)(2,1)S(1)}, u32[]{:S(2)}, u32[]{:S(2)}) collective-permute-start(bf16[640,256]{1,0:T(8,128)(2,1)S(1)} %collective-permute-done.23.refs_5_), channel_id=1, source_target_pairs={{2,0},{4,2},{6,4},{7,6},{5,7},{3,5},{1,3},{0,1},{10,8},{12,10},{14... | collective-permute-start | bytes 983048 | tf_op jit(solution)/shard_map/ppermute | solution.py:105
  107.8 5.0 %collective-permute-done.26.refs_8_ = bf16[640,256]{1,0:T(8,128)(2,1)S(1)} collective-permute-done((bf16[640,256]{1,0:T(8,128)(2,1)S(1)}, bf16[640,256]{1,0:T(8,128)(2,1)S(1)}, u32[]{:S(2)}, u32[]{:S(2)}) %collective-permute-start.26) | collective-permute-done | bytes 327712 | tf_op jit(solution)/shard_map/ppermute | solution.py:105
  112.8 0.1 collective-permute-start.27
  113.0 2.0 %collective-permute-start.28 = (bf16[256,256]{1,0:T(8,128)(2,1)S(1)}, bf16[256,256]{1,0:T(8,128)(2,1)S(1)}, u32[]{:S(2)}, u32[]{:S(2)}) collective-permute-start(bf16[256,256]{1,0:T(8,128)(2,1)S(1)} %slice.46), channel_id=1, source_target_pairs={{2,0},{4,2},{6,4},{7,6},{5,7},{3,5},{1,3},{0,1},{10,8},{12,10},{14... | collective-permute-start | bytes 393224 | tf_op jit(solution)/shard_map/ppermute | solution.py:111
  115.0 3.0 %collective-permute-done.28.refs_10_ = bf16[256,256]{1,0:T(8,128)(2,1)S(1)} collective-permute-done((bf16[256,256]{1,0:T(8,128)(2,1)S(1)}, bf16[256,256]{1,0:T(8,128)(2,1)S(1)}, u32[]{:S(2)}, u32[]{:S(2)}) %collective-permute-start.28) | collective-permute-done | bytes 131104 | tf_op jit(solution)/shard_map/ppermute | solution.py:111
  118.0 0.6 collective-permute-done.27.refs_9_
  118.6 1.4 shard_map.83
  120.0 0.1 collective-permute-start.29
  120.0 4.8 %shard_map.85 = (bf16[4,128,256]{2,1,0:T(8,128)(2,1)S(1)}, bf16[4,128,256]{2,1,0:T(8,128)(2,1)S(1)}) custom-call(s32[1]{0:T(128)} %bitcast.row_ref, s32[4]{0:T(128)S(1)} %bitcast.11, s32[16,8]{1,0:T(8,128)S(1)} %fusion.5.ids_ref, bf16[16,8,128,128]{3,2,1,0:T(8,128)(2,1)S(1)} %get-tuple-element.23.refs_3_.observed, ...), custom_call_target="tpu_custom_call" | custom-call | flops 1073741824 | bytes 16777216 | tf_op jit(solution)/shard_map/pallas_call | solution.py:367
  124.8 1.5 %collective-permute-start.30 = (bf16[4,128,256]{2,1,0:T(8,128)(2,1)S(1)}, bf16[4,128,256]{2,1,0:T(8,128)(2,1)S(1)}, u32[]{:S(2)}, u32[]{:S(2)}) collective-permute-start(bf16[4,128,256]{2,1,0:T(8,128)(2,1)S(1)} %get-tuple-element.41), channel_id=1, source_target_pairs={{0,16},{8,24},{16,0},{24,8},{1,17},{9,25},{17,1},{25,9},{2,18},{10... | collective-permute-start | bytes 786440 | tf_op jit(solution)/shard_map/ppermute | solution.py:502
  126.4 2.3 %shard_map.84 = (f32[16,128,256]{2,1,0:T(8,128)S(1)}, f32[16,128,256]{2,1,0:T(8,128)}) custom-call(s32[1]{0:T(128)} %bitcast.row_ref, s32[16]{0:T(128)S(1)} %copy-done.3, s32[16]{0:T(128)S(1)} %collective-permute-done.2.refs_1_, f32[16,128,256]{2,1,0:T(8,128)S(1)} %bitcast.8, bf16[4,128,256]{2,1,0:T(8,128)(2,1)S(1)} %get-tuple-element.38.refs_3_, ...), custom_call_target="tpu_custom_call" | custom-call | tf_op jit(solution)/shard_map/pallas_call | solution.py:408
  128.6 5.5 %collective-permute-done.30.refs_3_ = bf16[4,128,256]{2,1,0:T(8,128)(2,1)S(1)} collective-permute-done((bf16[4,128,256]{2,1,0:T(8,128)(2,1)S(1)}, bf16[4,128,256]{2,1,0:T(8,128)(2,1)S(1)}, u32[]{:S(2)}, u32[]{:S(2)}) %collective-permute-start.30) | collective-permute-done | bytes 262176 | tf_op jit(solution)/shard_map/ppermute | solution.py:502
  134.2 3.0 %collective-permute-done.31.refs_4_ = bf16[4,128,256]{2,1,0:T(8,128)(2,1)S(1)} collective-permute-done((bf16[4,128,256]{2,1,0:T(8,128)(2,1)S(1)}, bf16[4,128,256]{2,1,0:T(8,128)(2,1)S(1)}, u32[]{:S(2)}, u32[]{:S(2)}) %collective-permute-start.31) | collective-permute-done | bytes 262176 | tf_op jit(solution)/shard_map/ppermute | solution.py:502
  137.2 1.8 %shard_map.86 = f32[16,128,256]{2,1,0:T(8,128)} custom-call(s32[1]{0:T(128)} %bitcast.row_ref, s32[16]{0:T(128)S(1)} %collective-permute-done.refs_2_.refs_0_, s32[16]{0:T(128)S(1)} %collective-permute-done.1.refs_3_.refs_1_, f32[16,128,256]{2,1,0:T(8,128)S(1)} %get-tuple-element.40.refs_2_, ...), custom_call_target="tpu_custom_call", output_to_operand_aliasing={{}: (6, {})} | custom-call | tf_op jit(solution)/shard_map/pallas_call | solution.py:430
  (42 shorter events, 0.4 us)
Async XLA Ops:
  0.6 15.2 %copy-start.5 = (s32[16,8]{0,1:T(8,128)S(1)}, s32[16,8]{0,1:T(8,128)}, u32[]{:S(2)}) copy-start(s32[16,8]{0,1:T(8,128)} %param.8) | copy-start | bytes 1540
  0.6 15.3 %copy-start.1 = (s32[1,1,4]{2,1,0:T(1,128)S(1)}, s32[1,1,4]{2,1,0:T(1,128)}, u32[]{:S(2)}) copy-start(s32[1,1,4]{2,1,0:T(1,128)} %param.9) | copy-start | bytes 52
  1.8 12.0 %collective-permute-start.4 = (bf16[640,256]{1,0:T(8,128)(2,1)S(1)}, bf16[640,256]{1,0:T(8,128)(2,1)S(1)}, u32[]{:S(2)}, u32[]{:S(2)}) collective-permute-start(bf16[640,256]{1,0:T(8,128)(2,1)S(1)} %convert_element_type.69.refs_4_), channel_id=1, source_target_pairs={{0,2},{2,4},{4,6},{6,7},{7,5},{5,3},{3,1},{1,0},{8,10},{10,12},{12... | collective-permute-start | bytes 983048 | tf_op jit(solution)/shard_map/ppermute | solution.py:105
  4.9 10.9 %collective-permute-start.3 = (bf16[640,256]{1,0:T(8,128)(2,1)S(1)}, bf16[640,256]{1,0:T(8,128)(2,1)S(1)}, u32[]{:S(2)}, u32[]{:S(2)}) collective-permute-start(bf16[640,256]{1,0:T(8,128)(2,1)S(1)} %convert_element_type.69.refs_4_), channel_id=1, source_target_pairs={{2,0},{4,2},{6,4},{7,6},{5,7},{3,5},{1,3},{0,1},{10,8},{12,10},{14... | collective-permute-start | bytes 983048 | tf_op jit(solution)/shard_map/ppermute | solution.py:105
  4.9 2.1 %collective-permute-start.2 = (s32[16]{0:T(128)}, s32[16]{0:T(128)S(1)}, u32[]{:S(2)}, u32[]{:S(2)}) collective-permute-start(s32[16]{0:T(128)} %refs_0_.3), channel_id=1, source_target_pairs={{0,8},{8,0},{16,24},{24,16},{1,9},{9,1},{17,25},{25,17},{2,10},{10... | collective-permute-start | bytes 200 | tf_op jit(solution)/shard_map/ppermute | solution.py:457
  4.9 3.5 %collective-permute-start.1 = (s32[16]{0:T(128)}, s32[16]{0:T(128)S(1)}, u32[]{:S(2)}, u32[]{:S(2)}) collective-permute-start(s32[16]{0:T(128)} %refs_0_.3), channel_id=1, source_target_pairs={{0,24},{8,16},{16,8},{24,0},{1,25},{9,17},{17,9},{25,1},{2,26},{10... | collective-permute-start | bytes 200 | tf_op jit(solution)/shard_map/ppermute | solution.py:457
  6.9 3.7 %collective-permute-start = (s32[16]{0:T(128)}, s32[16]{0:T(128)S(1)}, u32[]{:S(2)}, u32[]{:S(2)}) collective-permute-start(s32[16]{0:T(128)} %refs_0_.3), channel_id=1, source_target_pairs={{0,16},{8,24},{16,0},{24,8},{1,17},{9,25},{17,1},{25,9},{2,18},{10... | collective-permute-start | bytes 200 | tf_op jit(solution)/shard_map/ppermute | solution.py:457
  10.6 0.7 copy-start.2
  13.6 13.0 %collective-permute-start.5 = (bf16[8,128,256]{2,1,0:T(8,128)(2,1)S(1)}, bf16[8,128,256]{2,1,0:T(8,128)(2,1)S(1)}, u32[]{:S(2)}, u32[]{:S(2)}) collective-permute-start(bf16[8,128,256]{2,1,0:T(8,128)(2,1)S(1)} %get-tuple-element.25), channel_id=1, source_target_pairs={{0,16},{8,24},{16,0},{24,8},{1,17},{9,25},{17,1},{25,9},{2,18},{10... | collective-permute-start | bytes 1572872 | tf_op jit(solution)/shard_map/ppermute | solution.py:460
  13.8 12.8 %collective-permute-start.7 = (bf16[640,256]{1,0:T(8,128)(2,1)S(1)}, bf16[640,256]{1,0:T(8,128)(2,1)S(1)}, u32[]{:S(2)}, u32[]{:S(2)}) collective-permute-start(bf16[640,256]{1,0:T(8,128)(2,1)S(1)} %collective-permute-done.4.refs_1_.refs_6_), channel_id=1, source_target_pairs={{0,2},{2,4},{4,6},{6,7},{7,5},{5,3},{3,1},{1,0},{8,10},{10,12},{12... | collective-permute-start | bytes 983048 | tf_op jit(solution)/shard_map/ppermute | solution.py:105
  15.8 10.9 %collective-permute-start.6 = (bf16[640,256]{1,0:T(8,128)(2,1)S(1)}, bf16[640,256]{1,0:T(8,128)(2,1)S(1)}, u32[]{:S(2)}, u32[]{:S(2)}) collective-permute-start(bf16[640,256]{1,0:T(8,128)(2,1)S(1)} %collective-permute-done.3.refs_0_.refs_5_), channel_id=1, source_target_pairs={{2,0},{4,2},{6,4},{7,6},{5,7},{3,5},{1,3},{0,1},{10,8},{12,10},{14... | collective-permute-start | bytes 983048 | tf_op jit(solution)/shard_map/ppermute | solution.py:105
  26.7 2.2 %collective-permute-start.8 = (bf16[8,128,256]{2,1,0:T(8,128)(2,1)S(1)}, bf16[8,128,256]{2,1,0:T(8,128)(2,1)S(1)}, u32[]{:S(2)}, u32[]{:S(2)}) collective-permute-start(bf16[8,128,256]{2,1,0:T(8,128)(2,1)S(1)} %shard_map.79), channel_id=1, source_target_pairs={{0,8},{8,0},{16,24},{24,16},{1,9},{9,1},{17,25},{25,17},{2,10},{10... | collective-permute-start | bytes 1572872 | tf_op jit(solution)/shard_map/ppermute | solution.py:478
  26.7 10.1 %collective-permute-start.10 = (bf16[640,256]{1,0:T(8,128)(2,1)S(1)}, bf16[640,256]{1,0:T(8,128)(2,1)S(1)}, u32[]{:S(2)}, u32[]{:S(2)}) collective-permute-start(bf16[640,256]{1,0:T(8,128)(2,1)S(1)} %collective-permute-done.7.refs_2_.refs_5_), channel_id=1, source_target_pairs={{0,2},{2,4},{4,6},{6,7},{7,5},{5,3},{3,1},{1,0},{8,10},{10,12},{12... | collective-permute-start | bytes 983048 | tf_op jit(solution)/shard_map/ppermute | solution.py:105
  28.4 10.1 %collective-permute-start.9 = (bf16[640,256]{1,0:T(8,128)(2,1)S(1)}, bf16[640,256]{1,0:T(8,128)(2,1)S(1)}, u32[]{:S(2)}, u32[]{:S(2)}) collective-permute-start(bf16[640,256]{1,0:T(8,128)(2,1)S(1)} %collective-permute-done.6.refs_1_.refs_4_), channel_id=1, source_target_pairs={{2,0},{4,2},{6,4},{7,6},{5,7},{3,5},{1,3},{0,1},{10,8},{12,10},{14... | collective-permute-start | bytes 983048 | tf_op jit(solution)/shard_map/ppermute | solution.py:105
  36.9 6.7 %collective-permute-start.11 = (bf16[384,256]{1,0:T(8,128)(2,1)S(1)}, bf16[384,256]{1,0:T(8,128)(2,1)S(1)}, u32[]{:S(2)}, u32[]{:S(2)}) collective-permute-start(bf16[384,256]{1,0:T(8,128)(2,1)S(1)} %slice_select_fusion), channel_id=1, source_target_pairs={{0,2},{2,4},{4,6},{6,7},{7,5},{5,3},{3,1},{1,0},{8,10},{10,12},{12... | collective-permute-start | bytes 589832 | tf_op jit(solution)/shard_map/ppermute | solution.py:111
  38.5 5.0 %collective-permute-start.12 = (bf16[256,256]{1,0:T(8,128)(2,1)S(1)}, bf16[256,256]{1,0:T(8,128)(2,1)S(1)}, u32[]{:S(2)}, u32[]{:S(2)}) collective-permute-start(bf16[256,256]{1,0:T(8,128)(2,1)S(1)} %slice_select_fusion.1), channel_id=1, source_target_pairs={{2,0},{4,2},{6,4},{7,6},{5,7},{3,5},{1,3},{0,1},{10,8},{12,10},{14... | collective-permute-start | bytes 393224 | tf_op jit(solution)/shard_map/ppermute | solution.py:111
  47.1 5.0 %collective-permute-start.17 = (bf16[256,256]{1,0:T(8,128)(2,1)S(1)}, bf16[256,256]{1,0:T(8,128)(2,1)S(1)}, u32[]{:S(2)}, u32[]{:S(2)}) collective-permute-start(bf16[256,256]{1,0:T(8,128)(2,1)S(1)} %get-tuple-element.35), channel_id=1, source_target_pairs={{2,0},{4,2},{6,4},{7,6},{5,7},{3,5},{1,3},{0,1},{10,8},{12,10},{14... | collective-permute-start | bytes 393224 | tf_op jit(solution)/shard_map/ppermute | solution.py:122
  47.9 5.9 %collective-permute-start.13 = (bf16[384,256]{1,0:T(8,128)(2,1)S(1)}, bf16[384,256]{1,0:T(8,128)(2,1)S(1)}, u32[]{:S(2)}, u32[]{:S(2)}) collective-permute-start(bf16[384,256]{1,0:T(8,128)(2,1)S(1)} %get-tuple-element.30), channel_id=1, source_target_pairs={{0,2},{2,4},{4,6},{6,7},{7,5},{5,3},{3,1},{1,0},{8,10},{10,12},{12... | collective-permute-start | bytes 589832 | tf_op jit(solution)/shard_map/ppermute | solution.py:122
  52.2 7.9 %collective-permute-start.18 = (bf16[640,256]{1,0:T(8,128)(2,1)S(1)}, bf16[640,256]{1,0:T(8,128)(2,1)S(1)}, u32[]{:S(2)}, u32[]{:S(2)}) collective-permute-start(bf16[640,256]{1,0:T(8,128)(2,1)S(1)} %pad_maximum_fusion.1), channel_id=1, source_target_pairs={{2,0},{4,2},{6,4},{7,6},{5,7},{3,5},{1,3},{0,1},{10,8},{12,10},{14... | collective-permute-start | bytes 983048 | tf_op jit(solution)/shard_map/ppermute | solution.py:132
  53.9 7.9 %collective-permute-start.14 = (bf16[640,256]{1,0:T(8,128)(2,1)S(1)}, bf16[640,256]{1,0:T(8,128)(2,1)S(1)}, u32[]{:S(2)}, u32[]{:S(2)}) collective-permute-start(bf16[640,256]{1,0:T(8,128)(2,1)S(1)} %pad_maximum_fusion), channel_id=1, source_target_pairs={{0,2},{2,4},{4,6},{6,7},{7,5},{5,3},{3,1},{1,0},{8,10},{10,12},{12... | collective-permute-start | bytes 983048 | tf_op jit(solution)/shard_map/ppermute | solution.py:132
  57.5 28.1 %copy-start.4 = (f32[640,256]{1,0:T(8,128)S(1)}, f32[640,256]{1,0:T(8,128)}, u32[]{:S(2)}) copy-start(f32[640,256]{1,0:T(8,128)} %param.11) | copy-start | bytes 1966084
  60.2 8.2 %collective-permute-start.19 = (bf16[640,256]{1,0:T(8,128)(2,1)S(1)}, bf16[640,256]{1,0:T(8,128)(2,1)S(1)}, u32[]{:S(2)}, u32[]{:S(2)}) collective-permute-start(bf16[640,256]{1,0:T(8,128)(2,1)S(1)} %add_convert_fusion.1), channel_id=1, source_target_pairs={{2,0},{4,2},{6,4},{7,6},{5,7},{3,5},{1,3},{0,1},{10,8},{12,10},{14... | collective-permute-start | bytes 983048 | tf_op jit(solution)/shard_map/ppermute | solution.py:132
  61.9 13.4 %collective-permute-start.15 = (bf16[640,256]{1,0:T(8,128)(2,1)S(1)}, bf16[640,256]{1,0:T(8,128)(2,1)S(1)}, u32[]{:S(2)}, u32[]{:S(2)}) collective-permute-start(bf16[640,256]{1,0:T(8,128)(2,1)S(1)} %add_convert_fusion.3), channel_id=1, source_target_pairs={{0,2},{2,4},{4,6},{6,7},{7,5},{5,3},{3,1},{1,0},{8,10},{10,12},{12... | collective-permute-start | bytes 983048 | tf_op jit(solution)/shard_map/ppermute | solution.py:132
  68.5 9.9 %collective-permute-start.20 = (bf16[640,256]{1,0:T(8,128)(2,1)S(1)}, bf16[640,256]{1,0:T(8,128)(2,1)S(1)}, u32[]{:S(2)}, u32[]{:S(2)}) collective-permute-start(bf16[640,256]{1,0:T(8,128)(2,1)S(1)} %add_convert_fusion), channel_id=1, source_target_pairs={{2,0},{4,2},{6,4},{7,6},{5,7},{3,5},{1,3},{0,1},{10,8},{12,10},{14... | collective-permute-start | bytes 983048 | tf_op jit(solution)/shard_map/ppermute | solution.py:132
  75.4 10.3 %collective-permute-start.16 = (bf16[640,256]{1,0:T(8,128)(2,1)S(1)}, bf16[640,256]{1,0:T(8,128)(2,1)S(1)}, u32[]{:S(2)}, u32[]{:S(2)}) collective-permute-start(bf16[640,256]{1,0:T(8,128)(2,1)S(1)} %add_convert_fusion.2), channel_id=1, source_target_pairs={{0,2},{2,4},{4,6},{6,7},{7,5},{5,3},{3,1},{1,0},{8,10},{10,12},{12... | collective-permute-start | bytes 983048 | tf_op jit(solution)/shard_map/ppermute | solution.py:132
  86.7 10.4 %collective-permute-start.22 = (bf16[640,256]{1,0:T(8,128)(2,1)S(1)}, bf16[640,256]{1,0:T(8,128)(2,1)S(1)}, u32[]{:S(2)}, u32[]{:S(2)}) collective-permute-start(bf16[640,256]{1,0:T(8,128)(2,1)S(1)} %get-tuple-element.44.refs_2_), channel_id=1, source_target_pairs={{0,2},{2,4},{4,6},{6,7},{7,5},{5,3},{3,1},{1,0},{8,10},{10,12},{12... | collective-permute-start | bytes 983048 | tf_op jit(solution)/shard_map/ppermute | solution.py:105
  86.7 10.4 %collective-permute-start.21 = (bf16[640,256]{1,0:T(8,128)(2,1)S(1)}, bf16[640,256]{1,0:T(8,128)(2,1)S(1)}, u32[]{:S(2)}, u32[]{:S(2)}) collective-permute-start(bf16[640,256]{1,0:T(8,128)(2,1)S(1)} %get-tuple-element.44.refs_2_), channel_id=1, source_target_pairs={{2,0},{4,2},{6,4},{7,6},{5,7},{3,5},{1,3},{0,1},{10,8},{12,10},{14... | collective-permute-start | bytes 983048 | tf_op jit(solution)/shard_map/ppermute | solution.py:105
  97.1 8.6 %collective-permute-start.24 = (bf16[640,256]{1,0:T(8,128)(2,1)S(1)}, bf16[640,256]{1,0:T(8,128)(2,1)S(1)}, u32[]{:S(2)}, u32[]{:S(2)}) collective-permute-start(bf16[640,256]{1,0:T(8,128)(2,1)S(1)} %collective-permute-done.22.refs_4_), channel_id=1, source_target_pairs={{0,2},{2,4},{4,6},{6,7},{7,5},{5,3},{3,1},{1,0},{8,10},{10,12},{12... | collective-permute-start | bytes 983048 | tf_op jit(solution)/shard_map/ppermute | solution.py:105
  97.1 8.7 %collective-permute-start.23 = (bf16[640,256]{1,0:T(8,128)(2,1)S(1)}, bf16[640,256]{1,0:T(8,128)(2,1)S(1)}, u32[]{:S(2)}, u32[]{:S(2)}) collective-permute-start(bf16[640,256]{1,0:T(8,128)(2,1)S(1)} %collective-permute-done.21.refs_3_), channel_id=1, source_target_pairs={{2,0},{4,2},{6,4},{7,6},{5,7},{3,5},{1,3},{0,1},{10,8},{12,10},{14... | collective-permute-start | bytes 983048 | tf_op jit(solution)/shard_map/ppermute | solution.py:105
  105.8 7.1 %collective-permute-start.26 = (bf16[640,256]{1,0:T(8,128)(2,1)S(1)}, bf16[640,256]{1,0:T(8,128)(2,1)S(1)}, u32[]{:S(2)}, u32[]{:S(2)}) collective-permute-start(bf16[640,256]{1,0:T(8,128)(2,1)S(1)} %collective-permute-done.24.refs_6_), channel_id=1, source_target_pairs={{0,2},{2,4},{4,6},{6,7},{7,5},{5,3},{3,1},{1,0},{8,10},{10,12},{12... | collective-permute-start | bytes 983048 | tf_op jit(solution)/shard_map/ppermute | solution.py:105
  105.8 7.1 %collective-permute-start.25 = (bf16[640,256]{1,0:T(8,128)(2,1)S(1)}, bf16[640,256]{1,0:T(8,128)(2,1)S(1)}, u32[]{:S(2)}, u32[]{:S(2)}) collective-permute-start(bf16[640,256]{1,0:T(8,128)(2,1)S(1)} %collective-permute-done.23.refs_5_), channel_id=1, source_target_pairs={{2,0},{4,2},{6,4},{7,6},{5,7},{3,5},{1,3},{0,1},{10,8},{12,10},{14... | collective-permute-start | bytes 983048 | tf_op jit(solution)/shard_map/ppermute | solution.py:105
  112.8 5.7 %collective-permute-start.27 = (bf16[384,256]{1,0:T(8,128)(2,1)S(1)}, bf16[384,256]{1,0:T(8,128)(2,1)S(1)}, u32[]{:S(2)}, u32[]{:S(2)}) collective-permute-start(bf16[384,256]{1,0:T(8,128)(2,1)S(1)} %slice.45), channel_id=1, source_target_pairs={{0,2},{2,4},{4,6},{6,7},{7,5},{5,3},{3,1},{1,0},{8,10},{10,12},{12... | collective-permute-start | bytes 589832 | tf_op jit(solution)/shard_map/ppermute | solution.py:111
  113.0 5.0 %collective-permute-start.28 = (bf16[256,256]{1,0:T(8,128)(2,1)S(1)}, bf16[256,256]{1,0:T(8,128)(2,1)S(1)}, u32[]{:S(2)}, u32[]{:S(2)}) collective-permute-start(bf16[256,256]{1,0:T(8,128)(2,1)S(1)} %slice.46), channel_id=1, source_target_pairs={{2,0},{4,2},{6,4},{7,6},{5,7},{3,5},{1,3},{0,1},{10,8},{12,10},{14... | collective-permute-start | bytes 393224 | tf_op jit(solution)/shard_map/ppermute | solution.py:111
  119.9 6.4 %copy-start = (f32[2048,256]{1,0:T(8,128)S(1)}, f32[2048,256]{1,0:T(8,128)}, u32[]{:S(2)}) copy-start(f32[2048,256]{1,0:T(8,128)} %param.10) | copy-start | bytes 6291460
  119.9 6.4 %copy-start.3 = (s32[16]{0:T(128)S(1)}, s32[16]{0:T(128)}, u32[]{:S(2)}) copy-start(s32[16]{0:T(128)} %refs_0_.3) | copy-start | bytes 196
  120.0 6.4 %collective-permute-start.29 = (bf16[4,128,256]{2,1,0:T(8,128)(2,1)S(1)}, bf16[4,128,256]{2,1,0:T(8,128)(2,1)S(1)}, u32[]{:S(2)}, u32[]{:S(2)}) collective-permute-start(bf16[4,128,256]{2,1,0:T(8,128)(2,1)S(1)} %get-tuple-element.39), channel_id=1, source_target_pairs={{0,8},{8,0},{16,24},{24,16},{1,9},{9,1},{17,25},{25,17},{2,10},{10... | collective-permute-start | bytes 786440 | tf_op jit(solution)/shard_map/ppermute | solution.py:502
  124.8 9.3 %collective-permute-start.30 = (bf16[4,128,256]{2,1,0:T(8,128)(2,1)S(1)}, bf16[4,128,256]{2,1,0:T(8,128)(2,1)S(1)}, u32[]{:S(2)}, u32[]{:S(2)}) collective-permute-start(bf16[4,128,256]{2,1,0:T(8,128)(2,1)S(1)} %get-tuple-element.41), channel_id=1, source_target_pairs={{0,16},{8,24},{16,0},{24,8},{1,17},{9,25},{17,1},{25,9},{2,18},{10... | collective-permute-start | bytes 786440 | tf_op jit(solution)/shard_map/ppermute | solution.py:502
  126.3 10.9 %collective-permute-start.31 = (bf16[4,128,256]{2,1,0:T(8,128)(2,1)S(1)}, bf16[4,128,256]{2,1,0:T(8,128)(2,1)S(1)}, u32[]{:S(2)}, u32[]{:S(2)}) collective-permute-start(bf16[4,128,256]{2,1,0:T(8,128)(2,1)S(1)} %get-tuple-element.42), channel_id=1, source_target_pairs={{0,24},{8,16},{16,8},{24,0},{1,25},{9,17},{17,9},{25,1},{2,26},{10... | collective-permute-start | bytes 786440 | tf_op jit(solution)/shard_map/ppermute | solution.py:502

commit v3 on v2

--- a/solution.py
+++ b/solution.py
@@ -73,7 +73,7 @@
         for m in range(1, self.far):
             self.order += [m, col_count - m]
         self.order.append(self.far)
-        self.groups = [self.order[:3], self.order[3:-3], self.order[-3:]]
+        self.groups = [self.order[:3], self.order[3:-3], self.order[-3:-1], self.order[-1:]]
         self.starts = [self.order.index(g[0]) * self.blocks for g in self.groups]
 
     def arrival(self, offset):
@@ -93,22 +93,26 @@
 
 
 def after(value, mark):
-    return jnp.where(mark[0, :1] < jnp.inf, value, jnp.zeros_like(value))
-
-
-def gather_ring(low, plan, mark_last=lambda pieces: None):
+    return jnp.where(mark[:1] < jnp.inf, value, jnp.zeros_like(value))
+
+
+def gather_ring(low, plan, marks=None, arrived=None):
     steps = ring_steps(plan.count)
     moved = [low, low]
     pieces = {0: [low]}
-    for step in range(1, plan.far):
-        for way in (0, 1):
-            moved[way] = lax.ppermute(moved[way], "col", steps[way])
-            pieces[step if way else plan.count - step] = [moved[way]]
-    mark = mark_last(pieces)
-    parts = [moved[way][a:b] for way, (a, b) in enumerate(plan.halves)]
-    if mark is not None:
-        parts = [after(part, mark) for part in parts]
-    pieces[plan.far] = [lax.ppermute(parts[way], "col", steps[way]) for way in (0, 1)]
+    for step in range(1, plan.far + 1):
+        if step == plan.far:
+            moved = [moved[way][a:b] for way, (a, b) in enumerate(plan.halves)]
+        if marks and step in marks:
+            moved = [after(value, marks[step]) for value in moved]
+        moved = [lax.ppermute(moved[way], "col", steps[way]) for way in (0, 1)]
+        if step == plan.far:
+            pieces[step] = moved
+        else:
+            pieces[plan.count - step] = moved[:1]
+            pieces[step] = moved[1:]
+        if arrived:
+            arrived(step, pieces)
     return pieces
 
 
@@ -153,16 +157,13 @@
         block_of(k, i).start()
     for k, i in order:
         block_of(k, i).wait()
-        out = outs[k] if k < 2 else outs[1 + k // 2]
-        at = i if k < 2 else k % 2 * per_owner + i
-        out[at] = held[k * per_owner + i].astype(jnp.bfloat16)
+        outs[k][i] = held[k * per_owner + i].astype(jnp.bfloat16)
 
 
 def pick(row, ids, table, per_owner):
     row_count = len(ids)
     block, rank = table.shape[1:]
-    heights = [per_owner] * 2 + [2 * per_owner] * (row_count // 2 - 1)
-    shapes = [VMEM((height, block, rank), jnp.bfloat16) for height in heights]
+    shapes = [VMEM((per_owner, block, rank), jnp.bfloat16)] * row_count
     asked = row_count * per_owner
     return pl.pallas_call(
         functools.partial(pick_kernel, row_count, per_owner),
@@ -181,7 +182,7 @@
     out = refs[-1]
     out[0:per_owner] = first[...]
     for x in range(1, out.shape[0] // per_owner):
-        out[x * per_owner : (x + 1) * per_owner] = refs[x - 1][per_owner:]
+        out[x * per_owner : (x + 1) * per_owner] = refs[x - 1][...]
 
 
 def join(first, moved, per_owner, marks):
@@ -198,7 +199,8 @@
 
 def list_kernel(cfg, row_ref, live_ref, ids_ref, observed, *refs):
     row_count, per_owner, kinds, starts, room = cfg
-    pairs_ref, counts_ref, held, sem = refs[-4:]
+    pairs_ref, counts_ref, held, mark, sem = refs[-5:]
+    mark[...] = jnp.zeros_like(mark)
     copy = pltpu.make_async_copy(observed, held, sem)
     copy.start()
     row = row_ref[0]
@@ -235,9 +237,10 @@
             jax.ShapeDtypeStruct((groups * room,), jnp.int32),
             jax.ShapeDtypeStruct((groups,), jnp.int32),
             VMEM(observed.shape, observed.dtype),
+            VMEM((8, marks[0].shape[1]), jnp.float32),
         ],
         in_specs=[spec(SMEM)] * 3 + [spec(pltpu.HBM)] + [spec(VMEM)] * len(marks),
-        out_specs=[spec(SMEM)] * 2 + [spec(VMEM)],
+        out_specs=[spec(SMEM)] * 2 + [spec(VMEM)] * 2,
         scratch_shapes=[pltpu.SemaphoreType.DMA],
         compiler_params=params(1),
     )(row, live, ids, away(observed), *map(near, marks))
@@ -331,48 +334,69 @@
     return {d: [out.pop(0) for _ in spans] for d, spans in zip(offsets, cuts)}
 
 
-def second_kernel(cfg, row_ref, live_ref, ids_ref, observed, *refs):
-    ks, sku_starts, per_owner, kinds, block = cfg
-    skus, pieces = refs[: len(ks)], refs[len(ks) : -1 - len(ks)]
-    outs, table = refs[-1 - len(ks) : -1], refs[-1]
+def second_kernel(cfg, pairs_ref, counts_ref, observed, *refs):
+    sku_starts, piece_count, room, groups, base, block, begins, ends = cfg
+    sku_count = len(sku_starts)
+    skus, refs = refs[:sku_count], refs[sku_count:]
+    pieces, refs = refs[:piece_count], refs[piece_count:]
+    total, mark, *outs = refs[0 if begins else 1 : -2]
+    held, table = refs[-2:]
+    mark[...] = jnp.zeros_like(mark)
+    load_skus(held, skus, sku_starts)
     load_table(table, pieces)
-    row = row_ref[0]
-    for k, sku_ref, start, out in zip(ks, skus, sku_starts, outs):
-        out[...] = jnp.zeros_like(out)
-        owner = row ^ k
-
-        @pl.loop(0, live_ref[owner])
-        def _(i):
-            slot = owner * per_owner + i
-            stores, measured = [], []
-            for n in range(kinds):
-                at = pl.multiple_of(ids_ref[slot, n] * block, block)
-                stores.append(table[pl.ds(at, block), :])
-                measured.append(observed[slot, n])
-            store = jnp.concatenate(stores, axis=0)
+    if begins:
+        total[...] = jnp.zeros_like(total)
+
+    def body(entries):
+        terms = []
+        for at, n, sku_at, slot in entries:
+            store = table[pl.ds(at, block), :]
             predicted = lax.dot_general(
-                sku_ref[start + i], store, NT, preferred_element_type=jnp.float32
+                held[sku_at], store, NT, preferred_element_type=jnp.float32
             )
-            misfit = predicted - jnp.concatenate(measured, axis=1).astype(jnp.float32)
-            out[i] = jnp.dot(
-                misfit.astype(jnp.bfloat16), store, preferred_element_type=jnp.float32
-            ).astype(jnp.bfloat16)
-
-
-def second_pass(ks, row, live, ids, observed, skus, pieces, plan, per_owner):
-    kept, sku_starts = zip(*[skus[k] for k in ks])
-    kinds, block, rank = observed.shape[1], plan.block, kept[0].shape[2]
-    shape = (per_owner, block, rank)
-    inputs = [observed, *kept, *[piece for d in plan.order for piece in pieces[d]]]
+            misfit = predicted - observed[slot, n].astype(jnp.float32)
+            terms.append(
+                jnp.dot(misfit.astype(jnp.bfloat16), store, preferred_element_type=jnp.float32)
+            )
+        for (_, _, sku_at, _), term in zip(entries, terms):
+            total[sku_at] += term
+
+    for_pairs(pairs_ref, counts_ref, room, groups, base, block, body)
+    for k, out in enumerate(outs):
+        count = out.shape[0]
+        out[...] = total[pl.ds(k * count, count)].astype(jnp.bfloat16)
+
+
+def second_pass(pairs, counts, observed, skus, pieces, plan, group, total, ends):
+    offsets = plan.groups[group]
+    given = [piece for d in offsets for piece in pieces[d]]
+    skus, sku_starts = zip(*skus)
+    block, rank = plan.block, skus[0].shape[2]
+    room = pairs.shape[0] // len(plan.groups)
+    per_owner = skus[0].shape[0]
+    slots = len(skus) * per_owner
+    begins = total is None
+    cfg = (
+        sku_starts, len(given), room, [group], plan.starts[group], block, begins, ends,
+    )
+    sums = (slots + 1, block, rank)
+    out_shape = [VMEM(sums, jnp.float32), VMEM((8, rank), jnp.float32)]
+    if ends:
+        out_shape += [VMEM((per_owner, block, rank), jnp.bfloat16)] * len(skus)
+    inputs = [observed, *skus, *given] + ([] if begins else [total])
     return pl.pallas_call(
-        functools.partial(second_kernel, (ks, sku_starts, per_owner, kinds, block)),
-        out_shape=[VMEM(shape, jnp.bfloat16)] * len(ks),
-        in_specs=[spec(SMEM)] * 3 + [spec(VMEM)] * len(inputs),
-        out_specs=[spec(VMEM)] * len(ks),
-        scratch_shapes=[VMEM((plan.count * plan.rows, rank), jnp.bfloat16)],
-        compiler_params=params(16),
-        cost_estimate=cost(len(ks) * per_owner * kinds, block, rank),
-    )(row, live, ids, *map(near, inputs))
+        functools.partial(second_kernel, cfg),
+        out_shape=out_shape,
+        in_specs=[spec(SMEM)] * 2 + [spec(VMEM)] * len(inputs),
+        out_specs=[spec(VMEM)] * len(out_shape),
+        scratch_shapes=[
+            VMEM(sums, jnp.bfloat16),
+            VMEM((len(offsets) * plan.rows, rank), jnp.bfloat16),
+        ],
+        input_output_aliases={} if begins else {1 + len(inputs): 0},
+        compiler_params=params(12),
+        cost_estimate=cost(len(offsets) * room // plan.count, block, rank),
+    )(pairs, counts, *map(near, inputs))
 
 
 def take_terms(held, ids, terms, row, per_owner):
@@ -456,50 +480,53 @@
     swaps = [[(r, r ^ k) for r in range(row_count)] for k in range(row_count)]
     asked = [sku_ids] + [lax.ppermute(sku_ids, "row", swaps[k]) for k in range(1, row_count)]
     picked = pick(row_vec, asked, sku, per_owner)
-    moved = [
-        lax.ppermute(picked[1 + x], "row", swaps[2 * x]) for x in range(1, row_count // 2)
-    ]
-
     place = ring_place(lax.axis_index("col"), plan.count)
     owner_place = ring_place(store_ids // plan.blocks, plan.count)
     arrival = plan.arrival((owner_place - place) % plan.count)
     ids = arrival * plan.blocks + store_ids % plan.blocks
-    made = []
-
-    def prepare(pieces):
-        early = pieces[1] + pieces[plan.count - 1]
-        made.extend(
-            list_pairs(
-                row_vec, live, ids, observed, plan, row_count, per_owner, kinds, early
-            )
-        )
-        late = pieces[plan.far - 2] + pieces[plan.far + 2] + [made[2]]
-        made.append(
-            lax.ppermute(join(picked[1], moved, per_owner, late), "row", swaps[1])
-        )
-        return made[3][0]
-
-    pieces = gather_ring(store_factors.astype(jnp.bfloat16), plan, prepare)
-    pairs, counts, observed, passed = made
+    pieces = gather_ring(store_factors.astype(jnp.bfloat16), plan)
+    early = pieces[1] + pieces[plan.count - 1]
+    pairs, counts, observed, listed = list_pairs(
+        row_vec, live, ids, observed, plan, row_count, per_owner, kinds, early
+    )
+
+    direct, through = [], []
+    for x in range(1, row_count // 2):
+        direct.append(lax.ppermute(picked[2 * x], "row", swaps[2 * x]))
+        onward = after(after(picked[2 * x + 1], direct[-1][0]), listed)
+        through.append(lax.ppermute(onward, "row", swaps[2 * x]))
+    late = pieces[plan.far - 1] + pieces[plan.far + 1]
+    passed = lax.ppermute(join(picked[1], through, per_owner, late), "row", swaps[1])
     skus = [(picked[0], 0), (passed, 0)]
-    for x, both in enumerate(moved, 1):
-        skus += [(both, 0), (passed, x * per_owner)]
+    for x, blocks in enumerate(direct, 1):
+        skus += [(blocks, 0), (passed, x * per_owner)]
 
     grads, marks = {}, []
-    for group in (0, 2, 1):
+    for group in (2, 3, 1, 0):
         if plan.groups[group]:
             some = first_pass(pairs, counts, observed, skus, pieces, plan, [group], marks)
             grads.update(some)
             marks = some[plan.groups[group][0]][:1]
     own_grad = scatter_ring(grads, plan)
     new_store = store_factors - learn_rate * (own_grad + weight_decay * store_factors)
-    new_pieces = gather_ring(new_store.astype(jnp.bfloat16), plan)
-
-    terms = [None] * row_count
-    for ks in (list(range(2, row_count)), [1, 0]):
-        out = second_pass(ks, row_vec, live, ids, observed, skus, new_pieces, plan, per_owner)
-        for k, term in zip(ks, out):
-            terms[k] = lax.ppermute(term, "row", swaps[k]) if k else term
+    made, ties = [], {}
+
+    def add_group(step, pieces):
+        due = {1: 0, plan.far - 2: 1, plan.far - 1: 2, plan.far: 3}
+        if step in due:
+            group = due[step]
+            total = made[-1][0] if made else None
+            made.append(
+                second_pass(
+                    pairs, counts, observed, skus, pieces, plan, group, total, group == 3
+                )
+            )
+            if group < 2:
+                ties[step + 2] = made[-1][1]
+
+    gather_ring(new_store.astype(jnp.bfloat16), plan, ties, add_group)
+    out = made[-1][2:]
+    terms = [out[0]] + [lax.ppermute(out[k], "row", swaps[k]) for k in range(1, row_count)]
     held, new_sku = base_step(row_vec, asked[:2], sku, terms[:2], per_owner)
     new_sku = finish_step(row_vec, asked[2:], held, new_sku, terms[2:], per_owner)
     return new_sku.reshape(sku_factors.shape), new_store

time: 141 us -> 129 us (0.915); the launches traced: 139 us -> 129 us
  waiting for transfers between devices: 73 us -> 57.5 us
  Pallas kernels: 26 us -> 33.3 us
    ppermute x6, waiting for transfers between devices: 20.6 us -> 10.2 us  [scatter_ring(): moved[way] = lax.ppermute(value, 'col', steps[way])]
    ppermute x21 -> x22, waiting for transfers between devices: 45.1 us -> 38.5 us  [the longest x16 18.2 us: gather_ring(): moved = [lax.ppermute(moved[way], 'col', steps[way]) for way in (0, 1)]]
    pallas_call x2 -> x4, Pallas kernels: 6.16 us -> 12.1 us  [second_pass(): pl.pallas_call(functools.partial(second_kernel, cfg), out_shape=out_shape...]
    ppermute x6, starting transfers between devices: 9.35 us -> 7.74 us  [scatter_ring(): moved[way] = lax.ppermute(value, 'col', steps[way])]
    ppermute x2, waiting for transfers between devices: 3.66 us -> 5.19 us  [scatter_ring(): lax.ppermute(pieces[plan.far][way], 'col', steps[way])]
    pallas_call x3 -> x4, Pallas kernels: 10 us -> 11.3 us  [first_pass(): pl.pallas_call(functools.partial(first_kernel, cfg), out_shape=[VMEM((hei...]
    ppermute x21 -> x22, starting transfers between devices: 20.7 us -> 21.5 us  [the longest x16 18.4 us: gather_ring(): moved = [lax.ppermute(moved[way], 'col', steps[way]) for way in (0, 1)]]
  transfers between devices with their start and end apart: 32 -> 33, of which waited for: 20 -> 20; matrix products, arithmetic and copies ran while one was open for 1% -> 1% of each run, Pallas kernels for 14% -> 22%
where the time goes in v3:
time: 129 us
  waiting for transfers between devices  57.5 us (45%)
  starting transfers between devices  33.8 us (26%)
  Pallas kernels  33.3 us (26%)
  other arithmetic  2.89 us (2%)
    ppermute x16, starting transfers between devices, gather_ring(): moved = [lax.ppermute(moved[way], 'col', steps[way]) for way in (0, 1)]  18.4 us
    ppermute x16, waiting for transfers between devices, gather_ring(): moved = [lax.ppermute(moved[way], 'col', steps[way]) for way in (0, 1)]  18.2 us
    pallas_call x4, Pallas kernels, second_pass(): pl.pallas_call(functools.partial(second_kernel, cfg), out_shape=out_shape...  12.1 us
    pallas_call x4, Pallas kernels, first_pass(): pl.pallas_call(functools.partial(first_kernel, cfg), out_shape=[VMEM((hei...  11.3 us
    ppermute x6, waiting for transfers between devices, scatter_ring(): moved[way] = lax.ppermute(value, 'col', steps[way])  10.2 us
    ppermute x3, waiting for transfers between devices, local(): lax.ppermute(out[k], 'row', swaps[k])  9.79 us
    ppermute x6, starting transfers between devices, scatter_ring(): moved[way] = lax.ppermute(value, 'col', steps[way])  7.74 us
    ppermute x1, waiting for transfers between devices, local(): through.append(lax.ppermute(onward, 'row', swaps[2 * x]))  5.4 us
  transfers between devices with their start and end apart: 33, of which 20 were waited for; matrix products, arithmetic and copies ran while one was open for 1% of the time, Pallas kernels for 22%

profile of v3, /device:TPU:0, one launch (start us, length us, event | category | flops | bytes accessed | tf_op | source)
XLA Modules:
  0.0 129.1 jit_solution(9703932341434096023)
XLA Ops:
  0.6 1.1 convert_element_type.69.refs_4_
  1.8 3.1 %collective-permute-start.4 = (bf16[640,256]{1,0:T(8,128)(2,1)S(1)}, bf16[640,256]{1,0:T(8,128)(2,1)S(1)}, u32[]{:S(2)}, u32[]{:S(2)}) collective-permute-start(bf16[640,256]{1,0:T(8,128)(2,1)S(1)} %convert_element_type.69.refs_4_), channel_id=1, source_target_pairs={{0,2},{2,4},{4,6},{6,7},{7,5},{5,3},{3,1},{1,0},{8,10},{10,12},{12... | collective-permute-start | bytes 983048 | tf_op jit(solution)/shard_map/ppermute | solution.py:108
  4.9 2.0 %collective-permute-start.1 = (s32[16]{0:T(128)}, s32[16]{0:T(128)S(1)}, u32[]{:S(2)}, u32[]{:S(2)}) collective-permute-start(s32[16]{0:T(128)} %refs_0_.3), channel_id=1, source_target_pairs={{0,24},{8,16},{16,8},{24,0},{1,25},{9,17},{17,9},{25,1},{2,26},{10... | collective-permute-start | bytes 200 | tf_op jit(solution)/shard_map/ppermute | solution.py:481
  6.9 0.1 collective-permute-start
  7.0 1.3 %collective-permute-done.1.refs_3_.refs_1_ = s32[16]{0:T(128)S(1)} collective-permute-done((s32[16]{0:T(128)}, s32[16]{0:T(128)S(1)}, u32[]{:S(2)}, u32[]{:S(2)}) %collective-permute-start.1) | collective-permute-done | bytes 96 | tf_op jit(solution)/shard_map/ppermute | solution.py:481
  8.3 2.2 %collective-permute-done.refs_2_.refs_0_ = s32[16]{0:T(128)S(1)} collective-permute-done((s32[16]{0:T(128)}, s32[16]{0:T(128)S(1)}, u32[]{:S(2)}, u32[]{:S(2)}) %collective-permute-start) | collective-permute-done | bytes 96 | tf_op jit(solution)/shard_map/ppermute | solution.py:481
  10.6 0.7 copy-done.1
  11.2 2.3 %shard_map.78 = (bf16[4,128,256]{2,1,0:T(8,128)(2,1)S(1)}, bf16[4,128,256]{2,1,0:T(8,128)(2,1)S(1)}, bf16[4,128,256]{2,1,0:T(8,128)(2,1)S(1)}, bf16[4,128,256]{2,1,0:T(8,128)(2,1)S(1)}) custom-call(s32[1]{0:T(128)} %bitcast.row_ref, s32[16]{0:T(128)S(1)} %copy-done.1, s32[16]{0:T(128)S(1)} %collective-permute-done.2.refs_1_, ...), custom_call_target="tpu_custom_call" | custom-call | tf_op jit(solution)/shard_map/pallas_call | solution.py:168
  13.6 0.2 collective-permute-start.5
  13.8 2.0 %collective-permute-start.9 = (bf16[640,256]{1,0:T(8,128)(2,1)S(1)}, bf16[640,256]{1,0:T(8,128)(2,1)S(1)}, u32[]{:S(2)}, u32[]{:S(2)}) collective-permute-start(bf16[640,256]{1,0:T(8,128)(2,1)S(1)} %collective-permute-done.4.refs_1_.refs_6_), channel_id=1, source_target_pairs={{0,2},{2,4},{4,6},{6,7},{7,5},{5,3},{3,1},{1,0},{8,10},{10,12},{12... | collective-permute-start | bytes 983048 | tf_op jit(solution)/shard_map/ppermute | solution.py:108
  15.9 5.1 %collective-permute-done.5.refs_2_ = bf16[4,128,256]{2,1,0:T(8,128)(2,1)S(1)} collective-permute-done((bf16[4,128,256]{2,1,0:T(8,128)(2,1)S(1)}, bf16[4,128,256]{2,1,0:T(8,128)(2,1)S(1)}, u32[]{:S(2)}, u32[]{:S(2)}) %collective-permute-start.5) | collective-permute-done | bytes 262176 | tf_op jit(solution)/shard_map/ppermute | solution.py:495
  21.0 3.5 %shard_map.77 = (s32[544]{0:T(1024)S(1)}, s32[4]{0:T(128)S(1)}, bf16[16,8,128,128]{3,2,1,0:T(8,128)(2,1)S(1)}, f32[8,256]{1,0:T(8,128)S(1)}) custom-call(s32[1]{0:T(128)} %bitcast.row_ref, s32[4]{0:T(128)S(1)} %bitcast.6, s32[16,8]{1,0:T(8,128)S(1)} %fusion.5.ids_ref, bf16[16,8,128,128]{3,2,1,0:T(8,128)(2,1)} %observed.1, ...), custom_call_target="tpu_custom_call" | custom-call | tf_op jit(solution)/shard_map/pallas_call | solution.py:234
  24.6 1.6 %collective-permute-start.10 = (bf16[640,256]{1,0:T(8,128)(2,1)S(1)}, bf16[640,256]{1,0:T(8,128)(2,1)S(1)}, u32[]{:S(2)}, u32[]{:S(2)}) collective-permute-start(bf16[640,256]{1,0:T(8,128)(2,1)S(1)} %collective-permute-done.9.refs_5_), channel_id=1, source_target_pairs={{0,2},{2,4},{4,6},{6,7},{7,5},{5,3},{3,1},{1,0},{8,10},{10,12},{12... | collective-permute-start | bytes 983048 | tf_op jit(solution)/shard_map/ppermute | solution.py:108
  26.2 0.5 collective-permute-start.8
  26.7 1.0 collective-permute-start.6
  27.7 5.4 %collective-permute-done.6.refs_0_ = bf16[4,128,256]{2,1,0:T(8,128)(2,1)S(1)} collective-permute-done((bf16[4,128,256]{2,1,0:T(8,128)(2,1)S(1)}, bf16[4,128,256]{2,1,0:T(8,128)(2,1)S(1)}, u32[]{:S(2)}, u32[]{:S(2)}) %collective-permute-start.6) | collective-permute-done | bytes 262176 | tf_op jit(solution)/shard_map/ppermute | solution.py:497
  33.1 0.6 collective-permute-done.8.refs_1_.refs_4_
  33.9 1.6 %collective-permute-start.12 = (bf16[384,256]{1,0:T(8,128)(2,1)S(1)}, bf16[384,256]{1,0:T(8,128)(2,1)S(1)}, u32[]{:S(2)}, u32[]{:S(2)}) collective-permute-start(bf16[384,256]{1,0:T(8,128)(2,1)S(1)} %slice.54), channel_id=1, source_target_pairs={{0,2},{2,4},{4,6},{6,7},{7,5},{5,3},{3,1},{1,0},{8,10},{10,12},{12... | collective-permute-start | bytes 589832 | tf_op jit(solution)/shard_map/ppermute | solution.py:108
  35.5 0.5 collective-permute-start.13
  36.0 2.8 %shard_map.80 = (bf16[640,256]{1,0:T(8,128)(2,1)S(1)}, bf16[640,256]{1,0:T(8,128)(2,1)S(1)}) custom-call(s32[544]{0:T(1024)S(1)} %get-tuple-element.30.pairs_ref, s32[4]{0:T(128)S(1)} %get-tuple-element.31.counts_ref, bf16[16,8,128,128]{3,2,1,0:T(8,128)(2,1)S(1)} %get-tuple-element.32.observed, bf16[4,128,256]{2,1,0:T(8,128)(2,1)S(1)} %get-tuple-element.33.refs_0_, ...), custom_call_target="tpu_custom_call" | custom-call | flops 570425344 | bytes 8912896 | tf_op jit(solution)/shard_map/pallas_call | solution.py:320
  38.9 2.3 %collective-permute-done.13.refs_5_ = bf16[256,256]{1,0:T(8,128)(2,1)S(1)} collective-permute-done((bf16[256,256]{1,0:T(8,128)(2,1)S(1)}, bf16[256,256]{1,0:T(8,128)(2,1)S(1)}, u32[]{:S(2)}, u32[]{:S(2)}) %collective-permute-start.13) | collective-permute-done | bytes 131104 | tf_op jit(solution)/shard_map/ppermute | solution.py:108
  41.2 1.4 %shard_map.81 = (bf16[384,256]{1,0:T(8,128)(2,1)S(1)}, bf16[256,256]{1,0:T(8,128)(2,1)S(1)}) custom-call(s32[544]{0:T(1024)S(1)} %get-tuple-element.30.pairs_ref, s32[4]{0:T(128)S(1)} %get-tuple-element.31.counts_ref, bf16[16,8,128,128]{3,2,1,0:T(8,128)(2,1)S(1)} %get-tuple-element.32.observed, bf16[4,128,256]{2,1,0:T(8,128)(2,1)S(1)} %get-tuple-element.33.refs_0_, ...), custom_call_target="tpu_custom_call" | custom-call | flops 285212672 | bytes 4456448 | tf_op jit(solution)/shard_map/pallas_call | solution.py:320
  42.7 1.6 %collective-permute-start.18 = (bf16[256,256]{1,0:T(8,128)(2,1)S(1)}, bf16[256,256]{1,0:T(8,128)(2,1)S(1)}, u32[]{:S(2)}, u32[]{:S(2)}) collective-permute-start(bf16[256,256]{1,0:T(8,128)(2,1)S(1)} %get-tuple-element.44), channel_id=1, source_target_pairs={{2,0},{4,2},{6,4},{7,6},{5,7},{3,5},{1,3},{0,1},{10,8},{12,10},{14... | collective-permute-start | bytes 393224 | tf_op jit(solution)/shard_map/ppermute | solution.py:126
  44.3 0.8 collective-permute-start.14
  45.1 4.1 %collective-permute-done.18 = bf16[256,256]{1,0:T(8,128)(2,1)S(1)} collective-permute-done((bf16[256,256]{1,0:T(8,128)(2,1)S(1)}, bf16[256,256]{1,0:T(8,128)(2,1)S(1)}, u32[]{:S(2)}, u32[]{:S(2)}) %collective-permute-start.18) | collective-permute-done | bytes 131104 | tf_op jit(solution)/shard_map/ppermute | solution.py:126
  49.2 0.3 collective-permute-start.19
  49.6 1.1 collective-permute-done.14
  50.8 1.8 %collective-permute-start.15 = (bf16[640,256]{1,0:T(8,128)(2,1)S(1)}, bf16[640,256]{1,0:T(8,128)(2,1)S(1)}, u32[]{:S(2)}, u32[]{:S(2)}) collective-permute-start(bf16[640,256]{1,0:T(8,128)(2,1)S(1)} %pad_maximum_fusion), channel_id=1, source_target_pairs={{0,2},{2,4},{4,6},{6,7},{7,5},{5,3},{3,1},{1,0},{8,10},{10,12},{12... | collective-permute-start | bytes 983048 | tf_op jit(solution)/shard_map/ppermute | solution.py:136
  52.5 2.8 %shard_map.82 = (bf16[640,256]{1,0:T(8,128)(2,1)S(1)}, bf16[640,256]{1,0:T(8,128)(2,1)S(1)}) custom-call(s32[544]{0:T(1024)S(1)} %get-tuple-element.30.pairs_ref, s32[4]{0:T(128)S(1)} %get-tuple-element.31.counts_ref, bf16[16,8,128,128]{3,2,1,0:T(8,128)(2,1)S(1)} %get-tuple-element.32.observed, bf16[4,128,256]{2,1,0:T(8,128)(2,1)S(1)} %get-tuple-element.33.refs_0_, ...), custom_call_target="tpu_custom_call" | custom-call | flops 570425344 | bytes 8912896 | tf_op jit(solution)/shard_map/pallas_call | solution.py:320
  55.4 3.5 %collective-permute-done.19 = bf16[640,256]{1,0:T(8,128)(2,1)S(1)} collective-permute-done((bf16[640,256]{1,0:T(8,128)(2,1)S(1)}, bf16[640,256]{1,0:T(8,128)(2,1)S(1)}, u32[]{:S(2)}, u32[]{:S(2)}) %collective-permute-start.19) | collective-permute-done | bytes 327712 | tf_op jit(solution)/shard_map/ppermute | solution.py:136
  58.8 0.1 add_convert_fusion.1
  58.9 0.3 collective-permute-start.20
  59.3 0.1 collective-permute-done.15
  59.4 0.1 add_convert_fusion.3
  59.5 2.5 %collective-permute-start.16 = (bf16[640,256]{1,0:T(8,128)(2,1)S(1)}, bf16[640,256]{1,0:T(8,128)(2,1)S(1)}, u32[]{:S(2)}, u32[]{:S(2)}) collective-permute-start(bf16[640,256]{1,0:T(8,128)(2,1)S(1)} %add_convert_fusion.3), channel_id=1, source_target_pairs={{0,2},{2,4},{4,6},{6,7},{7,5},{5,3},{3,1},{1,0},{8,10},{10,12},{12... | collective-permute-start | bytes 983048 | tf_op jit(solution)/shard_map/ppermute | solution.py:136
  62.0 4.3 %shard_map.83 = (bf16[640,256]{1,0:T(8,128)(2,1)S(1)}, bf16[640,256]{1,0:T(8,128)(2,1)S(1)}, bf16[640,256]{1,0:T(8,128)(2,1)S(1)}) custom-call(s32[544]{0:T(1024)S(1)} %get-tuple-element.30.pairs_ref, s32[4]{0:T(128)S(1)} %get-tuple-element.31.counts_ref, bf16[16,8,128,128]{3,2,1,0:T(8,128)(2,1)S(1)} %get-tuple-element.32.observed, ...), custom_call_target="tpu_custom_call" | custom-call | flops 855638016 | bytes 13369344 | tf_op jit(solution)/shard_map/pallas_call | solution.py:320
  66.3 1.4 %collective-permute-done.20 = bf16[640,256]{1,0:T(8,128)(2,1)S(1)} collective-permute-done((bf16[640,256]{1,0:T(8,128)(2,1)S(1)}, bf16[640,256]{1,0:T(8,128)(2,1)S(1)}, u32[]{:S(2)}, u32[]{:S(2)}) %collective-permute-start.20) | collective-permute-done | bytes 327712 | tf_op jit(solution)/shard_map/ppermute | solution.py:136
  67.7 0.1 add_convert_fusion
  67.8 0.3 collective-permute-start.21
  68.1 0.1 add_convert_fusion.2
  68.2 2.4 %collective-permute-start.17 = (bf16[640,256]{1,0:T(8,128)(2,1)S(1)}, bf16[640,256]{1,0:T(8,128)(2,1)S(1)}, u32[]{:S(2)}, u32[]{:S(2)}) collective-permute-start(bf16[640,256]{1,0:T(8,128)(2,1)S(1)} %add_convert_fusion.2), channel_id=1, source_target_pairs={{0,2},{2,4},{4,6},{6,7},{7,5},{5,3},{3,1},{1,0},{8,10},{10,12},{12... | collective-permute-start | bytes 983048 | tf_op jit(solution)/shard_map/ppermute | solution.py:136
  70.6 5.0 %collective-permute-done.21 = bf16[640,256]{1,0:T(8,128)(2,1)S(1)} collective-permute-done((bf16[640,256]{1,0:T(8,128)(2,1)S(1)}, bf16[640,256]{1,0:T(8,128)(2,1)S(1)}, u32[]{:S(2)}, u32[]{:S(2)}) %collective-permute-start.21) | collective-permute-done | bytes 327712 | tf_op jit(solution)/shard_map/ppermute | solution.py:136
  75.6 0.2 collective-permute-done.17
  75.8 1.0 fusion.10
  76.8 2.4 %collective-permute-start.24 = (bf16[640,256]{1,0:T(8,128)(2,1)S(1)}, bf16[640,256]{1,0:T(8,128)(2,1)S(1)}, u32[]{:S(2)}, u32[]{:S(2)}) collective-permute-start(bf16[640,256]{1,0:T(8,128)(2,1)S(1)} %get-tuple-element.58.refs_4_), channel_id=1, source_target_pairs={{0,2},{2,4},{4,6},{6,7},{7,5},{5,3},{3,1},{1,0},{8,10},{10,12},{12... | collective-permute-start | bytes 983048 | tf_op jit(solution)/shard_map/ppermute | solution.py:108
  79.2 6.1 %collective-permute-done.24.refs_6_ = bf16[640,256]{1,0:T(8,128)(2,1)S(1)} collective-permute-done((bf16[640,256]{1,0:T(8,128)(2,1)S(1)}, bf16[640,256]{1,0:T(8,128)(2,1)S(1)}, u32[]{:S(2)}, u32[]{:S(2)}) %collective-permute-start.24) | collective-permute-done | bytes 327712 | tf_op jit(solution)/shard_map/ppermute | solution.py:108
  85.3 2.5 %collective-permute-start.25 = (bf16[640,256]{1,0:T(8,128)(2,1)S(1)}, bf16[640,256]{1,0:T(8,128)(2,1)S(1)}, u32[]{:S(2)}, u32[]{:S(2)}) collective-permute-start(bf16[640,256]{1,0:T(8,128)(2,1)S(1)} %collective-permute-done.24.refs_6_), channel_id=1, source_target_pairs={{0,2},{2,4},{4,6},{6,7},{7,5},{5,3},{3,1},{1,0},{8,10},{10,12},{12... | collective-permute-start | bytes 983048 | tf_op jit(solution)/shard_map/ppermute | solution.py:108
  87.8 4.2 %shard_map.84 = (f32[17,128,256]{2,1,0:T(8,128)S(1)}, f32[8,256]{1,0:T(8,128)S(1)}) custom-call(s32[544]{0:T(1024)S(1)} %get-tuple-element.30.pairs_ref, s32[4]{0:T(128)S(1)} %get-tuple-element.31.counts_ref, bf16[16,8,128,128]{3,2,1,0:T(8,128)(2,1)S(1)} %get-tuple-element.32.observed, bf16[4,128,256]{2,1,0:T(8,128)(2,1)S(1)} %get-tuple-element.33.refs_0_, ...), custom_call_target="tpu_custom_call" | custom-call | flops 855638016 | bytes 13369344 | tf_op jit(solution)/shard_map/pallas_call | solution.py:387
  92.0 2.2 %collective-permute-done.25.refs_5_ = bf16[640,256]{1,0:T(8,128)(2,1)S(1)} collective-permute-done((bf16[640,256]{1,0:T(8,128)(2,1)S(1)}, bf16[640,256]{1,0:T(8,128)(2,1)S(1)}, u32[]{:S(2)}, u32[]{:S(2)}) %collective-permute-start.25) | collective-permute-done | bytes 327712 | tf_op jit(solution)/shard_map/ppermute | solution.py:108
  94.2 2.7 %collective-permute-done.23.refs_4_ = bf16[640,256]{1,0:T(8,128)(2,1)S(1)} collective-permute-done((bf16[640,256]{1,0:T(8,128)(2,1)S(1)}, bf16[640,256]{1,0:T(8,128)(2,1)S(1)}, u32[]{:S(2)}, u32[]{:S(2)}) %collective-permute-start.23) | collective-permute-done | bytes 327712 | tf_op jit(solution)/shard_map/ppermute | solution.py:108
  97.0 0.1 collective-permute-start.26
  97.2 1.9 %collective-permute-start.28 = (bf16[640,256]{1,0:T(8,128)(2,1)S(1)}, bf16[640,256]{1,0:T(8,128)(2,1)S(1)}, u32[]{:S(2)}, u32[]{:S(2)}) collective-permute-start(bf16[640,256]{1,0:T(8,128)(2,1)S(1)} %get-tuple-element.60), channel_id=1, source_target_pairs={{2,0},{4,2},{6,4},{7,6},{5,7},{3,5},{1,3},{0,1},{10,8},{12,10},{14... | collective-permute-start | bytes 983048 | tf_op jit(solution)/shard_map/ppermute | solution.py:108
  99.1 2.7 %shard_map.85 = (f32[17,128,256]{2,1,0:T(8,128)S(1)}, f32[8,256]{1,0:T(8,128)S(1)}) custom-call(s32[544]{0:T(1024)S(1)} %get-tuple-element.30.pairs_ref, s32[4]{0:T(128)S(1)} %get-tuple-element.31.counts_ref, bf16[16,8,128,128]{3,2,1,0:T(8,128)(2,1)S(1)} %get-tuple-element.32.observed, ...), custom_call_target="tpu_custom_call", output_to_operand_aliasing={{0}: (9, {})} | custom-call | flops 570425344 | bytes 8912896 | tf_op jit(solution)/shard_map/pallas_call | solution.py:387
  101.8 2.7 %collective-permute-done.26.refs_5_ = bf16[640,256]{1,0:T(8,128)(2,1)S(1)} collective-permute-done((bf16[640,256]{1,0:T(8,128)(2,1)S(1)}, bf16[640,256]{1,0:T(8,128)(2,1)S(1)}, u32[]{:S(2)}, u32[]{:S(2)}) %collective-permute-start.26) | collective-permute-done | bytes 327712 | tf_op jit(solution)/shard_map/ppermute | solution.py:108
  104.5 1.9 %collective-permute-start.27 = (bf16[384,256]{1,0:T(8,128)(2,1)S(1)}, bf16[384,256]{1,0:T(8,128)(2,1)S(1)}, u32[]{:S(2)}, u32[]{:S(2)}) collective-permute-start(bf16[384,256]{1,0:T(8,128)(2,1)S(1)} %slice_select_fusion), channel_id=1, source_target_pairs={{0,2},{2,4},{4,6},{6,7},{7,5},{5,3},{3,1},{1,0},{8,10},{10,12},{12... | collective-permute-start | bytes 589832 | tf_op jit(solution)/shard_map/ppermute | solution.py:108
  106.4 0.3 collective-permute-start.29
  106.7 3.3 %shard_map.86 = (f32[17,128,256]{2,1,0:T(8,128)S(1)}, f32[8,256]{1,0:T(8,128)}) custom-call(s32[544]{0:T(1024)S(1)} %get-tuple-element.30.pairs_ref, s32[4]{0:T(128)S(1)} %get-tuple-element.31.counts_ref, bf16[16,8,128,128]{3,2,1,0:T(8,128)(2,1)S(1)} %get-tuple-element.32.observed, ...), custom_call_target="tpu_custom_call", output_to_operand_aliasing={{0}: (9, {})} | custom-call | flops 570425344 | bytes 8912896 | tf_op jit(solution)/shard_map/pallas_call | solution.py:387
  110.0 1.5 %collective-permute-done.29.refs_5_ = bf16[256,256]{1,0:T(8,128)(2,1)S(1)} collective-permute-done((bf16[256,256]{1,0:T(8,128)(2,1)S(1)}, bf16[256,256]{1,0:T(8,128)(2,1)S(1)}, u32[]{:S(2)}, u32[]{:S(2)}) %collective-permute-start.29) | collective-permute-done | bytes 131104 | tf_op jit(solution)/shard_map/ppermute | solution.py:108
  111.5 1.9 %shard_map.87 = (f32[17,128,256]{2,1,0:T(8,128)S(1)}, f32[8,256]{1,0:T(8,128)}, bf16[4,128,256]{2,1,0:T(8,128)(2,1)S(1)}, bf16[4,128,256]{2,1,0:T(8,128)(2,1)S(1...) custom-call(s32[544]{0:T(1024)S(1)} %get-tuple-element.30.pairs_ref, ...), custom_call_target="tpu_custom_call", output_to_operand_aliasing={{0}: (9, {})} | custom-call | flops 285212672 | bytes 4456448 | tf_op jit(solution)/shard_map/pallas_call | solution.py:387
  113.4 1.9 %collective-permute-start.32 = (bf16[4,128,256]{2,1,0:T(8,128)(2,1)S(1)}, bf16[4,128,256]{2,1,0:T(8,128)(2,1)S(1)}, u32[]{:S(2)}, u32[]{:S(2)}) collective-permute-start(bf16[4,128,256]{2,1,0:T(8,128)(2,1)S(1)} %get-tuple-element.56), channel_id=1, source_target_pairs={{0,24},{8,16},{16,8},{24,0},{1,25},{9,17},{17,9},{25,1},{2,26},{10... | collective-permute-start | bytes 786440 | tf_op jit(solution)/shard_map/ppermute | solution.py:529
  115.3 2.3 %shard_map.88 = (f32[16,128,256]{2,1,0:T(8,128)S(1)}, f32[16,128,256]{2,1,0:T(8,128)}) custom-call(s32[1]{0:T(128)} %bitcast.row_ref, s32[16]{0:T(128)S(1)} %copy-done.2, s32[16]{0:T(128)S(1)} %collective-permute-done.2.refs_1_, f32[16,128,256]{2,1,0:T(8,128)S(1)} %bitcast.5, bf16[4,128,256]{2,1,0:T(8,128)(2,1)S(1)} %get-tuple-element.52.refs_3_, ...), custom_call_target="tpu_custom_call" | custom-call | tf_op jit(solution)/shard_map/pallas_call | solution.py:432
  117.6 4.9 %collective-permute-done.31.refs_3_ = bf16[4,128,256]{2,1,0:T(8,128)(2,1)S(1)} collective-permute-done((bf16[4,128,256]{2,1,0:T(8,128)(2,1)S(1)}, bf16[4,128,256]{2,1,0:T(8,128)(2,1)S(1)}, u32[]{:S(2)}, u32[]{:S(2)}) %collective-permute-start.31) | collective-permute-done | bytes 262176 | tf_op jit(solution)/shard_map/ppermute | solution.py:529
  122.5 4.8 %collective-permute-done.32.refs_4_ = bf16[4,128,256]{2,1,0:T(8,128)(2,1)S(1)} collective-permute-done((bf16[4,128,256]{2,1,0:T(8,128)(2,1)S(1)}, bf16[4,128,256]{2,1,0:T(8,128)(2,1)S(1)}, u32[]{:S(2)}, u32[]{:S(2)}) %collective-permute-start.32) | collective-permute-done | bytes 262176 | tf_op jit(solution)/shard_map/ppermute | solution.py:529
  127.4 1.8 %shard_map.89 = f32[16,128,256]{2,1,0:T(8,128)} custom-call(s32[1]{0:T(128)} %bitcast.row_ref, s32[16]{0:T(128)S(1)} %collective-permute-done.refs_2_.refs_0_, s32[16]{0:T(128)S(1)} %collective-permute-done.1.refs_3_.refs_1_, f32[16,128,256]{2,1,0:T(8,128)S(1)} %get-tuple-element.54.refs_2_, ...), custom_call_target="tpu_custom_call", output_to_operand_aliasing={{}: (6, {})} | custom-call | tf_op jit(solution)/shard_map/pallas_call | solution.py:454
  (51 shorter events, 0.7 us)
Async XLA Ops:
  0.6 13.1 %copy-start.5 = (s32[16,8]{0,1:T(8,128)S(1)}, s32[16,8]{0,1:T(8,128)}, u32[]{:S(2)}) copy-start(s32[16,8]{0,1:T(8,128)} %param.8) | copy-start | bytes 1540
  0.6 20.4 %copy-start.3 = (s32[1,1,4]{2,1,0:T(1,128)S(1)}, s32[1,1,4]{2,1,0:T(1,128)}, u32[]{:S(2)}) copy-start(s32[1,1,4]{2,1,0:T(1,128)} %param.9) | copy-start | bytes 52
  1.8 12.0 %collective-permute-start.4 = (bf16[640,256]{1,0:T(8,128)(2,1)S(1)}, bf16[640,256]{1,0:T(8,128)(2,1)S(1)}, u32[]{:S(2)}, u32[]{:S(2)}) collective-permute-start(bf16[640,256]{1,0:T(8,128)(2,1)S(1)} %convert_element_type.69.refs_4_), channel_id=1, source_target_pairs={{0,2},{2,4},{4,6},{6,7},{7,5},{5,3},{3,1},{1,0},{8,10},{10,12},{12... | collective-permute-start | bytes 983048 | tf_op jit(solution)/shard_map/ppermute | solution.py:108
  4.9 11.0 %collective-permute-start.3 = (bf16[640,256]{1,0:T(8,128)(2,1)S(1)}, bf16[640,256]{1,0:T(8,128)(2,1)S(1)}, u32[]{:S(2)}, u32[]{:S(2)}) collective-permute-start(bf16[640,256]{1,0:T(8,128)(2,1)S(1)} %convert_element_type.69.refs_4_), channel_id=1, source_target_pairs={{2,0},{4,2},{6,4},{7,6},{5,7},{3,5},{1,3},{0,1},{10,8},{12,10},{14... | collective-permute-start | bytes 983048 | tf_op jit(solution)/shard_map/ppermute | solution.py:108
  4.9 2.1 %collective-permute-start.2 = (s32[16]{0:T(128)}, s32[16]{0:T(128)S(1)}, u32[]{:S(2)}, u32[]{:S(2)}) collective-permute-start(s32[16]{0:T(128)} %refs_0_.3), channel_id=1, source_target_pairs={{0,8},{8,0},{16,24},{24,16},{1,9},{9,1},{17,25},{25,17},{2,10},{10... | collective-permute-start | bytes 200 | tf_op jit(solution)/shard_map/ppermute | solution.py:481
  4.9 3.5 %collective-permute-start.1 = (s32[16]{0:T(128)}, s32[16]{0:T(128)S(1)}, u32[]{:S(2)}, u32[]{:S(2)}) collective-permute-start(s32[16]{0:T(128)} %refs_0_.3), channel_id=1, source_target_pairs={{0,24},{8,16},{16,8},{24,0},{1,25},{9,17},{17,9},{25,1},{2,26},{10... | collective-permute-start | bytes 200 | tf_op jit(solution)/shard_map/ppermute | solution.py:481
  6.9 3.7 %collective-permute-start = (s32[16]{0:T(128)}, s32[16]{0:T(128)S(1)}, u32[]{:S(2)}, u32[]{:S(2)}) collective-permute-start(s32[16]{0:T(128)} %refs_0_.3), channel_id=1, source_target_pairs={{0,16},{8,24},{16,0},{24,8},{1,17},{9,25},{17,1},{25,9},{2,18},{10... | collective-permute-start | bytes 200 | tf_op jit(solution)/shard_map/ppermute | solution.py:481
  10.6 0.7 copy-start.1
  13.6 7.4 %collective-permute-start.5 = (bf16[4,128,256]{2,1,0:T(8,128)(2,1)S(1)}, bf16[4,128,256]{2,1,0:T(8,128)(2,1)S(1)}, u32[]{:S(2)}, u32[]{:S(2)}) collective-permute-start(bf16[4,128,256]{2,1,0:T(8,128)(2,1)S(1)} %get-tuple-element.36), channel_id=1, source_target_pairs={{0,16},{8,24},{16,0},{24,8},{1,17},{9,25},{17,1},{25,9},{2,18},{10... | collective-permute-start | bytes 786440 | tf_op jit(solution)/shard_map/ppermute | solution.py:495
  13.8 10.8 %collective-permute-start.9 = (bf16[640,256]{1,0:T(8,128)(2,1)S(1)}, bf16[640,256]{1,0:T(8,128)(2,1)S(1)}, u32[]{:S(2)}, u32[]{:S(2)}) collective-permute-start(bf16[640,256]{1,0:T(8,128)(2,1)S(1)} %collective-permute-done.4.refs_1_.refs_6_), channel_id=1, source_target_pairs={{0,2},{2,4},{4,6},{6,7},{7,5},{5,3},{3,1},{1,0},{8,10},{10,12},{12... | collective-permute-start | bytes 983048 | tf_op jit(solution)/shard_map/ppermute | solution.py:108
  15.8 10.4 %collective-permute-start.7 = (bf16[640,256]{1,0:T(8,128)(2,1)S(1)}, bf16[640,256]{1,0:T(8,128)(2,1)S(1)}, u32[]{:S(2)}, u32[]{:S(2)}) collective-permute-start(bf16[640,256]{1,0:T(8,128)(2,1)S(1)} %collective-permute-done.3.refs_0_.refs_5_), channel_id=1, source_target_pairs={{2,0},{4,2},{6,4},{7,6},{5,7},{3,5},{1,3},{0,1},{10,8},{12,10},{14... | collective-permute-start | bytes 983048 | tf_op jit(solution)/shard_map/ppermute | solution.py:108
  24.6 8.6 %collective-permute-start.10 = (bf16[640,256]{1,0:T(8,128)(2,1)S(1)}, bf16[640,256]{1,0:T(8,128)(2,1)S(1)}, u32[]{:S(2)}, u32[]{:S(2)}) collective-permute-start(bf16[640,256]{1,0:T(8,128)(2,1)S(1)} %collective-permute-done.9.refs_5_), channel_id=1, source_target_pairs={{0,2},{2,4},{4,6},{6,7},{7,5},{5,3},{3,1},{1,0},{8,10},{10,12},{12... | collective-permute-start | bytes 983048 | tf_op jit(solution)/shard_map/ppermute | solution.py:108
  26.2 7.6 %collective-permute-start.8 = (bf16[640,256]{1,0:T(8,128)(2,1)S(1)}, bf16[640,256]{1,0:T(8,128)(2,1)S(1)}, u32[]{:S(2)}, u32[]{:S(2)}) collective-permute-start(bf16[640,256]{1,0:T(8,128)(2,1)S(1)} %collective-permute-done.7.refs_4_), channel_id=1, source_target_pairs={{2,0},{4,2},{6,4},{7,6},{5,7},{3,5},{1,3},{0,1},{10,8},{12,10},{14... | collective-permute-start | bytes 983048 | tf_op jit(solution)/shard_map/ppermute | solution.py:108
  26.7 6.4 %collective-permute-start.6 = (bf16[4,128,256]{2,1,0:T(8,128)(2,1)S(1)}, bf16[4,128,256]{2,1,0:T(8,128)(2,1)S(1)}, u32[]{:S(2)}, u32[]{:S(2)}) collective-permute-start(bf16[4,128,256]{2,1,0:T(8,128)(2,1)S(1)} %select_select_fusion), channel_id=1, source_target_pairs={{0,16},{8,24},{16,0},{24,8},{1,17},{9,25},{17,1},{25,9},{2,18},{10... | collective-permute-start | bytes 786440 | tf_op jit(solution)/shard_map/ppermute | solution.py:497
  33.8 2.2 %collective-permute-start.11 = (bf16[8,128,256]{2,1,0:T(8,128)(2,1)S(1)}, bf16[8,128,256]{2,1,0:T(8,128)(2,1)S(1)}, u32[]{:S(2)}, u32[]{:S(2)}) collective-permute-start(bf16[8,128,256]{2,1,0:T(8,128)(2,1)S(1)} %shard_map.79), channel_id=1, source_target_pairs={{0,8},{8,0},{16,24},{24,16},{1,9},{9,1},{17,25},{25,17},{2,10},{10... | collective-permute-start | bytes 1572872 | tf_op jit(solution)/shard_map/ppermute | solution.py:499
  33.9 7.3 %collective-permute-start.12 = (bf16[384,256]{1,0:T(8,128)(2,1)S(1)}, bf16[384,256]{1,0:T(8,128)(2,1)S(1)}, u32[]{:S(2)}, u32[]{:S(2)}) collective-permute-start(bf16[384,256]{1,0:T(8,128)(2,1)S(1)} %slice.54), channel_id=1, source_target_pairs={{0,2},{2,4},{4,6},{6,7},{7,5},{5,3},{3,1},{1,0},{8,10},{10,12},{12... | collective-permute-start | bytes 589832 | tf_op jit(solution)/shard_map/ppermute | solution.py:108
  35.5 5.7 %collective-permute-start.13 = (bf16[256,256]{1,0:T(8,128)(2,1)S(1)}, bf16[256,256]{1,0:T(8,128)(2,1)S(1)}, u32[]{:S(2)}, u32[]{:S(2)}) collective-permute-start(bf16[256,256]{1,0:T(8,128)(2,1)S(1)} %slice.55), channel_id=1, source_target_pairs={{2,0},{4,2},{6,4},{7,6},{5,7},{3,5},{1,3},{0,1},{10,8},{12,10},{14... | collective-permute-start | bytes 393224 | tf_op jit(solution)/shard_map/ppermute | solution.py:108
  42.7 6.5 %collective-permute-start.18 = (bf16[256,256]{1,0:T(8,128)(2,1)S(1)}, bf16[256,256]{1,0:T(8,128)(2,1)S(1)}, u32[]{:S(2)}, u32[]{:S(2)}) collective-permute-start(bf16[256,256]{1,0:T(8,128)(2,1)S(1)} %get-tuple-element.44), channel_id=1, source_target_pairs={{2,0},{4,2},{6,4},{7,6},{5,7},{3,5},{1,3},{0,1},{10,8},{12,10},{14... | collective-permute-start | bytes 393224 | tf_op jit(solution)/shard_map/ppermute | solution.py:126
  44.3 6.4 %collective-permute-start.14 = (bf16[384,256]{1,0:T(8,128)(2,1)S(1)}, bf16[384,256]{1,0:T(8,128)(2,1)S(1)}, u32[]{:S(2)}, u32[]{:S(2)}) collective-permute-start(bf16[384,256]{1,0:T(8,128)(2,1)S(1)} %get-tuple-element.39.refs_6_), channel_id=1, source_target_pairs={{0,2},{2,4},{4,6},{6,7},{7,5},{5,3},{3,1},{1,0},{8,10},{10,12},{12... | collective-permute-start | bytes 589832 | tf_op jit(solution)/shard_map/ppermute | solution.py:126
  49.2 9.6 %collective-permute-start.19 = (bf16[640,256]{1,0:T(8,128)(2,1)S(1)}, bf16[640,256]{1,0:T(8,128)(2,1)S(1)}, u32[]{:S(2)}, u32[]{:S(2)}) collective-permute-start(bf16[640,256]{1,0:T(8,128)(2,1)S(1)} %pad_maximum_fusion.1), channel_id=1, source_target_pairs={{2,0},{4,2},{6,4},{7,6},{5,7},{3,5},{1,3},{0,1},{10,8},{12,10},{14... | collective-permute-start | bytes 983048 | tf_op jit(solution)/shard_map/ppermute | solution.py:136
  50.8 8.7 %collective-permute-start.15 = (bf16[640,256]{1,0:T(8,128)(2,1)S(1)}, bf16[640,256]{1,0:T(8,128)(2,1)S(1)}, u32[]{:S(2)}, u32[]{:S(2)}) collective-permute-start(bf16[640,256]{1,0:T(8,128)(2,1)S(1)} %pad_maximum_fusion), channel_id=1, source_target_pairs={{0,2},{2,4},{4,6},{6,7},{7,5},{5,3},{3,1},{1,0},{8,10},{10,12},{12... | collective-permute-start | bytes 983048 | tf_op jit(solution)/shard_map/ppermute | solution.py:136
  58.9 8.8 %collective-permute-start.20 = (bf16[640,256]{1,0:T(8,128)(2,1)S(1)}, bf16[640,256]{1,0:T(8,128)(2,1)S(1)}, u32[]{:S(2)}, u32[]{:S(2)}) collective-permute-start(bf16[640,256]{1,0:T(8,128)(2,1)S(1)} %add_convert_fusion.1), channel_id=1, source_target_pairs={{2,0},{4,2},{6,4},{7,6},{5,7},{3,5},{1,3},{0,1},{10,8},{12,10},{14... | collective-permute-start | bytes 983048 | tf_op jit(solution)/shard_map/ppermute | solution.py:136
  59.5 8.6 %collective-permute-start.16 = (bf16[640,256]{1,0:T(8,128)(2,1)S(1)}, bf16[640,256]{1,0:T(8,128)(2,1)S(1)}, u32[]{:S(2)}, u32[]{:S(2)}) collective-permute-start(bf16[640,256]{1,0:T(8,128)(2,1)S(1)} %add_convert_fusion.3), channel_id=1, source_target_pairs={{0,2},{2,4},{4,6},{6,7},{7,5},{5,3},{3,1},{1,0},{8,10},{10,12},{12... | collective-permute-start | bytes 983048 | tf_op jit(solution)/shard_map/ppermute | solution.py:136
  66.3 9.5 %copy-start.4 = (f32[640,256]{1,0:T(8,128)S(1)}, f32[640,256]{1,0:T(8,128)}, u32[]{:S(2)}) copy-start(f32[640,256]{1,0:T(8,128)} %param.11) | copy-start | bytes 1966084
  67.8 7.8 %collective-permute-start.21 = (bf16[640,256]{1,0:T(8,128)(2,1)S(1)}, bf16[640,256]{1,0:T(8,128)(2,1)S(1)}, u32[]{:S(2)}, u32[]{:S(2)}) collective-permute-start(bf16[640,256]{1,0:T(8,128)(2,1)S(1)} %add_convert_fusion), channel_id=1, source_target_pairs={{2,0},{4,2},{6,4},{7,6},{5,7},{3,5},{1,3},{0,1},{10,8},{12,10},{14... | collective-permute-start | bytes 983048 | tf_op jit(solution)/shard_map/ppermute | solution.py:136
  68.2 7.6 %collective-permute-start.17 = (bf16[640,256]{1,0:T(8,128)(2,1)S(1)}, bf16[640,256]{1,0:T(8,128)(2,1)S(1)}, u32[]{:S(2)}, u32[]{:S(2)}) collective-permute-start(bf16[640,256]{1,0:T(8,128)(2,1)S(1)} %add_convert_fusion.2), channel_id=1, source_target_pairs={{0,2},{2,4},{4,6},{6,7},{7,5},{5,3},{3,1},{1,0},{8,10},{10,12},{12... | collective-permute-start | bytes 983048 | tf_op jit(solution)/shard_map/ppermute | solution.py:136
  76.8 8.4 %collective-permute-start.24 = (bf16[640,256]{1,0:T(8,128)(2,1)S(1)}, bf16[640,256]{1,0:T(8,128)(2,1)S(1)}, u32[]{:S(2)}, u32[]{:S(2)}) collective-permute-start(bf16[640,256]{1,0:T(8,128)(2,1)S(1)} %get-tuple-element.58.refs_4_), channel_id=1, source_target_pairs={{0,2},{2,4},{4,6},{6,7},{7,5},{5,3},{3,1},{1,0},{8,10},{10,12},{12... | collective-permute-start | bytes 983048 | tf_op jit(solution)/shard_map/ppermute | solution.py:108
  79.2 8.6 %collective-permute-start.22 = (bf16[640,256]{1,0:T(8,128)(2,1)S(1)}, bf16[640,256]{1,0:T(8,128)(2,1)S(1)}, u32[]{:S(2)}, u32[]{:S(2)}) collective-permute-start(bf16[640,256]{1,0:T(8,128)(2,1)S(1)} %get-tuple-element.58.refs_4_), channel_id=1, source_target_pairs={{2,0},{4,2},{6,4},{7,6},{5,7},{3,5},{1,3},{0,1},{10,8},{12,10},{14... | collective-permute-start | bytes 983048 | tf_op jit(solution)/shard_map/ppermute | solution.py:108
  85.3 9.0 %collective-permute-start.25 = (bf16[640,256]{1,0:T(8,128)(2,1)S(1)}, bf16[640,256]{1,0:T(8,128)(2,1)S(1)}, u32[]{:S(2)}, u32[]{:S(2)}) collective-permute-start(bf16[640,256]{1,0:T(8,128)(2,1)S(1)} %collective-permute-done.24.refs_6_), channel_id=1, source_target_pairs={{0,2},{2,4},{4,6},{6,7},{7,5},{5,3},{3,1},{1,0},{8,10},{10,12},{12... | collective-permute-start | bytes 983048 | tf_op jit(solution)/shard_map/ppermute | solution.py:108
  87.8 9.2 %collective-permute-start.23 = (bf16[640,256]{1,0:T(8,128)(2,1)S(1)}, bf16[640,256]{1,0:T(8,128)(2,1)S(1)}, u32[]{:S(2)}, u32[]{:S(2)}) collective-permute-start(bf16[640,256]{1,0:T(8,128)(2,1)S(1)} %collective-permute-done.22.refs_5_), channel_id=1, source_target_pairs={{2,0},{4,2},{6,4},{7,6},{5,7},{3,5},{1,3},{0,1},{10,8},{12,10},{14... | collective-permute-start | bytes 983048 | tf_op jit(solution)/shard_map/ppermute | solution.py:108
  97.0 7.5 %collective-permute-start.26 = (bf16[640,256]{1,0:T(8,128)(2,1)S(1)}, bf16[640,256]{1,0:T(8,128)(2,1)S(1)}, u32[]{:S(2)}, u32[]{:S(2)}) collective-permute-start(bf16[640,256]{1,0:T(8,128)(2,1)S(1)} %get-tuple-element.61), channel_id=1, source_target_pairs={{0,2},{2,4},{4,6},{6,7},{7,5},{5,3},{3,1},{1,0},{8,10},{10,12},{12... | collective-permute-start | bytes 983048 | tf_op jit(solution)/shard_map/ppermute | solution.py:108
  97.2 9.3 %collective-permute-start.28 = (bf16[640,256]{1,0:T(8,128)(2,1)S(1)}, bf16[640,256]{1,0:T(8,128)(2,1)S(1)}, u32[]{:S(2)}, u32[]{:S(2)}) collective-permute-start(bf16[640,256]{1,0:T(8,128)(2,1)S(1)} %get-tuple-element.60), channel_id=1, source_target_pairs={{2,0},{4,2},{6,4},{7,6},{5,7},{3,5},{1,3},{0,1},{10,8},{12,10},{14... | collective-permute-start | bytes 983048 | tf_op jit(solution)/shard_map/ppermute | solution.py:108
  104.5 6.9 %collective-permute-start.27 = (bf16[384,256]{1,0:T(8,128)(2,1)S(1)}, bf16[384,256]{1,0:T(8,128)(2,1)S(1)}, u32[]{:S(2)}, u32[]{:S(2)}) collective-permute-start(bf16[384,256]{1,0:T(8,128)(2,1)S(1)} %slice_select_fusion), channel_id=1, source_target_pairs={{0,2},{2,4},{4,6},{6,7},{7,5},{5,3},{3,1},{1,0},{8,10},{10,12},{12... | collective-permute-start | bytes 589832 | tf_op jit(solution)/shard_map/ppermute | solution.py:108
  106.4 5.0 %collective-permute-start.29 = (bf16[256,256]{1,0:T(8,128)(2,1)S(1)}, bf16[256,256]{1,0:T(8,128)(2,1)S(1)}, u32[]{:S(2)}, u32[]{:S(2)}) collective-permute-start(bf16[256,256]{1,0:T(8,128)(2,1)S(1)} %slice_select_fusion.1), channel_id=1, source_target_pairs={{2,0},{4,2},{6,4},{7,6},{5,7},{3,5},{1,3},{0,1},{10,8},{12,10},{14... | collective-permute-start | bytes 393224 | tf_op jit(solution)/shard_map/ppermute | solution.py:108
  111.5 3.8 %copy-start = (f32[2048,256]{1,0:T(8,128)S(1)}, f32[2048,256]{1,0:T(8,128)}, u32[]{:S(2)}) copy-start(f32[2048,256]{1,0:T(8,128)} %param.10) | copy-start | bytes 6291460
  111.5 3.8 %copy-start.2 = (s32[16]{0:T(128)S(1)}, s32[16]{0:T(128)}, u32[]{:S(2)}) copy-start(s32[16]{0:T(128)} %refs_0_.3) | copy-start | bytes 196
  113.4 1.9 %collective-permute-start.30 = (bf16[4,128,256]{2,1,0:T(8,128)(2,1)S(1)}, bf16[4,128,256]{2,1,0:T(8,128)(2,1)S(1)}, u32[]{:S(2)}, u32[]{:S(2)}) collective-permute-start(bf16[4,128,256]{2,1,0:T(8,128)(2,1)S(1)} %get-tuple-element.53), channel_id=1, source_target_pairs={{0,8},{8,0},{16,24},{24,16},{1,9},{9,1},{17,25},{25,17},{2,10},{10... | collective-permute-start | bytes 786440 | tf_op jit(solution)/shard_map/ppermute | solution.py:529
  113.4 9.1 %collective-permute-start.31 = (bf16[4,128,256]{2,1,0:T(8,128)(2,1)S(1)}, bf16[4,128,256]{2,1,0:T(8,128)(2,1)S(1)}, u32[]{:S(2)}, u32[]{:S(2)}) collective-permute-start(bf16[4,128,256]{2,1,0:T(8,128)(2,1)S(1)} %get-tuple-element.55), channel_id=1, source_target_pairs={{0,16},{8,24},{16,0},{24,8},{1,17},{9,25},{17,1},{25,9},{2,18},{10... | collective-permute-start | bytes 786440 | tf_op jit(solution)/shard_map/ppermute | solution.py:529
  113.4 13.9 %collective-permute-start.32 = (bf16[4,128,256]{2,1,0:T(8,128)(2,1)S(1)}, bf16[4,128,256]{2,1,0:T(8,128)(2,1)S(1)}, u32[]{:S(2)}, u32[]{:S(2)}) collective-permute-start(bf16[4,128,256]{2,1,0:T(8,128)(2,1)S(1)} %get-tuple-element.56), channel_id=1, source_target_pairs={{0,24},{8,16},{16,8},{24,0},{1,25},{9,17},{17,9},{25,1},{2,26},{10... | collective-permute-start | bytes 786440 | tf_op jit(solution)/shard_map/ppermute | solution.py:529

commit v4 on v2

--- a/solution.py
+++ b/solution.py
@@ -11,6 +11,8 @@
 weight_decay = 0.05
 line_len = 4
 batch = 8
+split_sum = False
+split_gather = True
 
 VMEM = pltpu.VMEM
 SMEM = pltpu.SMEM
@@ -73,7 +75,7 @@
         for m in range(1, self.far):
             self.order += [m, col_count - m]
         self.order.append(self.far)
-        self.groups = [self.order[:3], self.order[3:-3], self.order[-3:]]
+        self.groups = [self.order[:3], self.order[3:-3], self.order[-3:-1], self.order[-1:]]
         self.starts = [self.order.index(g[0]) * self.blocks for g in self.groups]
 
     def arrival(self, offset):
@@ -89,26 +91,45 @@
         )
 
     def cuts(self, offset):
-        return self.halves if offset == self.far else [(0, self.rows)]
+        return self.halves if split_sum or offset == self.far else [(0, self.rows)]
 
 
 def after(value, mark):
-    return jnp.where(mark[0, :1] < jnp.inf, value, jnp.zeros_like(value))
-
-
-def gather_ring(low, plan, mark_last=lambda pieces: None):
+    return jnp.where(mark[:1] < jnp.inf, value, jnp.zeros_like(value))
+
+
+def gather_ring(low, plan, marks=None, arrived=None):
     steps = ring_steps(plan.count)
     moved = [low, low]
     pieces = {0: [low]}
-    for step in range(1, plan.far):
-        for way in (0, 1):
-            moved[way] = lax.ppermute(moved[way], "col", steps[way])
-            pieces[step if way else plan.count - step] = [moved[way]]
-    mark = mark_last(pieces)
-    parts = [moved[way][a:b] for way, (a, b) in enumerate(plan.halves)]
-    if mark is not None:
-        parts = [after(part, mark) for part in parts]
-    pieces[plan.far] = [lax.ppermute(parts[way], "col", steps[way]) for way in (0, 1)]
+    for step in range(1, plan.far + 1):
+        if step == plan.far:
+            moved = [moved[way][a:b] for way, (a, b) in enumerate(plan.halves)]
+        if marks is not None and step in marks:
+            moved = [after(value, marks[step]) for value in moved]
+        moved = [lax.ppermute(moved[way], "col", steps[way]) for way in (0, 1)]
+        if step == plan.far:
+            pieces[step] = moved
+        else:
+            pieces[plan.count - step] = moved[:1]
+            pieces[step] = moved[1:]
+        if arrived:
+            arrived(step, pieces)
+    return pieces
+
+
+def gather_split(low, plan):
+    steps = ring_steps(plan.count)
+    parts = [low[a:b] for a, b in plan.halves]
+    moved = {(way, h): parts[h] for way in (0, 1) for h in (0, 1)}
+    pieces = {offset: [None, None] for offset in plan.order}
+    pieces[0] = parts
+    for step in range(1, plan.far + 1):
+        for h in (0, 1):
+            for way in (0, 1):
+                if step < plan.far or way == h:
+                    moved[way, h] = lax.ppermute(moved[way, h], "col", steps[way])
+                    pieces[step if way else plan.count - step][h] = moved[way, h]
     return pieces
 
 
@@ -137,9 +158,31 @@
     )
 
 
+def scatter_split(pieces, plan):
+    steps = ring_steps(plan.count)
+    moved = {}
+    for step in range(plan.far, 0, -1):
+        for h in (0, 1):
+            for way in (0, 1):
+                if step < plan.far or way == h:
+                    value = pieces[plan.count - step if way else step][h]
+                    if (way, h) in moved:
+                        value = add_up(moved[way, h], value)
+                    moved[way, h] = lax.ppermute(value, "col", steps[way])
+    return jnp.concatenate(
+        [
+            pieces[0][h].astype(jnp.float32)
+            + moved[0, h].astype(jnp.float32)
+            + moved[1, h].astype(jnp.float32)
+            for h in (0, 1)
+        ],
+        axis=0,
+    )
+
+
 def pick_kernel(row_count, per_owner, row_ref, *refs):
     ids = refs[:row_count]
-    table, *outs = refs[row_count:-2]
+    table, _, *outs = refs[row_count:-2]
     held, sems = refs[-2:]
     row = row_ref[0]
 
@@ -153,35 +196,32 @@
         block_of(k, i).start()
     for k, i in order:
         block_of(k, i).wait()
-        out = outs[k] if k < 2 else outs[1 + k // 2]
-        at = i if k < 2 else k % 2 * per_owner + i
-        out[at] = held[k * per_owner + i].astype(jnp.bfloat16)
-
-
-def pick(row, ids, table, per_owner):
+        outs[k][i] = held[k * per_owner + i].astype(jnp.bfloat16)
+
+
+def pick(row, ids, table, per_owner, mark):
     row_count = len(ids)
     block, rank = table.shape[1:]
-    heights = [per_owner] * 2 + [2 * per_owner] * (row_count // 2 - 1)
-    shapes = [VMEM((height, block, rank), jnp.bfloat16) for height in heights]
+    shapes = [VMEM((per_owner, block, rank), jnp.bfloat16)] * row_count
     asked = row_count * per_owner
     return pl.pallas_call(
         functools.partial(pick_kernel, row_count, per_owner),
         out_shape=shapes,
-        in_specs=[spec(SMEM)] * (row_count + 1) + [spec(pltpu.HBM)],
+        in_specs=[spec(SMEM)] * (row_count + 1) + [spec(pltpu.HBM), spec(VMEM)],
         out_specs=[spec(VMEM)] * len(shapes),
         scratch_shapes=[
             VMEM((asked, block, rank), jnp.float32),
             pltpu.SemaphoreType.DMA((asked,)),
         ],
         compiler_params=params(8),
-    )(row, *ids, away(table))
+    )(row, *ids, away(table), near(mark))
 
 
 def join_kernel(per_owner, first, *refs):
     out = refs[-1]
     out[0:per_owner] = first[...]
     for x in range(1, out.shape[0] // per_owner):
-        out[x * per_owner : (x + 1) * per_owner] = refs[x - 1][per_owner:]
+        out[x * per_owner : (x + 1) * per_owner] = refs[x - 1][...]
 
 
 def join(first, moved, per_owner, marks):
@@ -198,35 +238,42 @@
 
 def list_kernel(cfg, row_ref, live_ref, ids_ref, observed, *refs):
     row_count, per_owner, kinds, starts, room = cfg
-    pairs_ref, counts_ref, held, sem = refs[-4:]
+    pairs_ref, counts_ref, held, mark, sem = refs[-5:]
+    mark[...] = jnp.zeros_like(mark)
     copy = pltpu.make_async_copy(observed, held, sem)
     copy.start()
     row = row_ref[0]
-    for g in range(len(starts)):
-        counts_ref[g] = 0
+    counts = (jnp.int32(0),) * len(starts)
     for owner in range(row_count):
 
-        @pl.loop(0, live_ref[owner])
-        def _(i):
+        def add_slot(i, counts):
             slot = owner * per_owner + i
             sku_at = (row ^ owner) * per_owner + i
+            tag = sku_at * 4096 + slot * 1048576
             for n in range(kinds):
-                at = ids_ref[slot, n]
-                group = jnp.int32(0)
-                for start in starts[1:]:
-                    group += (at >= start).astype(jnp.int32)
-                filled = counts_ref[group]
-                pairs_ref[group * room + filled] = at + n * 256 + sku_at * 4096 + slot * 1048576
-                counts_ref[group] = filled + 1
-
+                at = ids_ref[n, slot]
+                group, filled = jnp.int32(0), counts[0]
+                for g, start in enumerate(starts[1:], 1):
+                    group = jnp.where(at >= start, g, group)
+                    filled = jnp.where(at >= start, counts[g], filled)
+                pairs_ref[group * room + filled] = at + n * 256 + tag
+                counts = tuple(
+                    count + (group == g).astype(jnp.int32) for g, count in enumerate(counts)
+                )
+            return counts
+
+        counts = lax.fori_loop(0, live_ref[owner], add_slot, counts)
+
+    for g, count in enumerate(counts):
+        counts_ref[g] = count
     for g, start in enumerate(starts):
         for q in range(batch - 1):
             blank = start + row_count * per_owner * 4096
-            pairs_ref[g * room + counts_ref[g] + q] = jnp.int32(blank)
+            pairs_ref[g * room + counts[g] + q] = jnp.int32(blank)
     copy.wait()
 
 
-def list_pairs(row, live, ids, observed, plan, row_count, per_owner, kinds, marks):
+def list_pairs(row, live, ids, observed, plan, row_count, per_owner, kinds, rank):
     room = row_count * per_owner * kinds + batch
     groups = len(plan.groups)
     return pl.pallas_call(
@@ -235,12 +282,13 @@
             jax.ShapeDtypeStruct((groups * room,), jnp.int32),
             jax.ShapeDtypeStruct((groups,), jnp.int32),
             VMEM(observed.shape, observed.dtype),
+            VMEM((8, rank), jnp.float32),
         ],
-        in_specs=[spec(SMEM)] * 3 + [spec(pltpu.HBM)] + [spec(VMEM)] * len(marks),
-        out_specs=[spec(SMEM)] * 2 + [spec(VMEM)],
+        in_specs=[spec(SMEM)] * 3 + [spec(pltpu.HBM)],
+        out_specs=[spec(SMEM)] * 2 + [spec(VMEM)] * 2,
         scratch_shapes=[pltpu.SemaphoreType.DMA],
         compiler_params=params(1),
-    )(row, live, ids, away(observed), *map(near, marks))
+    )(row, live, ids, away(observed))
 
 
 def load_skus(held, refs, starts):
@@ -346,7 +394,7 @@
             slot = owner * per_owner + i
             stores, measured = [], []
             for n in range(kinds):
-                at = pl.multiple_of(ids_ref[slot, n] * block, block)
+                at = pl.multiple_of(ids_ref[n, slot] * block, block)
                 stores.append(table[pl.ds(at, block), :])
                 measured.append(observed[slot, n])
             store = jnp.concatenate(stores, axis=0)
@@ -455,45 +503,41 @@
 
     swaps = [[(r, r ^ k) for r in range(row_count)] for k in range(row_count)]
     asked = [sku_ids] + [lax.ppermute(sku_ids, "row", swaps[k]) for k in range(1, row_count)]
-    picked = pick(row_vec, asked, sku, per_owner)
-    moved = [
-        lax.ppermute(picked[1 + x], "row", swaps[2 * x]) for x in range(1, row_count // 2)
-    ]
-
     place = ring_place(lax.axis_index("col"), plan.count)
+    store_ids = store_ids.T
     owner_place = ring_place(store_ids // plan.blocks, plan.count)
     arrival = plan.arrival((owner_place - place) % plan.count)
     ids = arrival * plan.blocks + store_ids % plan.blocks
-    made = []
-
-    def prepare(pieces):
-        early = pieces[1] + pieces[plan.count - 1]
-        made.extend(
-            list_pairs(
-                row_vec, live, ids, observed, plan, row_count, per_owner, kinds, early
-            )
-        )
-        late = pieces[plan.far - 2] + pieces[plan.far + 2] + [made[2]]
-        made.append(
-            lax.ppermute(join(picked[1], moved, per_owner, late), "row", swaps[1])
-        )
-        return made[3][0]
-
-    pieces = gather_ring(store_factors.astype(jnp.bfloat16), plan, prepare)
-    pairs, counts, observed, passed = made
+    pairs, counts, observed, listed = list_pairs(
+        row_vec, live, ids, observed, plan, row_count, per_owner, kinds, rank
+    )
+    picked = pick(row_vec, asked, sku, per_owner, listed)
+    pieces = gather_ring(store_factors.astype(jnp.bfloat16), plan)
+
+    direct, through = [], []
+    for x in range(1, row_count // 2):
+        direct.append(lax.ppermute(picked[2 * x], "row", swaps[2 * x]))
+        onward = after(picked[2 * x + 1], direct[-1][0])
+        through.append(lax.ppermute(onward, "row", swaps[2 * x]))
+    late = pieces[plan.far - 1] + pieces[plan.far + 1]
+    passed = lax.ppermute(join(picked[1], through, per_owner, late), "row", swaps[1])
     skus = [(picked[0], 0), (passed, 0)]
-    for x, both in enumerate(moved, 1):
-        skus += [(both, 0), (passed, x * per_owner)]
+    for x, blocks in enumerate(direct, 1):
+        skus += [(blocks, 0), (passed, x * per_owner)]
 
     grads, marks = {}, []
-    for group in (0, 2, 1):
+    for group in (2, 3, 1, 0):
         if plan.groups[group]:
             some = first_pass(pairs, counts, observed, skus, pieces, plan, [group], marks)
             grads.update(some)
             marks = some[plan.groups[group][0]][:1]
-    own_grad = scatter_ring(grads, plan)
-    new_store = store_factors - learn_rate * (own_grad + weight_decay * store_factors)
-    new_pieces = gather_ring(new_store.astype(jnp.bfloat16), plan)
+    own_grad = (scatter_split if split_sum else scatter_ring)(grads, plan)
+
+    def step_of(grad):
+        return store_factors - learn_rate * (grad + weight_decay * store_factors)
+
+    new_low = step_of(own_grad).astype(jnp.bfloat16)
+    new_pieces = (gather_split if split_gather else gather_ring)(new_low, plan)
 
     terms = [None] * row_count
     for ks in (list(range(2, row_count)), [1, 0]):
@@ -502,6 +546,7 @@
             terms[k] = lax.ppermute(term, "row", swaps[k]) if k else term
     held, new_sku = base_step(row_vec, asked[:2], sku, terms[:2], per_owner)
     new_sku = finish_step(row_vec, asked[2:], held, new_sku, terms[2:], per_owner)
+    new_store = step_of(after(own_grad, new_pieces[plan.far][1]))
     return new_sku.reshape(sku_factors.shape), new_store
 
 

time: 141 us -> 125 us (0.89)
  waiting for transfers between devices: 73 us -> 51.6 us
  starting transfers between devices: 34.3 us -> 38.2 us
  Pallas kernels: 26 us -> 28.8 us
    ppermute x6, waiting for transfers between devices: 20.6 us -> 12.3 us  [scatter_ring(): moved[way] = lax.ppermute(value, 'col', steps[way])]
    ppermute x18 -> x25, starting transfers between devices: 19.1 us -> 27.1 us  [the longest x14 15.3 us: gather_split(): moved[way, h] = lax.ppermute(moved[way, h], 'col', steps[way])]
    ppermute x3, waiting for transfers between devices: 8.55 us -> 1.17 us  [local(): terms[k] = lax.ppermute(term, 'row', swaps[k]) if k else term]
    ppermute x6, starting transfers between devices: 9.35 us -> 4.12 us  [scatter_ring(): moved[way] = lax.ppermute(value, 'col', steps[way])]
    ppermute x3, waiting for transfers between devices: 3.58 us -> 0.01 us  [local(): lax.ppermute(sku_ids, 'row', swaps[k])]
    ppermute x18 -> x25, waiting for transfers between devices: 36.6 us -> 34 us  [the longest x14 17.1 us: gather_split(): moved[way, h] = lax.ppermute(moved[way, h], 'col', steps[way])]
    pallas_call x3 -> x4, Pallas kernels: 10 us -> 12 us  [first_pass(): pl.pallas_call(functools.partial(first_kernel, cfg), out_shape=[VMEM((hei...]
  transfers between devices with their start and end apart: 32 -> 39, of which waited for: 20 -> 25; matrix products, arithmetic and copies ran while one was open for 1% -> 2% of each run, Pallas kernels for 14% -> 16%
where the time goes in v4:
time: 125 us; the launch traced here: 124 us
  waiting for transfers between devices  51.6 us (41%)
  starting transfers between devices  38.2 us (31%)
  Pallas kernels  28.8 us (23%)
  other arithmetic  3.7 us (3%)
    ppermute x14, waiting for transfers between devices, gather_split(): moved[way, h] = lax.ppermute(moved[way, h], 'col', steps[way])  17.1 us
    ppermute x14, starting transfers between devices, gather_split(): moved[way, h] = lax.ppermute(moved[way, h], 'col', steps[way])  15.3 us
    ppermute x6, waiting for transfers between devices, scatter_ring(): moved[way] = lax.ppermute(value, 'col', steps[way])  12.3 us
    pallas_call x4, Pallas kernels, first_pass(): pl.pallas_call(functools.partial(first_kernel, cfg), out_shape=[VMEM((hei...  12 us
    ppermute x8, starting transfers between devices, gather_ring(): moved = [lax.ppermute(moved[way], 'col', steps[way]) for way in (0, 1)]  9.27 us
    pallas_call x2, Pallas kernels, second_pass(): pl.pallas_call(functools.partial(second_kernel, (ks, sku_starts, per_owne...  7.02 us
    ppermute x8, waiting for transfers between devices, gather_ring(): moved = [lax.ppermute(moved[way], 'col', steps[way]) for way in (0, 1)]  6.32 us
    ppermute x1, waiting for transfers between devices, local(): through.append(lax.ppermute(onward, 'row', swaps[2 * x]))  6.09 us
  transfers between devices with their start and end apart: 39, of which 25 were waited for; matrix products, arithmetic and copies ran while one was open for 2% of the time, Pallas kernels for 16%

profile of v4, /device:TPU:0, one launch (start us, length us, event | category | flops | bytes accessed | tf_op | source)
XLA Modules:
  0.0 124.0 jit_solution(12421629184641309491)
XLA Ops:
  0.6 1.1 convert_element_type.69.refs_4_
  1.8 3.1 %collective-permute-start.8 = (bf16[640,256]{1,0:T(8,128)(2,1)S(1)}, bf16[640,256]{1,0:T(8,128)(2,1)S(1)}, u32[]{:S(2)}, u32[]{:S(2)}) collective-permute-start(bf16[640,256]{1,0:T(8,128)(2,1)S(1)} %convert_element_type.69.refs_4_), channel_id=1, source_target_pairs={{0,2},{2,4},{4,6},{6,7},{7,5},{5,3},{3,1},{1,0},{8,10},{10,12},{12... | collective-permute-start | bytes 983048 | tf_op jit(solution)/shard_map/ppermute | solution.py:110
  4.8 1.9 %collective-permute-start = (s32[16]{0:T(128)}, s32[16]{0:T(128)S(1)}, u32[]{:S(2)}, u32[]{:S(2)}) collective-permute-start(s32[16]{0:T(128)} %refs_0_.3), channel_id=1, source_target_pairs={{0,16},{8,24},{16,0},{24,8},{1,17},{9,25},{17,1},{25,9},{2,18},{10... | collective-permute-start | bytes 200 | tf_op jit(solution)/shard_map/ppermute | solution.py:505
  7.0 0.7 fusion.5.ids_ref
  7.7 0.6 copy-done.1
  8.4 3.4 %shard_map.77 = (s32[544]{0:T(1024)S(1)}, s32[4]{0:T(128)S(1)}, bf16[16,8,128,128]{3,2,1,0:T(8,128)(2,1)S(1)}, f32[8,256]{1,0:T(8,128)S(1)}) custom-call(s32[1]{0:T(128)} %bitcast.row_ref, s32[4]{0:T(128)S(1)} %bitcast.28, s32[8,16]{1,0:T(8,128)S(1)} %fusion.5.ids_ref, bf16[16,8,128,128]{3,2,1,0:T(8,128)(2,1)} %observed.1), custom_call_target="tpu_custom_call" | custom-call | tf_op jit(solution)/shard_map/pallas_call | solution.py:279
  11.9 2.3 %shard_map.78 = (bf16[4,128,256]{2,1,0:T(8,128)(2,1)S(1)}, bf16[4,128,256]{2,1,0:T(8,128)(2,1)S(1)}, bf16[4,128,256]{2,1,0:T(8,128)(2,1)S(1)}, bf16[4,128,256]{2,1,0:T(8,128)(2,1)S(1)}) custom-call(s32[1]{0:T(128)} %bitcast.row_ref, s32[16]{0:T(128)S(1)} %copy-done.2, s32[16]{0:T(128)S(1)} %collective-permute-done.2.refs_1_, ...), custom_call_target="tpu_custom_call" | custom-call | tf_op jit(solution)/shard_map/pallas_call | solution.py:207
  14.2 2.0 %collective-permute-start.3 = (bf16[4,128,256]{2,1,0:T(8,128)(2,1)S(1)}, bf16[4,128,256]{2,1,0:T(8,128)(2,1)S(1)}, u32[]{:S(2)}, u32[]{:S(2)}) collective-permute-start(bf16[4,128,256]{2,1,0:T(8,128)(2,1)S(1)} %get-tuple-element.28), channel_id=1, source_target_pairs={{0,16},{8,24},{16,0},{24,8},{1,17},{9,25},{17,1},{25,9},{2,18},{10... | collective-permute-start | bytes 786440 | tf_op jit(solution)/shard_map/ppermute | solution.py:519
  16.2 1.6 %collective-permute-start.9 = (bf16[640,256]{1,0:T(8,128)(2,1)S(1)}, bf16[640,256]{1,0:T(8,128)(2,1)S(1)}, u32[]{:S(2)}, u32[]{:S(2)}) collective-permute-start(bf16[640,256]{1,0:T(8,128)(2,1)S(1)} %collective-permute-done.8.refs_6_), channel_id=1, source_target_pairs={{0,2},{2,4},{4,6},{6,7},{7,5},{5,3},{3,1},{1,0},{8,10},{10,12},{12... | collective-permute-start | bytes 983048 | tf_op jit(solution)/shard_map/ppermute | solution.py:110
  17.8 0.5 collective-permute-start.6
  18.2 4.5 %collective-permute-done.3.refs_2_.refs_0_ = bf16[4,128,256]{2,1,0:T(8,128)(2,1)S(1)} collective-permute-done((bf16[4,128,256]{2,1,0:T(8,128)(2,1)S(1)}, bf16[4,128,256]{2,1,0:T(8,128)(2,1)S(1)}, u32[]{:S(2)}, u32[]{:S(2)}) %collective-permute-start.3) | collective-permute-done | bytes 262176 | tf_op jit(solution)/shard_map/ppermute | solution.py:519
  22.8 2.7 %collective-permute-done.9.refs_5_ = bf16[640,256]{1,0:T(8,128)(2,1)S(1)} collective-permute-done((bf16[640,256]{1,0:T(8,128)(2,1)S(1)}, bf16[640,256]{1,0:T(8,128)(2,1)S(1)}, u32[]{:S(2)}, u32[]{:S(2)}) %collective-permute-start.9) | collective-permute-done | bytes 327712 | tf_op jit(solution)/shard_map/ppermute | solution.py:110
  25.5 1.6 %collective-permute-start.10 = (bf16[640,256]{1,0:T(8,128)(2,1)S(1)}, bf16[640,256]{1,0:T(8,128)(2,1)S(1)}, u32[]{:S(2)}, u32[]{:S(2)}) collective-permute-start(bf16[640,256]{1,0:T(8,128)(2,1)S(1)} %collective-permute-done.9.refs_5_), channel_id=1, source_target_pairs={{0,2},{2,4},{4,6},{6,7},{7,5},{5,3},{3,1},{1,0},{8,10},{10,12},{12... | collective-permute-start | bytes 983048 | tf_op jit(solution)/shard_map/ppermute | solution.py:110
  27.1 0.4 collective-permute-start.7
  27.6 0.5 collective-permute-start.4
  28.0 6.1 %collective-permute-done.4.refs_0_ = bf16[4,128,256]{2,1,0:T(8,128)(2,1)S(1)} collective-permute-done((bf16[4,128,256]{2,1,0:T(8,128)(2,1)S(1)}, bf16[4,128,256]{2,1,0:T(8,128)(2,1)S(1)}, u32[]{:S(2)}, u32[]{:S(2)}) %collective-permute-start.4) | collective-permute-done | bytes 262176 | tf_op jit(solution)/shard_map/ppermute | solution.py:521
  34.1 1.2 collective-permute-done.7.refs_1_.refs_4_
  35.5 1.6 %collective-permute-start.12 = (bf16[384,256]{1,0:T(8,128)(2,1)S(1)}, bf16[384,256]{1,0:T(8,128)(2,1)S(1)}, u32[]{:S(2)}, u32[]{:S(2)}) collective-permute-start(bf16[384,256]{1,0:T(8,128)(2,1)S(1)} %slice.44), channel_id=1, source_target_pairs={{0,2},{2,4},{4,6},{6,7},{7,5},{5,3},{3,1},{1,0},{8,10},{10,12},{12... | collective-permute-start | bytes 589832 | tf_op jit(solution)/shard_map/ppermute | solution.py:110
  37.0 0.6 collective-permute-start.13
  37.6 2.8 %shard_map.80 = (bf16[640,256]{1,0:T(8,128)(2,1)S(1)}, bf16[640,256]{1,0:T(8,128)(2,1)S(1)}) custom-call(s32[544]{0:T(1024)S(1)} %get-tuple-element.31.pairs_ref, s32[4]{0:T(128)S(1)} %get-tuple-element.32.counts_ref, bf16[16,8,128,128]{3,2,1,0:T(8,128)(2,1)S(1)} %get-tuple-element.25.observed, bf16[4,128,256]{2,1,0:T(8,128)(2,1)S(1)} %get-tuple-element.30.refs_0_.refs_1_, ...), custom_call_target="tpu_custom_call" | custom-call | flops 570425344 | bytes 8912896 | tf_op jit(solution)/shard_map/pallas_call | solution.py:365
  40.5 2.2 %collective-permute-done.13.refs_5_ = bf16[256,256]{1,0:T(8,128)(2,1)S(1)} collective-permute-done((bf16[256,256]{1,0:T(8,128)(2,1)S(1)}, bf16[256,256]{1,0:T(8,128)(2,1)S(1)}, u32[]{:S(2)}, u32[]{:S(2)}) %collective-permute-start.13) | collective-permute-done | bytes 131104 | tf_op jit(solution)/shard_map/ppermute | solution.py:110
  42.8 2.1 %shard_map.81 = (bf16[384,256]{1,0:T(8,128)(2,1)S(1)}, bf16[256,256]{1,0:T(8,128)(2,1)S(1)}) custom-call(s32[544]{0:T(1024)S(1)} %get-tuple-element.31.pairs_ref, s32[4]{0:T(128)S(1)} %get-tuple-element.32.counts_ref, bf16[16,8,128,128]{3,2,1,0:T(8,128)(2,1)S(1)} %get-tuple-element.25.observed, bf16[4,128,256]{2,1,0:T(8,128)(2,1)S(1)} %get-tuple-element.30.refs_0_.refs_1_, ...), custom_call_target="tpu_custom_call" | custom-call | flops 285212672 | bytes 4456448 | tf_op jit(solution)/shard_map/pallas_call | solution.py:365
  45.0 2.1 %collective-permute-start.14 = (bf16[384,256]{1,0:T(8,128)(2,1)S(1)}, bf16[384,256]{1,0:T(8,128)(2,1)S(1)}, u32[]{:S(2)}, u32[]{:S(2)}) collective-permute-start(bf16[384,256]{1,0:T(8,128)(2,1)S(1)} %get-tuple-element.34.refs_6_), channel_id=1, source_target_pairs={{0,2},{2,4},{4,6},{6,7},{7,5},{5,3},{3,1},{1,0},{8,10},{10,12},{12... | collective-permute-start | bytes 589832 | tf_op jit(solution)/shard_map/ppermute | solution.py:143
  47.1 2.9 %collective-permute-done.18 = bf16[256,256]{1,0:T(8,128)(2,1)S(1)} collective-permute-done((bf16[256,256]{1,0:T(8,128)(2,1)S(1)}, bf16[256,256]{1,0:T(8,128)(2,1)S(1)}, u32[]{:S(2)}, u32[]{:S(2)}) %collective-permute-start.18) | collective-permute-done | bytes 131104 | tf_op jit(solution)/shard_map/ppermute | solution.py:143
  50.2 1.3 %collective-permute-done.14 = bf16[384,256]{1,0:T(8,128)(2,1)S(1)} collective-permute-done((bf16[384,256]{1,0:T(8,128)(2,1)S(1)}, bf16[384,256]{1,0:T(8,128)(2,1)S(1)}, u32[]{:S(2)}, u32[]{:S(2)}) %collective-permute-start.14) | collective-permute-done | bytes 196640 | tf_op jit(solution)/shard_map/ppermute | solution.py:143
  51.5 1.4 %collective-permute-start.15 = (bf16[640,256]{1,0:T(8,128)(2,1)S(1)}, bf16[640,256]{1,0:T(8,128)(2,1)S(1)}, u32[]{:S(2)}, u32[]{:S(2)}) collective-permute-start(bf16[640,256]{1,0:T(8,128)(2,1)S(1)} %pad_maximum_fusion), channel_id=1, source_target_pairs={{0,2},{2,4},{4,6},{6,7},{7,5},{5,3},{3,1},{1,0},{8,10},{10,12},{12... | collective-permute-start | bytes 983048 | tf_op jit(solution)/shard_map/ppermute | solution.py:153
  52.9 2.8 %shard_map.82 = (bf16[640,256]{1,0:T(8,128)(2,1)S(1)}, bf16[640,256]{1,0:T(8,128)(2,1)S(1)}) custom-call(s32[544]{0:T(1024)S(1)} %get-tuple-element.31.pairs_ref, s32[4]{0:T(128)S(1)} %get-tuple-element.32.counts_ref, bf16[16,8,128,128]{3,2,1,0:T(8,128)(2,1)S(1)} %get-tuple-element.25.observed, bf16[4,128,256]{2,1,0:T(8,128)(2,1)S(1)} %get-tuple-element.30.refs_0_.refs_1_, ...), custom_call_target="tpu_custom_call" | custom-call | flops 570425344 | bytes 8912896 | tf_op jit(solution)/shard_map/pallas_call | solution.py:365
  55.7 1.9 %collective-permute-done.19 = bf16[640,256]{1,0:T(8,128)(2,1)S(1)} collective-permute-done((bf16[640,256]{1,0:T(8,128)(2,1)S(1)}, bf16[640,256]{1,0:T(8,128)(2,1)S(1)}, u32[]{:S(2)}, u32[]{:S(2)}) %collective-permute-start.19) | collective-permute-done | bytes 327712 | tf_op jit(solution)/shard_map/ppermute | solution.py:153
  57.7 0.5 collective-permute-start.20
  58.1 1.2 collective-permute-done.15
  59.4 1.1 collective-permute-start.16
  60.5 4.3 %shard_map.83 = (bf16[640,256]{1,0:T(8,128)(2,1)S(1)}, bf16[640,256]{1,0:T(8,128)(2,1)S(1)}, bf16[640,256]{1,0:T(8,128)(2,1)S(1)}) custom-call(s32[544]{0:T(1024)S(1)} %get-tuple-element.31.pairs_ref, s32[4]{0:T(128)S(1)} %get-tuple-element.32.counts_ref, bf16[16,8,128,128]{3,2,1,0:T(8,128)(2,1)S(1)} %get-tuple-element.25.observed, ...), custom_call_target="tpu_custom_call" | custom-call | flops 855638016 | bytes 13369344 | tf_op jit(solution)/shard_map/pallas_call | solution.py:365
  64.8 1.2 %collective-permute-done.20 = bf16[640,256]{1,0:T(8,128)(2,1)S(1)} collective-permute-done((bf16[640,256]{1,0:T(8,128)(2,1)S(1)}, bf16[640,256]{1,0:T(8,128)(2,1)S(1)}, u32[]{:S(2)}, u32[]{:S(2)}) %collective-permute-start.20) | collective-permute-done | bytes 327712 | tf_op jit(solution)/shard_map/ppermute | solution.py:153
  66.3 1.1 collective-permute-done.16
  67.5 0.9 collective-permute-start.17
  68.4 5.0 %collective-permute-done.21 = bf16[640,256]{1,0:T(8,128)(2,1)S(1)} collective-permute-done((bf16[640,256]{1,0:T(8,128)(2,1)S(1)}, bf16[640,256]{1,0:T(8,128)(2,1)S(1)}, u32[]{:S(2)}, u32[]{:S(2)}) %collective-permute-start.21) | collective-permute-done | bytes 327712 | tf_op jit(solution)/shard_map/ppermute | solution.py:153
  73.4 1.9 %collective-permute-done.17 = bf16[640,256]{1,0:T(8,128)(2,1)S(1)} collective-permute-done((bf16[640,256]{1,0:T(8,128)(2,1)S(1)}, bf16[640,256]{1,0:T(8,128)(2,1)S(1)}, u32[]{:S(2)}, u32[]{:S(2)}) %collective-permute-start.17) | collective-permute-done | bytes 327712 | tf_op jit(solution)/shard_map/ppermute | solution.py:153
  75.5 0.6 collective-permute-start.24
  76.1 1.5 %collective-permute-start.23 = (bf16[256,256]{1,0:T(8,128)(2,1)S(1)}, bf16[256,256]{1,0:T(8,128)(2,1)S(1)}, u32[]{:S(2)}, u32[]{:S(2)}) collective-permute-start(bf16[256,256]{1,0:T(8,128)(2,1)S(1)} %slice.47.refs_3_), channel_id=1, source_target_pairs={{2,0},{4,2},{6,4},{7,6},{5,7},{3,5},{1,3},{0,1},{10,8},{12,10},{14... | collective-permute-start | bytes 393224 | tf_op jit(solution)/shard_map/ppermute | solution.py:131
  77.7 2.0 %collective-permute-start.22 = (bf16[384,256]{1,0:T(8,128)(2,1)S(1)}, bf16[384,256]{1,0:T(8,128)(2,1)S(1)}, u32[]{:S(2)}, u32[]{:S(2)}) collective-permute-start(bf16[384,256]{1,0:T(8,128)(2,1)S(1)} %slice.46.refs_2_), channel_id=1, source_target_pairs={{2,0},{4,2},{6,4},{7,6},{5,7},{3,5},{1,3},{0,1},{10,8},{12,10},{14... | collective-permute-start | bytes 589832 | tf_op jit(solution)/shard_map/ppermute | solution.py:131
  79.7 3.1 %collective-permute-done.24.refs_6_ = bf16[384,256]{1,0:T(8,128)(2,1)S(1)} collective-permute-done((bf16[384,256]{1,0:T(8,128)(2,1)S(1)}, bf16[384,256]{1,0:T(8,128)(2,1)S(1)}, u32[]{:S(2)}, u32[]{:S(2)}) %collective-permute-start.24) | collective-permute-done | bytes 196640 | tf_op jit(solution)/shard_map/ppermute | solution.py:131
  82.8 1.1 collective-permute-start.28
  83.9 1.2 collective-permute-start.27
  85.1 1.3 %collective-permute-start.25 = (bf16[256,256]{1,0:T(8,128)(2,1)S(1)}, bf16[256,256]{1,0:T(8,128)(2,1)S(1)}, u32[]{:S(2)}, u32[]{:S(2)}) collective-permute-start(bf16[256,256]{1,0:T(8,128)(2,1)S(1)} %slice.47.refs_3_), channel_id=1, source_target_pairs={{0,2},{2,4},{4,6},{6,7},{7,5},{5,3},{3,1},{1,0},{8,10},{10,12},{12... | collective-permute-start | bytes 393224 | tf_op jit(solution)/shard_map/ppermute | solution.py:131
  86.4 0.9 collective-permute-done.22.refs_4_
  87.2 0.8 collective-permute-start.26
  88.0 2.8 %collective-permute-done.28.refs_10_ = bf16[384,256]{1,0:T(8,128)(2,1)S(1)} collective-permute-done((bf16[384,256]{1,0:T(8,128)(2,1)S(1)}, bf16[384,256]{1,0:T(8,128)(2,1)S(1)}, u32[]{:S(2)}, u32[]{:S(2)}) %collective-permute-start.28) | collective-permute-done | bytes 196640 | tf_op jit(solution)/shard_map/ppermute | solution.py:131
  90.8 0.8 collective-permute-start.32
  91.6 1.2 collective-permute-start.31
  92.8 0.5 collective-permute-done.25.refs_7_
  93.4 0.8 collective-permute-start.29
  94.2 4.0 %collective-permute-done.31.refs_13_ = bf16[256,256]{1,0:T(8,128)(2,1)S(1)} collective-permute-done((bf16[256,256]{1,0:T(8,128)(2,1)S(1)}, bf16[256,256]{1,0:T(8,128)(2,1)S(1)}, u32[]{:S(2)}, u32[]{:S(2)}) %collective-permute-start.31) | collective-permute-done | bytes 131104 | tf_op jit(solution)/shard_map/ppermute | solution.py:131
  98.2 0.4 collective-permute-start.35
  98.6 2.3 %collective-permute-start.30 = (bf16[384,256]{1,0:T(8,128)(2,1)S(1)}, bf16[384,256]{1,0:T(8,128)(2,1)S(1)}, u32[]{:S(2)}, u32[]{:S(2)}) collective-permute-start(bf16[384,256]{1,0:T(8,128)(2,1)S(1)} %collective-permute-done.26.refs_8_), channel_id=1, source_target_pairs={{2,0},{4,2},{6,4},{7,6},{5,7},{3,5},{1,3},{0,1},{10,8},{12,10},{14... | collective-permute-start | bytes 589832 | tf_op jit(solution)/shard_map/ppermute | solution.py:131
  101.0 1.3 %collective-permute-start.33 = (bf16[256,256]{1,0:T(8,128)(2,1)S(1)}, bf16[256,256]{1,0:T(8,128)(2,1)S(1)}, u32[]{:S(2)}, u32[]{:S(2)}) collective-permute-start(bf16[256,256]{1,0:T(8,128)(2,1)S(1)} %collective-permute-done.29.refs_11_), channel_id=1, source_target_pairs={{0,2},{2,4},{4,6},{6,7},{7,5},{5,3},{3,1},{1,0},{8,10},{10,12},{12... | collective-permute-start | bytes 393224 | tf_op jit(solution)/shard_map/ppermute | solution.py:131
  102.3 0.8 collective-permute-done.35.refs_17_
  103.2 4.8 %collective-permute-done.33.refs_15_ = bf16[256,256]{1,0:T(8,128)(2,1)S(1)} collective-permute-done((bf16[256,256]{1,0:T(8,128)(2,1)S(1)}, bf16[256,256]{1,0:T(8,128)(2,1)S(1)}, u32[]{:S(2)}, u32[]{:S(2)}) %collective-permute-start.33) | collective-permute-done | bytes 131104 | tf_op jit(solution)/shard_map/ppermute | solution.py:131
  107.9 4.7 %shard_map.86 = (bf16[4,128,256]{2,1,0:T(8,128)(2,1)S(1)}, bf16[4,128,256]{2,1,0:T(8,128)(2,1)S(1)}) custom-call(s32[1]{0:T(128)} %bitcast.row_ref, s32[4]{0:T(128)S(1)} %bitcast.29, s32[8,16]{1,0:T(8,128)S(1)} %fusion.5.ids_ref, bf16[16,8,128,128]{3,2,1,0:T(8,128)(2,1)S(1)} %get-tuple-element.25.observed, ...), custom_call_target="tpu_custom_call" | custom-call | flops 1073741824 | bytes 16777216 | tf_op jit(solution)/shard_map/pallas_call | solution.py:415
  112.8 2.3 %shard_map.84 = (bf16[4,128,256]{2,1,0:T(8,128)(2,1)S(1)}, bf16[4,128,256]{2,1,0:T(8,128)(2,1)S(1)}) custom-call(s32[1]{0:T(128)} %bitcast.row_ref, s32[4]{0:T(128)S(1)} %bitcast.30, s32[8,16]{1,0:T(8,128)S(1)} %fusion.5.ids_ref, bf16[16,8,128,128]{3,2,1,0:T(8,128)(2,1)S(1)} %get-tuple-element.25.observed, ...), custom_call_target="tpu_custom_call" | custom-call | flops 1073741824 | bytes 16777216 | tf_op jit(solution)/shard_map/pallas_call | solution.py:415
  115.2 2.6 %collective-permute-start.36 = (bf16[4,128,256]{2,1,0:T(8,128)(2,1)S(1)}, bf16[4,128,256]{2,1,0:T(8,128)(2,1)S(1)}, u32[]{:S(2)}, u32[]{:S(2)}) collective-permute-start(bf16[4,128,256]{2,1,0:T(8,128)(2,1)S(1)} %get-tuple-element.43), channel_id=1, source_target_pairs={{0,8},{8,0},{16,24},{24,16},{1,9},{9,1},{17,25},{25,17},{2,10},{10... | collective-permute-start | bytes 786440 | tf_op jit(solution)/shard_map/ppermute | solution.py:546
  117.7 1.1 multiply_subtract_fusion
  118.9 2.3 %shard_map.85 = (f32[16,128,256]{2,1,0:T(8,128)S(1)}, f32[16,128,256]{2,1,0:T(8,128)}) custom-call(s32[1]{0:T(128)} %bitcast.row_ref, s32[16]{0:T(128)S(1)} %copy-done.2, s32[16]{0:T(128)S(1)} %collective-permute-done.2.refs_1_, f32[16,128,256]{2,1,0:T(8,128)S(1)} %bitcast.27, bf16[4,128,256]{2,1,0:T(8,128)(2,1)S(1)} %get-tuple-element.42.refs_3_, ...), custom_call_target="tpu_custom_call" | custom-call | tf_op jit(solution)/shard_map/pallas_call | solution.py:456
  121.4 0.8 collective-permute-done.38.refs_4_
  122.3 1.8 %shard_map.87 = f32[16,128,256]{2,1,0:T(8,128)} custom-call(s32[1]{0:T(128)} %bitcast.row_ref, s32[16]{0:T(128)S(1)} %collective-permute-done.refs_2_.refs_0_, s32[16]{0:T(128)S(1)} %collective-permute-done.1.refs_3_.refs_1_, f32[16,128,256]{2,1,0:T(8,128)S(1)} %get-tuple-element.44.refs_2_, ...), custom_call_target="tpu_custom_call", output_to_operand_aliasing={{}: (6, {})} | custom-call | tf_op jit(solution)/shard_map/pallas_call | solution.py:478
  (54 shorter events, 2.3 us)
Async XLA Ops:
  1.8 14.4 %collective-permute-start.8 = (bf16[640,256]{1,0:T(8,128)(2,1)S(1)}, bf16[640,256]{1,0:T(8,128)(2,1)S(1)}, u32[]{:S(2)}, u32[]{:S(2)}) collective-permute-start(bf16[640,256]{1,0:T(8,128)(2,1)S(1)} %convert_element_type.69.refs_4_), channel_id=1, source_target_pairs={{0,2},{2,4},{4,6},{6,7},{7,5},{5,3},{3,1},{1,0},{8,10},{10,12},{12... | collective-permute-start | bytes 983048 | tf_op jit(solution)/shard_map/ppermute | solution.py:110
  4.8 12.9 %collective-permute-start.5 = (bf16[640,256]{1,0:T(8,128)(2,1)S(1)}, bf16[640,256]{1,0:T(8,128)(2,1)S(1)}, u32[]{:S(2)}, u32[]{:S(2)}) collective-permute-start(bf16[640,256]{1,0:T(8,128)(2,1)S(1)} %convert_element_type.69.refs_4_), channel_id=1, source_target_pairs={{2,0},{4,2},{6,4},{7,6},{5,7},{3,5},{1,3},{0,1},{10,8},{12,10},{14... | collective-permute-start | bytes 983048 | tf_op jit(solution)/shard_map/ppermute | solution.py:110
  4.8 7.0 %collective-permute-start = (s32[16]{0:T(128)}, s32[16]{0:T(128)S(1)}, u32[]{:S(2)}, u32[]{:S(2)}) collective-permute-start(s32[16]{0:T(128)} %refs_0_.3), channel_id=1, source_target_pairs={{0,16},{8,24},{16,0},{24,8},{1,17},{9,25},{17,1},{25,9},{2,18},{10... | collective-permute-start | bytes 200 | tf_op jit(solution)/shard_map/ppermute | solution.py:505
  6.8 5.1 %collective-permute-start.1 = (s32[16]{0:T(128)}, s32[16]{0:T(128)S(1)}, u32[]{:S(2)}, u32[]{:S(2)}) collective-permute-start(s32[16]{0:T(128)} %refs_0_.3), channel_id=1, source_target_pairs={{0,24},{8,16},{16,8},{24,0},{1,25},{9,17},{17,9},{25,1},{2,26},{10... | collective-permute-start | bytes 200 | tf_op jit(solution)/shard_map/ppermute | solution.py:505
  6.8 5.1 %collective-permute-start.2 = (s32[16]{0:T(128)}, s32[16]{0:T(128)S(1)}, u32[]{:S(2)}, u32[]{:S(2)}) collective-permute-start(s32[16]{0:T(128)} %refs_0_.3), channel_id=1, source_target_pairs={{0,8},{8,0},{16,24},{24,16},{1,9},{9,1},{17,25},{25,17},{2,10},{10... | collective-permute-start | bytes 200 | tf_op jit(solution)/shard_map/ppermute | solution.py:505
  7.7 0.7 copy-start.1
  8.4 3.5 %copy-start.2 = (s32[16]{0:T(128)S(1)}, s32[16]{0:T(128)}, u32[]{:S(2)}) copy-start(s32[16]{0:T(128)} %refs_0_.3) | copy-start | bytes 196
  14.2 8.6 %collective-permute-start.3 = (bf16[4,128,256]{2,1,0:T(8,128)(2,1)S(1)}, bf16[4,128,256]{2,1,0:T(8,128)(2,1)S(1)}, u32[]{:S(2)}, u32[]{:S(2)}) collective-permute-start(bf16[4,128,256]{2,1,0:T(8,128)(2,1)S(1)} %get-tuple-element.28), channel_id=1, source_target_pairs={{0,16},{8,24},{16,0},{24,8},{1,17},{9,25},{17,1},{25,9},{2,18},{10... | collective-permute-start | bytes 786440 | tf_op jit(solution)/shard_map/ppermute | solution.py:519
  16.2 9.3 %collective-permute-start.9 = (bf16[640,256]{1,0:T(8,128)(2,1)S(1)}, bf16[640,256]{1,0:T(8,128)(2,1)S(1)}, u32[]{:S(2)}, u32[]{:S(2)}) collective-permute-start(bf16[640,256]{1,0:T(8,128)(2,1)S(1)} %collective-permute-done.8.refs_6_), channel_id=1, source_target_pairs={{0,2},{2,4},{4,6},{6,7},{7,5},{5,3},{3,1},{1,0},{8,10},{10,12},{12... | collective-permute-start | bytes 983048 | tf_op jit(solution)/shard_map/ppermute | solution.py:110
  17.8 9.4 %collective-permute-start.6 = (bf16[640,256]{1,0:T(8,128)(2,1)S(1)}, bf16[640,256]{1,0:T(8,128)(2,1)S(1)}, u32[]{:S(2)}, u32[]{:S(2)}) collective-permute-start(bf16[640,256]{1,0:T(8,128)(2,1)S(1)} %collective-permute-done.5.refs_5_), channel_id=1, source_target_pairs={{2,0},{4,2},{6,4},{7,6},{5,7},{3,5},{1,3},{0,1},{10,8},{12,10},{14... | collective-permute-start | bytes 983048 | tf_op jit(solution)/shard_map/ppermute | solution.py:110
  25.5 8.6 %collective-permute-start.10 = (bf16[640,256]{1,0:T(8,128)(2,1)S(1)}, bf16[640,256]{1,0:T(8,128)(2,1)S(1)}, u32[]{:S(2)}, u32[]{:S(2)}) collective-permute-start(bf16[640,256]{1,0:T(8,128)(2,1)S(1)} %collective-permute-done.9.refs_5_), channel_id=1, source_target_pairs={{0,2},{2,4},{4,6},{6,7},{7,5},{5,3},{3,1},{1,0},{8,10},{10,12},{12... | collective-permute-start | bytes 983048 | tf_op jit(solution)/shard_map/ppermute | solution.py:110
  27.1 8.2 %collective-permute-start.7 = (bf16[640,256]{1,0:T(8,128)(2,1)S(1)}, bf16[640,256]{1,0:T(8,128)(2,1)S(1)}, u32[]{:S(2)}, u32[]{:S(2)}) collective-permute-start(bf16[640,256]{1,0:T(8,128)(2,1)S(1)} %collective-permute-done.6.refs_4_), channel_id=1, source_target_pairs={{2,0},{4,2},{6,4},{7,6},{5,7},{3,5},{1,3},{0,1},{10,8},{12,10},{14... | collective-permute-start | bytes 983048 | tf_op jit(solution)/shard_map/ppermute | solution.py:110
  27.6 6.5 %collective-permute-start.4 = (bf16[4,128,256]{2,1,0:T(8,128)(2,1)S(1)}, bf16[4,128,256]{2,1,0:T(8,128)(2,1)S(1)}, u32[]{:S(2)}, u32[]{:S(2)}) collective-permute-start(bf16[4,128,256]{2,1,0:T(8,128)(2,1)S(1)} %broadcast_select_fusion), channel_id=1, source_target_pairs={{0,16},{8,24},{16,0},{24,8},{1,17},{9,25},{17,1},{25,9},{2,18},{10... | collective-permute-start | bytes 786440 | tf_op jit(solution)/shard_map/ppermute | solution.py:521
  35.4 2.2 %collective-permute-start.11 = (bf16[8,128,256]{2,1,0:T(8,128)(2,1)S(1)}, bf16[8,128,256]{2,1,0:T(8,128)(2,1)S(1)}, u32[]{:S(2)}, u32[]{:S(2)}) collective-permute-start(bf16[8,128,256]{2,1,0:T(8,128)(2,1)S(1)} %shard_map.79), channel_id=1, source_target_pairs={{0,8},{8,0},{16,24},{24,16},{1,9},{9,1},{17,25},{25,17},{2,10},{10... | collective-permute-start | bytes 1572872 | tf_op jit(solution)/shard_map/ppermute | solution.py:523
  35.5 7.3 %collective-permute-start.12 = (bf16[384,256]{1,0:T(8,128)(2,1)S(1)}, bf16[384,256]{1,0:T(8,128)(2,1)S(1)}, u32[]{:S(2)}, u32[]{:S(2)}) collective-permute-start(bf16[384,256]{1,0:T(8,128)(2,1)S(1)} %slice.44), channel_id=1, source_target_pairs={{0,2},{2,4},{4,6},{6,7},{7,5},{5,3},{3,1},{1,0},{8,10},{10,12},{12... | collective-permute-start | bytes 589832 | tf_op jit(solution)/shard_map/ppermute | solution.py:110
  37.0 5.7 %collective-permute-start.13 = (bf16[256,256]{1,0:T(8,128)(2,1)S(1)}, bf16[256,256]{1,0:T(8,128)(2,1)S(1)}, u32[]{:S(2)}, u32[]{:S(2)}) collective-permute-start(bf16[256,256]{1,0:T(8,128)(2,1)S(1)} %slice.45), channel_id=1, source_target_pairs={{2,0},{4,2},{6,4},{7,6},{5,7},{3,5},{1,3},{0,1},{10,8},{12,10},{14... | collective-permute-start | bytes 393224 | tf_op jit(solution)/shard_map/ppermute | solution.py:110
  44.9 5.0 %collective-permute-start.18 = (bf16[256,256]{1,0:T(8,128)(2,1)S(1)}, bf16[256,256]{1,0:T(8,128)(2,1)S(1)}, u32[]{:S(2)}, u32[]{:S(2)}) collective-permute-start(bf16[256,256]{1,0:T(8,128)(2,1)S(1)} %get-tuple-element.39), channel_id=1, source_target_pairs={{2,0},{4,2},{6,4},{7,6},{5,7},{3,5},{1,3},{0,1},{10,8},{12,10},{14... | collective-permute-start | bytes 393224 | tf_op jit(solution)/shard_map/ppermute | solution.py:143
  45.0 6.4 %collective-permute-start.14 = (bf16[384,256]{1,0:T(8,128)(2,1)S(1)}, bf16[384,256]{1,0:T(8,128)(2,1)S(1)}, u32[]{:S(2)}, u32[]{:S(2)}) collective-permute-start(bf16[384,256]{1,0:T(8,128)(2,1)S(1)} %get-tuple-element.34.refs_6_), channel_id=1, source_target_pairs={{0,2},{2,4},{4,6},{6,7},{7,5},{5,3},{3,1},{1,0},{8,10},{10,12},{12... | collective-permute-start | bytes 589832 | tf_op jit(solution)/shard_map/ppermute | solution.py:143
  50.0 7.6 %collective-permute-start.19 = (bf16[640,256]{1,0:T(8,128)(2,1)S(1)}, bf16[640,256]{1,0:T(8,128)(2,1)S(1)}, u32[]{:S(2)}, u32[]{:S(2)}) collective-permute-start(bf16[640,256]{1,0:T(8,128)(2,1)S(1)} %pad_maximum_fusion.1), channel_id=1, source_target_pairs={{2,0},{4,2},{6,4},{7,6},{5,7},{3,5},{1,3},{0,1},{10,8},{12,10},{14... | collective-permute-start | bytes 983048 | tf_op jit(solution)/shard_map/ppermute | solution.py:153
  51.5 7.8 %collective-permute-start.15 = (bf16[640,256]{1,0:T(8,128)(2,1)S(1)}, bf16[640,256]{1,0:T(8,128)(2,1)S(1)}, u32[]{:S(2)}, u32[]{:S(2)}) collective-permute-start(bf16[640,256]{1,0:T(8,128)(2,1)S(1)} %pad_maximum_fusion), channel_id=1, source_target_pairs={{0,2},{2,4},{4,6},{6,7},{7,5},{5,3},{3,1},{1,0},{8,10},{10,12},{12... | collective-permute-start | bytes 983048 | tf_op jit(solution)/shard_map/ppermute | solution.py:153
  57.7 8.4 %collective-permute-start.20 = (bf16[640,256]{1,0:T(8,128)(2,1)S(1)}, bf16[640,256]{1,0:T(8,128)(2,1)S(1)}, u32[]{:S(2)}, u32[]{:S(2)}) collective-permute-start(bf16[640,256]{1,0:T(8,128)(2,1)S(1)} %add_convert_fusion.1), channel_id=1, source_target_pairs={{2,0},{4,2},{6,4},{7,6},{5,7},{3,5},{1,3},{0,1},{10,8},{12,10},{14... | collective-permute-start | bytes 983048 | tf_op jit(solution)/shard_map/ppermute | solution.py:153
  59.4 8.0 %collective-permute-start.16 = (bf16[640,256]{1,0:T(8,128)(2,1)S(1)}, bf16[640,256]{1,0:T(8,128)(2,1)S(1)}, u32[]{:S(2)}, u32[]{:S(2)}) collective-permute-start(bf16[640,256]{1,0:T(8,128)(2,1)S(1)} %add_convert_fusion.3), channel_id=1, source_target_pairs={{0,2},{2,4},{4,6},{6,7},{7,5},{5,3},{3,1},{1,0},{8,10},{10,12},{12... | collective-permute-start | bytes 983048 | tf_op jit(solution)/shard_map/ppermute | solution.py:153
  64.8 10.5 %copy-start.3 = (f32[640,256]{1,0:T(8,128)S(1)}, f32[640,256]{1,0:T(8,128)}, u32[]{:S(2)}) copy-start(f32[640,256]{1,0:T(8,128)} %param.11) | copy-start | bytes 1966084
  66.2 7.2 %collective-permute-start.21 = (bf16[640,256]{1,0:T(8,128)(2,1)S(1)}, bf16[640,256]{1,0:T(8,128)(2,1)S(1)}, u32[]{:S(2)}, u32[]{:S(2)}) collective-permute-start(bf16[640,256]{1,0:T(8,128)(2,1)S(1)} %add_convert_fusion), channel_id=1, source_target_pairs={{2,0},{4,2},{6,4},{7,6},{5,7},{3,5},{1,3},{0,1},{10,8},{12,10},{14... | collective-permute-start | bytes 983048 | tf_op jit(solution)/shard_map/ppermute | solution.py:153
  67.5 7.8 %collective-permute-start.17 = (bf16[640,256]{1,0:T(8,128)(2,1)S(1)}, bf16[640,256]{1,0:T(8,128)(2,1)S(1)}, u32[]{:S(2)}, u32[]{:S(2)}) collective-permute-start(bf16[640,256]{1,0:T(8,128)(2,1)S(1)} %add_convert_fusion.2), channel_id=1, source_target_pairs={{0,2},{2,4},{4,6},{6,7},{7,5},{5,3},{3,1},{1,0},{8,10},{10,12},{12... | collective-permute-start | bytes 983048 | tf_op jit(solution)/shard_map/ppermute | solution.py:153
  75.5 7.3 %collective-permute-start.24 = (bf16[384,256]{1,0:T(8,128)(2,1)S(1)}, bf16[384,256]{1,0:T(8,128)(2,1)S(1)}, u32[]{:S(2)}, u32[]{:S(2)}) collective-permute-start(bf16[384,256]{1,0:T(8,128)(2,1)S(1)} %slice.46.refs_2_), channel_id=1, source_target_pairs={{0,2},{2,4},{4,6},{6,7},{7,5},{5,3},{3,1},{1,0},{8,10},{10,12},{12... | collective-permute-start | bytes 589832 | tf_op jit(solution)/shard_map/ppermute | solution.py:131
  76.1 7.8 %collective-permute-start.23 = (bf16[256,256]{1,0:T(8,128)(2,1)S(1)}, bf16[256,256]{1,0:T(8,128)(2,1)S(1)}, u32[]{:S(2)}, u32[]{:S(2)}) collective-permute-start(bf16[256,256]{1,0:T(8,128)(2,1)S(1)} %slice.47.refs_3_), channel_id=1, source_target_pairs={{2,0},{4,2},{6,4},{7,6},{5,7},{3,5},{1,3},{0,1},{10,8},{12,10},{14... | collective-permute-start | bytes 393224 | tf_op jit(solution)/shard_map/ppermute | solution.py:131
  77.7 9.6 %collective-permute-start.22 = (bf16[384,256]{1,0:T(8,128)(2,1)S(1)}, bf16[384,256]{1,0:T(8,128)(2,1)S(1)}, u32[]{:S(2)}, u32[]{:S(2)}) collective-permute-start(bf16[384,256]{1,0:T(8,128)(2,1)S(1)} %slice.46.refs_2_), channel_id=1, source_target_pairs={{2,0},{4,2},{6,4},{7,6},{5,7},{3,5},{1,3},{0,1},{10,8},{12,10},{14... | collective-permute-start | bytes 589832 | tf_op jit(solution)/shard_map/ppermute | solution.py:131
  82.8 8.0 %collective-permute-start.28 = (bf16[384,256]{1,0:T(8,128)(2,1)S(1)}, bf16[384,256]{1,0:T(8,128)(2,1)S(1)}, u32[]{:S(2)}, u32[]{:S(2)}) collective-permute-start(bf16[384,256]{1,0:T(8,128)(2,1)S(1)} %collective-permute-done.24.refs_6_), channel_id=1, source_target_pairs={{0,2},{2,4},{4,6},{6,7},{7,5},{5,3},{3,1},{1,0},{8,10},{10,12},{12... | collective-permute-start | bytes 589832 | tf_op jit(solution)/shard_map/ppermute | solution.py:131
  83.9 7.8 %collective-permute-start.27 = (bf16[256,256]{1,0:T(8,128)(2,1)S(1)}, bf16[256,256]{1,0:T(8,128)(2,1)S(1)}, u32[]{:S(2)}, u32[]{:S(2)}) collective-permute-start(bf16[256,256]{1,0:T(8,128)(2,1)S(1)} %collective-permute-done.23.refs_5_), channel_id=1, source_target_pairs={{2,0},{4,2},{6,4},{7,6},{5,7},{3,5},{1,3},{0,1},{10,8},{12,10},{14... | collective-permute-start | bytes 393224 | tf_op jit(solution)/shard_map/ppermute | solution.py:131
  85.1 8.3 %collective-permute-start.25 = (bf16[256,256]{1,0:T(8,128)(2,1)S(1)}, bf16[256,256]{1,0:T(8,128)(2,1)S(1)}, u32[]{:S(2)}, u32[]{:S(2)}) collective-permute-start(bf16[256,256]{1,0:T(8,128)(2,1)S(1)} %slice.47.refs_3_), channel_id=1, source_target_pairs={{0,2},{2,4},{4,6},{6,7},{7,5},{5,3},{3,1},{1,0},{8,10},{10,12},{12... | collective-permute-start | bytes 393224 | tf_op jit(solution)/shard_map/ppermute | solution.py:131
  87.2 11.4 %collective-permute-start.26 = (bf16[384,256]{1,0:T(8,128)(2,1)S(1)}, bf16[384,256]{1,0:T(8,128)(2,1)S(1)}, u32[]{:S(2)}, u32[]{:S(2)}) collective-permute-start(bf16[384,256]{1,0:T(8,128)(2,1)S(1)} %collective-permute-done.22.refs_4_), channel_id=1, source_target_pairs={{2,0},{4,2},{6,4},{7,6},{5,7},{3,5},{1,3},{0,1},{10,8},{12,10},{14... | collective-permute-start | bytes 589832 | tf_op jit(solution)/shard_map/ppermute | solution.py:131
  90.8 10.1 %collective-permute-start.32 = (bf16[384,256]{1,0:T(8,128)(2,1)S(1)}, bf16[384,256]{1,0:T(8,128)(2,1)S(1)}, u32[]{:S(2)}, u32[]{:S(2)}) collective-permute-start(bf16[384,256]{1,0:T(8,128)(2,1)S(1)} %collective-permute-done.28.refs_10_), channel_id=1, source_target_pairs={{0,2},{2,4},{4,6},{6,7},{7,5},{5,3},{3,1},{1,0},{8,10},{10,12},{12... | collective-permute-start | bytes 589832 | tf_op jit(solution)/shard_map/ppermute | solution.py:131
  91.6 6.5 %collective-permute-start.31 = (bf16[256,256]{1,0:T(8,128)(2,1)S(1)}, bf16[256,256]{1,0:T(8,128)(2,1)S(1)}, u32[]{:S(2)}, u32[]{:S(2)}) collective-permute-start(bf16[256,256]{1,0:T(8,128)(2,1)S(1)} %collective-permute-done.27.refs_9_), channel_id=1, source_target_pairs={{2,0},{4,2},{6,4},{7,6},{5,7},{3,5},{1,3},{0,1},{10,8},{12,10},{14... | collective-permute-start | bytes 393224 | tf_op jit(solution)/shard_map/ppermute | solution.py:131
  93.4 7.7 %collective-permute-start.29 = (bf16[256,256]{1,0:T(8,128)(2,1)S(1)}, bf16[256,256]{1,0:T(8,128)(2,1)S(1)}, u32[]{:S(2)}, u32[]{:S(2)}) collective-permute-start(bf16[256,256]{1,0:T(8,128)(2,1)S(1)} %collective-permute-done.25.refs_7_), channel_id=1, source_target_pairs={{0,2},{2,4},{4,6},{6,7},{7,5},{5,3},{3,1},{1,0},{8,10},{10,12},{12... | collective-permute-start | bytes 393224 | tf_op jit(solution)/shard_map/ppermute | solution.py:131
  98.2 5.0 %collective-permute-start.35 = (bf16[256,256]{1,0:T(8,128)(2,1)S(1)}, bf16[256,256]{1,0:T(8,128)(2,1)S(1)}, u32[]{:S(2)}, u32[]{:S(2)}) collective-permute-start(bf16[256,256]{1,0:T(8,128)(2,1)S(1)} %collective-permute-done.31.refs_13_), channel_id=1, source_target_pairs={{2,0},{4,2},{6,4},{7,6},{5,7},{3,5},{1,3},{0,1},{10,8},{12,10},{14... | collective-permute-start | bytes 393224 | tf_op jit(solution)/shard_map/ppermute | solution.py:131
  98.6 9.3 %collective-permute-start.30 = (bf16[384,256]{1,0:T(8,128)(2,1)S(1)}, bf16[384,256]{1,0:T(8,128)(2,1)S(1)}, u32[]{:S(2)}, u32[]{:S(2)}) collective-permute-start(bf16[384,256]{1,0:T(8,128)(2,1)S(1)} %collective-permute-done.26.refs_8_), channel_id=1, source_target_pairs={{2,0},{4,2},{6,4},{7,6},{5,7},{3,5},{1,3},{0,1},{10,8},{12,10},{14... | collective-permute-start | bytes 589832 | tf_op jit(solution)/shard_map/ppermute | solution.py:131
  100.9 7.1 %collective-permute-start.34 = (bf16[384,256]{1,0:T(8,128)(2,1)S(1)}, bf16[384,256]{1,0:T(8,128)(2,1)S(1)}, u32[]{:S(2)}, u32[]{:S(2)}) collective-permute-start(bf16[384,256]{1,0:T(8,128)(2,1)S(1)} %collective-permute-done.32.refs_14_), channel_id=1, source_target_pairs={{0,2},{2,4},{4,6},{6,7},{7,5},{5,3},{3,1},{1,0},{8,10},{10,12},{12... | collective-permute-start | bytes 589832 | tf_op jit(solution)/shard_map/ppermute | solution.py:131
  101.0 6.9 %collective-permute-start.33 = (bf16[256,256]{1,0:T(8,128)(2,1)S(1)}, bf16[256,256]{1,0:T(8,128)(2,1)S(1)}, u32[]{:S(2)}, u32[]{:S(2)}) collective-permute-start(bf16[256,256]{1,0:T(8,128)(2,1)S(1)} %collective-permute-done.29.refs_11_), channel_id=1, source_target_pairs={{0,2},{2,4},{4,6},{6,7},{7,5},{5,3},{3,1},{1,0},{8,10},{10,12},{12... | collective-permute-start | bytes 393224 | tf_op jit(solution)/shard_map/ppermute | solution.py:131
  112.7 8.8 %collective-permute-start.37 = (bf16[4,128,256]{2,1,0:T(8,128)(2,1)S(1)}, bf16[4,128,256]{2,1,0:T(8,128)(2,1)S(1)}, u32[]{:S(2)}, u32[]{:S(2)}) collective-permute-start(bf16[4,128,256]{2,1,0:T(8,128)(2,1)S(1)} %get-tuple-element.45), channel_id=1, source_target_pairs={{0,16},{8,24},{16,0},{24,8},{1,17},{9,25},{17,1},{25,9},{2,18},{10... | collective-permute-start | bytes 786440 | tf_op jit(solution)/shard_map/ppermute | solution.py:546
  112.8 9.5 %collective-permute-start.38 = (bf16[4,128,256]{2,1,0:T(8,128)(2,1)S(1)}, bf16[4,128,256]{2,1,0:T(8,128)(2,1)S(1)}, u32[]{:S(2)}, u32[]{:S(2)}) collective-permute-start(bf16[4,128,256]{2,1,0:T(8,128)(2,1)S(1)} %get-tuple-element.46), channel_id=1, source_target_pairs={{0,24},{8,16},{16,8},{24,0},{1,25},{9,17},{17,9},{25,1},{2,26},{10... | collective-permute-start | bytes 786440 | tf_op jit(solution)/shard_map/ppermute | solution.py:546
  115.1 3.8 %copy-start = (f32[2048,256]{1,0:T(8,128)S(1)}, f32[2048,256]{1,0:T(8,128)}, u32[]{:S(2)}) copy-start(f32[2048,256]{1,0:T(8,128)} %param.10) | copy-start | bytes 6291460
  115.2 3.7 %collective-permute-start.36 = (bf16[4,128,256]{2,1,0:T(8,128)(2,1)S(1)}, bf16[4,128,256]{2,1,0:T(8,128)(2,1)S(1)}, u32[]{:S(2)}, u32[]{:S(2)}) collective-permute-start(bf16[4,128,256]{2,1,0:T(8,128)(2,1)S(1)} %get-tuple-element.43), channel_id=1, source_target_pairs={{0,8},{8,0},{16,24},{24,16},{1,9},{9,1},{17,25},{25,17},{2,10},{10... | collective-permute-start | bytes 786440 | tf_op jit(solution)/shard_map/ppermute | solution.py:546

commit v5 on v4

--- a/solution.py
+++ b/solution.py
@@ -236,12 +236,9 @@
     )(*map(near, inputs))
 
 
-def list_kernel(cfg, row_ref, live_ref, ids_ref, observed, *refs):
+def list_kernel(cfg, row_ref, live_ref, ids_ref, pairs_ref, counts_ref, mark):
     row_count, per_owner, kinds, starts, room = cfg
-    pairs_ref, counts_ref, held, mark, sem = refs[-5:]
     mark[...] = jnp.zeros_like(mark)
-    copy = pltpu.make_async_copy(observed, held, sem)
-    copy.start()
     row = row_ref[0]
     counts = (jnp.int32(0),) * len(starts)
     for owner in range(row_count):
@@ -270,10 +267,9 @@
         for q in range(batch - 1):
             blank = start + row_count * per_owner * 4096
             pairs_ref[g * room + counts[g] + q] = jnp.int32(blank)
-    copy.wait()
-
-
-def list_pairs(row, live, ids, observed, plan, row_count, per_owner, kinds, rank):
+
+
+def list_pairs(row, live, ids, plan, row_count, per_owner, kinds, rank):
     room = row_count * per_owner * kinds + batch
     groups = len(plan.groups)
     return pl.pallas_call(
@@ -281,14 +277,39 @@
         out_shape=[
             jax.ShapeDtypeStruct((groups * room,), jnp.int32),
             jax.ShapeDtypeStruct((groups,), jnp.int32),
-            VMEM(observed.shape, observed.dtype),
             VMEM((8, rank), jnp.float32),
         ],
-        in_specs=[spec(SMEM)] * 3 + [spec(pltpu.HBM)],
-        out_specs=[spec(SMEM)] * 2 + [spec(VMEM)] * 2,
-        scratch_shapes=[pltpu.SemaphoreType.DMA],
+        in_specs=[spec(SMEM)] * 3,
+        out_specs=[spec(SMEM)] * 2 + [spec(VMEM)],
         compiler_params=params(1),
-    )(row, live, ids, away(observed))
+    )(row, live, ids)
+
+
+def hold_kernel(observed, *refs):
+    held, mark, sems = refs[-3:]
+    copies = [
+        pltpu.make_async_copy(observed.at[slot], held.at[slot], sems.at[slot])
+        for slot in range(observed.shape[0])
+    ]
+    for copy in copies:
+        copy.start()
+    mark[...] = jnp.zeros_like(mark)
+    for copy in copies:
+        copy.wait()
+
+
+def hold(observed, marks):
+    return pl.pallas_call(
+        hold_kernel,
+        out_shape=[
+            VMEM(observed.shape, observed.dtype),
+            VMEM((8, marks[0].shape[1]), jnp.float32),
+        ],
+        in_specs=[spec(pltpu.HBM)] + [spec(VMEM)] * len(marks),
+        out_specs=[spec(VMEM)] * 2,
+        scratch_shapes=[pltpu.SemaphoreType.DMA((observed.shape[0],))],
+        compiler_params=params(1),
+    )(away(observed), *map(near, marks))
 
 
 def load_skus(held, refs, starts):
@@ -508,16 +529,17 @@
     owner_place = ring_place(store_ids // plan.blocks, plan.count)
     arrival = plan.arrival((owner_place - place) % plan.count)
     ids = arrival * plan.blocks + store_ids % plan.blocks
-    pairs, counts, observed, listed = list_pairs(
-        row_vec, live, ids, observed, plan, row_count, per_owner, kinds, rank
+    pairs, counts, listed = list_pairs(
+        row_vec, live, ids, plan, row_count, per_owner, kinds, rank
     )
     picked = pick(row_vec, asked, sku, per_owner, listed)
     pieces = gather_ring(store_factors.astype(jnp.bfloat16), plan)
 
+    observed, is_held = hold(observed, pieces[1] + pieces[plan.count - 1])
     direct, through = [], []
     for x in range(1, row_count // 2):
         direct.append(lax.ppermute(picked[2 * x], "row", swaps[2 * x]))
-        onward = after(picked[2 * x + 1], direct[-1][0])
+        onward = after(after(picked[2 * x + 1], direct[-1][0]), is_held)
         through.append(lax.ppermute(onward, "row", swaps[2 * x]))
     late = pieces[plan.far - 1] + pieces[plan.far + 1]
     passed = lax.ppermute(join(picked[1], through, per_owner, late), "row", swaps[1])

time: 125 us -> 125 us (level)
  starting transfers between devices: 38.2 us -> 40.7 us
  Pallas kernels: 28.8 us -> 26.8 us
  waiting for transfers between devices: 51.6 us -> 50.2 us
    pallas_call x0 -> x1, Pallas kernels: none -> 2.27 us  [hold(): pl.pallas_call(hold_kernel, out_shape=[VMEM(observed.shape, observed.dtyp...]
    pallas_call x4, Pallas kernels: 12 us -> 10 us  [first_pass(): pl.pallas_call(functools.partial(first_kernel, cfg), out_shape=[VMEM((hei...]
    pallas_call x1, Pallas kernels: 3.43 us -> 2.05 us  [list_pairs(): pl.pallas_call(functools.partial(list_kernel, (row_count, per_owner, kind...]
    ppermute x1, waiting for transfers between devices: 4.55 us -> 3.23 us  [local(): direct.append(lax.ppermute(picked[2 * x], 'row', swaps[2 * x]))]
    ppermute x6, starting transfers between devices: 4.12 us -> 5.38 us  [scatter_ring(): moved[way] = lax.ppermute(value, 'col', steps[way])]
  transfers between devices with their start and end apart: 39 -> 39, of which waited for: 25 -> 25; matrix products, arithmetic and copies ran while one was open for 2% -> 3% of each run, Pallas kernels for 16% -> 15%
where the time goes in v5:
time: 125 us; the launch traced here: 124 us
  waiting for transfers between devices  50.2 us (40%)
  starting transfers between devices  40.7 us (33%)
  Pallas kernels  26.8 us (21%)
  other arithmetic  3.75 us (3%)
  local copies, waits for them, and re-layouts  1.39 us (1%)
    ppermute x14, waiting for transfers between devices, gather_split(): moved[way, h] = lax.ppermute(moved[way, h], 'col', steps[way])  17.3 us
    ppermute x14, starting transfers between devices, gather_split(): moved[way, h] = lax.ppermute(moved[way, h], 'col', steps[way])  14.8 us
    ppermute x6, waiting for transfers between devices, scatter_ring(): moved[way] = lax.ppermute(value, 'col', steps[way])  13.2 us
    pallas_call x4, Pallas kernels, first_pass(): pl.pallas_call(functools.partial(first_kernel, cfg), out_shape=[VMEM((hei...  10 us
    ppermute x8, starting transfers between devices, gather_ring(): moved = [lax.ppermute(moved[way], 'col', steps[way]) for way in (0, 1)]  8.33 us
    pallas_call x2, Pallas kernels, second_pass(): pl.pallas_call(functools.partial(second_kernel, (ks, sku_starts, per_owne...  6.06 us
    ppermute x8, waiting for transfers between devices, gather_ring(): moved = [lax.ppermute(moved[way], 'col', steps[way]) for way in (0, 1)]  5.62 us
    ppermute x6, starting transfers between devices, scatter_ring(): moved[way] = lax.ppermute(value, 'col', steps[way])  5.38 us
  transfers between devices with their start and end apart: 39, of which 25 were waited for; matrix products, arithmetic and copies ran while one was open for 3% of the time, Pallas kernels for 15%

profile of v5, /device:TPU:0, one launch (start us, length us, event | category | flops | bytes accessed | tf_op | source)
XLA Modules:
  0.0 123.7 jit_solution(485394876840021951)
XLA Ops:
  0.6 3.0 %collective-permute-start = (s32[16]{0:T(128)}, s32[16]{0:T(128)S(1)}, u32[]{:S(2)}, u32[]{:S(2)}) collective-permute-start(s32[16]{0:T(128)} %refs_0_.3), channel_id=1, source_target_pairs={{0,16},{8,24},{16,0},{24,8},{1,17},{9,25},{17,1},{25,9},{2,18},{10... | collective-permute-start | bytes 200 | tf_op jit(solution)/shard_map/ppermute | solution.py:526
  3.8 1.1 convert_element_type.69.refs_4_
  5.0 2.0 %collective-permute-start.3 = (bf16[640,256]{1,0:T(8,128)(2,1)S(1)}, bf16[640,256]{1,0:T(8,128)(2,1)S(1)}, u32[]{:S(2)}, u32[]{:S(2)}) collective-permute-start(bf16[640,256]{1,0:T(8,128)(2,1)S(1)} %convert_element_type.69.refs_4_), channel_id=1, source_target_pairs={{2,0},{4,2},{6,4},{7,6},{5,7},{3,5},{1,3},{0,1},{10,8},{12,10},{14... | collective-permute-start | bytes 983048 | tf_op jit(solution)/shard_map/ppermute | solution.py:110
  7.1 0.7 fusion.5.ids_ref
  7.8 0.6 copy-done.1
  8.5 2.1 %shard_map.78 = (s32[544]{0:T(1024)S(1)}, s32[4]{0:T(128)S(1)}, f32[8,256]{1,0:T(8,128)S(1)}) custom-call(s32[1]{0:T(128)} %bitcast.row_ref, s32[4]{0:T(128)S(1)} %bitcast.28, s32[8,16]{1,0:T(8,128)S(1)} %fusion.5.ids_ref), custom_call_target="tpu_custom_call" | custom-call | tf_op jit(solution)/shard_map/pallas_call | solution.py:275
  10.6 0.6 copy-done.3
  11.2 2.3 %shard_map.79 = (bf16[4,128,256]{2,1,0:T(8,128)(2,1)S(1)}, bf16[4,128,256]{2,1,0:T(8,128)(2,1)S(1)}, bf16[4,128,256]{2,1,0:T(8,128)(2,1)S(1)}, bf16[4,128,256]{2,1,0:T(8,128)(2,1)S(1)}) custom-call(s32[1]{0:T(128)} %bitcast.row_ref, s32[16]{0:T(128)S(1)} %copy-done.3, s32[16]{0:T(128)S(1)} %collective-permute-done.2.refs_1_, ...), custom_call_target="tpu_custom_call" | custom-call | tf_op jit(solution)/shard_map/pallas_call | solution.py:207
  13.6 1.8 %collective-permute-start.5 = (bf16[4,128,256]{2,1,0:T(8,128)(2,1)S(1)}, bf16[4,128,256]{2,1,0:T(8,128)(2,1)S(1)}, u32[]{:S(2)}, u32[]{:S(2)}) collective-permute-start(bf16[4,128,256]{2,1,0:T(8,128)(2,1)S(1)} %get-tuple-element.30), channel_id=1, source_target_pairs={{0,16},{8,24},{16,0},{24,8},{1,17},{9,25},{17,1},{25,9},{2,18},{10... | collective-permute-start | bytes 786440 | tf_op jit(solution)/shard_map/ppermute | solution.py:541
  15.3 1.0 collective-permute-done.4.refs_1_.refs_6_
  16.3 1.0 collective-permute-start.9
  17.3 1.0 collective-permute-start.7
  18.3 3.2 %collective-permute-done.5.refs_2_.refs_0_ = bf16[4,128,256]{2,1,0:T(8,128)(2,1)S(1)} collective-permute-done((bf16[4,128,256]{2,1,0:T(8,128)(2,1)S(1)}, bf16[4,128,256]{2,1,0:T(8,128)(2,1)S(1)}, u32[]{:S(2)}, u32[]{:S(2)}) %collective-permute-start.5) | collective-permute-done | bytes 262176 | tf_op jit(solution)/shard_map/ppermute | solution.py:541
  21.6 2.3 %shard_map.77 = (bf16[16,8,128,128]{3,2,1,0:T(8,128)(2,1)S(1)}, f32[8,256]{1,0:T(8,128)S(1)}) custom-call(bf16[16,8,128,128]{3,2,1,0:T(8,128)(2,1)} %observed.1, bf16[640,256]{1,0:T(8,128)(2,1)S(1)} %collective-permute-done.3.refs_0_.refs_5_, bf16[640,256]{1,0:T(8,128)(2,1)S(1)} %collective-permute-done.4.refs_1_.refs_6_), custom_call_target="tpu_custom_call" | custom-call | tf_op jit(solution)/shard_map/pallas_call | solution.py:302
  23.9 0.9 collective-permute-done.9.refs_5_
  24.8 1.4 %collective-permute-start.10 = (bf16[640,256]{1,0:T(8,128)(2,1)S(1)}, bf16[640,256]{1,0:T(8,128)(2,1)S(1)}, u32[]{:S(2)}, u32[]{:S(2)}) collective-permute-start(bf16[640,256]{1,0:T(8,128)(2,1)S(1)} %collective-permute-done.9.refs_5_), channel_id=1, source_target_pairs={{0,2},{2,4},{4,6},{6,7},{7,5},{5,3},{3,1},{1,0},{8,10},{10,12},{12... | collective-permute-start | bytes 983048 | tf_op jit(solution)/shard_map/ppermute | solution.py:110
  26.2 0.6 collective-permute-start.8
  26.8 1.6 %collective-permute-start.6 = (bf16[4,128,256]{2,1,0:T(8,128)(2,1)S(1)}, bf16[4,128,256]{2,1,0:T(8,128)(2,1)S(1)}, u32[]{:S(2)}, u32[]{:S(2)}) collective-permute-start(bf16[4,128,256]{2,1,0:T(8,128)(2,1)S(1)} %select_select_fusion), channel_id=1, source_target_pairs={{0,16},{8,24},{16,0},{24,8},{1,17},{9,25},{17,1},{25,9},{2,18},{10... | collective-permute-start | bytes 786440 | tf_op jit(solution)/shard_map/ppermute | solution.py:543
  28.4 4.9 %collective-permute-done.6.refs_0_ = bf16[4,128,256]{2,1,0:T(8,128)(2,1)S(1)} collective-permute-done((bf16[4,128,256]{2,1,0:T(8,128)(2,1)S(1)}, bf16[4,128,256]{2,1,0:T(8,128)(2,1)S(1)}, u32[]{:S(2)}, u32[]{:S(2)}) %collective-permute-start.6) | collective-permute-done | bytes 262176 | tf_op jit(solution)/shard_map/ppermute | solution.py:543
  33.3 0.6 collective-permute-done.8.refs_1_.refs_4_
  34.0 1.8 %collective-permute-start.12 = (bf16[384,256]{1,0:T(8,128)(2,1)S(1)}, bf16[384,256]{1,0:T(8,128)(2,1)S(1)}, u32[]{:S(2)}, u32[]{:S(2)}) collective-permute-start(bf16[384,256]{1,0:T(8,128)(2,1)S(1)} %slice.48), channel_id=1, source_target_pairs={{0,2},{2,4},{4,6},{6,7},{7,5},{5,3},{3,1},{1,0},{8,10},{10,12},{12... | collective-permute-start | bytes 589832 | tf_op jit(solution)/shard_map/ppermute | solution.py:110
  36.2 2.2 %shard_map.81 = (bf16[640,256]{1,0:T(8,128)(2,1)S(1)}, bf16[640,256]{1,0:T(8,128)(2,1)S(1)}) custom-call(s32[544]{0:T(1024)S(1)} %get-tuple-element.33.pairs_ref, s32[4]{0:T(128)S(1)} %get-tuple-element.34.counts_ref, bf16[16,8,128,128]{3,2,1,0:T(8,128)(2,1)S(1)} %get-tuple-element.26.observed, bf16[4,128,256]{2,1,0:T(8,128)(2,1)S(1)} %get-tuple-element.32.refs_0_.refs_1_, ...), custom_call_target="tpu_custom_call" | custom-call | flops 570425344 | bytes 8912896 | tf_op jit(solution)/shard_map/pallas_call | solution.py:386
  38.4 3.1 %collective-permute-done.13.refs_5_ = bf16[256,256]{1,0:T(8,128)(2,1)S(1)} collective-permute-done((bf16[256,256]{1,0:T(8,128)(2,1)S(1)}, bf16[256,256]{1,0:T(8,128)(2,1)S(1)}, u32[]{:S(2)}, u32[]{:S(2)}) %collective-permute-start.13) | collective-permute-done | bytes 131104 | tf_op jit(solution)/shard_map/ppermute | solution.py:110
  41.5 1.4 %shard_map.82 = (bf16[384,256]{1,0:T(8,128)(2,1)S(1)}, bf16[256,256]{1,0:T(8,128)(2,1)S(1)}) custom-call(s32[544]{0:T(1024)S(1)} %get-tuple-element.33.pairs_ref, s32[4]{0:T(128)S(1)} %get-tuple-element.34.counts_ref, bf16[16,8,128,128]{3,2,1,0:T(8,128)(2,1)S(1)} %get-tuple-element.26.observed, bf16[4,128,256]{2,1,0:T(8,128)(2,1)S(1)} %get-tuple-element.32.refs_0_.refs_1_, ...), custom_call_target="tpu_custom_call" | custom-call | flops 285212672 | bytes 4456448 | tf_op jit(solution)/shard_map/pallas_call | solution.py:386
  42.9 0.9 collective-permute-start.18
  43.8 1.5 %collective-permute-start.14 = (bf16[384,256]{1,0:T(8,128)(2,1)S(1)}, bf16[384,256]{1,0:T(8,128)(2,1)S(1)}, u32[]{:S(2)}, u32[]{:S(2)}) collective-permute-start(bf16[384,256]{1,0:T(8,128)(2,1)S(1)} %get-tuple-element.36.refs_6_), channel_id=1, source_target_pairs={{0,2},{2,4},{4,6},{6,7},{7,5},{5,3},{3,1},{1,0},{8,10},{10,12},{12... | collective-permute-start | bytes 589832 | tf_op jit(solution)/shard_map/ppermute | solution.py:143
  45.4 3.3 %collective-permute-done.18 = bf16[256,256]{1,0:T(8,128)(2,1)S(1)} collective-permute-done((bf16[256,256]{1,0:T(8,128)(2,1)S(1)}, bf16[256,256]{1,0:T(8,128)(2,1)S(1)}, u32[]{:S(2)}, u32[]{:S(2)}) %collective-permute-start.18) | collective-permute-done | bytes 131104 | tf_op jit(solution)/shard_map/ppermute | solution.py:143
  49.0 1.1 collective-permute-done.14
  50.2 1.8 %collective-permute-start.15 = (bf16[640,256]{1,0:T(8,128)(2,1)S(1)}, bf16[640,256]{1,0:T(8,128)(2,1)S(1)}, u32[]{:S(2)}, u32[]{:S(2)}) collective-permute-start(bf16[640,256]{1,0:T(8,128)(2,1)S(1)} %pad_maximum_fusion), channel_id=1, source_target_pairs={{0,2},{2,4},{4,6},{6,7},{7,5},{5,3},{3,1},{1,0},{8,10},{10,12},{12... | collective-permute-start | bytes 983048 | tf_op jit(solution)/shard_map/ppermute | solution.py:153
  52.0 2.8 %shard_map.83 = (bf16[640,256]{1,0:T(8,128)(2,1)S(1)}, bf16[640,256]{1,0:T(8,128)(2,1)S(1)}) custom-call(s32[544]{0:T(1024)S(1)} %get-tuple-element.33.pairs_ref, s32[4]{0:T(128)S(1)} %get-tuple-element.34.counts_ref, bf16[16,8,128,128]{3,2,1,0:T(8,128)(2,1)S(1)} %get-tuple-element.26.observed, bf16[4,128,256]{2,1,0:T(8,128)(2,1)S(1)} %get-tuple-element.32.refs_0_.refs_1_, ...), custom_call_target="tpu_custom_call" | custom-call | flops 570425344 | bytes 8912896 | tf_op jit(solution)/shard_map/pallas_call | solution.py:386
  54.8 2.7 %collective-permute-done.19 = bf16[640,256]{1,0:T(8,128)(2,1)S(1)} collective-permute-done((bf16[640,256]{1,0:T(8,128)(2,1)S(1)}, bf16[640,256]{1,0:T(8,128)(2,1)S(1)}, u32[]{:S(2)}, u32[]{:S(2)}) %collective-permute-start.19) | collective-permute-done | bytes 327712 | tf_op jit(solution)/shard_map/ppermute | solution.py:153
  57.9 0.6 collective-permute-done.15
  58.6 1.9 %collective-permute-start.16 = (bf16[640,256]{1,0:T(8,128)(2,1)S(1)}, bf16[640,256]{1,0:T(8,128)(2,1)S(1)}, u32[]{:S(2)}, u32[]{:S(2)}) collective-permute-start(bf16[640,256]{1,0:T(8,128)(2,1)S(1)} %add_convert_fusion.3), channel_id=1, source_target_pairs={{0,2},{2,4},{4,6},{6,7},{7,5},{5,3},{3,1},{1,0},{8,10},{10,12},{12... | collective-permute-start | bytes 983048 | tf_op jit(solution)/shard_map/ppermute | solution.py:153
  60.6 3.6 %shard_map.84 = (bf16[640,256]{1,0:T(8,128)(2,1)S(1)}, bf16[640,256]{1,0:T(8,128)(2,1)S(1)}, bf16[640,256]{1,0:T(8,128)(2,1)S(1)}) custom-call(s32[544]{0:T(1024)S(1)} %get-tuple-element.33.pairs_ref, s32[4]{0:T(128)S(1)} %get-tuple-element.34.counts_ref, bf16[16,8,128,128]{3,2,1,0:T(8,128)(2,1)S(1)} %get-tuple-element.26.observed, ...), custom_call_target="tpu_custom_call" | custom-call | flops 855638016 | bytes 13369344 | tf_op jit(solution)/shard_map/pallas_call | solution.py:386
  64.2 1.3 %collective-permute-done.20 = bf16[640,256]{1,0:T(8,128)(2,1)S(1)} collective-permute-done((bf16[640,256]{1,0:T(8,128)(2,1)S(1)}, bf16[640,256]{1,0:T(8,128)(2,1)S(1)}, u32[]{:S(2)}, u32[]{:S(2)}) %collective-permute-start.20) | collective-permute-done | bytes 327712 | tf_op jit(solution)/shard_map/ppermute | solution.py:153
  65.9 1.6 %collective-permute-done.16 = bf16[640,256]{1,0:T(8,128)(2,1)S(1)} collective-permute-done((bf16[640,256]{1,0:T(8,128)(2,1)S(1)}, bf16[640,256]{1,0:T(8,128)(2,1)S(1)}, u32[]{:S(2)}, u32[]{:S(2)}) %collective-permute-start.16) | collective-permute-done | bytes 327712 | tf_op jit(solution)/shard_map/ppermute | solution.py:153
  67.6 0.6 collective-permute-start.17
  68.2 4.5 %collective-permute-done.21 = bf16[640,256]{1,0:T(8,128)(2,1)S(1)} collective-permute-done((bf16[640,256]{1,0:T(8,128)(2,1)S(1)}, bf16[640,256]{1,0:T(8,128)(2,1)S(1)}, u32[]{:S(2)}, u32[]{:S(2)}) %collective-permute-start.21) | collective-permute-done | bytes 327712 | tf_op jit(solution)/shard_map/ppermute | solution.py:153
  72.7 2.5 %collective-permute-done.17 = bf16[640,256]{1,0:T(8,128)(2,1)S(1)} collective-permute-done((bf16[640,256]{1,0:T(8,128)(2,1)S(1)}, bf16[640,256]{1,0:T(8,128)(2,1)S(1)}, u32[]{:S(2)}, u32[]{:S(2)}) %collective-permute-start.17) | collective-permute-done | bytes 327712 | tf_op jit(solution)/shard_map/ppermute | solution.py:153
  76.0 1.7 %collective-permute-start.23 = (bf16[256,256]{1,0:T(8,128)(2,1)S(1)}, bf16[256,256]{1,0:T(8,128)(2,1)S(1)}, u32[]{:S(2)}, u32[]{:S(2)}) collective-permute-start(bf16[256,256]{1,0:T(8,128)(2,1)S(1)} %slice.51.refs_3_), channel_id=1, source_target_pairs={{2,0},{4,2},{6,4},{7,6},{5,7},{3,5},{1,3},{0,1},{10,8},{12,10},{14... | collective-permute-start | bytes 393224 | tf_op jit(solution)/shard_map/ppermute | solution.py:131
  77.6 1.7 %collective-permute-start.22 = (bf16[384,256]{1,0:T(8,128)(2,1)S(1)}, bf16[384,256]{1,0:T(8,128)(2,1)S(1)}, u32[]{:S(2)}, u32[]{:S(2)}) collective-permute-start(bf16[384,256]{1,0:T(8,128)(2,1)S(1)} %slice.50.refs_2_), channel_id=1, source_target_pairs={{2,0},{4,2},{6,4},{7,6},{5,7},{3,5},{1,3},{0,1},{10,8},{12,10},{14... | collective-permute-start | bytes 589832 | tf_op jit(solution)/shard_map/ppermute | solution.py:131
  79.4 3.7 %collective-permute-done.24.refs_6_ = bf16[384,256]{1,0:T(8,128)(2,1)S(1)} collective-permute-done((bf16[384,256]{1,0:T(8,128)(2,1)S(1)}, bf16[384,256]{1,0:T(8,128)(2,1)S(1)}, u32[]{:S(2)}, u32[]{:S(2)}) %collective-permute-start.24) | collective-permute-done | bytes 196640 | tf_op jit(solution)/shard_map/ppermute | solution.py:131
  83.0 0.6 collective-permute-start.28
  83.6 1.4 %collective-permute-start.27 = (bf16[256,256]{1,0:T(8,128)(2,1)S(1)}, bf16[256,256]{1,0:T(8,128)(2,1)S(1)}, u32[]{:S(2)}, u32[]{:S(2)}) collective-permute-start(bf16[256,256]{1,0:T(8,128)(2,1)S(1)} %collective-permute-done.23.refs_5_), channel_id=1, source_target_pairs={{2,0},{4,2},{6,4},{7,6},{5,7},{3,5},{1,3},{0,1},{10,8},{12,10},{14... | collective-permute-start | bytes 393224 | tf_op jit(solution)/shard_map/ppermute | solution.py:131
  85.1 1.1 collective-permute-start.25
  86.1 0.8 collective-permute-done.22.refs_4_
  87.0 1.2 collective-permute-start.26
  88.2 2.5 %collective-permute-done.28.refs_10_ = bf16[384,256]{1,0:T(8,128)(2,1)S(1)} collective-permute-done((bf16[384,256]{1,0:T(8,128)(2,1)S(1)}, bf16[384,256]{1,0:T(8,128)(2,1)S(1)}, u32[]{:S(2)}, u32[]{:S(2)}) %collective-permute-start.28) | collective-permute-done | bytes 196640 | tf_op jit(solution)/shard_map/ppermute | solution.py:131
  90.7 0.6 collective-permute-start.32
  91.4 1.4 %collective-permute-start.31 = (bf16[256,256]{1,0:T(8,128)(2,1)S(1)}, bf16[256,256]{1,0:T(8,128)(2,1)S(1)}, u32[]{:S(2)}, u32[]{:S(2)}) collective-permute-start(bf16[256,256]{1,0:T(8,128)(2,1)S(1)} %collective-permute-done.27.refs_9_), channel_id=1, source_target_pairs={{2,0},{4,2},{6,4},{7,6},{5,7},{3,5},{1,3},{0,1},{10,8},{12,10},{14... | collective-permute-start | bytes 393224 | tf_op jit(solution)/shard_map/ppermute | solution.py:131
  93.6 3.9 %collective-permute-done.31.refs_13_ = bf16[256,256]{1,0:T(8,128)(2,1)S(1)} collective-permute-done((bf16[256,256]{1,0:T(8,128)(2,1)S(1)}, bf16[256,256]{1,0:T(8,128)(2,1)S(1)}, u32[]{:S(2)}, u32[]{:S(2)}) %collective-permute-start.31) | collective-permute-done | bytes 131104 | tf_op jit(solution)/shard_map/ppermute | solution.py:131
  97.5 1.2 collective-permute-start.35
  98.8 1.8 %collective-permute-start.30 = (bf16[384,256]{1,0:T(8,128)(2,1)S(1)}, bf16[384,256]{1,0:T(8,128)(2,1)S(1)}, u32[]{:S(2)}, u32[]{:S(2)}) collective-permute-start(bf16[384,256]{1,0:T(8,128)(2,1)S(1)} %collective-permute-done.26.refs_8_), channel_id=1, source_target_pairs={{2,0},{4,2},{6,4},{7,6},{5,7},{3,5},{1,3},{0,1},{10,8},{12,10},{14... | collective-permute-start | bytes 589832 | tf_op jit(solution)/shard_map/ppermute | solution.py:131
  101.0 0.8 collective-permute-start.33
  101.8 0.7 collective-permute-done.35.refs_17_
  102.5 5.1 %collective-permute-done.33.refs_15_ = bf16[256,256]{1,0:T(8,128)(2,1)S(1)} collective-permute-done((bf16[256,256]{1,0:T(8,128)(2,1)S(1)}, bf16[256,256]{1,0:T(8,128)(2,1)S(1)}, u32[]{:S(2)}, u32[]{:S(2)}) %collective-permute-start.33) | collective-permute-done | bytes 131104 | tf_op jit(solution)/shard_map/ppermute | solution.py:131
  107.6 4.7 %shard_map.87 = (bf16[4,128,256]{2,1,0:T(8,128)(2,1)S(1)}, bf16[4,128,256]{2,1,0:T(8,128)(2,1)S(1)}) custom-call(s32[1]{0:T(128)} %bitcast.row_ref, s32[4]{0:T(128)S(1)} %bitcast.29, s32[8,16]{1,0:T(8,128)S(1)} %fusion.5.ids_ref, bf16[16,8,128,128]{3,2,1,0:T(8,128)(2,1)S(1)} %get-tuple-element.26.observed, ...), custom_call_target="tpu_custom_call" | custom-call | flops 1073741824 | bytes 16777216 | tf_op jit(solution)/shard_map/pallas_call | solution.py:436
  112.5 1.3 %shard_map.85 = (bf16[4,128,256]{2,1,0:T(8,128)(2,1)S(1)}, bf16[4,128,256]{2,1,0:T(8,128)(2,1)S(1)}) custom-call(s32[1]{0:T(128)} %bitcast.row_ref, s32[4]{0:T(128)S(1)} %bitcast.30, s32[8,16]{1,0:T(8,128)S(1)} %fusion.5.ids_ref, bf16[16,8,128,128]{3,2,1,0:T(8,128)(2,1)S(1)} %get-tuple-element.26.observed, ...), custom_call_target="tpu_custom_call" | custom-call | flops 1073741824 | bytes 16777216 | tf_op jit(solution)/shard_map/pallas_call | solution.py:436
  113.9 3.1 %collective-permute-start.36 = (bf16[4,128,256]{2,1,0:T(8,128)(2,1)S(1)}, bf16[4,128,256]{2,1,0:T(8,128)(2,1)S(1)}, u32[]{:S(2)}, u32[]{:S(2)}) collective-permute-start(bf16[4,128,256]{2,1,0:T(8,128)(2,1)S(1)} %get-tuple-element.45), channel_id=1, source_target_pairs={{0,8},{8,0},{16,24},{24,16},{1,9},{9,1},{17,25},{25,17},{2,10},{10... | collective-permute-start | bytes 786440 | tf_op jit(solution)/shard_map/ppermute | solution.py:568
  117.0 1.1 multiply_subtract_fusion
  118.1 2.3 %shard_map.86 = (f32[16,128,256]{2,1,0:T(8,128)S(1)}, f32[16,128,256]{2,1,0:T(8,128)}) custom-call(s32[1]{0:T(128)} %bitcast.row_ref, s32[16]{0:T(128)S(1)} %copy-done.4, s32[16]{0:T(128)S(1)} %collective-permute-done.2.refs_1_, f32[16,128,256]{2,1,0:T(8,128)S(1)} %bitcast.27, bf16[4,128,256]{2,1,0:T(8,128)(2,1)S(1)} %get-tuple-element.44.refs_3_, ...), custom_call_target="tpu_custom_call" | custom-call | tf_op jit(solution)/shard_map/pallas_call | solution.py:477
  120.4 0.7 collective-permute-done.37.refs_3_
  121.1 0.8 collective-permute-done.38.refs_4_
  122.0 1.8 %shard_map.88 = f32[16,128,256]{2,1,0:T(8,128)} custom-call(s32[1]{0:T(128)} %bitcast.row_ref, s32[16]{0:T(128)S(1)} %collective-permute-done.refs_2_.refs_0_, s32[16]{0:T(128)S(1)} %collective-permute-done.1.refs_3_.refs_1_, f32[16,128,256]{2,1,0:T(8,128)S(1)} %get-tuple-element.46.refs_2_, ...), custom_call_target="tpu_custom_call", output_to_operand_aliasing={{}: (6, {})} | custom-call | tf_op jit(solution)/shard_map/pallas_call | solution.py:499
  (60 shorter events, 4.8 us)
Async XLA Ops:
  0.6 9.9 %collective-permute-start = (s32[16]{0:T(128)}, s32[16]{0:T(128)S(1)}, u32[]{:S(2)}, u32[]{:S(2)}) collective-permute-start(s32[16]{0:T(128)} %refs_0_.3), channel_id=1, source_target_pairs={{0,16},{8,24},{16,0},{24,8},{1,17},{9,25},{17,1},{25,9},{2,18},{10... | collective-permute-start | bytes 200 | tf_op jit(solution)/shard_map/ppermute | solution.py:526
  3.6 6.9 %collective-permute-start.1 = (s32[16]{0:T(128)}, s32[16]{0:T(128)S(1)}, u32[]{:S(2)}, u32[]{:S(2)}) collective-permute-start(s32[16]{0:T(128)} %refs_0_.3), channel_id=1, source_target_pairs={{0,24},{8,16},{16,8},{24,0},{1,25},{9,17},{17,9},{25,1},{2,26},{10... | collective-permute-start | bytes 200 | tf_op jit(solution)/shard_map/ppermute | solution.py:526
  3.6 6.9 %collective-permute-start.2 = (s32[16]{0:T(128)}, s32[16]{0:T(128)S(1)}, u32[]{:S(2)}, u32[]{:S(2)}) collective-permute-start(s32[16]{0:T(128)} %refs_0_.3), channel_id=1, source_target_pairs={{0,8},{8,0},{16,24},{24,16},{1,9},{9,1},{17,25},{25,17},{2,10},{10... | collective-permute-start | bytes 200 | tf_op jit(solution)/shard_map/ppermute | solution.py:526
  5.0 12.4 %collective-permute-start.3 = (bf16[640,256]{1,0:T(8,128)(2,1)S(1)}, bf16[640,256]{1,0:T(8,128)(2,1)S(1)}, u32[]{:S(2)}, u32[]{:S(2)}) collective-permute-start(bf16[640,256]{1,0:T(8,128)(2,1)S(1)} %convert_element_type.69.refs_4_), channel_id=1, source_target_pairs={{2,0},{4,2},{6,4},{7,6},{5,7},{3,5},{1,3},{0,1},{10,8},{12,10},{14... | collective-permute-start | bytes 983048 | tf_op jit(solution)/shard_map/ppermute | solution.py:110
  7.0 9.3 %collective-permute-start.4 = (bf16[640,256]{1,0:T(8,128)(2,1)S(1)}, bf16[640,256]{1,0:T(8,128)(2,1)S(1)}, u32[]{:S(2)}, u32[]{:S(2)}) collective-permute-start(bf16[640,256]{1,0:T(8,128)(2,1)S(1)} %convert_element_type.69.refs_4_), channel_id=1, source_target_pairs={{0,2},{2,4},{4,6},{6,7},{7,5},{5,3},{3,1},{1,0},{8,10},{10,12},{12... | collective-permute-start | bytes 983048 | tf_op jit(solution)/shard_map/ppermute | solution.py:110
  7.8 0.7 copy-start.1
  10.6 0.7 copy-start.3
  13.6 8.0 %collective-permute-start.5 = (bf16[4,128,256]{2,1,0:T(8,128)(2,1)S(1)}, bf16[4,128,256]{2,1,0:T(8,128)(2,1)S(1)}, u32[]{:S(2)}, u32[]{:S(2)}) collective-permute-start(bf16[4,128,256]{2,1,0:T(8,128)(2,1)S(1)} %get-tuple-element.30), channel_id=1, source_target_pairs={{0,16},{8,24},{16,0},{24,8},{1,17},{9,25},{17,1},{25,9},{2,18},{10... | collective-permute-start | bytes 786440 | tf_op jit(solution)/shard_map/ppermute | solution.py:541
  16.3 8.4 %collective-permute-start.9 = (bf16[640,256]{1,0:T(8,128)(2,1)S(1)}, bf16[640,256]{1,0:T(8,128)(2,1)S(1)}, u32[]{:S(2)}, u32[]{:S(2)}) collective-permute-start(bf16[640,256]{1,0:T(8,128)(2,1)S(1)} %collective-permute-done.4.refs_1_.refs_6_), channel_id=1, source_target_pairs={{0,2},{2,4},{4,6},{6,7},{7,5},{5,3},{3,1},{1,0},{8,10},{10,12},{12... | collective-permute-start | bytes 983048 | tf_op jit(solution)/shard_map/ppermute | solution.py:110
  17.3 8.9 %collective-permute-start.7 = (bf16[640,256]{1,0:T(8,128)(2,1)S(1)}, bf16[640,256]{1,0:T(8,128)(2,1)S(1)}, u32[]{:S(2)}, u32[]{:S(2)}) collective-permute-start(bf16[640,256]{1,0:T(8,128)(2,1)S(1)} %collective-permute-done.3.refs_0_.refs_5_), channel_id=1, source_target_pairs={{2,0},{4,2},{6,4},{7,6},{5,7},{3,5},{1,3},{0,1},{10,8},{12,10},{14... | collective-permute-start | bytes 983048 | tf_op jit(solution)/shard_map/ppermute | solution.py:110
  24.8 8.5 %collective-permute-start.10 = (bf16[640,256]{1,0:T(8,128)(2,1)S(1)}, bf16[640,256]{1,0:T(8,128)(2,1)S(1)}, u32[]{:S(2)}, u32[]{:S(2)}) collective-permute-start(bf16[640,256]{1,0:T(8,128)(2,1)S(1)} %collective-permute-done.9.refs_5_), channel_id=1, source_target_pairs={{0,2},{2,4},{4,6},{6,7},{7,5},{5,3},{3,1},{1,0},{8,10},{10,12},{12... | collective-permute-start | bytes 983048 | tf_op jit(solution)/shard_map/ppermute | solution.py:110
  26.2 7.7 %collective-permute-start.8 = (bf16[640,256]{1,0:T(8,128)(2,1)S(1)}, bf16[640,256]{1,0:T(8,128)(2,1)S(1)}, u32[]{:S(2)}, u32[]{:S(2)}) collective-permute-start(bf16[640,256]{1,0:T(8,128)(2,1)S(1)} %collective-permute-done.7.refs_4_), channel_id=1, source_target_pairs={{2,0},{4,2},{6,4},{7,6},{5,7},{3,5},{1,3},{0,1},{10,8},{12,10},{14... | collective-permute-start | bytes 983048 | tf_op jit(solution)/shard_map/ppermute | solution.py:110
  26.8 6.4 %collective-permute-start.6 = (bf16[4,128,256]{2,1,0:T(8,128)(2,1)S(1)}, bf16[4,128,256]{2,1,0:T(8,128)(2,1)S(1)}, u32[]{:S(2)}, u32[]{:S(2)}) collective-permute-start(bf16[4,128,256]{2,1,0:T(8,128)(2,1)S(1)} %select_select_fusion), channel_id=1, source_target_pairs={{0,16},{8,24},{16,0},{24,8},{1,17},{9,25},{17,1},{25,9},{2,18},{10... | collective-permute-start | bytes 786440 | tf_op jit(solution)/shard_map/ppermute | solution.py:543
  33.9 2.2 %collective-permute-start.11 = (bf16[8,128,256]{2,1,0:T(8,128)(2,1)S(1)}, bf16[8,128,256]{2,1,0:T(8,128)(2,1)S(1)}, u32[]{:S(2)}, u32[]{:S(2)}) collective-permute-start(bf16[8,128,256]{2,1,0:T(8,128)(2,1)S(1)} %shard_map.80), channel_id=1, source_target_pairs={{0,8},{8,0},{16,24},{24,16},{1,9},{9,1},{17,25},{25,17},{2,10},{10... | collective-permute-start | bytes 1572872 | tf_op jit(solution)/shard_map/ppermute | solution.py:545
  34.0 7.5 %collective-permute-start.12 = (bf16[384,256]{1,0:T(8,128)(2,1)S(1)}, bf16[384,256]{1,0:T(8,128)(2,1)S(1)}, u32[]{:S(2)}, u32[]{:S(2)}) collective-permute-start(bf16[384,256]{1,0:T(8,128)(2,1)S(1)} %slice.48), channel_id=1, source_target_pairs={{0,2},{2,4},{4,6},{6,7},{7,5},{5,3},{3,1},{1,0},{8,10},{10,12},{12... | collective-permute-start | bytes 589832 | tf_op jit(solution)/shard_map/ppermute | solution.py:110
  35.8 5.7 %collective-permute-start.13 = (bf16[256,256]{1,0:T(8,128)(2,1)S(1)}, bf16[256,256]{1,0:T(8,128)(2,1)S(1)}, u32[]{:S(2)}, u32[]{:S(2)}) collective-permute-start(bf16[256,256]{1,0:T(8,128)(2,1)S(1)} %slice.49), channel_id=1, source_target_pairs={{2,0},{4,2},{6,4},{7,6},{5,7},{3,5},{1,3},{0,1},{10,8},{12,10},{14... | collective-permute-start | bytes 393224 | tf_op jit(solution)/shard_map/ppermute | solution.py:110
  42.9 5.7 %collective-permute-start.18 = (bf16[256,256]{1,0:T(8,128)(2,1)S(1)}, bf16[256,256]{1,0:T(8,128)(2,1)S(1)}, u32[]{:S(2)}, u32[]{:S(2)}) collective-permute-start(bf16[256,256]{1,0:T(8,128)(2,1)S(1)} %get-tuple-element.41), channel_id=1, source_target_pairs={{2,0},{4,2},{6,4},{7,6},{5,7},{3,5},{1,3},{0,1},{10,8},{12,10},{14... | collective-permute-start | bytes 393224 | tf_op jit(solution)/shard_map/ppermute | solution.py:143
  43.8 6.3 %collective-permute-start.14 = (bf16[384,256]{1,0:T(8,128)(2,1)S(1)}, bf16[384,256]{1,0:T(8,128)(2,1)S(1)}, u32[]{:S(2)}, u32[]{:S(2)}) collective-permute-start(bf16[384,256]{1,0:T(8,128)(2,1)S(1)} %get-tuple-element.36.refs_6_), channel_id=1, source_target_pairs={{0,2},{2,4},{4,6},{6,7},{7,5},{5,3},{3,1},{1,0},{8,10},{10,12},{12... | collective-permute-start | bytes 589832 | tf_op jit(solution)/shard_map/ppermute | solution.py:143
  48.7 8.8 %collective-permute-start.19 = (bf16[640,256]{1,0:T(8,128)(2,1)S(1)}, bf16[640,256]{1,0:T(8,128)(2,1)S(1)}, u32[]{:S(2)}, u32[]{:S(2)}) collective-permute-start(bf16[640,256]{1,0:T(8,128)(2,1)S(1)} %pad_maximum_fusion.1), channel_id=1, source_target_pairs={{2,0},{4,2},{6,4},{7,6},{5,7},{3,5},{1,3},{0,1},{10,8},{12,10},{14... | collective-permute-start | bytes 983048 | tf_op jit(solution)/shard_map/ppermute | solution.py:153
  50.2 8.3 %collective-permute-start.15 = (bf16[640,256]{1,0:T(8,128)(2,1)S(1)}, bf16[640,256]{1,0:T(8,128)(2,1)S(1)}, u32[]{:S(2)}, u32[]{:S(2)}) collective-permute-start(bf16[640,256]{1,0:T(8,128)(2,1)S(1)} %pad_maximum_fusion), channel_id=1, source_target_pairs={{0,2},{2,4},{4,6},{6,7},{7,5},{5,3},{3,1},{1,0},{8,10},{10,12},{12... | collective-permute-start | bytes 983048 | tf_op jit(solution)/shard_map/ppermute | solution.py:153
  57.6 7.9 %collective-permute-start.20 = (bf16[640,256]{1,0:T(8,128)(2,1)S(1)}, bf16[640,256]{1,0:T(8,128)(2,1)S(1)}, u32[]{:S(2)}, u32[]{:S(2)}) collective-permute-start(bf16[640,256]{1,0:T(8,128)(2,1)S(1)} %add_convert_fusion.1), channel_id=1, source_target_pairs={{2,0},{4,2},{6,4},{7,6},{5,7},{3,5},{1,3},{0,1},{10,8},{12,10},{14... | collective-permute-start | bytes 983048 | tf_op jit(solution)/shard_map/ppermute | solution.py:153
  58.6 8.9 %collective-permute-start.16 = (bf16[640,256]{1,0:T(8,128)(2,1)S(1)}, bf16[640,256]{1,0:T(8,128)(2,1)S(1)}, u32[]{:S(2)}, u32[]{:S(2)}) collective-permute-start(bf16[640,256]{1,0:T(8,128)(2,1)S(1)} %add_convert_fusion.3), channel_id=1, source_target_pairs={{0,2},{2,4},{4,6},{6,7},{7,5},{5,3},{3,1},{1,0},{8,10},{10,12},{12... | collective-permute-start | bytes 983048 | tf_op jit(solution)/shard_map/ppermute | solution.py:153
  64.2 11.0 %copy-start.5 = (f32[640,256]{1,0:T(8,128)S(1)}, f32[640,256]{1,0:T(8,128)}, u32[]{:S(2)}) copy-start(f32[640,256]{1,0:T(8,128)} %param.11) | copy-start | bytes 1966084
  65.5 42.2 %copy-start.2 = (s32[1,1,4]{2,1,0:T(1,128)S(1)}, s32[1,1,4]{2,1,0:T(1,128)}, u32[]{:S(2)}) copy-start(s32[1,1,4]{2,1,0:T(1,128)} %param.9) | copy-start | bytes 52
  65.6 7.1 %collective-permute-start.21 = (bf16[640,256]{1,0:T(8,128)(2,1)S(1)}, bf16[640,256]{1,0:T(8,128)(2,1)S(1)}, u32[]{:S(2)}, u32[]{:S(2)}) collective-permute-start(bf16[640,256]{1,0:T(8,128)(2,1)S(1)} %add_convert_fusion), channel_id=1, source_target_pairs={{2,0},{4,2},{6,4},{7,6},{5,7},{3,5},{1,3},{0,1},{10,8},{12,10},{14... | collective-permute-start | bytes 983048 | tf_op jit(solution)/shard_map/ppermute | solution.py:153
  67.6 7.6 %collective-permute-start.17 = (bf16[640,256]{1,0:T(8,128)(2,1)S(1)}, bf16[640,256]{1,0:T(8,128)(2,1)S(1)}, u32[]{:S(2)}, u32[]{:S(2)}) collective-permute-start(bf16[640,256]{1,0:T(8,128)(2,1)S(1)} %add_convert_fusion.2), channel_id=1, source_target_pairs={{0,2},{2,4},{4,6},{6,7},{7,5},{5,3},{3,1},{1,0},{8,10},{10,12},{12... | collective-permute-start | bytes 983048 | tf_op jit(solution)/shard_map/ppermute | solution.py:153
  75.5 7.5 %collective-permute-start.24 = (bf16[384,256]{1,0:T(8,128)(2,1)S(1)}, bf16[384,256]{1,0:T(8,128)(2,1)S(1)}, u32[]{:S(2)}, u32[]{:S(2)}) collective-permute-start(bf16[384,256]{1,0:T(8,128)(2,1)S(1)} %slice.50.refs_2_), channel_id=1, source_target_pairs={{0,2},{2,4},{4,6},{6,7},{7,5},{5,3},{3,1},{1,0},{8,10},{10,12},{12... | collective-permute-start | bytes 589832 | tf_op jit(solution)/shard_map/ppermute | solution.py:131
  76.0 7.6 %collective-permute-start.23 = (bf16[256,256]{1,0:T(8,128)(2,1)S(1)}, bf16[256,256]{1,0:T(8,128)(2,1)S(1)}, u32[]{:S(2)}, u32[]{:S(2)}) collective-permute-start(bf16[256,256]{1,0:T(8,128)(2,1)S(1)} %slice.51.refs_3_), channel_id=1, source_target_pairs={{2,0},{4,2},{6,4},{7,6},{5,7},{3,5},{1,3},{0,1},{10,8},{12,10},{14... | collective-permute-start | bytes 393224 | tf_op jit(solution)/shard_map/ppermute | solution.py:131
  77.6 9.3 %collective-permute-start.22 = (bf16[384,256]{1,0:T(8,128)(2,1)S(1)}, bf16[384,256]{1,0:T(8,128)(2,1)S(1)}, u32[]{:S(2)}, u32[]{:S(2)}) collective-permute-start(bf16[384,256]{1,0:T(8,128)(2,1)S(1)} %slice.50.refs_2_), channel_id=1, source_target_pairs={{2,0},{4,2},{6,4},{7,6},{5,7},{3,5},{1,3},{0,1},{10,8},{12,10},{14... | collective-permute-start | bytes 589832 | tf_op jit(solution)/shard_map/ppermute | solution.py:131
  83.0 7.7 %collective-permute-start.28 = (bf16[384,256]{1,0:T(8,128)(2,1)S(1)}, bf16[384,256]{1,0:T(8,128)(2,1)S(1)}, u32[]{:S(2)}, u32[]{:S(2)}) collective-permute-start(bf16[384,256]{1,0:T(8,128)(2,1)S(1)} %collective-permute-done.24.refs_6_), channel_id=1, source_target_pairs={{0,2},{2,4},{4,6},{6,7},{7,5},{5,3},{3,1},{1,0},{8,10},{10,12},{12... | collective-permute-start | bytes 589832 | tf_op jit(solution)/shard_map/ppermute | solution.py:131
  83.6 7.7 %collective-permute-start.27 = (bf16[256,256]{1,0:T(8,128)(2,1)S(1)}, bf16[256,256]{1,0:T(8,128)(2,1)S(1)}, u32[]{:S(2)}, u32[]{:S(2)}) collective-permute-start(bf16[256,256]{1,0:T(8,128)(2,1)S(1)} %collective-permute-done.23.refs_5_), channel_id=1, source_target_pairs={{2,0},{4,2},{6,4},{7,6},{5,7},{3,5},{1,3},{0,1},{10,8},{12,10},{14... | collective-permute-start | bytes 393224 | tf_op jit(solution)/shard_map/ppermute | solution.py:131
  85.1 8.0 %collective-permute-start.25 = (bf16[256,256]{1,0:T(8,128)(2,1)S(1)}, bf16[256,256]{1,0:T(8,128)(2,1)S(1)}, u32[]{:S(2)}, u32[]{:S(2)}) collective-permute-start(bf16[256,256]{1,0:T(8,128)(2,1)S(1)} %slice.51.refs_3_), channel_id=1, source_target_pairs={{0,2},{2,4},{4,6},{6,7},{7,5},{5,3},{3,1},{1,0},{8,10},{10,12},{12... | collective-permute-start | bytes 393224 | tf_op jit(solution)/shard_map/ppermute | solution.py:131
  87.0 11.8 %collective-permute-start.26 = (bf16[384,256]{1,0:T(8,128)(2,1)S(1)}, bf16[384,256]{1,0:T(8,128)(2,1)S(1)}, u32[]{:S(2)}, u32[]{:S(2)}) collective-permute-start(bf16[384,256]{1,0:T(8,128)(2,1)S(1)} %collective-permute-done.22.refs_4_), channel_id=1, source_target_pairs={{2,0},{4,2},{6,4},{7,6},{5,7},{3,5},{1,3},{0,1},{10,8},{12,10},{14... | collective-permute-start | bytes 589832 | tf_op jit(solution)/shard_map/ppermute | solution.py:131
  90.7 9.8 %collective-permute-start.32 = (bf16[384,256]{1,0:T(8,128)(2,1)S(1)}, bf16[384,256]{1,0:T(8,128)(2,1)S(1)}, u32[]{:S(2)}, u32[]{:S(2)}) collective-permute-start(bf16[384,256]{1,0:T(8,128)(2,1)S(1)} %collective-permute-done.28.refs_10_), channel_id=1, source_target_pairs={{0,2},{2,4},{4,6},{6,7},{7,5},{5,3},{3,1},{1,0},{8,10},{10,12},{12... | collective-permute-start | bytes 589832 | tf_op jit(solution)/shard_map/ppermute | solution.py:131
  91.4 6.2 %collective-permute-start.31 = (bf16[256,256]{1,0:T(8,128)(2,1)S(1)}, bf16[256,256]{1,0:T(8,128)(2,1)S(1)}, u32[]{:S(2)}, u32[]{:S(2)}) collective-permute-start(bf16[256,256]{1,0:T(8,128)(2,1)S(1)} %collective-permute-done.27.refs_9_), channel_id=1, source_target_pairs={{2,0},{4,2},{6,4},{7,6},{5,7},{3,5},{1,3},{0,1},{10,8},{12,10},{14... | collective-permute-start | bytes 393224 | tf_op jit(solution)/shard_map/ppermute | solution.py:131
  93.1 7.9 %collective-permute-start.29 = (bf16[256,256]{1,0:T(8,128)(2,1)S(1)}, bf16[256,256]{1,0:T(8,128)(2,1)S(1)}, u32[]{:S(2)}, u32[]{:S(2)}) collective-permute-start(bf16[256,256]{1,0:T(8,128)(2,1)S(1)} %collective-permute-done.25.refs_7_), channel_id=1, source_target_pairs={{0,2},{2,4},{4,6},{6,7},{7,5},{5,3},{3,1},{1,0},{8,10},{10,12},{12... | collective-permute-start | bytes 393224 | tf_op jit(solution)/shard_map/ppermute | solution.py:131
  97.5 5.0 %collective-permute-start.35 = (bf16[256,256]{1,0:T(8,128)(2,1)S(1)}, bf16[256,256]{1,0:T(8,128)(2,1)S(1)}, u32[]{:S(2)}, u32[]{:S(2)}) collective-permute-start(bf16[256,256]{1,0:T(8,128)(2,1)S(1)} %collective-permute-done.31.refs_13_), channel_id=1, source_target_pairs={{2,0},{4,2},{6,4},{7,6},{5,7},{3,5},{1,3},{0,1},{10,8},{12,10},{14... | collective-permute-start | bytes 393224 | tf_op jit(solution)/shard_map/ppermute | solution.py:131
  98.8 8.9 %collective-permute-start.30 = (bf16[384,256]{1,0:T(8,128)(2,1)S(1)}, bf16[384,256]{1,0:T(8,128)(2,1)S(1)}, u32[]{:S(2)}, u32[]{:S(2)}) collective-permute-start(bf16[384,256]{1,0:T(8,128)(2,1)S(1)} %collective-permute-done.26.refs_8_), channel_id=1, source_target_pairs={{2,0},{4,2},{6,4},{7,6},{5,7},{3,5},{1,3},{0,1},{10,8},{12,10},{14... | collective-permute-start | bytes 589832 | tf_op jit(solution)/shard_map/ppermute | solution.py:131
  100.5 7.1 %collective-permute-start.34 = (bf16[384,256]{1,0:T(8,128)(2,1)S(1)}, bf16[384,256]{1,0:T(8,128)(2,1)S(1)}, u32[]{:S(2)}, u32[]{:S(2)}) collective-permute-start(bf16[384,256]{1,0:T(8,128)(2,1)S(1)} %collective-permute-done.32.refs_14_), channel_id=1, source_target_pairs={{0,2},{2,4},{4,6},{6,7},{7,5},{5,3},{3,1},{1,0},{8,10},{10,12},{12... | collective-permute-start | bytes 589832 | tf_op jit(solution)/shard_map/ppermute | solution.py:131
  101.0 6.6 %collective-permute-start.33 = (bf16[256,256]{1,0:T(8,128)(2,1)S(1)}, bf16[256,256]{1,0:T(8,128)(2,1)S(1)}, u32[]{:S(2)}, u32[]{:S(2)}) collective-permute-start(bf16[256,256]{1,0:T(8,128)(2,1)S(1)} %collective-permute-done.29.refs_11_), channel_id=1, source_target_pairs={{0,2},{2,4},{4,6},{6,7},{7,5},{5,3},{3,1},{1,0},{8,10},{10,12},{12... | collective-permute-start | bytes 393224 | tf_op jit(solution)/shard_map/ppermute | solution.py:131
  112.4 8.8 %collective-permute-start.37 = (bf16[4,128,256]{2,1,0:T(8,128)(2,1)S(1)}, bf16[4,128,256]{2,1,0:T(8,128)(2,1)S(1)}, u32[]{:S(2)}, u32[]{:S(2)}) collective-permute-start(bf16[4,128,256]{2,1,0:T(8,128)(2,1)S(1)} %get-tuple-element.47), channel_id=1, source_target_pairs={{0,16},{8,24},{16,0},{24,8},{1,17},{9,25},{17,1},{25,9},{2,18},{10... | collective-permute-start | bytes 786440 | tf_op jit(solution)/shard_map/ppermute | solution.py:568
  112.5 9.5 %collective-permute-start.38 = (bf16[4,128,256]{2,1,0:T(8,128)(2,1)S(1)}, bf16[4,128,256]{2,1,0:T(8,128)(2,1)S(1)}, u32[]{:S(2)}, u32[]{:S(2)}) collective-permute-start(bf16[4,128,256]{2,1,0:T(8,128)(2,1)S(1)} %get-tuple-element.48), channel_id=1, source_target_pairs={{0,24},{8,16},{16,8},{24,0},{1,25},{9,17},{17,9},{25,1},{2,26},{10... | collective-permute-start | bytes 786440 | tf_op jit(solution)/shard_map/ppermute | solution.py:568
  113.9 4.3 %copy-start = (f32[2048,256]{1,0:T(8,128)S(1)}, f32[2048,256]{1,0:T(8,128)}, u32[]{:S(2)}) copy-start(f32[2048,256]{1,0:T(8,128)} %param.10) | copy-start | bytes 6291460
  113.9 4.3 %copy-start.4 = (s32[16]{0:T(128)S(1)}, s32[16]{0:T(128)}, u32[]{:S(2)}) copy-start(s32[16]{0:T(128)} %refs_0_.3) | copy-start | bytes 196
  113.9 4.2 %collective-permute-start.36 = (bf16[4,128,256]{2,1,0:T(8,128)(2,1)S(1)}, bf16[4,128,256]{2,1,0:T(8,128)(2,1)S(1)}, u32[]{:S(2)}, u32[]{:S(2)}) collective-permute-start(bf16[4,128,256]{2,1,0:T(8,128)(2,1)S(1)} %get-tuple-element.45), channel_id=1, source_target_pairs={{0,8},{8,0},{16,24},{24,16},{1,9},{9,1},{17,25},{25,17},{2,10},{10... | collective-permute-start | bytes 786440 | tf_op jit(solution)/shard_map/ppermute | solution.py:568

commit v6 on v5

--- a/solution.py
+++ b/solution.py
@@ -401,10 +401,13 @@
 
 
 def second_kernel(cfg, row_ref, live_ref, ids_ref, observed, *refs):
-    ks, sku_starts, per_owner, kinds, block = cfg
-    skus, pieces = refs[: len(ks)], refs[len(ks) : -1 - len(ks)]
-    outs, table = refs[-1 - len(ks) : -1], refs[-1]
-    load_table(table, pieces)
+    ks, sku_starts, piece_count, per_owner, kinds, block = cfg
+    skus, pieces = refs[: len(ks)], refs[len(ks) : len(ks) + piece_count]
+    if piece_count > 1:
+        *outs, table = refs[-1 - len(ks) :]
+        load_table(table, pieces)
+    else:
+        outs, (table,) = refs[-len(ks) :], pieces
     row = row_ref[0]
     for k, sku_ref, start, out in zip(ks, skus, sku_starts, outs):
         out[...] = jnp.zeros_like(out)
@@ -428,18 +431,22 @@
             ).astype(jnp.bfloat16)
 
 
-def second_pass(ks, row, live, ids, observed, skus, pieces, plan, per_owner):
+def second_pass(ks, row, live, ids, observed, skus, pieces, plan, per_owner, marks):
     kept, sku_starts = zip(*[skus[k] for k in ks])
     kinds, block, rank = observed.shape[1], plan.block, kept[0].shape[2]
     shape = (per_owner, block, rank)
-    inputs = [observed, *kept, *[piece for d in plan.order for piece in pieces[d]]]
-    return pl.pallas_call(
-        functools.partial(second_kernel, (ks, sku_starts, per_owner, kinds, block)),
-        out_shape=[VMEM(shape, jnp.bfloat16)] * len(ks),
+    given = [pieces]
+    out_shape = [VMEM(shape, jnp.bfloat16)] * len(ks)
+    if isinstance(pieces, dict):
+        given = [piece for d in plan.order for piece in pieces[d]]
+        out_shape.append(VMEM((plan.count * plan.rows, rank), jnp.bfloat16))
+    inputs = [observed, *kept, *given, *marks]
+    return pl.pallas_call(
+        functools.partial(second_kernel, (ks, sku_starts, len(given), per_owner, kinds, block)),
+        out_shape=out_shape,
         in_specs=[spec(SMEM)] * 3 + [spec(VMEM)] * len(inputs),
-        out_specs=[spec(VMEM)] * len(ks),
-        scratch_shapes=[VMEM((plan.count * plan.rows, rank), jnp.bfloat16)],
-        compiler_params=params(16),
+        out_specs=[spec(VMEM)] * len(out_shape),
+        compiler_params=params(8),
         cost_estimate=cost(len(ks) * per_owner * kinds, block, rank),
     )(row, live, ids, *map(near, inputs))
 
@@ -484,32 +491,22 @@
     )(row, *ids, sku, *map(near, terms))
 
 
-def finish_kernel(count, per_owner, row_ref, *refs):
-    ids, sku, terms = refs[:count], refs[count], refs[count + 1 : 2 * count + 1]
-    out, held, sems = refs[-3:]
-    for block_ids in ids:
-        for i in range(per_owner):
-            block = block_ids[row_ref[0] * per_owner + i]
-            held[block] = sku[block]
-    blocks = take_terms(held, ids, terms, row_ref[0], per_owner)
+def finish_kernel(per_owner, row_ref, ids, term, *refs):
+    held, out, sems = refs[-3:]
+    blocks = take_terms(held, [ids], [term], row_ref[0], per_owner)
     copy_out(held, out, blocks, sems)
 
 
-def finish_step(row, ids, held, out, terms, per_owner):
-    return pl.pallas_call(
-        functools.partial(finish_kernel, len(ids), per_owner),
-        out_shape=pltpu.HBM(out.shape, jnp.float32),
-        in_specs=[spec(SMEM)] * (len(ids) + 1)
-        + [spec(VMEM)] * (1 + len(ids))
-        + [spec(pltpu.HBM)],
-        out_specs=spec(pltpu.HBM),
-        scratch_shapes=[
-            VMEM(out.shape, jnp.float32),
-            pltpu.SemaphoreType.DMA((len(ids) * per_owner,)),
-        ],
-        input_output_aliases={2 + 2 * len(ids): 0},
-        compiler_params=params(4),
-    )(row, *ids, near(held), *map(near, terms), away(out))
+def finish_step(row, ids, held, out, term, per_owner):
+    return pl.pallas_call(
+        functools.partial(finish_kernel, per_owner),
+        out_shape=[VMEM(held.shape, jnp.float32), pltpu.HBM(out.shape, jnp.float32)],
+        in_specs=[spec(SMEM)] * 2 + [spec(VMEM)] * 2 + [spec(pltpu.HBM)],
+        out_specs=[spec(VMEM), spec(pltpu.HBM)],
+        scratch_shapes=[pltpu.SemaphoreType.DMA((per_owner,))],
+        input_output_aliases={3: 0, 4: 1},
+        compiler_params=params(1),
+    )(row, ids, near(term), near(held), away(out))
 
 
 def local(observed, sku_ids, store_ids, live_slot_counts, sku_factors, store_factors):
@@ -561,13 +558,19 @@
     new_low = step_of(own_grad).astype(jnp.bfloat16)
     new_pieces = (gather_split if split_gather else gather_ring)(new_low, plan)
 
-    terms = [None] * row_count
-    for ks in (list(range(2, row_count)), [1, 0]):
-        out = second_pass(ks, row_vec, live, ids, observed, skus, new_pieces, plan, per_owner)
+    terms, table, marks = [None] * row_count, new_pieces, []
+    for ks in [[k] for k in range(row_count - 1, 1, -1)] + [[1, 0]]:
+        out = second_pass(
+            ks, row_vec, live, ids, observed, skus, table, plan, per_owner, marks
+        )
+        marks = out[:1]
+        if len(out) > len(ks):
+            table = out[-1]
         for k, term in zip(ks, out):
             terms[k] = lax.ppermute(term, "row", swaps[k]) if k else term
     held, new_sku = base_step(row_vec, asked[:2], sku, terms[:2], per_owner)
-    new_sku = finish_step(row_vec, asked[2:], held, new_sku, terms[2:], per_owner)
+    for k in range(row_count - 1, 1, -1):
+        held, new_sku = finish_step(row_vec, asked[k], held, new_sku, terms[k], per_owner)
     new_store = step_of(after(own_grad, new_pieces[plan.far][1]))
     return new_sku.reshape(sku_factors.shape), new_store
 

time: 125 us -> 124 us (level); the launches traced: 124 us -> 125 us
  waiting for transfers between devices: 50.2 us -> 43.3 us
  Pallas kernels: 26.8 us -> 30.8 us
  starting transfers between devices: 40.7 us -> 44.2 us
    ppermute x6, waiting for transfers between devices: 13.2 us -> 9.76 us  [scatter_ring(): moved[way] = lax.ppermute(value, 'col', steps[way])]
    pallas_call x3 -> x5, Pallas kernels: 7.82 us -> 10.3 us  [the longest x3 7.48 us: second_pass(): pl.pallas_call(functools.partial(second_kernel, (ks, sku_starts, len(give...]
    ppermute x6, starting transfers between devices: 5.38 us -> 7.6 us  [scatter_ring(): moved[way] = lax.ppermute(value, 'col', steps[way])]
    ppermute x14, waiting for transfers between devices: 17.3 us -> 15.3 us  [gather_split(): moved[way, h] = lax.ppermute(moved[way, h], 'col', steps[way])]
    ppermute x8, waiting for transfers between devices: 5.62 us -> 3.91 us  [gather_ring(): moved = [lax.ppermute(moved[way], 'col', steps[way]) for way in (0, 1)]]
    ppermute x14, starting transfers between devices: 14.8 us -> 16.2 us  [gather_split(): moved[way, h] = lax.ppermute(moved[way, h], 'col', steps[way])]
    pallas_call x4, Pallas kernels: 10 us -> 11.3 us  [first_pass(): pl.pallas_call(functools.partial(first_kernel, cfg), out_shape=[VMEM((hei...]
  transfers between devices with their start and end apart: 39 -> 39, of which waited for: 25 -> 20; matrix products, arithmetic and copies ran while one was open for 3% -> 3% of each run, Pallas kernels for 15% -> 21%
where the time goes in v6:
time: 124 us; the launch traced here: 125 us
  starting transfers between devices  44.2 us (36%)
  waiting for transfers between devices  43.3 us (35%)
  Pallas kernels  30.8 us (25%)
  other arithmetic  3.71 us (3%)
  local copies, waits for them, and re-layouts  1.6 us (1%)
    ppermute x14, starting transfers between devices, gather_split(): moved[way, h] = lax.ppermute(moved[way, h], 'col', steps[way])  16.2 us
    ppermute x14, waiting for transfers between devices, gather_split(): moved[way, h] = lax.ppermute(moved[way, h], 'col', steps[way])  15.3 us
    pallas_call x4, Pallas kernels, first_pass(): pl.pallas_call(functools.partial(first_kernel, cfg), out_shape=[VMEM((hei...  11.3 us
    ppermute x6, waiting for transfers between devices, scatter_ring(): moved[way] = lax.ppermute(value, 'col', steps[way])  9.76 us
    ppermute x8, starting transfers between devices, gather_ring(): moved = [lax.ppermute(moved[way], 'col', steps[way]) for way in (0, 1)]  8.41 us
    ppermute x6, starting transfers between devices, scatter_ring(): moved[way] = lax.ppermute(value, 'col', steps[way])  7.6 us
    pallas_call x3, Pallas kernels, second_pass(): pl.pallas_call(functools.partial(second_kernel, (ks, sku_starts, len(give...  7.48 us
    ppermute x1, waiting for transfers between devices, local(): through.append(lax.ppermute(onward, 'row', swaps[2 * x]))  5.12 us
  transfers between devices with their start and end apart: 39, of which 20 were waited for; matrix products, arithmetic and copies ran while one was open for 3% of the time, Pallas kernels for 21%

profile of v6, /device:TPU:0, one launch (start us, length us, event | category | flops | bytes accessed | tf_op | source)
XLA Modules:
  0.0 124.5 jit_solution(13201783804663840072)
XLA Ops:
  0.6 2.4 %collective-permute-start.4 = (s32[16]{0:T(128)}, s32[16]{0:T(128)S(1)}, u32[]{:S(2)}, u32[]{:S(2)}) collective-permute-start(s32[16]{0:T(128)} %refs_0_.3), channel_id=1, source_target_pairs={{0,24},{8,16},{16,8},{24,0},{1,25},{9,17},{17,9},{25,1},{2,26},{10... | collective-permute-start | bytes 200 | tf_op jit(solution)/shard_map/ppermute | solution.py:523
  3.1 0.7 collective-permute-start.3
  3.8 1.1 convert_element_type.69.refs_4_
  4.9 2.1 %collective-permute-start.2 = (bf16[640,256]{1,0:T(8,128)(2,1)S(1)}, bf16[640,256]{1,0:T(8,128)(2,1)S(1)}, u32[]{:S(2)}, u32[]{:S(2)}) collective-permute-start(bf16[640,256]{1,0:T(8,128)(2,1)S(1)} %convert_element_type.69.refs_4_), channel_id=1, source_target_pairs={{0,2},{2,4},{4,6},{6,7},{7,5},{5,3},{3,1},{1,0},{8,10},{10,12},{12... | collective-permute-start | bytes 983048 | tf_op jit(solution)/shard_map/ppermute | solution.py:110
  7.0 0.7 fusion.5.ids_ref
  7.8 0.6 copy-done.1
  8.4 2.2 %shard_map.78 = (s32[544]{0:T(1024)S(1)}, s32[4]{0:T(128)S(1)}, f32[8,256]{1,0:T(8,128)S(1)}) custom-call(s32[1]{0:T(128)} %bitcast.row_ref, s32[4]{0:T(128)S(1)} %bitcast.28, s32[8,16]{1,0:T(8,128)S(1)} %fusion.5.ids_ref), custom_call_target="tpu_custom_call" | custom-call | tf_op jit(solution)/shard_map/pallas_call | solution.py:275
  10.7 0.6 copy-done.3
  11.4 2.3 %shard_map.79 = (bf16[4,128,256]{2,1,0:T(8,128)(2,1)S(1)}, bf16[4,128,256]{2,1,0:T(8,128)(2,1)S(1)}, bf16[4,128,256]{2,1,0:T(8,128)(2,1)S(1)}, bf16[4,128,256]{2,1,0:T(8,128)(2,1)S(1)}) custom-call(s32[1]{0:T(128)} %bitcast.row_ref, s32[16]{0:T(128)S(1)} %copy-done.3, s32[16]{0:T(128)S(1)} %collective-permute-done.3.refs_1_, ...), custom_call_target="tpu_custom_call" | custom-call | tf_op jit(solution)/shard_map/pallas_call | solution.py:207
  13.7 1.7 %collective-permute-start.5 = (bf16[4,128,256]{2,1,0:T(8,128)(2,1)S(1)}, bf16[4,128,256]{2,1,0:T(8,128)(2,1)S(1)}, u32[]{:S(2)}, u32[]{:S(2)}) collective-permute-start(bf16[4,128,256]{2,1,0:T(8,128)(2,1)S(1)} %get-tuple-element.31), channel_id=1, source_target_pairs={{0,16},{8,24},{16,0},{24,8},{1,17},{9,25},{17,1},{25,9},{2,18},{10... | collective-permute-start | bytes 786440 | tf_op jit(solution)/shard_map/ppermute | solution.py:538
  15.4 2.1 %collective-permute-start.9 = (bf16[640,256]{1,0:T(8,128)(2,1)S(1)}, bf16[640,256]{1,0:T(8,128)(2,1)S(1)}, u32[]{:S(2)}, u32[]{:S(2)}) collective-permute-start(bf16[640,256]{1,0:T(8,128)(2,1)S(1)} %collective-permute-done.2.refs_1_.refs_6_), channel_id=1, source_target_pairs={{0,2},{2,4},{4,6},{6,7},{7,5},{5,3},{3,1},{1,0},{8,10},{10,12},{12... | collective-permute-start | bytes 983048 | tf_op jit(solution)/shard_map/ppermute | solution.py:110
  17.5 3.9 %collective-permute-done.5.refs_2_.refs_0_ = bf16[4,128,256]{2,1,0:T(8,128)(2,1)S(1)} collective-permute-done((bf16[4,128,256]{2,1,0:T(8,128)(2,1)S(1)}, bf16[4,128,256]{2,1,0:T(8,128)(2,1)S(1)}, u32[]{:S(2)}, u32[]{:S(2)}) %collective-permute-start.5) | collective-permute-done | bytes 262176 | tf_op jit(solution)/shard_map/ppermute | solution.py:538
  21.4 2.3 %shard_map.77 = (bf16[16,8,128,128]{3,2,1,0:T(8,128)(2,1)S(1)}, f32[8,256]{1,0:T(8,128)S(1)}) custom-call(bf16[16,8,128,128]{3,2,1,0:T(8,128)(2,1)} %observed.1, bf16[640,256]{1,0:T(8,128)(2,1)S(1)} %collective-permute-done.1.refs_0_.refs_5_, bf16[640,256]{1,0:T(8,128)(2,1)S(1)} %collective-permute-done.2.refs_1_.refs_6_), custom_call_target="tpu_custom_call" | custom-call | tf_op jit(solution)/shard_map/pallas_call | solution.py:302
  23.7 0.3 collective-permute-done.9.refs_5_
  24.0 1.9 %collective-permute-start.10 = (bf16[640,256]{1,0:T(8,128)(2,1)S(1)}, bf16[640,256]{1,0:T(8,128)(2,1)S(1)}, u32[]{:S(2)}, u32[]{:S(2)}) collective-permute-start(bf16[640,256]{1,0:T(8,128)(2,1)S(1)} %collective-permute-done.9.refs_5_), channel_id=1, source_target_pairs={{0,2},{2,4},{4,6},{6,7},{7,5},{5,3},{3,1},{1,0},{8,10},{10,12},{12... | collective-permute-start | bytes 983048 | tf_op jit(solution)/shard_map/ppermute | solution.py:110
  26.1 1.3 %collective-permute-start.6 = (bf16[4,128,256]{2,1,0:T(8,128)(2,1)S(1)}, bf16[4,128,256]{2,1,0:T(8,128)(2,1)S(1)}, u32[]{:S(2)}, u32[]{:S(2)}) collective-permute-start(bf16[4,128,256]{2,1,0:T(8,128)(2,1)S(1)} %select_select_fusion), channel_id=1, source_target_pairs={{0,16},{8,24},{16,0},{24,8},{1,17},{9,25},{17,1},{25,9},{2,18},{10... | collective-permute-start | bytes 786440 | tf_op jit(solution)/shard_map/ppermute | solution.py:540
  27.4 5.1 %collective-permute-done.6.refs_0_ = bf16[4,128,256]{2,1,0:T(8,128)(2,1)S(1)} collective-permute-done((bf16[4,128,256]{2,1,0:T(8,128)(2,1)S(1)}, bf16[4,128,256]{2,1,0:T(8,128)(2,1)S(1)}, u32[]{:S(2)}, u32[]{:S(2)}) %collective-permute-start.6) | collective-permute-done | bytes 262176 | tf_op jit(solution)/shard_map/ppermute | solution.py:540
  32.5 1.3 %collective-permute-done.8.refs_1_.refs_4_ = bf16[640,256]{1,0:T(8,128)(2,1)S(1)} collective-permute-done((bf16[640,256]{1,0:T(8,128)(2,1)S(1)}, bf16[640,256]{1,0:T(8,128)(2,1)S(1)}, u32[]{:S(2)}, u32[]{:S(2)}) %collective-permute-start.8) | collective-permute-done | bytes 327712 | tf_op jit(solution)/shard_map/ppermute | solution.py:110
  33.9 1.2 collective-permute-start.12
  35.2 0.9 collective-permute-start.13
  36.1 2.8 %shard_map.81 = (bf16[640,256]{1,0:T(8,128)(2,1)S(1)}, bf16[640,256]{1,0:T(8,128)(2,1)S(1)}) custom-call(s32[544]{0:T(1024)S(1)} %get-tuple-element.35.pairs_ref, s32[4]{0:T(128)S(1)} %get-tuple-element.36.counts_ref, bf16[16,8,128,128]{3,2,1,0:T(8,128)(2,1)S(1)} %get-tuple-element.29.observed, bf16[4,128,256]{2,1,0:T(8,128)(2,1)S(1)} %get-tuple-element.37.refs_0_.refs_1_, ...), custom_call_target="tpu_custom_call" | custom-call | flops 570425344 | bytes 8912896 | tf_op jit(solution)/shard_map/pallas_call | solution.py:386
  38.9 1.9 %collective-permute-done.13.refs_5_ = bf16[256,256]{1,0:T(8,128)(2,1)S(1)} collective-permute-done((bf16[256,256]{1,0:T(8,128)(2,1)S(1)}, bf16[256,256]{1,0:T(8,128)(2,1)S(1)}, u32[]{:S(2)}, u32[]{:S(2)}) %collective-permute-start.13) | collective-permute-done | bytes 131104 | tf_op jit(solution)/shard_map/ppermute | solution.py:110
  40.8 0.5 collective-permute-done.12.refs_4_
  41.3 1.4 %shard_map.82 = (bf16[384,256]{1,0:T(8,128)(2,1)S(1)}, bf16[256,256]{1,0:T(8,128)(2,1)S(1)}) custom-call(s32[544]{0:T(1024)S(1)} %get-tuple-element.35.pairs_ref, s32[4]{0:T(128)S(1)} %get-tuple-element.36.counts_ref, bf16[16,8,128,128]{3,2,1,0:T(8,128)(2,1)S(1)} %get-tuple-element.29.observed, bf16[4,128,256]{2,1,0:T(8,128)(2,1)S(1)} %get-tuple-element.37.refs_0_.refs_1_, ...), custom_call_target="tpu_custom_call" | custom-call | flops 285212672 | bytes 4456448 | tf_op jit(solution)/shard_map/pallas_call | solution.py:386
  42.7 1.1 collective-permute-start.18
  43.9 1.0 collective-permute-start.14
  44.9 3.8 %collective-permute-done.18 = bf16[256,256]{1,0:T(8,128)(2,1)S(1)} collective-permute-done((bf16[256,256]{1,0:T(8,128)(2,1)S(1)}, bf16[256,256]{1,0:T(8,128)(2,1)S(1)}, u32[]{:S(2)}, u32[]{:S(2)}) %collective-permute-start.18) | collective-permute-done | bytes 131104 | tf_op jit(solution)/shard_map/ppermute | solution.py:143
  48.7 0.3 collective-permute-start.19
  49.0 1.1 collective-permute-done.14
  50.2 1.8 %collective-permute-start.15 = (bf16[640,256]{1,0:T(8,128)(2,1)S(1)}, bf16[640,256]{1,0:T(8,128)(2,1)S(1)}, u32[]{:S(2)}, u32[]{:S(2)}) collective-permute-start(bf16[640,256]{1,0:T(8,128)(2,1)S(1)} %pad_maximum_fusion), channel_id=1, source_target_pairs={{0,2},{2,4},{4,6},{6,7},{7,5},{5,3},{3,1},{1,0},{8,10},{10,12},{12... | collective-permute-start | bytes 983048 | tf_op jit(solution)/shard_map/ppermute | solution.py:153
  52.0 2.8 %shard_map.83 = (bf16[640,256]{1,0:T(8,128)(2,1)S(1)}, bf16[640,256]{1,0:T(8,128)(2,1)S(1)}) custom-call(s32[544]{0:T(1024)S(1)} %get-tuple-element.35.pairs_ref, s32[4]{0:T(128)S(1)} %get-tuple-element.36.counts_ref, bf16[16,8,128,128]{3,2,1,0:T(8,128)(2,1)S(1)} %get-tuple-element.29.observed, bf16[4,128,256]{2,1,0:T(8,128)(2,1)S(1)} %get-tuple-element.37.refs_0_.refs_1_, ...), custom_call_target="tpu_custom_call" | custom-call | flops 570425344 | bytes 8912896 | tf_op jit(solution)/shard_map/pallas_call | solution.py:386
  54.8 3.2 %collective-permute-done.19 = bf16[640,256]{1,0:T(8,128)(2,1)S(1)} collective-permute-done((bf16[640,256]{1,0:T(8,128)(2,1)S(1)}, bf16[640,256]{1,0:T(8,128)(2,1)S(1)}, u32[]{:S(2)}, u32[]{:S(2)}) %collective-permute-start.19) | collective-permute-done | bytes 327712 | tf_op jit(solution)/shard_map/ppermute | solution.py:153
  58.1 0.3 collective-permute-start.20
  58.6 2.5 %collective-permute-start.16 = (bf16[640,256]{1,0:T(8,128)(2,1)S(1)}, bf16[640,256]{1,0:T(8,128)(2,1)S(1)}, u32[]{:S(2)}, u32[]{:S(2)}) collective-permute-start(bf16[640,256]{1,0:T(8,128)(2,1)S(1)} %add_convert_fusion.3), channel_id=1, source_target_pairs={{0,2},{2,4},{4,6},{6,7},{7,5},{5,3},{3,1},{1,0},{8,10},{10,12},{12... | collective-permute-start | bytes 983048 | tf_op jit(solution)/shard_map/ppermute | solution.py:153
  61.1 4.3 %shard_map.84 = (bf16[640,256]{1,0:T(8,128)(2,1)S(1)}, bf16[640,256]{1,0:T(8,128)(2,1)S(1)}, bf16[640,256]{1,0:T(8,128)(2,1)S(1)}) custom-call(s32[544]{0:T(1024)S(1)} %get-tuple-element.35.pairs_ref, s32[4]{0:T(128)S(1)} %get-tuple-element.36.counts_ref, bf16[16,8,128,128]{3,2,1,0:T(8,128)(2,1)S(1)} %get-tuple-element.29.observed, ...), custom_call_target="tpu_custom_call" | custom-call | flops 855638016 | bytes 13369344 | tf_op jit(solution)/shard_map/pallas_call | solution.py:386
  65.4 1.2 collective-permute-done.20
  66.7 0.4 collective-permute-start.21
  67.1 2.2 %collective-permute-start.17 = (bf16[640,256]{1,0:T(8,128)(2,1)S(1)}, bf16[640,256]{1,0:T(8,128)(2,1)S(1)}, u32[]{:S(2)}, u32[]{:S(2)}) collective-permute-start(bf16[640,256]{1,0:T(8,128)(2,1)S(1)} %add_convert_fusion.2), channel_id=1, source_target_pairs={{0,2},{2,4},{4,6},{6,7},{7,5},{5,3},{3,1},{1,0},{8,10},{10,12},{12... | collective-permute-start | bytes 983048 | tf_op jit(solution)/shard_map/ppermute | solution.py:153
  69.3 4.9 %collective-permute-done.21 = bf16[640,256]{1,0:T(8,128)(2,1)S(1)} collective-permute-done((bf16[640,256]{1,0:T(8,128)(2,1)S(1)}, bf16[640,256]{1,0:T(8,128)(2,1)S(1)}, u32[]{:S(2)}, u32[]{:S(2)}) %collective-permute-start.21) | collective-permute-done | bytes 327712 | tf_op jit(solution)/shard_map/ppermute | solution.py:153
  74.2 0.5 collective-permute-done.17
  74.9 2.3 %collective-permute-start.24 = (bf16[384,256]{1,0:T(8,128)(2,1)S(1)}, bf16[384,256]{1,0:T(8,128)(2,1)S(1)}, u32[]{:S(2)}, u32[]{:S(2)}) collective-permute-start(bf16[384,256]{1,0:T(8,128)(2,1)S(1)} %slice.50.refs_1_), channel_id=1, source_target_pairs={{0,2},{2,4},{4,6},{6,7},{7,5},{5,3},{3,1},{1,0},{8,10},{10,12},{12... | collective-permute-start | bytes 589832 | tf_op jit(solution)/shard_map/ppermute | solution.py:131
  77.3 1.0 collective-permute-start.22
  78.3 4.3 %collective-permute-done.24.refs_5_ = bf16[384,256]{1,0:T(8,128)(2,1)S(1)} collective-permute-done((bf16[384,256]{1,0:T(8,128)(2,1)S(1)}, bf16[384,256]{1,0:T(8,128)(2,1)S(1)}, u32[]{:S(2)}, u32[]{:S(2)}) %collective-permute-start.24) | collective-permute-done | bytes 196640 | tf_op jit(solution)/shard_map/ppermute | solution.py:131
  82.5 2.2 %collective-permute-start.28 = (bf16[384,256]{1,0:T(8,128)(2,1)S(1)}, bf16[384,256]{1,0:T(8,128)(2,1)S(1)}, u32[]{:S(2)}, u32[]{:S(2)}) collective-permute-start(bf16[384,256]{1,0:T(8,128)(2,1)S(1)} %collective-permute-done.24.refs_5_), channel_id=1, source_target_pairs={{0,2},{2,4},{4,6},{6,7},{7,5},{5,3},{3,1},{1,0},{8,10},{10,12},{12... | collective-permute-start | bytes 589832 | tf_op jit(solution)/shard_map/ppermute | solution.py:131
  84.8 2.0 %collective-permute-start.25 = (bf16[256,256]{1,0:T(8,128)(2,1)S(1)}, bf16[256,256]{1,0:T(8,128)(2,1)S(1)}, u32[]{:S(2)}, u32[]{:S(2)}) collective-permute-start(bf16[256,256]{1,0:T(8,128)(2,1)S(1)} %slice.51.refs_2_), channel_id=1, source_target_pairs={{0,2},{2,4},{4,6},{6,7},{7,5},{5,3},{3,1},{1,0},{8,10},{10,12},{12... | collective-permute-start | bytes 393224 | tf_op jit(solution)/shard_map/ppermute | solution.py:131
  86.8 1.1 collective-permute-done.22.refs_3_
  87.9 2.4 %collective-permute-done.28.refs_9_ = bf16[384,256]{1,0:T(8,128)(2,1)S(1)} collective-permute-done((bf16[384,256]{1,0:T(8,128)(2,1)S(1)}, bf16[384,256]{1,0:T(8,128)(2,1)S(1)}, u32[]{:S(2)}, u32[]{:S(2)}) %collective-permute-start.28) | collective-permute-done | bytes 196640 | tf_op jit(solution)/shard_map/ppermute | solution.py:131
  90.2 2.2 %collective-permute-start.32 = (bf16[384,256]{1,0:T(8,128)(2,1)S(1)}, bf16[384,256]{1,0:T(8,128)(2,1)S(1)}, u32[]{:S(2)}, u32[]{:S(2)}) collective-permute-start(bf16[384,256]{1,0:T(8,128)(2,1)S(1)} %collective-permute-done.28.refs_9_), channel_id=1, source_target_pairs={{0,2},{2,4},{4,6},{6,7},{7,5},{5,3},{3,1},{1,0},{8,10},{10,12},{12... | collective-permute-start | bytes 589832 | tf_op jit(solution)/shard_map/ppermute | solution.py:131
  92.5 2.4 %collective-permute-start.29 = (bf16[256,256]{1,0:T(8,128)(2,1)S(1)}, bf16[256,256]{1,0:T(8,128)(2,1)S(1)}, u32[]{:S(2)}, u32[]{:S(2)}) collective-permute-start(bf16[256,256]{1,0:T(8,128)(2,1)S(1)} %collective-permute-done.25.refs_6_), channel_id=1, source_target_pairs={{0,2},{2,4},{4,6},{6,7},{7,5},{5,3},{3,1},{1,0},{8,10},{10,12},{12... | collective-permute-start | bytes 393224 | tf_op jit(solution)/shard_map/ppermute | solution.py:131
  94.9 3.5 %collective-permute-done.31.refs_12_ = bf16[256,256]{1,0:T(8,128)(2,1)S(1)} collective-permute-done((bf16[256,256]{1,0:T(8,128)(2,1)S(1)}, bf16[256,256]{1,0:T(8,128)(2,1)S(1)}, u32[]{:S(2)}, u32[]{:S(2)}) %collective-permute-start.31) | collective-permute-done | bytes 131104 | tf_op jit(solution)/shard_map/ppermute | solution.py:131
  98.4 1.0 collective-permute-start.30
  99.4 1.1 collective-permute-start.34
  100.5 2.0 %collective-permute-start.33 = (bf16[256,256]{1,0:T(8,128)(2,1)S(1)}, bf16[256,256]{1,0:T(8,128)(2,1)S(1)}, u32[]{:S(2)}, u32[]{:S(2)}) collective-permute-start(bf16[256,256]{1,0:T(8,128)(2,1)S(1)} %collective-permute-done.29.refs_10_), channel_id=1, source_target_pairs={{0,2},{2,4},{4,6},{6,7},{7,5},{5,3},{3,1},{1,0},{8,10},{10,12},{12... | collective-permute-start | bytes 393224 | tf_op jit(solution)/shard_map/ppermute | solution.py:131
  102.5 0.9 collective-permute-done.35.refs_16_
  103.4 3.1 %collective-permute-done.33.refs_14_ = bf16[256,256]{1,0:T(8,128)(2,1)S(1)} collective-permute-done((bf16[256,256]{1,0:T(8,128)(2,1)S(1)}, bf16[256,256]{1,0:T(8,128)(2,1)S(1)}, u32[]{:S(2)}, u32[]{:S(2)}) %collective-permute-start.33) | collective-permute-done | bytes 131104 | tf_op jit(solution)/shard_map/ppermute | solution.py:131
  106.5 2.3 %shard_map.85 = (bf16[4,128,256]{2,1,0:T(8,128)(2,1)S(1)}, bf16[5120,256]{1,0:T(8,128)(2,1)S(1)}) custom-call(s32[1]{0:T(128)} %bitcast.row_ref, s32[4]{0:T(128)S(1)} %bitcast.29, s32[8,16]{1,0:T(8,128)S(1)} %fusion.5.ids_ref, bf16[16,8,128,128]{3,2,1,0:T(8,128)(2,1)S(1)} %get-tuple-element.29.observed, ...), custom_call_target="tpu_custom_call" | custom-call | flops 536870912 | bytes 8388608 | tf_op jit(solution)/shard_map/pallas_call | solution.py:444
  108.9 0.6 shard_map.86.refs_3_
  109.5 3.4 %collective-permute-start.36 = (bf16[4,128,256]{2,1,0:T(8,128)(2,1)S(1)}, bf16[4,128,256]{2,1,0:T(8,128)(2,1)S(1)}, u32[]{:S(2)}, u32[]{:S(2)}) collective-permute-start(bf16[4,128,256]{2,1,0:T(8,128)(2,1)S(1)} %shard_map.86.refs_3_), channel_id=1, source_target_pairs={{0,16},{8,24},{16,0},{24,8},{1,17},{9,25},{17,1},{25,9},{2,18},{10... | collective-permute-start | bytes 786440 | tf_op jit(solution)/shard_map/ppermute | solution.py:570
  112.9 4.6 %shard_map.87 = (bf16[4,128,256]{2,1,0:T(8,128)(2,1)S(1)}, bf16[4,128,256]{2,1,0:T(8,128)(2,1)S(1)}) custom-call(s32[1]{0:T(128)} %bitcast.row_ref, s32[4]{0:T(128)S(1)} %bitcast.31, s32[8,16]{1,0:T(8,128)S(1)} %fusion.5.ids_ref, bf16[16,8,128,128]{3,2,1,0:T(8,128)(2,1)S(1)} %get-tuple-element.29.observed, ...), custom_call_target="tpu_custom_call" | custom-call | flops 1073741824 | bytes 16777216 | tf_op jit(solution)/shard_map/pallas_call | solution.py:444
  117.6 1.1 multiply_subtract_fusion
  118.6 0.4 collective-permute-done.38.refs_4_
  119.3 2.3 %shard_map.88 = (f32[16,128,256]{2,1,0:T(8,128)S(1)}, f32[16,128,256]{2,1,0:T(8,128)}) custom-call(s32[1]{0:T(128)} %bitcast.row_ref, s32[16]{0:T(128)S(1)} %copy-done.4, s32[16]{0:T(128)S(1)} %collective-permute-done.3.refs_1_, f32[16,128,256]{2,1,0:T(8,128)S(1)} %bitcast.27, bf16[4,128,256]{2,1,0:T(8,128)(2,1)S(1)} %get-tuple-element.49.refs_3_, ...), custom_call_target="tpu_custom_call" | custom-call | tf_op jit(solution)/shard_map/pallas_call | solution.py:484
  121.6 1.4 %shard_map.89 = (f32[16,128,256]{2,1,0:T(8,128)S(1)}, f32[16,128,256]{2,1,0:T(8,128)}) custom-call(s32[1]{0:T(128)} %bitcast.row_ref, s32[16]{0:T(128)S(1)} %collective-permute-done.4.refs_3_.ids, bf16[4,128,256]{2,1,0:T(8,128)(2,1)S(1)} %collective-permute-done.37.term, ...), custom_call_target="tpu_custom_call", output_to_operand_aliasing={{0}: (3, {}), {1}: (4, {})} | custom-call | tf_op jit(solution)/shard_map/pallas_call | solution.py:501
  123.1 1.4 %shard_map.90 = (f32[16,128,256]{2,1,0:T(8,128)S(1)}, f32[16,128,256]{2,1,0:T(8,128)}) custom-call(s32[1]{0:T(128)} %bitcast.row_ref, s32[16]{0:T(128)S(1)} %collective-permute-done.refs_2_.ids, bf16[4,128,256]{2,1,0:T(8,128)(2,1)S(1)} %collective-permute-done.36.term, ...), custom_call_target="tpu_custom_call", output_to_operand_aliasing={{0}: (3, {}), {1}: (4, {})} | custom-call | tf_op jit(solution)/shard_map/pallas_call | solution.py:501
  (62 shorter events, 1.8 us)
Async XLA Ops:
  0.6 10.0 %collective-permute-start.4 = (s32[16]{0:T(128)}, s32[16]{0:T(128)S(1)}, u32[]{:S(2)}, u32[]{:S(2)}) collective-permute-start(s32[16]{0:T(128)} %refs_0_.3), channel_id=1, source_target_pairs={{0,24},{8,16},{16,8},{24,0},{1,25},{9,17},{17,9},{25,1},{2,26},{10... | collective-permute-start | bytes 200 | tf_op jit(solution)/shard_map/ppermute | solution.py:523
  3.1 7.6 %collective-permute-start.3 = (s32[16]{0:T(128)}, s32[16]{0:T(128)S(1)}, u32[]{:S(2)}, u32[]{:S(2)}) collective-permute-start(s32[16]{0:T(128)} %refs_0_.3), channel_id=1, source_target_pairs={{0,8},{8,0},{16,24},{24,16},{1,9},{9,1},{17,25},{25,17},{2,10},{10... | collective-permute-start | bytes 200 | tf_op jit(solution)/shard_map/ppermute | solution.py:523
  3.7 6.9 %collective-permute-start = (s32[16]{0:T(128)}, s32[16]{0:T(128)S(1)}, u32[]{:S(2)}, u32[]{:S(2)}) collective-permute-start(s32[16]{0:T(128)} %refs_0_.3), channel_id=1, source_target_pairs={{0,16},{8,24},{16,0},{24,8},{1,17},{9,25},{17,1},{25,9},{2,18},{10... | collective-permute-start | bytes 200 | tf_op jit(solution)/shard_map/ppermute | solution.py:523
  4.9 10.5 %collective-permute-start.2 = (bf16[640,256]{1,0:T(8,128)(2,1)S(1)}, bf16[640,256]{1,0:T(8,128)(2,1)S(1)}, u32[]{:S(2)}, u32[]{:S(2)}) collective-permute-start(bf16[640,256]{1,0:T(8,128)(2,1)S(1)} %convert_element_type.69.refs_4_), channel_id=1, source_target_pairs={{0,2},{2,4},{4,6},{6,7},{7,5},{5,3},{3,1},{1,0},{8,10},{10,12},{12... | collective-permute-start | bytes 983048 | tf_op jit(solution)/shard_map/ppermute | solution.py:110
  7.0 10.5 %collective-permute-start.1 = (bf16[640,256]{1,0:T(8,128)(2,1)S(1)}, bf16[640,256]{1,0:T(8,128)(2,1)S(1)}, u32[]{:S(2)}, u32[]{:S(2)}) collective-permute-start(bf16[640,256]{1,0:T(8,128)(2,1)S(1)} %convert_element_type.69.refs_4_), channel_id=1, source_target_pairs={{2,0},{4,2},{6,4},{7,6},{5,7},{3,5},{1,3},{0,1},{10,8},{12,10},{14... | collective-permute-start | bytes 983048 | tf_op jit(solution)/shard_map/ppermute | solution.py:110
  7.8 0.7 copy-start.1
  10.7 0.7 copy-start.3
  13.7 7.7 %collective-permute-start.5 = (bf16[4,128,256]{2,1,0:T(8,128)(2,1)S(1)}, bf16[4,128,256]{2,1,0:T(8,128)(2,1)S(1)}, u32[]{:S(2)}, u32[]{:S(2)}) collective-permute-start(bf16[4,128,256]{2,1,0:T(8,128)(2,1)S(1)} %get-tuple-element.31), channel_id=1, source_target_pairs={{0,16},{8,24},{16,0},{24,8},{1,17},{9,25},{17,1},{25,9},{2,18},{10... | collective-permute-start | bytes 786440 | tf_op jit(solution)/shard_map/ppermute | solution.py:538
  15.4 8.6 %collective-permute-start.9 = (bf16[640,256]{1,0:T(8,128)(2,1)S(1)}, bf16[640,256]{1,0:T(8,128)(2,1)S(1)}, u32[]{:S(2)}, u32[]{:S(2)}) collective-permute-start(bf16[640,256]{1,0:T(8,128)(2,1)S(1)} %collective-permute-done.2.refs_1_.refs_6_), channel_id=1, source_target_pairs={{0,2},{2,4},{4,6},{6,7},{7,5},{5,3},{3,1},{1,0},{8,10},{10,12},{12... | collective-permute-start | bytes 983048 | tf_op jit(solution)/shard_map/ppermute | solution.py:110
  17.5 8.4 %collective-permute-start.7 = (bf16[640,256]{1,0:T(8,128)(2,1)S(1)}, bf16[640,256]{1,0:T(8,128)(2,1)S(1)}, u32[]{:S(2)}, u32[]{:S(2)}) collective-permute-start(bf16[640,256]{1,0:T(8,128)(2,1)S(1)} %collective-permute-done.1.refs_0_.refs_5_), channel_id=1, source_target_pairs={{2,0},{4,2},{6,4},{7,6},{5,7},{3,5},{1,3},{0,1},{10,8},{12,10},{14... | collective-permute-start | bytes 983048 | tf_op jit(solution)/shard_map/ppermute | solution.py:110
  24.0 8.5 %collective-permute-start.10 = (bf16[640,256]{1,0:T(8,128)(2,1)S(1)}, bf16[640,256]{1,0:T(8,128)(2,1)S(1)}, u32[]{:S(2)}, u32[]{:S(2)}) collective-permute-start(bf16[640,256]{1,0:T(8,128)(2,1)S(1)} %collective-permute-done.9.refs_5_), channel_id=1, source_target_pairs={{0,2},{2,4},{4,6},{6,7},{7,5},{5,3},{3,1},{1,0},{8,10},{10,12},{12... | collective-permute-start | bytes 983048 | tf_op jit(solution)/shard_map/ppermute | solution.py:110
  25.9 7.9 %collective-permute-start.8 = (bf16[640,256]{1,0:T(8,128)(2,1)S(1)}, bf16[640,256]{1,0:T(8,128)(2,1)S(1)}, u32[]{:S(2)}, u32[]{:S(2)}) collective-permute-start(bf16[640,256]{1,0:T(8,128)(2,1)S(1)} %collective-permute-done.7.refs_4_), channel_id=1, source_target_pairs={{2,0},{4,2},{6,4},{7,6},{5,7},{3,5},{1,3},{0,1},{10,8},{12,10},{14... | collective-permute-start | bytes 983048 | tf_op jit(solution)/shard_map/ppermute | solution.py:110
  26.1 6.4 %collective-permute-start.6 = (bf16[4,128,256]{2,1,0:T(8,128)(2,1)S(1)}, bf16[4,128,256]{2,1,0:T(8,128)(2,1)S(1)}, u32[]{:S(2)}, u32[]{:S(2)}) collective-permute-start(bf16[4,128,256]{2,1,0:T(8,128)(2,1)S(1)} %select_select_fusion), channel_id=1, source_target_pairs={{0,16},{8,24},{16,0},{24,8},{1,17},{9,25},{17,1},{25,9},{2,18},{10... | collective-permute-start | bytes 786440 | tf_op jit(solution)/shard_map/ppermute | solution.py:540
  33.8 2.2 %collective-permute-start.11 = (bf16[8,128,256]{2,1,0:T(8,128)(2,1)S(1)}, bf16[8,128,256]{2,1,0:T(8,128)(2,1)S(1)}, u32[]{:S(2)}, u32[]{:S(2)}) collective-permute-start(bf16[8,128,256]{2,1,0:T(8,128)(2,1)S(1)} %shard_map.80), channel_id=1, source_target_pairs={{0,8},{8,0},{16,24},{24,16},{1,9},{9,1},{17,25},{25,17},{2,10},{10... | collective-permute-start | bytes 1572872 | tf_op jit(solution)/shard_map/ppermute | solution.py:542
  33.9 7.3 %collective-permute-start.12 = (bf16[384,256]{1,0:T(8,128)(2,1)S(1)}, bf16[384,256]{1,0:T(8,128)(2,1)S(1)}, u32[]{:S(2)}, u32[]{:S(2)}) collective-permute-start(bf16[384,256]{1,0:T(8,128)(2,1)S(1)} %slice.48), channel_id=1, source_target_pairs={{0,2},{2,4},{4,6},{6,7},{7,5},{5,3},{3,1},{1,0},{8,10},{10,12},{12... | collective-permute-start | bytes 589832 | tf_op jit(solution)/shard_map/ppermute | solution.py:110
  35.2 5.7 %collective-permute-start.13 = (bf16[256,256]{1,0:T(8,128)(2,1)S(1)}, bf16[256,256]{1,0:T(8,128)(2,1)S(1)}, u32[]{:S(2)}, u32[]{:S(2)}) collective-permute-start(bf16[256,256]{1,0:T(8,128)(2,1)S(1)} %slice.49), channel_id=1, source_target_pairs={{2,0},{4,2},{6,4},{7,6},{5,7},{3,5},{1,3},{0,1},{10,8},{12,10},{14... | collective-permute-start | bytes 393224 | tf_op jit(solution)/shard_map/ppermute | solution.py:110
  42.7 5.9 %collective-permute-start.18 = (bf16[256,256]{1,0:T(8,128)(2,1)S(1)}, bf16[256,256]{1,0:T(8,128)(2,1)S(1)}, u32[]{:S(2)}, u32[]{:S(2)}) collective-permute-start(bf16[256,256]{1,0:T(8,128)(2,1)S(1)} %get-tuple-element.44), channel_id=1, source_target_pairs={{2,0},{4,2},{6,4},{7,6},{5,7},{3,5},{1,3},{0,1},{10,8},{12,10},{14... | collective-permute-start | bytes 393224 | tf_op jit(solution)/shard_map/ppermute | solution.py:143
  43.9 6.2 %collective-permute-start.14 = (bf16[384,256]{1,0:T(8,128)(2,1)S(1)}, bf16[384,256]{1,0:T(8,128)(2,1)S(1)}, u32[]{:S(2)}, u32[]{:S(2)}) collective-permute-start(bf16[384,256]{1,0:T(8,128)(2,1)S(1)} %get-tuple-element.39.refs_6_), channel_id=1, source_target_pairs={{0,2},{2,4},{4,6},{6,7},{7,5},{5,3},{3,1},{1,0},{8,10},{10,12},{12... | collective-permute-start | bytes 589832 | tf_op jit(solution)/shard_map/ppermute | solution.py:143
  48.7 9.3 %collective-permute-start.19 = (bf16[640,256]{1,0:T(8,128)(2,1)S(1)}, bf16[640,256]{1,0:T(8,128)(2,1)S(1)}, u32[]{:S(2)}, u32[]{:S(2)}) collective-permute-start(bf16[640,256]{1,0:T(8,128)(2,1)S(1)} %pad_maximum_fusion.1), channel_id=1, source_target_pairs={{2,0},{4,2},{6,4},{7,6},{5,7},{3,5},{1,3},{0,1},{10,8},{12,10},{14... | collective-permute-start | bytes 983048 | tf_op jit(solution)/shard_map/ppermute | solution.py:153
  50.2 8.3 %collective-permute-start.15 = (bf16[640,256]{1,0:T(8,128)(2,1)S(1)}, bf16[640,256]{1,0:T(8,128)(2,1)S(1)}, u32[]{:S(2)}, u32[]{:S(2)}) collective-permute-start(bf16[640,256]{1,0:T(8,128)(2,1)S(1)} %pad_maximum_fusion), channel_id=1, source_target_pairs={{0,2},{2,4},{4,6},{6,7},{7,5},{5,3},{3,1},{1,0},{8,10},{10,12},{12... | collective-permute-start | bytes 983048 | tf_op jit(solution)/shard_map/ppermute | solution.py:153
  58.1 8.4 %collective-permute-start.20 = (bf16[640,256]{1,0:T(8,128)(2,1)S(1)}, bf16[640,256]{1,0:T(8,128)(2,1)S(1)}, u32[]{:S(2)}, u32[]{:S(2)}) collective-permute-start(bf16[640,256]{1,0:T(8,128)(2,1)S(1)} %add_convert_fusion.1), channel_id=1, source_target_pairs={{2,0},{4,2},{6,4},{7,6},{5,7},{3,5},{1,3},{0,1},{10,8},{12,10},{14... | collective-permute-start | bytes 983048 | tf_op jit(solution)/shard_map/ppermute | solution.py:153
  58.6 8.4 %collective-permute-start.16 = (bf16[640,256]{1,0:T(8,128)(2,1)S(1)}, bf16[640,256]{1,0:T(8,128)(2,1)S(1)}, u32[]{:S(2)}, u32[]{:S(2)}) collective-permute-start(bf16[640,256]{1,0:T(8,128)(2,1)S(1)} %add_convert_fusion.3), channel_id=1, source_target_pairs={{0,2},{2,4},{4,6},{6,7},{7,5},{5,3},{3,1},{1,0},{8,10},{10,12},{12... | collective-permute-start | bytes 983048 | tf_op jit(solution)/shard_map/ppermute | solution.py:153
  65.4 9.3 %copy-start.5 = (f32[640,256]{1,0:T(8,128)S(1)}, f32[640,256]{1,0:T(8,128)}, u32[]{:S(2)}) copy-start(f32[640,256]{1,0:T(8,128)} %param.11) | copy-start | bytes 1966084
  66.6 40.0 %copy-start.2 = (s32[1,1,4]{2,1,0:T(1,128)S(1)}, s32[1,1,4]{2,1,0:T(1,128)}, u32[]{:S(2)}) copy-start(s32[1,1,4]{2,1,0:T(1,128)} %param.9) | copy-start | bytes 52
  66.7 7.5 %collective-permute-start.21 = (bf16[640,256]{1,0:T(8,128)(2,1)S(1)}, bf16[640,256]{1,0:T(8,128)(2,1)S(1)}, u32[]{:S(2)}, u32[]{:S(2)}) collective-permute-start(bf16[640,256]{1,0:T(8,128)(2,1)S(1)} %add_convert_fusion), channel_id=1, source_target_pairs={{2,0},{4,2},{6,4},{7,6},{5,7},{3,5},{1,3},{0,1},{10,8},{12,10},{14... | collective-permute-start | bytes 983048 | tf_op jit(solution)/shard_map/ppermute | solution.py:153
  67.1 7.6 %collective-permute-start.17 = (bf16[640,256]{1,0:T(8,128)(2,1)S(1)}, bf16[640,256]{1,0:T(8,128)(2,1)S(1)}, u32[]{:S(2)}, u32[]{:S(2)}) collective-permute-start(bf16[640,256]{1,0:T(8,128)(2,1)S(1)} %add_convert_fusion.2), channel_id=1, source_target_pairs={{0,2},{2,4},{4,6},{6,7},{7,5},{5,3},{3,1},{1,0},{8,10},{10,12},{12... | collective-permute-start | bytes 983048 | tf_op jit(solution)/shard_map/ppermute | solution.py:153
  74.9 7.6 %collective-permute-start.24 = (bf16[384,256]{1,0:T(8,128)(2,1)S(1)}, bf16[384,256]{1,0:T(8,128)(2,1)S(1)}, u32[]{:S(2)}, u32[]{:S(2)}) collective-permute-start(bf16[384,256]{1,0:T(8,128)(2,1)S(1)} %slice.50.refs_1_), channel_id=1, source_target_pairs={{0,2},{2,4},{4,6},{6,7},{7,5},{5,3},{3,1},{1,0},{8,10},{10,12},{12... | collective-permute-start | bytes 589832 | tf_op jit(solution)/shard_map/ppermute | solution.py:131
  77.2 7.5 %collective-permute-start.23 = (bf16[256,256]{1,0:T(8,128)(2,1)S(1)}, bf16[256,256]{1,0:T(8,128)(2,1)S(1)}, u32[]{:S(2)}, u32[]{:S(2)}) collective-permute-start(bf16[256,256]{1,0:T(8,128)(2,1)S(1)} %slice.51.refs_2_), channel_id=1, source_target_pairs={{2,0},{4,2},{6,4},{7,6},{5,7},{3,5},{1,3},{0,1},{10,8},{12,10},{14... | collective-permute-start | bytes 393224 | tf_op jit(solution)/shard_map/ppermute | solution.py:131
  77.3 10.6 %collective-permute-start.22 = (bf16[384,256]{1,0:T(8,128)(2,1)S(1)}, bf16[384,256]{1,0:T(8,128)(2,1)S(1)}, u32[]{:S(2)}, u32[]{:S(2)}) collective-permute-start(bf16[384,256]{1,0:T(8,128)(2,1)S(1)} %slice.50.refs_1_), channel_id=1, source_target_pairs={{2,0},{4,2},{6,4},{7,6},{5,7},{3,5},{1,3},{0,1},{10,8},{12,10},{14... | collective-permute-start | bytes 589832 | tf_op jit(solution)/shard_map/ppermute | solution.py:131
  82.5 7.7 %collective-permute-start.28 = (bf16[384,256]{1,0:T(8,128)(2,1)S(1)}, bf16[384,256]{1,0:T(8,128)(2,1)S(1)}, u32[]{:S(2)}, u32[]{:S(2)}) collective-permute-start(bf16[384,256]{1,0:T(8,128)(2,1)S(1)} %collective-permute-done.24.refs_5_), channel_id=1, source_target_pairs={{0,2},{2,4},{4,6},{6,7},{7,5},{5,3},{3,1},{1,0},{8,10},{10,12},{12... | collective-permute-start | bytes 589832 | tf_op jit(solution)/shard_map/ppermute | solution.py:131
  84.7 7.7 %collective-permute-start.27 = (bf16[256,256]{1,0:T(8,128)(2,1)S(1)}, bf16[256,256]{1,0:T(8,128)(2,1)S(1)}, u32[]{:S(2)}, u32[]{:S(2)}) collective-permute-start(bf16[256,256]{1,0:T(8,128)(2,1)S(1)} %collective-permute-done.23.refs_4_), channel_id=1, source_target_pairs={{2,0},{4,2},{6,4},{7,6},{5,7},{3,5},{1,3},{0,1},{10,8},{12,10},{14... | collective-permute-start | bytes 393224 | tf_op jit(solution)/shard_map/ppermute | solution.py:131
  84.8 7.8 %collective-permute-start.25 = (bf16[256,256]{1,0:T(8,128)(2,1)S(1)}, bf16[256,256]{1,0:T(8,128)(2,1)S(1)}, u32[]{:S(2)}, u32[]{:S(2)}) collective-permute-start(bf16[256,256]{1,0:T(8,128)(2,1)S(1)} %slice.51.refs_2_), channel_id=1, source_target_pairs={{0,2},{2,4},{4,6},{6,7},{7,5},{5,3},{3,1},{1,0},{8,10},{10,12},{12... | collective-permute-start | bytes 393224 | tf_op jit(solution)/shard_map/ppermute | solution.py:131
  87.8 10.6 %collective-permute-start.26 = (bf16[384,256]{1,0:T(8,128)(2,1)S(1)}, bf16[384,256]{1,0:T(8,128)(2,1)S(1)}, u32[]{:S(2)}, u32[]{:S(2)}) collective-permute-start(bf16[384,256]{1,0:T(8,128)(2,1)S(1)} %collective-permute-done.22.refs_3_), channel_id=1, source_target_pairs={{2,0},{4,2},{6,4},{7,6},{5,7},{3,5},{1,3},{0,1},{10,8},{12,10},{14... | collective-permute-start | bytes 589832 | tf_op jit(solution)/shard_map/ppermute | solution.py:131
  90.2 9.2 %collective-permute-start.32 = (bf16[384,256]{1,0:T(8,128)(2,1)S(1)}, bf16[384,256]{1,0:T(8,128)(2,1)S(1)}, u32[]{:S(2)}, u32[]{:S(2)}) collective-permute-start(bf16[384,256]{1,0:T(8,128)(2,1)S(1)} %collective-permute-done.28.refs_9_), channel_id=1, source_target_pairs={{0,2},{2,4},{4,6},{6,7},{7,5},{5,3},{3,1},{1,0},{8,10},{10,12},{12... | collective-permute-start | bytes 589832 | tf_op jit(solution)/shard_map/ppermute | solution.py:131
  92.5 6.0 %collective-permute-start.31 = (bf16[256,256]{1,0:T(8,128)(2,1)S(1)}, bf16[256,256]{1,0:T(8,128)(2,1)S(1)}, u32[]{:S(2)}, u32[]{:S(2)}) collective-permute-start(bf16[256,256]{1,0:T(8,128)(2,1)S(1)} %collective-permute-done.27.refs_8_), channel_id=1, source_target_pairs={{2,0},{4,2},{6,4},{7,6},{5,7},{3,5},{1,3},{0,1},{10,8},{12,10},{14... | collective-permute-start | bytes 393224 | tf_op jit(solution)/shard_map/ppermute | solution.py:131
  92.5 8.0 %collective-permute-start.29 = (bf16[256,256]{1,0:T(8,128)(2,1)S(1)}, bf16[256,256]{1,0:T(8,128)(2,1)S(1)}, u32[]{:S(2)}, u32[]{:S(2)}) collective-permute-start(bf16[256,256]{1,0:T(8,128)(2,1)S(1)} %collective-permute-done.25.refs_6_), channel_id=1, source_target_pairs={{0,2},{2,4},{4,6},{6,7},{7,5},{5,3},{3,1},{1,0},{8,10},{10,12},{12... | collective-permute-start | bytes 393224 | tf_op jit(solution)/shard_map/ppermute | solution.py:131
  98.4 5.0 %collective-permute-start.35 = (bf16[256,256]{1,0:T(8,128)(2,1)S(1)}, bf16[256,256]{1,0:T(8,128)(2,1)S(1)}, u32[]{:S(2)}, u32[]{:S(2)}) collective-permute-start(bf16[256,256]{1,0:T(8,128)(2,1)S(1)} %collective-permute-done.31.refs_12_), channel_id=1, source_target_pairs={{2,0},{4,2},{6,4},{7,6},{5,7},{3,5},{1,3},{0,1},{10,8},{12,10},{14... | collective-permute-start | bytes 393224 | tf_op jit(solution)/shard_map/ppermute | solution.py:131
  98.4 8.1 %collective-permute-start.30 = (bf16[384,256]{1,0:T(8,128)(2,1)S(1)}, bf16[384,256]{1,0:T(8,128)(2,1)S(1)}, u32[]{:S(2)}, u32[]{:S(2)}) collective-permute-start(bf16[384,256]{1,0:T(8,128)(2,1)S(1)} %collective-permute-done.26.refs_7_), channel_id=1, source_target_pairs={{2,0},{4,2},{6,4},{7,6},{5,7},{3,5},{1,3},{0,1},{10,8},{12,10},{14... | collective-permute-start | bytes 589832 | tf_op jit(solution)/shard_map/ppermute | solution.py:131
  99.4 7.1 %collective-permute-start.34 = (bf16[384,256]{1,0:T(8,128)(2,1)S(1)}, bf16[384,256]{1,0:T(8,128)(2,1)S(1)}, u32[]{:S(2)}, u32[]{:S(2)}) collective-permute-start(bf16[384,256]{1,0:T(8,128)(2,1)S(1)} %collective-permute-done.32.refs_13_), channel_id=1, source_target_pairs={{0,2},{2,4},{4,6},{6,7},{7,5},{5,3},{3,1},{1,0},{8,10},{10,12},{12... | collective-permute-start | bytes 589832 | tf_op jit(solution)/shard_map/ppermute | solution.py:131
  100.5 6.0 %collective-permute-start.33 = (bf16[256,256]{1,0:T(8,128)(2,1)S(1)}, bf16[256,256]{1,0:T(8,128)(2,1)S(1)}, u32[]{:S(2)}, u32[]{:S(2)}) collective-permute-start(bf16[256,256]{1,0:T(8,128)(2,1)S(1)} %collective-permute-done.29.refs_10_), channel_id=1, source_target_pairs={{0,2},{2,4},{4,6},{6,7},{7,5},{5,3},{3,1},{1,0},{8,10},{10,12},{12... | collective-permute-start | bytes 393224 | tf_op jit(solution)/shard_map/ppermute | solution.py:131
  108.8 12.8 %collective-permute-start.37 = (bf16[4,128,256]{2,1,0:T(8,128)(2,1)S(1)}, bf16[4,128,256]{2,1,0:T(8,128)(2,1)S(1)}, u32[]{:S(2)}, u32[]{:S(2)}) collective-permute-start(bf16[4,128,256]{2,1,0:T(8,128)(2,1)S(1)} %get-tuple-element.48.refs_2_), channel_id=1, source_target_pairs={{0,24},{8,16},{16,8},{24,0},{1,25},{9,17},{17,9},{25,1},{2,26},{10... | collective-permute-start | bytes 786440 | tf_op jit(solution)/shard_map/ppermute | solution.py:570
  109.5 13.6 %collective-permute-start.36 = (bf16[4,128,256]{2,1,0:T(8,128)(2,1)S(1)}, bf16[4,128,256]{2,1,0:T(8,128)(2,1)S(1)}, u32[]{:S(2)}, u32[]{:S(2)}) collective-permute-start(bf16[4,128,256]{2,1,0:T(8,128)(2,1)S(1)} %shard_map.86.refs_3_), channel_id=1, source_target_pairs={{0,16},{8,24},{16,0},{24,8},{1,17},{9,25},{17,1},{25,9},{2,18},{10... | collective-permute-start | bytes 786440 | tf_op jit(solution)/shard_map/ppermute | solution.py:570
  117.5 1.8 %copy-start = (f32[2048,256]{1,0:T(8,128)S(1)}, f32[2048,256]{1,0:T(8,128)}, u32[]{:S(2)}) copy-start(f32[2048,256]{1,0:T(8,128)} %param.10) | copy-start | bytes 6291460
  117.5 1.8 %copy-start.4 = (s32[16]{0:T(128)S(1)}, s32[16]{0:T(128)}, u32[]{:S(2)}) copy-start(s32[16]{0:T(128)} %refs_0_.3) | copy-start | bytes 196
  117.5 1.6 %collective-permute-start.38 = (bf16[4,128,256]{2,1,0:T(8,128)(2,1)S(1)}, bf16[4,128,256]{2,1,0:T(8,128)(2,1)S(1)}, u32[]{:S(2)}, u32[]{:S(2)}) collective-permute-start(bf16[4,128,256]{2,1,0:T(8,128)(2,1)S(1)} %get-tuple-element.50), channel_id=1, source_target_pairs={{0,8},{8,0},{16,24},{24,16},{1,9},{9,1},{17,25},{25,17},{2,10},{10... | collective-permute-start | bytes 786440 | tf_op jit(solution)/shard_map/ppermute | solution.py:570
